TPU v7x, 256 devices: a whole 4x4x8 slice. The times are simulated.
256 devices in a mesh: pack: 32 (over x, y, core), tp: 8 (over z).
Axes of the slice: x: 4, y: 4, z: 8, core: 2. Of those that a mesh axis runs over, the one named last changes fastest.
Arguments:
- queries: bfloat16 [16384, 2048], P('pack', 'tp'), may hold values from -11.5 to 11.5
- keys_values: bfloat16 [16384, 8, 256], P('pack', 'tp'), may hold values from -11.5 to 11.5
- ssm_values: bfloat16 [16384, 4096], P('pack', 'tp'), may hold values from -6 to 6
- ssm_gates: bfloat16 [16384, 4096], P('pack', 'tp'), may hold values from -6 to 6
- ssm_maps: bfloat16 [16384, 512], P('pack'), may hold values from -0.375 to 0.375
- step_size: float32 [16384, 64], P('pack', 'tp'), may hold values from 0.45 to 14000
- decay_log: float32 [64], P('tp'), may hold values from -10 to -3.5
- skip_gain: float32 [64], P('tp'), may hold values from 0.5 to 1.5
- attn_out_weight: bfloat16 [2048, 5120], P('tp'), may hold values from -0.078125 to 0.078125
- ssd_out_weight: bfloat16 [4096, 5120], P('tp'), may hold values from -0.078125 to 0.078125
- lengths: int32 [4], replicated, may hold values from 1 to 8704, 16384 in all
Outputs:
- mixed: bfloat16 [16384, 5120], P(('pack', 'tp'))
Inputs may be any that keep to these rules, and one draw needn't show every extreme that they name: The lengths of the 4 requests in packed order; they sum to 16384, and the longest is exactly 8704.
All inputs are finite; a program needn't handle non-finite values.
Results may differ from a plain program's by a relative error of at most 0.023.
Values may be sent and summed in bfloat16 or wider, within the bound.
No kernel may reach another device: no remote copies, remote signals or barrier semaphores. Data moves between devices by JAX's collectives and lax.ppermute only.
A program may use at most 128 MiB of HBM per device.

v0:
```python
import jax
import jax.numpy as jnp
from jax import lax
from jax.sharding import PartitionSpec as P

BLOCK = 256


masked_value = -1e30


def as_sent(value):
    return jax.tree.map(lambda a: a.astype(jnp.bfloat16) if a.dtype == jnp.float32 else a, value)


def shifted(block, axis, distance):
    devices = range(lax.axis_size(axis))
    route = [(i - distance, i) for i in devices if i - distance in devices]
    return lax.ppermute(block, axis, route)


def segment_of(positions, lengths):
    ends = jnp.cumsum(lengths)
    return jnp.sum((positions[:, None] >= ends[None, :]).astype(jnp.int32), axis=1)


def scan_block(recurrent_memory, values, maps, steps, fading_rates, skip, segs, prior_seg):
    block_size = values.shape[0]
    state_width = maps.shape[1] // 2
    write_map = maps[:, :state_width]
    read_map = maps[:, state_width:]
    decay_logarithm = -fading_rates[None, :] * steps
    cumulative = jnp.cumsum(decay_logarithm, axis=0)
    indices = jnp.arange(block_size, dtype=jnp.int32)
    allowed = (segs[:, None] == segs[None, :]) & (indices[None, :] <= indices[:, None])
    products = jnp.dot(read_map, write_map.T, preferred_element_type=jnp.float32)
    decay_gap = jnp.where(
        allowed[None], cumulative.T[:, :, None] - cumulative.T[:, None, :], masked_value
    )
    block_weights = (jnp.exp(decay_gap) * products[None]).astype(jnp.bfloat16)
    within = jnp.einsum("htu,uhp->thp", block_weights, values, preferred_element_type=jnp.float32)
    continuing = segs == prior_seg
    reads = jnp.einsum(
        "ln,hpn->lhp",
        read_map.astype(jnp.float32),
        recurrent_memory,
        precision=lax.Precision.HIGHEST,
    )
    carried_in = jnp.where(continuing[:, None, None], reads * jnp.exp(cumulative)[:, :, None], 0.0)
    last_seg = segs[block_size - 1]
    tail_decay = jnp.where(
        (segs == last_seg)[:, None], jnp.exp(cumulative[block_size - 1][None, :] - cumulative), 0.0
    )
    weighted = (values.astype(jnp.float32) * tail_decay[:, :, None]).astype(jnp.bfloat16)
    new_part = jnp.einsum("lhp,ln->hpn", weighted, write_map, preferred_element_type=jnp.float32)
    keep_old = jnp.where(last_seg == prior_seg, jnp.exp(cumulative[block_size - 1]), 0.0)
    new_state = new_part + keep_old[:, None, None] * recurrent_memory
    ssm_y = within + carried_in + skip[None, :, None] * values.astype(jnp.float32)
    return (new_state, ssm_y)


def combine_carry(earlier, later):
    return (earlier[0] * later[0], later[0][:, None, None] * earlier[1] + later[1])


def local(
    queries,
    keys_values,
    ssm_values,
    ssm_gates,
    ssm_maps,
    step_size,
    decay_log,
    skip_gain,
    attn_out_weight,
    ssd_out_weight,
    lengths,
):
    row_count = queries.shape[0]
    packed_length = lax.axis_size("pack")
    device_rank = lax.axis_index("pack")
    first_row = device_rank * row_count
    positions = first_row + jnp.arange(row_count, dtype=jnp.int32)
    segments = segment_of(positions, lengths)
    key_heads = keys_values.shape[1]
    head_size = keys_values.shape[2] // 2
    group_size = queries.shape[1] // (key_heads * head_size)
    query_heads = queries.reshape(row_count, key_heads, group_size, head_size)
    scaling = head_size ** (-0.5)
    longest = packed_length * row_count // 2 + row_count
    reach = min(packed_length - 1, (longest - 1) // row_count + 1)

    def absorb_rows(running, portion, offset):
        row_max, totals, accumulated = running
        key_pos = offset + jnp.arange(portion.shape[0], dtype=jnp.int32)
        key_seg = segment_of(key_pos, lengths)
        allowed = (
            (key_pos[None, :] >= 0)
            & (key_seg[None, :] == segments[:, None])
            & (key_pos[None, :] <= positions[:, None])
        )
        wide_mask = allowed[:, None, None, :]
        scores = (
            jnp.einsum(
                "rkgd,skd->rkgs",
                query_heads,
                portion[:, :, :head_size],
                preferred_element_type=jnp.float32,
            )
            * scaling
        )
        scores = jnp.where(wide_mask, scores, masked_value)
        new_max = jnp.maximum(row_max, jnp.max(scores, axis=-1))
        raw_weights = jnp.where(wide_mask, jnp.exp(scores - new_max[..., None]), 0.0)
        rescale = jnp.exp(row_max - new_max)
        totals = totals * rescale + jnp.sum(raw_weights, axis=-1)
        accumulated = accumulated * rescale[..., None] + jnp.einsum(
            "rkgs,skd->rkgd",
            raw_weights.astype(jnp.bfloat16),
            portion[:, :, head_size:],
            preferred_element_type=jnp.float32,
        )
        return (new_max, totals, accumulated)

    start_state = (
        jnp.full((row_count, key_heads, group_size), masked_value, jnp.float32),
        jnp.zeros((row_count, key_heads, group_size), jnp.float32),
        jnp.zeros((row_count, key_heads, group_size, head_size), jnp.float32),
    )
    portion = lax.all_gather(keys_values, "pack", axis=0, tiled=True)
    token_count = portion.shape[0]

    def one_step(step_index, inner):
        cut_portion = lax.dynamic_slice_in_dim(portion, step_index * row_count, row_count, 0)
        return absorb_rows(inner, cut_portion, step_index * row_count)

    row_max, totals, accumulated = lax.fori_loop(0, token_count // row_count, one_step, start_state)
    attended = (
        (accumulated / totals[..., None])
        .astype(jnp.bfloat16)
        .reshape(row_count, key_heads * group_size * head_size)
    )
    ssm_heads = step_size.shape[1]
    head_width = ssm_values.shape[1] // ssm_heads
    state_width = ssm_maps.shape[1] // 2
    local_blocks = row_count // BLOCK
    fading_rates = jnp.exp(decay_log)
    seg_blocks = segments.reshape(local_blocks, BLOCK)
    priors = jnp.concatenate([jnp.full((1,), -1, jnp.int32), seg_blocks[:-1, BLOCK - 1]])

    def advance(recurrent_memory, pieces):
        values, maps, steps, segs, prior_seg = pieces
        return scan_block(
            recurrent_memory, values, maps, steps, fading_rates, skip_gain, segs, prior_seg
        )

    inputs_seq = (
        ssm_values.reshape(local_blocks, BLOCK, ssm_heads, head_width),
        ssm_maps.reshape(local_blocks, BLOCK, 2 * state_width),
        step_size.reshape(local_blocks, BLOCK, ssm_heads),
        seg_blocks,
        priors,
    )
    zero_state = jnp.zeros((ssm_heads, head_width, state_width), jnp.float32)
    end_state, ssm_y = lax.scan(advance, zero_state, inputs_seq)
    ssm_y = ssm_y.reshape(row_count, ssm_heads, head_width)
    cumulative = jnp.cumsum(-fading_rates[None, :] * step_size, axis=0)
    before_row = segment_of(jnp.reshape(first_row - 1, (1,)), lengths)[0]
    prior_device = jnp.where(device_rank == 0, -1, before_row)
    through = jnp.where(
        segments[row_count - 1] == prior_device, jnp.exp(cumulative[row_count - 1]), 0.0
    )
    summary = (through, end_state)
    outgoing = summary
    received = summary
    for step_index in range(reach):
        received = shifted((as_sent(outgoing[0]), as_sent(outgoing[1])), "pack", 1)
        outgoing = combine_carry(received, summary)
    incoming = received[1]
    read_map = ssm_maps[:, state_width:].astype(jnp.float32)
    reads = jnp.einsum("ln,hpn->lhp", read_map, incoming, precision=lax.Precision.HIGHEST)
    continuing = segments == prior_device
    ssm_y = ssm_y + jnp.where(
        continuing[:, None, None], reads * jnp.exp(cumulative)[:, :, None], 0.0
    )
    gated = ssm_y * jax.nn.silu(
        ssm_gates.reshape(row_count, ssm_heads, head_width).astype(jnp.float32)
    )
    ssd_out = gated.astype(jnp.bfloat16).reshape(row_count, ssm_heads * head_width)
    return lax.psum_scatter(
        (
            jnp.dot(attended, attn_out_weight, preferred_element_type=jnp.float32)
            + jnp.dot(ssd_out, ssd_out_weight, preferred_element_type=jnp.float32)
        ).astype(jnp.bfloat16),
        "tp",
        scatter_dimension=0,
        tiled=True,
    )


def solution(mesh):
    return jax.shard_map(
        local,
        mesh=mesh,
        in_specs=(
            P("pack", "tp"),
            P("pack", "tp", None),
            P("pack", "tp"),
            P("pack", "tp"),
            P("pack", None),
            P("pack", "tp"),
            P("tp"),
            P("tp"),
            P("tp", None),
            P("tp", None),
            P(),
        ),
        out_specs=P(("pack", "tp"), None),
        check_vma=False,
    )
```

profile of v0, /device:TPU:1, one launch (start us, length us, event | category | flops | bytes accessed | tf_op | source)
XLA Modules:
  0.0 492.9 jit_solution(17382598982491738724)
XLA Ops:
  14.6 41.4 %while.36 = (s32[]{:T(128)}, f32[8,64,256]{2,1,0:T(8,128)S(1)}, f32[2,256,8,64]{1,0,3,2:T(2,128)}, bf16[2,256,8,64]{1,3,2,0:T(8,128)(2,1)}, s32[2,256]{1,0:T(2,1...) while((s32[]{:T(128)}, f32[8,64,256]{2,1,0:T(8,128)S(1)}, ...), condition=%wide.region_11.12_spmd.clone, body=%wide.region_8.11_spmd.clone.sunk | while | flops 574693888 | bytes 9961702 | solution.py:165
  23.7 11.6 %dynamic_update_slice.8 = f32[2,256,8,64]{1,0,3,2:T(2,128)} dynamic-update-slice(f32[2,256,8,64]{1,0,3,2:T(2,128)} %get-tuple-element.666, f32[1,256,8,64]{1,0,3,2:T(1,128)} %copy.55, s32[]{:T(128)S(6)} %copy.60, s32[]{:T(128)} %constant.131.clone.1..sunk.1, s32[]{:T(128)} %constant.131.clone.1..sunk.1, s32[]{:T(128)} %constant.131.clone.1..sunk.1) | dynamic-update-slice | bytes 1048580 | tf_op jit(solution)/shard_map/while/body/jit(dynamic_update_index_in_dim)/dynamic_update_slice | solution.py:165
  44.3 11.6 %dynamic_update_slice.8 = f32[2,256,8,64]{1,0,3,2:T(2,128)} dynamic-update-slice(f32[2,256,8,64]{1,0,3,2:T(2,128)} %get-tuple-element.666, f32[1,256,8,64]{1,0,3,2:T(1,128)} %copy.55, s32[]{:T(128)S(6)} %copy.60, s32[]{:T(128)} %constant.131.clone.1..sunk.1, s32[]{:T(128)} %constant.131.clone.1..sunk.1, s32[]{:T(128)} %constant.131.clone.1..sunk.1) | dynamic-update-slice | bytes 1048580 | tf_op jit(solution)/shard_map/while/body/jit(dynamic_update_index_in_dim)/dynamic_update_slice | solution.py:165
  56.0 4.6 collective-permute-start
  70.2 4.5 collective-permute-start.1
  78.1 4.4 collective-permute-start.2
  85.9 4.4 collective-permute-start.3
  93.8 4.4 collective-permute-start.4
  101.6 4.4 collective-permute-start.5
  109.4 4.4 collective-permute-start.6
  117.2 4.4 collective-permute-start.7
  125.1 4.4 collective-permute-start.8
  132.9 4.4 collective-permute-start.9
  140.7 4.4 collective-permute-start.10
  148.5 4.4 collective-permute-start.11
  156.4 4.5 collective-permute-start.12
  164.3 4.4 collective-permute-start.13
  172.1 4.6 collective-permute-start.14
  180.2 6.5 %collective-permute-start.15 = (bf16[8,64,256]{2,1,0:T(8,128)(2,1)S(1)}, bf16[8,64,256]{2,1,0:T(8,128)(2,1)S(1)}, u32[]{:S(2)}, u32[]{:S(2)}) collective-permute-start(bf16[8,64,256]{2,1,0:T(8,128)(2,1)S(1)} %add_convert_fusion.2), channel_id=1, source_target_pairs={{0,8},{8,16},{16,24},{24,32},{32,40},{40,48},{48,56},{56,64},{64,7... | collective-permute-start | bytes 786440 | tf_op jit(solution)/shard_map/ppermute | solution.py:19
  190.8 6.7 %collective-permute-start.16 = (bf16[8,64,256]{2,1,0:T(8,128)(2,1)}, bf16[8,64,256]{2,1,0:T(8,128)(2,1)}, u32[]{:S(2)}, u32[]{:S(2)}) collective-permute-start(bf16[8,64,256]{2,1,0:T(8,128)(2,1)} %add_convert_fusion.1), channel_id=1, source_target_pairs={{0,8},{8,16},{16,24},{24,32},{32,40},{40,48},{48,56},{56,64},{64,7... | collective-permute-start | bytes 786440 | tf_op jit(solution)/shard_map/ppermute | solution.py:19
  205.6 8.1 %fusion.66 = f32[512,5120]{1,0:T(8,128)} fusion(bf16[512,512]{0,1:T(8,128)(2,1)S(1)} %bitcast.191, bf16[512,5120]{1,0:T(8,128)(2,1)} %param.24), kind=kOutput, calls=%fused_computation.126 | convolution fusion | flops 2684354560 | bytes 16252928 | tf_op jit(solution)/shard_map/dot_general | solution.py:193
  213.7 167.5 %while.35 = (s32[]{:T(128)}, f32[512,1,2]{0,2,1:T(2,128)S(1)}, f32[512,1,2]{0,2,1:T(2,128)S(1)}, f32[512,1,2,128]{0,3,2,1:T(8,128)}, s32[1,4]{1,0:T(1,128)S(1)},...) while((s32[]{:T(128)}, f32[512,1,2]{0,2,1:T(2,128)S(1)}, ...), condition=%wide.region_7.8_spmd.clone, body=%wide.region_3.7_spmd.clone.sunk | while | flops 276706816 | bytes 13190451 | solution.py:137
  382.3 7.9 %add_convert_fusion = bf16[512,5120]{1,0:T(8,128)(2,1)} fusion(f32[512,5120]{1,0:T(8,128)} %fusion.66, bf16[512,256]{0,1:T(8,128)(2,1)S(1)} %bitcast.194, bf16[256,5120]{1,0:T(8,128)(2,1)S(1)} %copy-done), kind=kOutput, calls=%fused_computation.84 | convolution fusion | flops 1347420160 | bytes 18612224 | tf_op jit(solution)/shard_map/dot_general | solution.py:192
  390.2 95.8 %reduce-scatter.2.cloned.1.call-done = bf16[64,5120]{1,0:T(8,128)(2,1)} async-done(((bf16[512,5120]{1,0:T(8,128)(2,1)}), bf16[64,5120]{1,0:T(8,128)(2,1)}) %reduce-scatter.2.cloned.1.call-update) | async-done | bytes 655376 | tf_op jit(solution)/shard_map/reduce_scatter | solution.py:190
  (576 shorter events, 258.5 us)
Async XLA Ops:
  6.5 375.7 %copy-start = (bf16[256,5120]{1,0:T(8,128)(2,1)S(1)}, bf16[256,5120]{1,0:T(8,128)(2,1)}, u32[]{:S(2)}) copy-start(bf16[256,5120]{1,0:T(8,128)(2,1)} %param.23) | copy-start | bytes 7864324
  6.5 8.0 %copy-start.5 = (f32[512,8]{0,1:T(8,128)S(1)}, f32[512,8]{0,1:T(8,128)}, u32[]{:S(2)}) copy-start(f32[512,8]{0,1:T(8,128)} %param.20) | copy-start | bytes 49156
  6.5 8.0 %copy-start.7 = (f32[8]{0:T(128)S(1)}, f32[8]{0:T(128)}, u32[]{:S(2)}) copy-start(f32[8]{0:T(128)} %param.22) | copy-start | bytes 100
  6.5 207.1 %all-gather.2.cloned.1.call-start = ((), (), s32[]{:S(2)}) async-start(), calls=%async_computation.1 | async-start | bytes 8650752 | tf_op jit(solution)/shard_map/all_gather | solution.py:130
  7.3 478.8 %reduce-scatter.2.cloned.1.call-start = ((), (), s32[]{:S(2)}) async-start(), calls=%async_computation.2 | async-start | bytes 5898240 | tf_op jit(solution)/shard_map/reduce_scatter | solution.py:190
  56.0 13.1 %collective-permute-start = (bf16[8,64,256]{2,1,0:T(8,128)(2,1)S(1)}, bf16[8,64,256]{2,1,0:T(8,128)(2,1)}, u32[]{:S(2)}, u32[]{:S(2)}) collective-permute-start(bf16[8,64,256]{2,1,0:T(8,128)(2,1)S(1)} %convert_element_type.168), channel_id=1, source_target_pairs={{0,8},{8,16},{16,24},{24,32},{32,40},{40,48},{48,56},{56,64},{64,7... | collective-permute-start | bytes 786440 | tf_op jit(solution)/shard_map/ppermute | solution.py:19
  70.2 7.8 %collective-permute-start.1 = (bf16[8,64,256]{2,1,0:T(8,128)(2,1)S(1)}, bf16[8,64,256]{2,1,0:T(8,128)(2,1)S(1)}, u32[]{:S(2)}, u32[]{:S(2)}) collective-permute-start(bf16[8,64,256]{2,1,0:T(8,128)(2,1)S(1)} %add_convert_fusion.16), channel_id=1, source_target_pairs={{0,8},{8,16},{16,24},{24,32},{32,40},{40,48},{48,56},{56,64},{64,7... | collective-permute-start | bytes 786440 | tf_op jit(solution)/shard_map/ppermute | solution.py:19
  78.1 7.7 %collective-permute-start.2 = (bf16[8,64,256]{2,1,0:T(8,128)(2,1)S(1)}, bf16[8,64,256]{2,1,0:T(8,128)(2,1)S(1)}, u32[]{:S(2)}, u32[]{:S(2)}) collective-permute-start(bf16[8,64,256]{2,1,0:T(8,128)(2,1)S(1)} %add_convert_fusion.15), channel_id=1, source_target_pairs={{0,8},{8,16},{16,24},{24,32},{32,40},{40,48},{48,56},{56,64},{64,7... | collective-permute-start | bytes 786440 | tf_op jit(solution)/shard_map/ppermute | solution.py:19
  85.9 7.7 %collective-permute-start.3 = (bf16[8,64,256]{2,1,0:T(8,128)(2,1)S(1)}, bf16[8,64,256]{2,1,0:T(8,128)(2,1)S(1)}, u32[]{:S(2)}, u32[]{:S(2)}) collective-permute-start(bf16[8,64,256]{2,1,0:T(8,128)(2,1)S(1)} %add_convert_fusion.14), channel_id=1, source_target_pairs={{0,8},{8,16},{16,24},{24,32},{32,40},{40,48},{48,56},{56,64},{64,7... | collective-permute-start | bytes 786440 | tf_op jit(solution)/shard_map/ppermute | solution.py:19
  93.8 7.7 %collective-permute-start.4 = (bf16[8,64,256]{2,1,0:T(8,128)(2,1)S(1)}, bf16[8,64,256]{2,1,0:T(8,128)(2,1)S(1)}, u32[]{:S(2)}, u32[]{:S(2)}) collective-permute-start(bf16[8,64,256]{2,1,0:T(8,128)(2,1)S(1)} %add_convert_fusion.13), channel_id=1, source_target_pairs={{0,8},{8,16},{16,24},{24,32},{32,40},{40,48},{48,56},{56,64},{64,7... | collective-permute-start | bytes 786440 | tf_op jit(solution)/shard_map/ppermute | solution.py:19
  101.6 7.7 %collective-permute-start.5 = (bf16[8,64,256]{2,1,0:T(8,128)(2,1)S(1)}, bf16[8,64,256]{2,1,0:T(8,128)(2,1)S(1)}, u32[]{:S(2)}, u32[]{:S(2)}) collective-permute-start(bf16[8,64,256]{2,1,0:T(8,128)(2,1)S(1)} %add_convert_fusion.12), channel_id=1, source_target_pairs={{0,8},{8,16},{16,24},{24,32},{32,40},{40,48},{48,56},{56,64},{64,7... | collective-permute-start | bytes 786440 | tf_op jit(solution)/shard_map/ppermute | solution.py:19
  109.4 7.7 %collective-permute-start.6 = (bf16[8,64,256]{2,1,0:T(8,128)(2,1)S(1)}, bf16[8,64,256]{2,1,0:T(8,128)(2,1)S(1)}, u32[]{:S(2)}, u32[]{:S(2)}) collective-permute-start(bf16[8,64,256]{2,1,0:T(8,128)(2,1)S(1)} %add_convert_fusion.11), channel_id=1, source_target_pairs={{0,8},{8,16},{16,24},{24,32},{32,40},{40,48},{48,56},{56,64},{64,7... | collective-permute-start | bytes 786440 | tf_op jit(solution)/shard_map/ppermute | solution.py:19
  117.2 7.7 %collective-permute-start.7 = (bf16[8,64,256]{2,1,0:T(8,128)(2,1)S(1)}, bf16[8,64,256]{2,1,0:T(8,128)(2,1)S(1)}, u32[]{:S(2)}, u32[]{:S(2)}) collective-permute-start(bf16[8,64,256]{2,1,0:T(8,128)(2,1)S(1)} %add_convert_fusion.10), channel_id=1, source_target_pairs={{0,8},{8,16},{16,24},{24,32},{32,40},{40,48},{48,56},{56,64},{64,7... | collective-permute-start | bytes 786440 | tf_op jit(solution)/shard_map/ppermute | solution.py:19
  125.1 7.7 %collective-permute-start.8 = (bf16[8,64,256]{2,1,0:T(8,128)(2,1)S(1)}, bf16[8,64,256]{2,1,0:T(8,128)(2,1)S(1)}, u32[]{:S(2)}, u32[]{:S(2)}) collective-permute-start(bf16[8,64,256]{2,1,0:T(8,128)(2,1)S(1)} %add_convert_fusion.9), channel_id=1, source_target_pairs={{0,8},{8,16},{16,24},{24,32},{32,40},{40,48},{48,56},{56,64},{64,7... | collective-permute-start | bytes 786440 | tf_op jit(solution)/shard_map/ppermute | solution.py:19
  132.9 7.7 %collective-permute-start.9 = (bf16[8,64,256]{2,1,0:T(8,128)(2,1)S(1)}, bf16[8,64,256]{2,1,0:T(8,128)(2,1)S(1)}, u32[]{:S(2)}, u32[]{:S(2)}) collective-permute-start(bf16[8,64,256]{2,1,0:T(8,128)(2,1)S(1)} %add_convert_fusion.8), channel_id=1, source_target_pairs={{0,8},{8,16},{16,24},{24,32},{32,40},{40,48},{48,56},{56,64},{64,7... | collective-permute-start | bytes 786440 | tf_op jit(solution)/shard_map/ppermute | solution.py:19
  140.7 7.7 %collective-permute-start.10 = (bf16[8,64,256]{2,1,0:T(8,128)(2,1)S(1)}, bf16[8,64,256]{2,1,0:T(8,128)(2,1)S(1)}, u32[]{:S(2)}, u32[]{:S(2)}) collective-permute-start(bf16[8,64,256]{2,1,0:T(8,128)(2,1)S(1)} %add_convert_fusion.7), channel_id=1, source_target_pairs={{0,8},{8,16},{16,24},{24,32},{32,40},{40,48},{48,56},{56,64},{64,7... | collective-permute-start | bytes 786440 | tf_op jit(solution)/shard_map/ppermute | solution.py:19
  148.5 7.7 %collective-permute-start.11 = (bf16[8,64,256]{2,1,0:T(8,128)(2,1)S(1)}, bf16[8,64,256]{2,1,0:T(8,128)(2,1)S(1)}, u32[]{:S(2)}, u32[]{:S(2)}) collective-permute-start(bf16[8,64,256]{2,1,0:T(8,128)(2,1)S(1)} %add_convert_fusion.6), channel_id=1, source_target_pairs={{0,8},{8,16},{16,24},{24,32},{32,40},{40,48},{48,56},{56,64},{64,7... | collective-permute-start | bytes 786440 | tf_op jit(solution)/shard_map/ppermute | solution.py:19
  156.3 41.2 %copy-start.8 = (s32[4]{0:T(128)S(1)}, s32[4]{0:T(128)}, u32[]{:S(2)}) copy-start(s32[4]{0:T(128)} %param.25) | copy-start | bytes 52
  156.4 41.4 %copy-start.4 = (bf16[512,256]{1,0:T(8,128)(2,1)S(1)}, bf16[512,256]{1,0:T(8,128)(2,1)}, u32[]{:S(2)}) copy-start(bf16[512,256]{1,0:T(8,128)(2,1)} %param.15) | copy-start | bytes 786436
  156.4 7.8 %collective-permute-start.12 = (bf16[8,64,256]{2,1,0:T(8,128)(2,1)S(1)}, bf16[8,64,256]{2,1,0:T(8,128)(2,1)S(1)}, u32[]{:S(2)}, u32[]{:S(2)}) collective-permute-start(bf16[8,64,256]{2,1,0:T(8,128)(2,1)S(1)} %add_convert_fusion.5), channel_id=1, source_target_pairs={{0,8},{8,16},{16,24},{24,32},{32,40},{40,48},{48,56},{56,64},{64,7... | collective-permute-start | bytes 786440 | tf_op jit(solution)/shard_map/ppermute | solution.py:19
  164.3 7.7 %collective-permute-start.13 = (bf16[8,64,256]{2,1,0:T(8,128)(2,1)S(1)}, bf16[8,64,256]{2,1,0:T(8,128)(2,1)S(1)}, u32[]{:S(2)}, u32[]{:S(2)}) collective-permute-start(bf16[8,64,256]{2,1,0:T(8,128)(2,1)S(1)} %add_convert_fusion.4), channel_id=1, source_target_pairs={{0,8},{8,16},{16,24},{24,32},{32,40},{40,48},{48,56},{56,64},{64,7... | collective-permute-start | bytes 786440 | tf_op jit(solution)/shard_map/ppermute | solution.py:19
  172.1 7.9 %collective-permute-start.14 = (bf16[8,64,256]{2,1,0:T(8,128)(2,1)S(1)}, bf16[8,64,256]{2,1,0:T(8,128)(2,1)S(1)}, u32[]{:S(2)}, u32[]{:S(2)}) collective-permute-start(bf16[8,64,256]{2,1,0:T(8,128)(2,1)S(1)} %add_convert_fusion.3), channel_id=1, source_target_pairs={{0,8},{8,16},{16,24},{24,32},{32,40},{40,48},{48,56},{56,64},{64,7... | collective-permute-start | bytes 786440 | tf_op jit(solution)/shard_map/ppermute | solution.py:19
  180.2 9.8 %collective-permute-start.15 = (bf16[8,64,256]{2,1,0:T(8,128)(2,1)S(1)}, bf16[8,64,256]{2,1,0:T(8,128)(2,1)S(1)}, u32[]{:S(2)}, u32[]{:S(2)}) collective-permute-start(bf16[8,64,256]{2,1,0:T(8,128)(2,1)S(1)} %add_convert_fusion.2), channel_id=1, source_target_pairs={{0,8},{8,16},{16,24},{24,32},{32,40},{40,48},{48,56},{56,64},{64,7... | collective-permute-start | bytes 786440 | tf_op jit(solution)/shard_map/ppermute | solution.py:19
  190.8 12.6 %collective-permute-start.16 = (bf16[8,64,256]{2,1,0:T(8,128)(2,1)}, bf16[8,64,256]{2,1,0:T(8,128)(2,1)}, u32[]{:S(2)}, u32[]{:S(2)}) collective-permute-start(bf16[8,64,256]{2,1,0:T(8,128)(2,1)} %add_convert_fusion.1), channel_id=1, source_target_pairs={{0,8},{8,16},{16,24},{24,32},{32,40},{40,48},{48,56},{56,64},{64,7... | collective-permute-start | bytes 786440 | tf_op jit(solution)/shard_map/ppermute | solution.py:19
  (67 other events, 106.0 us)
Sparse Core Ops, SparseCore 0:
  9.9 62.1 all-gather.1
  390.3 95.6 reduce-scatter.1
where the time goes:
time: 497 us; the launch traced here: 493 us
  waiting for transfers between devices  150 us (30%)
  matrix products  129 us (26%)
  starting transfers between devices  79.8 us (16%)
  local copies, waits for them, and re-layouts  67.5 us (14%)
  other arithmetic  47 us (9%)
  between operations  15 us (3%)
    reduce_scatter x1, waiting for transfers between devices, local(): lax.psum_scatter((jnp.dot(attended, attn_out_weight, preferred_element_ty...  95.8 us
    ppermute x17, starting transfers between devices, shifted(): return lax.ppermute(block, axis, route)  79.7 us
    dot_general x32, matrix products, absorb_rows(): jnp.einsum('rkgs,skd->rkgd', raw_weights.astype(jnp.bfloat16), portion[:,...  59 us
    ppermute x17, waiting for transfers between devices, shifted(): return lax.ppermute(block, axis, route)  53.7 us
    dot_general x32, matrix products, absorb_rows(): jnp.einsum('rkgd,skd->rkgs', query_heads, portion[:, :, :head_size], pref...  48.5 us
    dynamic_update_slice x4, local copies, waits for them, and re-layouts, local(): end_state, ssm_y = lax.scan(advance, zero_state, inputs_seq)  25.9 us
    while x164, local copies, waits for them, and re-layouts  24.4 us
    reduce_sum x32, other arithmetic, absorb_rows(): totals = totals * rescale + jnp.sum(raw_weights, axis=-1)  18.4 us
  transfers between devices with their start and end apart: 19, of which 17 were waited for; matrix products, arithmetic and copies ran while one was open for 14% of the time, Pallas kernels for 0%

commit v1 on v0

v1 whole, which is shorter than its diff:
```python
import functools

import jax
import jax.numpy as jnp
from jax import lax
from jax.experimental import pallas as pl
from jax.experimental.pallas import tpu as pltpu
from jax.sharding import PartitionSpec as P

ROWS = 512
BLOCK = 256
HD = 128
HEADS = 8
HP = 512
SN = 256
DM = 5120
CHUNK = 512
LOW = -1e30
LOG2E = 1.4426950408889634
HIGH = lax.Precision.HIGHEST
STATE_ROWS = SN + 16
VMEM = pl.BlockSpec(memory_space=pltpu.VMEM)
SMEM = pl.BlockSpec(memory_space=pltpu.SMEM)


def iota(shape, dim):
    return lax.broadcasted_iota(jnp.int32, shape, dim)


def ends_of(len_ref):
    e0 = len_ref[0]
    e1 = e0 + len_ref[1]
    return e0, e1, e1 + len_ref[2]


def start_of(pos, ends):
    e0, e1, e2 = ends
    zero = jnp.zeros_like(pos)
    out = jnp.where(pos >= e0, zero + e0, zero)
    out = jnp.where(pos >= e1, zero + e1, out)
    return jnp.where(pos >= e2, zero + e2, out)


def spread():
    return (iota((HEADS, HP), 1) // (HP // HEADS) == iota((HEADS, HP), 0)).astype(jnp.float32)


def widen(a, expand):
    return jnp.dot(a, expand, precision=HIGH, preferred_element_type=jnp.float32)


def ssd_kernel(len_ref, dl_ref, skip_ref, first_ref, x_ref, maps_ref, step_ref, y_ref, st_ref, fac_ref):
    first = first_ref[0]
    ends = ends_of(len_ref)
    expand = spread()
    head_lane = iota((1, HEADS), 1)
    wide_lane = iota((1, HP), 1) // (HP // HEADS)
    rate = jnp.zeros((1, HEADS), jnp.float32)
    skip = jnp.zeros((1, HP), jnp.float32)
    for h in range(HEADS):
        rate = jnp.where(head_lane == h, dl_ref[h], rate)
        skip = jnp.where(wide_lane == h, skip_ref[h], skip)
    rate = -jnp.exp(rate)
    row = iota((BLOCK, 1), 0)
    col = iota((1, BLOCK), 1)
    tri = (row >= col).astype(jnp.float32)
    half = iota((1, 128), 1) < 64
    state = None
    before = None
    for n in range(ROWS // BLOCK):
        rows = slice(n * BLOCK, (n + 1) * BLOCK)
        base = first + n * BLOCK
        start_col = start_of(base + row, ends)
        last_start = start_of(base + (BLOCK - 1), ends)
        cum = jnp.dot(tri, rate * step_ref[rows, :], precision=HIGH, preferred_element_type=jnp.float32)
        cum_t = cum.T
        write = maps_ref[rows, :SN]
        read = maps_ref[rows, SN:]
        prod = lax.dot_general(read, write, (((1,), (1,)), ((), ())), preferred_element_type=jnp.float32)
        allowed = (base + col >= start_col) & (col <= row)
        for pair in range(HEADS // 2):
            lanes = slice(pair * 128, (pair + 1) * 128)
            x = x_ref[rows, lanes]
            total = skip[:, lanes] * x.astype(jnp.float32)
            for which in range(2):
                h = pair * 2 + which
                gap = jnp.where(allowed, cum[:, h : h + 1] - cum_t[h : h + 1, :], LOW)
                weights = (jnp.exp(gap) * prod).astype(jnp.bfloat16)
                part = jnp.where(half if which == 0 else ~half, x, jnp.zeros_like(x))
                total = total + jnp.dot(weights, part, preferred_element_type=jnp.float32)
            y_ref[rows, lanes] = total
        ecum = jnp.exp(cum)
        if state is not None:
            local = widen(jnp.where(start_col < base, ecum, 0.0), expand)
            reads = jnp.dot(read, state.astype(jnp.bfloat16), preferred_element_type=jnp.float32)
            y_ref[rows, :] += reads * local
        carry = jnp.where(start_col < first, ecum, 0.0)
        if before is not None:
            carry = carry * before
        fac_ref[rows, :] = carry
        tail = jnp.exp(cum[BLOCK - 1 : BLOCK, :] - cum)
        tail = widen(jnp.where(base + row >= last_start, tail, 0.0), expand)
        weighted = (x_ref[rows, :].astype(jnp.float32) * tail).astype(jnp.bfloat16)
        new = lax.dot_general(write, weighted, (((0,), (0,)), ((), ())), preferred_element_type=jnp.float32)
        end = ecum[BLOCK - 8 :, :]
        if state is not None:
            keep = jnp.where(last_start < base, 1.0, 0.0)
            new = new + (keep * widen(end, expand)[7:8, :]) * state
            end = end * before
        state = new
        before = end[7:8, :]
    through = jnp.where(last_start < first, 1.0, 0.0) * widen(end, expand)[7:8, :]
    st_ref[:SN, :] = state.astype(jnp.bfloat16)
    store_through(st_ref, through)


def store_through(ref, through):
    high = through.astype(jnp.bfloat16).astype(jnp.float32)
    low = through - high
    sub = iota((16, 1), 0)
    ref[SN:, :] = jnp.where(sub == 0, high, jnp.where(sub == 1, low, 0.0)).astype(jnp.bfloat16)


def through_of(ref):
    tail = ref[SN:, :].astype(jnp.float32)
    return tail[0:1, :] + tail[1:2, :]


def join_kernel(*refs):
    out = refs[-1]
    state = refs[0][:SN, :].astype(jnp.float32)
    through = through_of(refs[0])
    for ref in refs[1:-1]:
        t = through_of(ref)
        state = ref[:SN, :].astype(jnp.float32) + t * state
        through = through * t
    out[:SN, :] = state.astype(jnp.bfloat16)
    store_through(out, through)


def attn_kernel(len_ref, first_ref, q_ref, kv_ref, o_ref, q_scr, m_scr, l_scr, acc_scr):
    first = first_ref[0]
    ends = ends_of(len_ref)
    tile = 256
    tiles = 2 * ROWS // tile
    q_scr[:ROWS, :] = q_ref[:, :HD]
    q_scr[ROWS:, :] = q_ref[:, HD:]
    factor = LOG2E * HD**-0.5

    def step(j, masked, opening):
        base = j * CHUNK
        k = kv_ref[pl.ds(pl.multiple_of(base, CHUNK), CHUNK), :HD]
        v = kv_ref[pl.ds(pl.multiple_of(base, CHUNK), CHUNK), HD:]
        for r in range(tiles):
            rows = slice(r * tile, (r + 1) * tile)
            s = lax.dot_general(q_scr[rows, :], k, (((1,), (1,)), ((), ())), preferred_element_type=jnp.float32)
            s = s * factor
            if masked:
                pos = first + (r * tile) % ROWS + iota((tile, 1), 0)
                key = base + iota((1, CHUNK), 1)
                s = jnp.where((key >= start_of(pos, ends)) & (key <= pos), s, LOW)
            m = jnp.max(s, axis=1, keepdims=True)
            if opening:
                m = jnp.broadcast_to(m, (tile, 128))
            else:
                old = m_scr[rows, :]
                m = jnp.maximum(old, m)
                alpha = jnp.exp2(old - m)
            p = jnp.exp2(s - jnp.concatenate([m] * (CHUNK // 128), axis=1))
            total = p[:, :128]
            for i in range(1, CHUNK // 128):
                total = total + p[:, i * 128 : (i + 1) * 128]
            out = jnp.dot(p.astype(jnp.bfloat16), v, preferred_element_type=jnp.float32)
            if not opening:
                total = total + l_scr[rows, :] * alpha
                out = out + acc_scr[rows, :] * alpha
            m_scr[rows, :] = m
            l_scr[rows, :] = total
            acc_scr[rows, :] = out

    mine = first // CHUNK
    low = start_of(first, ends) // CHUNK
    clear = jnp.clip((start_of(first + ROWS - 1, ends) + CHUNK - 1) // CHUNK, low, mine)
    step(mine, True, True)
    lax.fori_loop(low, clear, lambda j, _: (step(j, True, False), 0)[1], 0)
    lax.fori_loop(clear, mine, lambda j, _: (step(j, False, False), 0)[1], 0)
    for g in range(2):
        rows = slice(g * ROWS, (g + 1) * ROWS)
        total = jnp.sum(l_scr[rows, :], axis=1, keepdims=True)
        o_ref[:, g * HD : (g + 1) * HD] = (acc_scr[rows, :] / total).astype(jnp.bfloat16)


def proj_kernel(att_ref, y_ref, z_ref, read_ref, fac_ref, far_ref, near_ref, wa_ref, ws_ref, o_ref, act):
    @pl.when(pl.program_id(0) == 0)
    def _():
        state = near_ref[:SN, :].astype(jnp.float32)
        state = state + through_of(near_ref) * far_ref[:SN, :].astype(jnp.float32)
        reads = jnp.dot(read_ref[...], state.astype(jnp.bfloat16), preferred_element_type=jnp.float32)
        y = y_ref[...] + reads * widen(fac_ref[...], spread())
        z = z_ref[...].astype(jnp.float32)
        act[:, : 2 * HD] = att_ref[...]
        act[:, 2 * HD :] = (y * (z / (1.0 + jnp.exp(-z)))).astype(jnp.bfloat16)

    out = jnp.dot(act[:, : 2 * HD], wa_ref[...], preferred_element_type=jnp.float32)
    out = out + jnp.dot(act[:, 2 * HD :], ws_ref[...], preferred_element_type=jnp.float32)
    o_ref[...] = out.astype(jnp.bfloat16)


def big(**more):
    return pltpu.CompilerParams(vmem_limit_bytes=56 * 2**20, **more)


def shifted(block, distance):
    n = lax.axis_size("pack")
    return lax.ppermute(block, "pack", [(i, i + distance) for i in range(n - distance)])


def join(*runs):
    return pl.pallas_call(
        join_kernel,
        out_shape=jax.ShapeDtypeStruct((STATE_ROWS, HP), jnp.bfloat16),
        in_specs=[VMEM] * len(runs),
        out_specs=VMEM,
        compiler_params=big(),
    )(*runs)


def local(
    queries,
    keys_values,
    ssm_values,
    ssm_gates,
    ssm_maps,
    step_size,
    decay_log,
    skip_gain,
    attn_out_weight,
    ssd_out_weight,
    lengths,
):
    first = jnp.reshape(lax.axis_index("pack") * ROWS, (1,)).astype(jnp.int32)
    kv = lax.all_gather(keys_values.reshape(ROWS, 2 * HD), "pack", axis=0, tiled=True)

    y_local, summary, fac = pl.pallas_call(
        ssd_kernel,
        out_shape=(
            jax.ShapeDtypeStruct((ROWS, HP), jnp.float32),
            jax.ShapeDtypeStruct((STATE_ROWS, HP), jnp.bfloat16),
            jax.ShapeDtypeStruct((ROWS, HEADS), jnp.float32),
        ),
        in_specs=[SMEM] * 4 + [VMEM] * 3,
        out_specs=(VMEM, VMEM, VMEM),
        compiler_params=big(),
        cost_estimate=pl.CostEstimate(flops=10**9, bytes_accessed=4 * 10**6, transcendentals=10**6),
        name="ssd_local",
    )(lengths, decay_log, skip_gain, first, ssm_values, ssm_maps, step_size)

    three = join(shifted(summary, 3), shifted(summary, 2), shifted(summary, 1))
    nine = join(shifted(three, 6), shifted(three, 3), three)
    far = shifted(nine, 9)

    attended = pl.pallas_call(
        attn_kernel,
        out_shape=jax.ShapeDtypeStruct((ROWS, 2 * HD), jnp.bfloat16),
        in_specs=[SMEM] * 2 + [VMEM] * 2,
        out_specs=VMEM,
        scratch_shapes=[
            pltpu.VMEM((2 * ROWS, HD), jnp.bfloat16),
            pltpu.VMEM((2 * ROWS, 128), jnp.float32),
            pltpu.VMEM((2 * ROWS, 128), jnp.float32),
            pltpu.VMEM((2 * ROWS, HD), jnp.float32),
        ],
        compiler_params=big(),
        cost_estimate=pl.CostEstimate(flops=5 * 10**9, bytes_accessed=9 * 10**6, transcendentals=9 * 10**6),
        name="attention",
    )(lengths, first, queries, kv)

    cols = 1280
    whole = lambda *shape: pl.BlockSpec(shape, lambda i: (0,) * len(shape))
    terms = pl.pallas_call(
        proj_kernel,
        out_shape=jax.ShapeDtypeStruct((ROWS, DM), jnp.bfloat16),
        grid=(DM // cols,),
        in_specs=[
            whole(ROWS, 2 * HD),
            whole(ROWS, HP),
            whole(ROWS, HP),
            pl.BlockSpec((ROWS, SN), lambda i: (0, 1)),
            whole(ROWS, HEADS),
            whole(STATE_ROWS, HP),
            whole(STATE_ROWS, HP),
            pl.BlockSpec((2 * HD, cols), lambda i: (0, i)),
            pl.BlockSpec((HP, cols), lambda i: (0, i)),
        ],
        out_specs=pl.BlockSpec((ROWS, cols), lambda i: (0, i)),
        scratch_shapes=[pltpu.VMEM((ROWS, 2 * HD + HP), jnp.bfloat16)],
        compiler_params=big(),
        cost_estimate=pl.CostEstimate(flops=4 * 10**9, bytes_accessed=16 * 10**6, transcendentals=10**6),
        name="project",
    )(attended, y_local, ssm_gates, ssm_maps, fac, far, nine, attn_out_weight, ssd_out_weight)
    return lax.psum_scatter(terms, "tp", scatter_dimension=0, tiled=True)


def solution(mesh):
    return jax.shard_map(
        local,
        mesh=mesh,
        in_specs=(
            P("pack", "tp"),
            P("pack", "tp", None),
            P("pack", "tp"),
            P("pack", "tp"),
            P("pack", None),
            P("pack", "tp"),
            P("tp"),
            P("tp"),
            P("tp", None),
            P("tp", None),
            P(),
        ),
        out_specs=P(("pack", "tp"), None),
        check_vma=False,
    )
```

time: 497 us -> 199 us (0.40); the launches traced: 493 us -> 200 us
  matrix products: 129 us -> 0 us
  local copies, waits for them, and re-layouts: 67.5 us -> 3.7 us
  starting transfers between devices: 79.8 us -> 26 us
  other arithmetic: 47 us -> 0 us
  Pallas kernels: 0 us -> 28.3 us
  waiting for transfers between devices: 150 us -> 129 us
    dot_general x75 -> x0, matrix products: 129 us -> none  [the longest x32 59 us: absorb_rows(): jnp.einsum('rkgs,skd->rkgd', raw_weights.astype(jnp.bfloat16), portion[:,...]
    ppermute x17 -> x6, starting transfers between devices: 79.7 us -> 26 us  [shifted(): lax.ppermute(block, 'pack', [(i, i + distance) for i in range(n - distanc...]
    ppermute x17 -> x6, waiting for transfers between devices: 53.7 us -> 21.9 us  [shifted(): lax.ppermute(block, 'pack', [(i, i + distance) for i in range(n - distanc...]
    pallas_call x0 -> x5, Pallas kernels: none -> 28.3 us  [the longest x1 10.7 us: local(): pl.pallas_call(proj_kernel, out_shape=jax.ShapeDtypeStruct((ROWS, DM), jn...]
    dynamic_update_slice x4 -> x0, local copies, waits for them, and re-layouts: 25.9 us -> none  [local(): end_state, ssm_y = lax.scan(advance, zero_state, inputs_seq)]
    while x164 -> x0, local copies, waits for them, and re-layouts: 24.4 us -> none
    reduce_sum x66 -> x0, other arithmetic: 22 us -> none  [the longest x32 18.4 us: absorb_rows(): totals = totals * rescale + jnp.sum(raw_weights, axis=-1)]
    all_gather x1, waiting for transfers between devices: 0.01 us -> 13.3 us  [local(): lax.all_gather(keys_values.reshape(ROWS, 2 * HD), 'pack', axis=0, tiled=T...]
  transfers between devices with their start and end apart: 19 -> 8, of which waited for: 17 -> 5; matrix products, arithmetic and copies ran while one was open for 14% -> 1% of each run, Pallas kernels for 0% -> 9%
where the time goes in v1:
time: 199 us; the launch traced here: 200 us
  waiting for transfers between devices  129 us (65%)
  Pallas kernels  28.3 us (14%)
  starting transfers between devices  26 us (13%)
  between operations  13.5 us (7%)
  local copies, waits for them, and re-layouts  3.7 us (2%)
    reduce_scatter x1, waiting for transfers between devices, local(): return lax.psum_scatter(terms, 'tp', scatter_dimension=0, tiled=True)  92.8 us
    ppermute x6, starting transfers between devices, shifted(): lax.ppermute(block, 'pack', [(i, i + distance) for i in range(n - distanc...  26 us
    ppermute x6, waiting for transfers between devices, shifted(): lax.ppermute(block, 'pack', [(i, i + distance) for i in range(n - distanc...  21.9 us
    all_gather x1, waiting for transfers between devices, local(): lax.all_gather(keys_values.reshape(ROWS, 2 * HD), 'pack', axis=0, tiled=T...  13.3 us
    pallas_call x1, Pallas kernels, local(): pl.pallas_call(proj_kernel, out_shape=jax.ShapeDtypeStruct((ROWS, DM), jn...  10.7 us
    pallas_call x1, Pallas kernels, local(): pl.pallas_call(attn_kernel, out_shape=jax.ShapeDtypeStruct((ROWS, 2 * HD)...  7.32 us
    pallas_call x1, Pallas kernels, local(): pl.pallas_call(ssd_kernel, out_shape=(jax.ShapeDtypeStruct((ROWS, HP), jn...  6.2 us
    pallas_call x2, Pallas kernels, join(): pl.pallas_call(join_kernel, out_shape=jax.ShapeDtypeStruct((STATE_ROWS, H...  4.09 us
  transfers between devices with their start and end apart: 8, of which 5 were waited for; matrix products, arithmetic and copies ran while one was open for 1% of the time, Pallas kernels for 9%

profile of v1, /device:TPU:1, one launch (start us, length us, event | category | flops | bytes accessed | tf_op | source)
XLA Modules:
  0.0 200.2 jit_solution(3278101939531715781)
XLA Ops:
  6.5 0.7 all-gather.3.cloned.1.call-update
  7.3 0.0 reduce-scatter.2.cloned.1.call-start
  7.3 1.6 copy.12.step_ref
  8.9 6.2 %ssd_local.1 = (f32[512,512]{1,0:T(8,128)}, bf16[272,512]{1,0:T(8,128)(2,1)}, f32[512,8]{1,0:T(8,128)}) custom-call(s32[4]{0:T(128)} %len_ref.3, f32[8]{0:T(128)} %dl_ref.1, f32[8]{0:T(128)} %skip_ref.1, s32[1]{0:T(128)} %bitcast.first_ref, bf16[512,512]{1,0:T(8,128)(2,1)} %x_ref.1, bf16[512,512]{1,0:T(8,128)(2,1)} %read_ref.1, f32[512,8]{1,0:T(8,128)} %copy.12.step_ref), custom_call_target="tpu_custom_call" | custom-call | flops 1000000000 | bytes 4000000 | tf_op jit(solution)/shard_map/ssd_local/pallas_call | solution.py:244
  15.1 4.6 %collective-permute-start.2 = (bf16[272,512]{1,0:T(8,128)(2,1)}, bf16[272,512]{1,0:T(8,128)(2,1)S(1)}, u32[]{:S(2)}, u32[]{:S(2)}) collective-permute-start(bf16[272,512]{1,0:T(8,128)(2,1)} %get-tuple-element.10), channel_id=1, source_target_pairs={{0,8},{8,16},{16,24},{24,32},{32,40},{40,48},{48,56},{56,64},{64,7... | collective-permute-start | bytes 835592 | tf_op jit(solution)/shard_map/ppermute | solution.py:215
  19.7 3.2 %collective-permute-start.1 = (bf16[272,512]{1,0:T(8,128)(2,1)}, bf16[272,512]{1,0:T(8,128)(2,1)S(1)}, u32[]{:S(2)}, u32[]{:S(2)}) collective-permute-start(bf16[272,512]{1,0:T(8,128)(2,1)} %get-tuple-element.10), channel_id=1, source_target_pairs={{0,16},{8,24},{16,32},{24,40},{32,48},{40,56},{48,64},{56,72},{64,... | collective-permute-start | bytes 835592 | tf_op jit(solution)/shard_map/ppermute | solution.py:215
  22.9 3.5 %collective-permute-start = (bf16[272,512]{1,0:T(8,128)(2,1)}, bf16[272,512]{1,0:T(8,128)(2,1)S(1)}, u32[]{:S(2)}, u32[]{:S(2)}) collective-permute-start(bf16[272,512]{1,0:T(8,128)(2,1)} %get-tuple-element.10), channel_id=1, source_target_pairs={{0,24},{8,32},{16,40},{24,48},{32,56},{40,64},{48,72},{56,80},{64,... | collective-permute-start | bytes 835592 | tf_op jit(solution)/shard_map/ppermute | solution.py:215
  26.4 0.0 collective-permute-done.2.refs_2_
  26.4 4.8 %collective-permute-done.1.refs_1_ = bf16[272,512]{1,0:T(8,128)(2,1)S(1)} collective-permute-done((bf16[272,512]{1,0:T(8,128)(2,1)}, bf16[272,512]{1,0:T(8,128)(2,1)S(1)}, u32[]{:S(2)}, u32[]{:S(2)}) %collective-permute-start.1) | collective-permute-done | bytes 278560 | tf_op jit(solution)/shard_map/ppermute | solution.py:215
  31.2 7.3 %collective-permute-done.refs_0_ = bf16[272,512]{1,0:T(8,128)(2,1)S(1)} collective-permute-done((bf16[272,512]{1,0:T(8,128)(2,1)}, bf16[272,512]{1,0:T(8,128)(2,1)S(1)}, u32[]{:S(2)}, u32[]{:S(2)}) %collective-permute-start) | collective-permute-done | bytes 278560 | tf_op jit(solution)/shard_map/ppermute | solution.py:215
  38.6 0.7 copy-done.2
  39.3 2.0 shard_map.109.refs_2_
  41.2 5.9 %collective-permute-start.4 = (bf16[272,512]{1,0:T(8,128)(2,1)}, bf16[272,512]{1,0:T(8,128)(2,1)S(1)}, u32[]{:S(2)}, u32[]{:S(2)}) collective-permute-start(bf16[272,512]{1,0:T(8,128)(2,1)} %shard_map.109.refs_2_), channel_id=1, source_target_pairs={{0,24},{8,32},{16,40},{24,48},{32,56},{40,64},{48,72},{56,80},{64,... | collective-permute-start | bytes 835592 | tf_op jit(solution)/shard_map/ppermute | solution.py:215
  47.2 7.5 %collective-permute-start.3 = (bf16[272,512]{1,0:T(8,128)(2,1)}, bf16[272,512]{1,0:T(8,128)(2,1)S(1)}, u32[]{:S(2)}, u32[]{:S(2)}) collective-permute-start(bf16[272,512]{1,0:T(8,128)(2,1)} %shard_map.109.refs_2_), channel_id=1, source_target_pairs={{0,48},{8,56},{16,64},{24,72},{32,80},{40,88},{48,96},{56,104},{64... | collective-permute-start | bytes 835592 | tf_op jit(solution)/shard_map/ppermute | solution.py:215
  54.6 9.7 %collective-permute-done.3.refs_0_ = bf16[272,512]{1,0:T(8,128)(2,1)S(1)} collective-permute-done((bf16[272,512]{1,0:T(8,128)(2,1)}, bf16[272,512]{1,0:T(8,128)(2,1)S(1)}, u32[]{:S(2)}, u32[]{:S(2)}) %collective-permute-start.3) | collective-permute-done | bytes 278560 | tf_op jit(solution)/shard_map/ppermute | solution.py:215
  64.4 0.7 copy-done.4
  65.1 2.1 %shard_map.110.near_ref = bf16[272,512]{1,0:T(8,128)(2,1)} custom-call(bf16[272,512]{1,0:T(8,128)(2,1)} %copy-done.4, bf16[272,512]{1,0:T(8,128)(2,1)} %copy-done.3, bf16[272,512]{1,0:T(8,128)(2,1)} %shard_map.109.refs_2_), custom_call_target="tpu_custom_call" | custom-call | tf_op jit(solution)/shard_map/pallas_call | solution.py:219
  67.2 1.3 collective-permute-start.5
  68.5 13.3 %all-gather.3.cloned.1.call-done = bf16[16384,1,256]{2,0,1:T(8,128)(2,1)} async-done(((bf16[512,1,256]{2,0,1:T(8,128)(2,1)}), bf16[16384,1,256]{2,0,1:T(8,128)(2,1)}) %all-gather.3.cloned.1.call-update) | async-done | bytes 8388624 | tf_op jit(solution)/shard_map/all_gather | solution.py:242
  81.8 7.3 %attention.1.att_ref = bf16[512,256]{1,0:T(8,128)(2,1)} custom-call(s32[4]{0:T(128)} %len_ref.3, s32[1]{0:T(128)} %bitcast.first_ref, bf16[512,256]{1,0:T(8,128)(2,1)} %q_ref.1, bf16[16384,256]{1,0:T(8,128)(2,1)} %bitcast.2), custom_call_target="tpu_custom_call" | custom-call | flops 5000000000 | bytes 9000000 | tf_op jit(solution)/shard_map/attention/pallas_call | solution.py:262
  89.1 0.7 copy-done.5
  89.8 10.7 %project.1 = bf16[512,5120]{1,0:T(8,128)(2,1)} custom-call(bf16[512,256]{1,0:T(8,128)(2,1)} %attention.1.att_ref, f32[512,512]{1,0:T(8,128)} %get-tuple-element.8.y_ref, bf16[512,512]{1,0:T(8,128)(2,1)} %z_ref.1, bf16[512,512]{1,0:T(8,128)(2,1)} %read_ref.1, f32[512,8]{1,0:T(8,128)} %get-tuple-element.9.fac_ref, bf16[272,512]{1,0:T(8,128)(2,1)} %copy-done.5, ...), custom_call_target="tpu_custom_call" | custom-call | flops 4000000000 | bytes 16000000 | tf_op jit(solution)/shard_map/project/pallas_call | solution.py:280
  100.5 0.0 reduce-scatter.2.cloned.1.call-update
  100.5 92.8 %reduce-scatter.2.cloned.1.call-done = bf16[64,5120]{1,0:T(8,128)(2,1)} async-done(((bf16[512,5120]{1,0:T(8,128)(2,1)}), bf16[64,5120]{1,0:T(8,128)(2,1)}) %reduce-scatter.2.cloned.1.call-update) | async-done | bytes 655376 | tf_op jit(solution)/shard_map/reduce_scatter | solution.py:301
  (12 shorter events, 0.0 us)
Async XLA Ops:
  6.5 75.2 %all-gather.3.cloned.1.call-start = ((), (), s32[]{:S(2)}) async-start(), calls=%async_computation.2 | async-start | bytes 8650752 | tf_op jit(solution)/shard_map/all_gather | solution.py:242
  7.3 186.1 %reduce-scatter.2.cloned.1.call-start = ((), (), s32[]{:S(2)}) async-start(), calls=%async_computation.1 | async-start | bytes 5898240 | tf_op jit(solution)/shard_map/reduce_scatter | solution.py:301
  15.1 11.3 %collective-permute-start.2 = (bf16[272,512]{1,0:T(8,128)(2,1)}, bf16[272,512]{1,0:T(8,128)(2,1)S(1)}, u32[]{:S(2)}, u32[]{:S(2)}) collective-permute-start(bf16[272,512]{1,0:T(8,128)(2,1)} %get-tuple-element.10), channel_id=1, source_target_pairs={{0,8},{8,16},{16,24},{24,32},{32,40},{40,48},{48,56},{56,64},{64,7... | collective-permute-start | bytes 835592 | tf_op jit(solution)/shard_map/ppermute | solution.py:215
  19.7 11.6 %collective-permute-start.1 = (bf16[272,512]{1,0:T(8,128)(2,1)}, bf16[272,512]{1,0:T(8,128)(2,1)S(1)}, u32[]{:S(2)}, u32[]{:S(2)}) collective-permute-start(bf16[272,512]{1,0:T(8,128)(2,1)} %get-tuple-element.10), channel_id=1, source_target_pairs={{0,16},{8,24},{16,32},{24,40},{32,48},{40,56},{48,64},{56,72},{64,... | collective-permute-start | bytes 835592 | tf_op jit(solution)/shard_map/ppermute | solution.py:215
  22.9 15.7 %collective-permute-start = (bf16[272,512]{1,0:T(8,128)(2,1)}, bf16[272,512]{1,0:T(8,128)(2,1)S(1)}, u32[]{:S(2)}, u32[]{:S(2)}) collective-permute-start(bf16[272,512]{1,0:T(8,128)(2,1)} %get-tuple-element.10), channel_id=1, source_target_pairs={{0,24},{8,32},{16,40},{24,48},{32,56},{40,64},{48,72},{56,80},{64,... | collective-permute-start | bytes 835592 | tf_op jit(solution)/shard_map/ppermute | solution.py:215
  26.4 12.1 %copy-start = (bf16[272,512]{1,0:T(8,128)(2,1)}, bf16[272,512]{1,0:T(8,128)(2,1)S(1)}, u32[]{:S(2)}) copy-start(bf16[272,512]{1,0:T(8,128)(2,1)S(1)} %collective-permute-done.2.refs_2_) | copy-start | bytes 835588
  31.2 7.3 %copy-start.1 = (bf16[272,512]{1,0:T(8,128)(2,1)}, bf16[272,512]{1,0:T(8,128)(2,1)S(1)}, u32[]{:S(2)}) copy-start(bf16[272,512]{1,0:T(8,128)(2,1)S(1)} %collective-permute-done.1.refs_1_) | copy-start | bytes 835588
  38.5 0.7 copy-start.2
  41.2 13.4 %collective-permute-start.4 = (bf16[272,512]{1,0:T(8,128)(2,1)}, bf16[272,512]{1,0:T(8,128)(2,1)S(1)}, u32[]{:S(2)}, u32[]{:S(2)}) collective-permute-start(bf16[272,512]{1,0:T(8,128)(2,1)} %shard_map.109.refs_2_), channel_id=1, source_target_pairs={{0,24},{8,32},{16,40},{24,48},{32,56},{40,64},{48,72},{56,80},{64,... | collective-permute-start | bytes 835592 | tf_op jit(solution)/shard_map/ppermute | solution.py:215
  47.2 17.2 %collective-permute-start.3 = (bf16[272,512]{1,0:T(8,128)(2,1)}, bf16[272,512]{1,0:T(8,128)(2,1)S(1)}, u32[]{:S(2)}, u32[]{:S(2)}) collective-permute-start(bf16[272,512]{1,0:T(8,128)(2,1)} %shard_map.109.refs_2_), channel_id=1, source_target_pairs={{0,48},{8,56},{16,64},{24,72},{32,80},{40,88},{48,96},{56,104},{64... | collective-permute-start | bytes 835592 | tf_op jit(solution)/shard_map/ppermute | solution.py:215
  54.6 9.8 %copy-start.3 = (bf16[272,512]{1,0:T(8,128)(2,1)}, bf16[272,512]{1,0:T(8,128)(2,1)S(1)}, u32[]{:S(2)}) copy-start(bf16[272,512]{1,0:T(8,128)(2,1)S(1)} %collective-permute-done.4.refs_1_) | copy-start | bytes 835588
  64.4 0.7 copy-start.4
  67.2 21.9 %collective-permute-start.5 = (bf16[272,512]{1,0:T(8,128)(2,1)}, bf16[272,512]{1,0:T(8,128)(2,1)S(1)}, u32[]{:S(2)}, u32[]{:S(2)}) collective-permute-start(bf16[272,512]{1,0:T(8,128)(2,1)} %shard_map.110.near_ref), channel_id=1, source_target_pairs={{0,72},{8,80},{16,88},{24,96},{32,104},{40,112},{48,120},{56,128},... | collective-permute-start | bytes 835592 | tf_op jit(solution)/shard_map/ppermute | solution.py:215
  89.1 0.7 copy-start.5
Sparse Core Ops, SparseCore 0:
  9.9 71.8 all-gather.2
  100.6 92.6 reduce-scatter.1

commit v2 on v1

--- a/solution.py
+++ b/solution.py
@@ -1,5 +1,3 @@
-import functools
-
 import jax
 import jax.numpy as jnp
 from jax import lax
@@ -15,12 +13,16 @@
 SN = 256
 DM = 5120
 CHUNK = 512
+SLOTS = 18
+TILE = 256
+COLS = 1280
 LOW = -1e30
 LOG2E = 1.4426950408889634
 HIGH = lax.Precision.HIGHEST
 STATE_ROWS = SN + 16
 VMEM = pl.BlockSpec(memory_space=pltpu.VMEM)
 SMEM = pl.BlockSpec(memory_space=pltpu.SMEM)
+ANY = pl.BlockSpec(memory_space=pl.ANY)
 
 
 def iota(shape, dim):
@@ -138,72 +140,137 @@
     store_through(out, through)
 
 
-def attn_kernel(len_ref, first_ref, q_ref, kv_ref, o_ref, q_scr, m_scr, l_scr, acc_scr):
+def gate_kernel(y_ref, z_ref, read_ref, fac_ref, far_ref, near_ref, act_ref):
+    state = near_ref[:SN, :].astype(jnp.float32)
+    state = state + through_of(near_ref) * far_ref[:SN, :].astype(jnp.float32)
+    reads = jnp.dot(read_ref[...], state.astype(jnp.bfloat16), preferred_element_type=jnp.float32)
+    y = y_ref[...] + reads * widen(fac_ref[...], spread())
+    z = z_ref[...].astype(jnp.float32)
+    act_ref[...] = (y * (z / (1.0 + jnp.exp(-z)))).astype(jnp.bfloat16)
+
+
+def mix_kernel(
+    len_ref,
+    first_ref,
+    q_ref,
+    act_ref,
+    kv_hbm,
+    wa_hbm,
+    ws_hbm,
+    o_hbm,
+    q_scr,
+    kv_scr,
+    acc_scr,
+    m_scr,
+    w_scr,
+    in_scr,
+    o_scr,
+    kv_sem,
+    w_sem,
+    o_sem,
+):
     first = first_ref[0]
     ends = ends_of(len_ref)
-    tile = 256
-    tiles = 2 * ROWS // tile
-    q_scr[:ROWS, :] = q_ref[:, :HD]
-    q_scr[ROWS:, :] = q_ref[:, HD:]
-    factor = LOG2E * HD**-0.5
-
-    def step(j, masked, opening):
-        base = j * CHUNK
-        k = kv_ref[pl.ds(pl.multiple_of(base, CHUNK), CHUNK), :HD]
-        v = kv_ref[pl.ds(pl.multiple_of(base, CHUNK), CHUNK), HD:]
-        for r in range(tiles):
-            rows = slice(r * tile, (r + 1) * tile)
-            s = lax.dot_general(q_scr[rows, :], k, (((1,), (1,)), ((), ())), preferred_element_type=jnp.float32)
-            s = s * factor
-            if masked:
-                pos = first + (r * tile) % ROWS + iota((tile, 1), 0)
-                key = base + iota((1, CHUNK), 1)
-                s = jnp.where((key >= start_of(pos, ends)) & (key <= pos), s, LOW)
-            m = jnp.max(s, axis=1, keepdims=True)
-            if opening:
-                m = jnp.broadcast_to(m, (tile, 128))
-            else:
-                old = m_scr[rows, :]
-                m = jnp.maximum(old, m)
-                alpha = jnp.exp2(old - m)
-            p = jnp.exp2(s - jnp.concatenate([m] * (CHUNK // 128), axis=1))
-            total = p[:, :128]
-            for i in range(1, CHUNK // 128):
-                total = total + p[:, i * 128 : (i + 1) * 128]
-            out = jnp.dot(p.astype(jnp.bfloat16), v, preferred_element_type=jnp.float32)
-            if not opening:
-                total = total + l_scr[rows, :] * alpha
-                out = out + acc_scr[rows, :] * alpha
-            m_scr[rows, :] = m
-            l_scr[rows, :] = total
-            acc_scr[rows, :] = out
-
     mine = first // CHUNK
     low = start_of(first, ends) // CHUNK
-    clear = jnp.clip((start_of(first + ROWS - 1, ends) + CHUNK - 1) // CHUNK, low, mine)
-    step(mine, True, True)
-    lax.fori_loop(low, clear, lambda j, _: (step(j, True, False), 0)[1], 0)
-    lax.fori_loop(clear, mine, lambda j, _: (step(j, False, False), 0)[1], 0)
+    last_start = start_of(first + ROWS - 1, ends)
+    count = mine - low + 1
+
+    def chunk_of(i):
+        return jnp.where(i == 0, mine, low + i - 1)
+
+    def kv_copy(i):
+        rows = pl.ds(pl.multiple_of(chunk_of(i) * CHUNK, CHUNK), CHUNK)
+        return pltpu.make_async_copy(kv_hbm.at[rows], kv_scr.at[i], kv_sem.at[i])
+
+    lax.fori_loop(0, count, lambda i, _: (kv_copy(i).start(), 0)[1], 0)
+    weights = [
+        pltpu.make_async_copy(wa_hbm, w_scr.at[pl.ds(0, 2 * HD)], w_sem.at[0]),
+        pltpu.make_async_copy(ws_hbm, w_scr.at[pl.ds(2 * HD, HP)], w_sem.at[1]),
+    ]
+    for copy in weights:
+        copy.start()
     for g in range(2):
         rows = slice(g * ROWS, (g + 1) * ROWS)
-        total = jnp.sum(l_scr[rows, :], axis=1, keepdims=True)
-        o_ref[:, g * HD : (g + 1) * HD] = (acc_scr[rows, :] / total).astype(jnp.bfloat16)
-
-
-def proj_kernel(att_ref, y_ref, z_ref, read_ref, fac_ref, far_ref, near_ref, wa_ref, ws_ref, o_ref, act):
-    @pl.when(pl.program_id(0) == 0)
+        scaled = q_ref[:, g * HD : (g + 1) * HD].astype(jnp.float32) * (LOG2E * HD**-0.5)
+        high = scaled.astype(jnp.bfloat16)
+        q_scr[rows, :HD] = high
+        q_scr[rows, HD:] = (scaled - high.astype(jnp.float32)).astype(jnp.bfloat16)
+    one = jnp.ones((CHUNK, HD), jnp.bfloat16)
+
+    def scores(i, rows, masked):
+        k = kv_scr[i, :, :HD]
+        s = lax.dot_general(
+            q_scr[rows, :],
+            jnp.concatenate([k, k], axis=1),
+            (((1,), (1,)), ((), ())),
+            preferred_element_type=jnp.float32,
+        )
+        if masked:
+            pos = first + rows.start % ROWS + iota((rows.stop - rows.start, 1), 0)
+            key = chunk_of(i) * CHUNK + iota((1, CHUNK), 1)
+            s = jnp.where((key >= start_of(pos, ends)) & (key <= pos), s, LOW)
+        return s
+
+    def plain(i, masked):
+        v = jnp.concatenate([kv_scr[i, :, HD:], one], axis=1)
+        for r in range(2 * ROWS // TILE):
+            rows = slice(r * TILE, (r + 1) * TILE)
+            p = jnp.exp2(scores(i, rows, masked)).astype(jnp.bfloat16)
+            acc_scr[rows, :] += jnp.dot(p, v, preferred_element_type=jnp.float32)
+
+    def guarded(i, masked):
+        v = jnp.concatenate([kv_scr[i, :, HD:], one], axis=1)
+        for r in range(2 * ROWS // TILE):
+            rows = slice(r * TILE, (r + 1) * TILE)
+            s = scores(i, rows, masked)
+            old = m_scr[rows, :]
+            m = jnp.maximum(old, jnp.max(s, axis=1, keepdims=True))
+            alpha = jnp.exp2(old - m)
+            p = jnp.exp2(s - jnp.concatenate([m] * (CHUNK // 128), axis=1)).astype(jnp.bfloat16)
+            out = jnp.dot(p, v, preferred_element_type=jnp.float32)
+            acc_scr[rows, :] = acc_scr[rows, :] * jnp.concatenate([alpha, alpha], axis=1) + out
+            m_scr[rows, :] = m
+
+    def over_chunks(step, wait):
+        def one_chunk(i, _):
+            if wait:
+                kv_copy(i).wait()
+            masked = (i == 0) | (chunk_of(i) * CHUNK < last_start)
+            pl.when(masked)(lambda: step(i, True))
+            pl.when(jnp.logical_not(masked))(lambda: step(i, False))
+            return 0
+
+        lax.fori_loop(0, count, one_chunk, 0)
+
+    acc_scr[...] = jnp.zeros_like(acc_scr)
+    over_chunks(plain, True)
+    total = acc_scr[:, HD:]
+    fine = (jnp.min(total) > 2.0**-60) & (jnp.max(total) < 2.0**110)
+
+    @pl.when(jnp.logical_not(fine))
     def _():
-        state = near_ref[:SN, :].astype(jnp.float32)
-        state = state + through_of(near_ref) * far_ref[:SN, :].astype(jnp.float32)
-        reads = jnp.dot(read_ref[...], state.astype(jnp.bfloat16), preferred_element_type=jnp.float32)
-        y = y_ref[...] + reads * widen(fac_ref[...], spread())
-        z = z_ref[...].astype(jnp.float32)
-        act[:, : 2 * HD] = att_ref[...]
-        act[:, 2 * HD :] = (y * (z / (1.0 + jnp.exp(-z)))).astype(jnp.bfloat16)
-
-    out = jnp.dot(act[:, : 2 * HD], wa_ref[...], preferred_element_type=jnp.float32)
-    out = out + jnp.dot(act[:, 2 * HD :], ws_ref[...], preferred_element_type=jnp.float32)
-    o_ref[...] = out.astype(jnp.bfloat16)
+        acc_scr[...] = jnp.zeros_like(acc_scr)
+        m_scr[...] = jnp.full(m_scr.shape, LOW, jnp.float32)
+        over_chunks(guarded, False)
+
+    for g in range(2):
+        rows = slice(g * ROWS, (g + 1) * ROWS)
+        in_scr[:, g * HD : (g + 1) * HD] = (acc_scr[rows, :HD] / acc_scr[rows, HD:]).astype(jnp.bfloat16)
+    in_scr[:, 2 * HD :] = act_ref[...]
+    for copy in weights:
+        copy.wait()
+
+    def out_copy(i):
+        cols = pl.ds(i * COLS, COLS)
+        return pltpu.make_async_copy(o_scr.at[:, cols], o_hbm.at[:, cols], o_sem.at[i])
+
+    for i in range(DM // COLS):
+        cols = slice(i * COLS, (i + 1) * COLS)
+        o_scr[:, cols] = jnp.dot(in_scr[...], w_scr[:, cols], preferred_element_type=jnp.float32).astype(jnp.bfloat16)
+        out_copy(i).start()
+    for i in range(DM // COLS):
+        out_copy(i).wait()
 
 
 def big(**more):
@@ -259,45 +326,45 @@
     nine = join(shifted(three, 6), shifted(three, 3), three)
     far = shifted(nine, 9)
 
-    attended = pl.pallas_call(
-        attn_kernel,
-        out_shape=jax.ShapeDtypeStruct((ROWS, 2 * HD), jnp.bfloat16),
-        in_specs=[SMEM] * 2 + [VMEM] * 2,
-        out_specs=VMEM,
+    act = pl.pallas_call(
+        gate_kernel,
+        out_shape=jax.ShapeDtypeStruct((ROWS, HP), jnp.bfloat16),
+        grid=(1,),
+        in_specs=[
+            pl.BlockSpec((ROWS, HP), lambda i: (0, 0)),
+            pl.BlockSpec((ROWS, HP), lambda i: (0, 0)),
+            pl.BlockSpec((ROWS, SN), lambda i: (0, 1)),
+            pl.BlockSpec((ROWS, HEADS), lambda i: (0, 0)),
+            pl.BlockSpec((STATE_ROWS, HP), lambda i: (0, 0)),
+            pl.BlockSpec((STATE_ROWS, HP), lambda i: (0, 0)),
+        ],
+        out_specs=pl.BlockSpec((ROWS, HP), lambda i: (0, 0)),
+        compiler_params=big(),
+        cost_estimate=pl.CostEstimate(flops=10**8, bytes_accessed=3 * 10**6, transcendentals=3 * 10**5),
+        name="gate",
+    )(y_local, ssm_gates, ssm_maps, fac, far, nine)
+
+    terms = pl.pallas_call(
+        mix_kernel,
+        out_shape=jax.ShapeDtypeStruct((ROWS, DM), jnp.bfloat16),
+        in_specs=[SMEM] * 2 + [VMEM] * 2 + [ANY] * 3,
+        out_specs=ANY,
         scratch_shapes=[
-            pltpu.VMEM((2 * ROWS, HD), jnp.bfloat16),
-            pltpu.VMEM((2 * ROWS, 128), jnp.float32),
-            pltpu.VMEM((2 * ROWS, 128), jnp.float32),
+            pltpu.VMEM((2 * ROWS, 2 * HD), jnp.bfloat16),
+            pltpu.VMEM((SLOTS, CHUNK, 2 * HD), jnp.bfloat16),
+            pltpu.VMEM((2 * ROWS, 2 * HD), jnp.float32),
             pltpu.VMEM((2 * ROWS, HD), jnp.float32),
+            pltpu.VMEM((2 * HD + HP, DM), jnp.bfloat16),
+            pltpu.VMEM((ROWS, 2 * HD + HP), jnp.bfloat16),
+            pltpu.VMEM((ROWS, DM), jnp.bfloat16),
+            pltpu.SemaphoreType.DMA((SLOTS,)),
+            pltpu.SemaphoreType.DMA((2,)),
+            pltpu.SemaphoreType.DMA((DM // COLS,)),
         ],
         compiler_params=big(),
-        cost_estimate=pl.CostEstimate(flops=5 * 10**9, bytes_accessed=9 * 10**6, transcendentals=9 * 10**6),
-        name="attention",
-    )(lengths, first, queries, kv)
-
-    cols = 1280
-    whole = lambda *shape: pl.BlockSpec(shape, lambda i: (0,) * len(shape))
-    terms = pl.pallas_call(
-        proj_kernel,
-        out_shape=jax.ShapeDtypeStruct((ROWS, DM), jnp.bfloat16),
-        grid=(DM // cols,),
-        in_specs=[
-            whole(ROWS, 2 * HD),
-            whole(ROWS, HP),
-            whole(ROWS, HP),
-            pl.BlockSpec((ROWS, SN), lambda i: (0, 1)),
-            whole(ROWS, HEADS),
-            whole(STATE_ROWS, HP),
-            whole(STATE_ROWS, HP),
-            pl.BlockSpec((2 * HD, cols), lambda i: (0, i)),
-            pl.BlockSpec((HP, cols), lambda i: (0, i)),
-        ],
-        out_specs=pl.BlockSpec((ROWS, cols), lambda i: (0, i)),
-        scratch_shapes=[pltpu.VMEM((ROWS, 2 * HD + HP), jnp.bfloat16)],
-        compiler_params=big(),
-        cost_estimate=pl.CostEstimate(flops=4 * 10**9, bytes_accessed=16 * 10**6, transcendentals=10**6),
-        name="project",
-    )(attended, y_local, ssm_gates, ssm_maps, fac, far, nine, attn_out_weight, ssd_out_weight)
+        cost_estimate=pl.CostEstimate(flops=9 * 10**9, bytes_accessed=25 * 10**6, transcendentals=9 * 10**6),
+        name="mix",
+    )(lengths, first, queries, act, kv, attn_out_weight, ssd_out_weight)
     return lax.psum_scatter(terms, "tp", scatter_dimension=0, tiled=True)
 
 

time: 199 us -> 204 us (1.025)
  waiting for transfers between devices: 129 us -> 137 us
    all_gather x1, waiting for transfers between devices: 13.3 us -> 0.01 us  [local(): lax.all_gather(keys_values.reshape(ROWS, 2 * HD), 'pack', axis=0, tiled=T...]
    ppermute x6, waiting for transfers between devices: 21.9 us -> 33.6 us  [shifted(): lax.ppermute(block, 'pack', [(i, i + distance) for i in range(n - distanc...]
    reduce_scatter x1, waiting for transfers between devices: 92.8 us -> 102 us  [local(): return lax.psum_scatter(terms, 'tp', scatter_dimension=0, tiled=True)]
  transfers between devices with their start and end apart: 8 -> 8, of which waited for: 5 -> 5; matrix products, arithmetic and copies ran while one was open for 1% -> 1% of each run, Pallas kernels for 9% -> 7%
where the time goes in v2:
time: 204 us; the launch traced here: 206 us
  waiting for transfers between devices  137 us (67%)
  Pallas kernels  26.5 us (13%)
  starting transfers between devices  26 us (13%)
  between operations  13.5 us (7%)
  local copies, waits for them, and re-layouts  3.71 us (2%)
    reduce_scatter x1, waiting for transfers between devices, local(): return lax.psum_scatter(terms, 'tp', scatter_dimension=0, tiled=True)  102 us
    ppermute x6, waiting for transfers between devices, shifted(): lax.ppermute(block, 'pack', [(i, i + distance) for i in range(n - distanc...  33.6 us
    ppermute x6, starting transfers between devices, shifted(): lax.ppermute(block, 'pack', [(i, i + distance) for i in range(n - distanc...  26 us
    pallas_call x1, Pallas kernels, local(): pl.pallas_call(mix_kernel, out_shape=jax.ShapeDtypeStruct((ROWS, DM), jnp...  12.4 us
    pallas_call x1, Pallas kernels, local(): pl.pallas_call(ssd_kernel, out_shape=(jax.ShapeDtypeStruct((ROWS, HP), jn...  6.2 us
    pallas_call x2, Pallas kernels, join(): pl.pallas_call(join_kernel, out_shape=jax.ShapeDtypeStruct((STATE_ROWS, H...  4.08 us
  transfers between devices with their start and end apart: 8, of which 5 were waited for; matrix products, arithmetic and copies ran while one was open for 1% of the time, Pallas kernels for 7%

profile of v2, /device:TPU:1, one launch (start us, length us, event | category | flops | bytes accessed | tf_op | source)
XLA Modules:
  0.0 206.5 jit_solution(2887354038388497920)
XLA Ops:
  6.5 0.7 all-gather.3.cloned.1.call-update
  7.3 0.0 reduce-scatter.2.cloned.1.call-start
  7.3 1.6 copy.12.step_ref
  8.9 6.2 %ssd_local.1 = (f32[512,512]{1,0:T(8,128)}, bf16[272,512]{1,0:T(8,128)(2,1)}, f32[512,8]{1,0:T(8,128)}) custom-call(s32[4]{0:T(128)} %len_ref.3, f32[8]{0:T(128)} %dl_ref.1, f32[8]{0:T(128)} %skip_ref.1, s32[1]{0:T(128)} %bitcast.first_ref, bf16[512,512]{1,0:T(8,128)(2,1)} %x_ref.1, bf16[512,512]{1,0:T(8,128)(2,1)} %read_ref.1, f32[512,8]{1,0:T(8,128)} %copy.12.step_ref), custom_call_target="tpu_custom_call" | custom-call | flops 1000000000 | bytes 4000000 | tf_op jit(solution)/shard_map/ssd_local/pallas_call | solution.py:311
  15.1 4.6 %collective-permute-start.2 = (bf16[272,512]{1,0:T(8,128)(2,1)}, bf16[272,512]{1,0:T(8,128)(2,1)S(1)}, u32[]{:S(2)}, u32[]{:S(2)}) collective-permute-start(bf16[272,512]{1,0:T(8,128)(2,1)} %get-tuple-element.10), channel_id=1, source_target_pairs={{0,8},{8,16},{16,24},{24,32},{32,40},{40,48},{48,56},{56,64},{64,7... | collective-permute-start | bytes 835592 | tf_op jit(solution)/shard_map/ppermute | solution.py:282
  19.7 3.2 %collective-permute-start.1 = (bf16[272,512]{1,0:T(8,128)(2,1)}, bf16[272,512]{1,0:T(8,128)(2,1)S(1)}, u32[]{:S(2)}, u32[]{:S(2)}) collective-permute-start(bf16[272,512]{1,0:T(8,128)(2,1)} %get-tuple-element.10), channel_id=1, source_target_pairs={{0,16},{8,24},{16,32},{24,40},{32,48},{40,56},{48,64},{56,72},{64,... | collective-permute-start | bytes 835592 | tf_op jit(solution)/shard_map/ppermute | solution.py:282
  22.9 3.5 %collective-permute-start = (bf16[272,512]{1,0:T(8,128)(2,1)}, bf16[272,512]{1,0:T(8,128)(2,1)S(1)}, u32[]{:S(2)}, u32[]{:S(2)}) collective-permute-start(bf16[272,512]{1,0:T(8,128)(2,1)} %get-tuple-element.10), channel_id=1, source_target_pairs={{0,24},{8,32},{16,40},{24,48},{32,56},{40,64},{48,72},{56,80},{64,... | collective-permute-start | bytes 835592 | tf_op jit(solution)/shard_map/ppermute | solution.py:282
  26.4 4.8 %collective-permute-done.1.refs_1_ = bf16[272,512]{1,0:T(8,128)(2,1)S(1)} collective-permute-done((bf16[272,512]{1,0:T(8,128)(2,1)}, bf16[272,512]{1,0:T(8,128)(2,1)S(1)}, u32[]{:S(2)}, u32[]{:S(2)}) %collective-permute-start.1) | collective-permute-done | bytes 278560 | tf_op jit(solution)/shard_map/ppermute | solution.py:282
  31.2 7.3 %collective-permute-done.refs_0_ = bf16[272,512]{1,0:T(8,128)(2,1)S(1)} collective-permute-done((bf16[272,512]{1,0:T(8,128)(2,1)}, bf16[272,512]{1,0:T(8,128)(2,1)S(1)}, u32[]{:S(2)}, u32[]{:S(2)}) %collective-permute-start) | collective-permute-done | bytes 278560 | tf_op jit(solution)/shard_map/ppermute | solution.py:282
  38.6 0.7 copy-done.2
  39.3 2.0 shard_map.109.refs_2_
  41.3 5.9 %collective-permute-start.4 = (bf16[272,512]{1,0:T(8,128)(2,1)}, bf16[272,512]{1,0:T(8,128)(2,1)S(1)}, u32[]{:S(2)}, u32[]{:S(2)}) collective-permute-start(bf16[272,512]{1,0:T(8,128)(2,1)} %shard_map.109.refs_2_), channel_id=1, source_target_pairs={{0,24},{8,32},{16,40},{24,48},{32,56},{40,64},{48,72},{56,80},{64,... | collective-permute-start | bytes 835592 | tf_op jit(solution)/shard_map/ppermute | solution.py:282
  47.2 7.5 %collective-permute-start.3 = (bf16[272,512]{1,0:T(8,128)(2,1)}, bf16[272,512]{1,0:T(8,128)(2,1)S(1)}, u32[]{:S(2)}, u32[]{:S(2)}) collective-permute-start(bf16[272,512]{1,0:T(8,128)(2,1)} %shard_map.109.refs_2_), channel_id=1, source_target_pairs={{0,48},{8,56},{16,64},{24,72},{32,80},{40,88},{48,96},{56,104},{64... | collective-permute-start | bytes 835592 | tf_op jit(solution)/shard_map/ppermute | solution.py:282
  54.6 0.0 collective-permute-done.4.refs_1_
  54.6 9.7 %collective-permute-done.3.refs_0_ = bf16[272,512]{1,0:T(8,128)(2,1)S(1)} collective-permute-done((bf16[272,512]{1,0:T(8,128)(2,1)}, bf16[272,512]{1,0:T(8,128)(2,1)S(1)}, u32[]{:S(2)}, u32[]{:S(2)}) %collective-permute-start.3) | collective-permute-done | bytes 278560 | tf_op jit(solution)/shard_map/ppermute | solution.py:282
  64.4 0.7 copy-done.4
  65.1 2.1 %shard_map.110.near_ref = bf16[272,512]{1,0:T(8,128)(2,1)} custom-call(bf16[272,512]{1,0:T(8,128)(2,1)} %copy-done.4, bf16[272,512]{1,0:T(8,128)(2,1)} %copy-done.3, bf16[272,512]{1,0:T(8,128)(2,1)} %shard_map.109.refs_2_), custom_call_target="tpu_custom_call" | custom-call | tf_op jit(solution)/shard_map/pallas_call | solution.py:286
  67.2 1.3 collective-permute-start.5
  68.5 11.8 %collective-permute-done.5.far_ref = bf16[272,512]{1,0:T(8,128)(2,1)S(1)} collective-permute-done((bf16[272,512]{1,0:T(8,128)(2,1)}, bf16[272,512]{1,0:T(8,128)(2,1)S(1)}, u32[]{:S(2)}, u32[]{:S(2)}) %collective-permute-start.5) | collective-permute-done | bytes 278560 | tf_op jit(solution)/shard_map/ppermute | solution.py:282
  80.3 0.7 copy-done.5
  81.0 3.8 %gate.1.act_ref = bf16[512,512]{1,0:T(8,128)(2,1)} custom-call(f32[512,512]{1,0:T(8,128)} %get-tuple-element.8.y_ref, bf16[512,512]{1,0:T(8,128)(2,1)} %z_ref.1, bf16[512,512]{1,0:T(8,128)(2,1)} %read_ref.1, f32[512,8]{1,0:T(8,128)} %get-tuple-element.9.fac_ref, bf16[272,512]{1,0:T(8,128)(2,1)} %copy-done.5, bf16[272,512]{1,0:T(8,128)(2,1)} %shard_map.110.near_ref), custom_call_target="tpu_custom_call" | custom-call | flops 100000000 | bytes 3000000 | tf_op jit(solution)/shard_map/gate/pallas_call | solution.py:329
  84.8 12.4 %mix.1 = bf16[512,5120]{1,0:T(8,128)(2,1)} custom-call(s32[4]{0:T(128)} %len_ref.3, s32[1]{0:T(128)} %bitcast.first_ref, bf16[512,256]{1,0:T(8,128)(2,1)} %q_ref.1, bf16[512,512]{1,0:T(8,128)(2,1)} %gate.1.act_ref, bf16[16384,256]{1,0:T(8,128)(2,1)} %bitcast.2, bf16[256,5120]{1,0:T(8,128)(2,1)} %wa_hbm.1, bf16[512,5120]{1,0:T(8,128)(2,1)} %ws_hbm.1), custom_call_target="tpu_custom_call" | custom-call | flops 8999999488 | bytes 25000000 | tf_op jit(solution)/shard_map/mix/pallas_call | solution.py:347
  97.2 0.0 reduce-scatter.2.cloned.1.call-update
  97.2 102.4 %reduce-scatter.2.cloned.1.call-done = bf16[64,5120]{1,0:T(8,128)(2,1)} async-done(((bf16[512,5120]{1,0:T(8,128)(2,1)}), bf16[64,5120]{1,0:T(8,128)(2,1)}) %reduce-scatter.2.cloned.1.call-update) | async-done | bytes 655376 | tf_op jit(solution)/shard_map/reduce_scatter | solution.py:368
  (12 shorter events, 0.0 us)
Async XLA Ops:
  6.5 78.3 %all-gather.3.cloned.1.call-start = ((), (), s32[]{:S(2)}) async-start(), calls=%async_computation.2 | async-start | bytes 8650752 | tf_op jit(solution)/shard_map/all_gather | solution.py:309
  7.3 192.4 %reduce-scatter.2.cloned.1.call-start = ((), (), s32[]{:S(2)}) async-start(), calls=%async_computation.1 | async-start | bytes 5898240 | tf_op jit(solution)/shard_map/reduce_scatter | solution.py:368
  15.1 11.4 %collective-permute-start.2 = (bf16[272,512]{1,0:T(8,128)(2,1)}, bf16[272,512]{1,0:T(8,128)(2,1)S(1)}, u32[]{:S(2)}, u32[]{:S(2)}) collective-permute-start(bf16[272,512]{1,0:T(8,128)(2,1)} %get-tuple-element.10), channel_id=1, source_target_pairs={{0,8},{8,16},{16,24},{24,32},{32,40},{40,48},{48,56},{56,64},{64,7... | collective-permute-start | bytes 835592 | tf_op jit(solution)/shard_map/ppermute | solution.py:282
  19.7 11.6 %collective-permute-start.1 = (bf16[272,512]{1,0:T(8,128)(2,1)}, bf16[272,512]{1,0:T(8,128)(2,1)S(1)}, u32[]{:S(2)}, u32[]{:S(2)}) collective-permute-start(bf16[272,512]{1,0:T(8,128)(2,1)} %get-tuple-element.10), channel_id=1, source_target_pairs={{0,16},{8,24},{16,32},{24,40},{32,48},{40,56},{48,64},{56,72},{64,... | collective-permute-start | bytes 835592 | tf_op jit(solution)/shard_map/ppermute | solution.py:282
  22.9 15.7 %collective-permute-start = (bf16[272,512]{1,0:T(8,128)(2,1)}, bf16[272,512]{1,0:T(8,128)(2,1)S(1)}, u32[]{:S(2)}, u32[]{:S(2)}) collective-permute-start(bf16[272,512]{1,0:T(8,128)(2,1)} %get-tuple-element.10), channel_id=1, source_target_pairs={{0,24},{8,32},{16,40},{24,48},{32,56},{40,64},{48,72},{56,80},{64,... | collective-permute-start | bytes 835592 | tf_op jit(solution)/shard_map/ppermute | solution.py:282
  26.4 12.1 %copy-start = (bf16[272,512]{1,0:T(8,128)(2,1)}, bf16[272,512]{1,0:T(8,128)(2,1)S(1)}, u32[]{:S(2)}) copy-start(bf16[272,512]{1,0:T(8,128)(2,1)S(1)} %collective-permute-done.2.refs_2_) | copy-start | bytes 835588
  31.2 7.3 %copy-start.1 = (bf16[272,512]{1,0:T(8,128)(2,1)}, bf16[272,512]{1,0:T(8,128)(2,1)S(1)}, u32[]{:S(2)}) copy-start(bf16[272,512]{1,0:T(8,128)(2,1)S(1)} %collective-permute-done.1.refs_1_) | copy-start | bytes 835588
  38.6 0.7 copy-start.2
  41.3 13.4 %collective-permute-start.4 = (bf16[272,512]{1,0:T(8,128)(2,1)}, bf16[272,512]{1,0:T(8,128)(2,1)S(1)}, u32[]{:S(2)}, u32[]{:S(2)}) collective-permute-start(bf16[272,512]{1,0:T(8,128)(2,1)} %shard_map.109.refs_2_), channel_id=1, source_target_pairs={{0,24},{8,32},{16,40},{24,48},{32,56},{40,64},{48,72},{56,80},{64,... | collective-permute-start | bytes 835592 | tf_op jit(solution)/shard_map/ppermute | solution.py:282
  47.2 17.2 %collective-permute-start.3 = (bf16[272,512]{1,0:T(8,128)(2,1)}, bf16[272,512]{1,0:T(8,128)(2,1)S(1)}, u32[]{:S(2)}, u32[]{:S(2)}) collective-permute-start(bf16[272,512]{1,0:T(8,128)(2,1)} %shard_map.109.refs_2_), channel_id=1, source_target_pairs={{0,48},{8,56},{16,64},{24,72},{32,80},{40,88},{48,96},{56,104},{64... | collective-permute-start | bytes 835592 | tf_op jit(solution)/shard_map/ppermute | solution.py:282
  54.6 9.8 %copy-start.3 = (bf16[272,512]{1,0:T(8,128)(2,1)}, bf16[272,512]{1,0:T(8,128)(2,1)S(1)}, u32[]{:S(2)}) copy-start(bf16[272,512]{1,0:T(8,128)(2,1)S(1)} %collective-permute-done.4.refs_1_) | copy-start | bytes 835588
  64.4 0.7 copy-start.4
  67.2 13.1 %collective-permute-start.5 = (bf16[272,512]{1,0:T(8,128)(2,1)}, bf16[272,512]{1,0:T(8,128)(2,1)S(1)}, u32[]{:S(2)}, u32[]{:S(2)}) collective-permute-start(bf16[272,512]{1,0:T(8,128)(2,1)} %shard_map.110.near_ref), channel_id=1, source_target_pairs={{0,72},{8,80},{16,88},{24,96},{32,104},{40,112},{48,120},{56,128},... | collective-permute-start | bytes 835592 | tf_op jit(solution)/shard_map/ppermute | solution.py:282
  80.3 0.7 copy-start.5
Sparse Core Ops, SparseCore 0:
  9.9 71.8 all-gather.2
  97.4 102.2 reduce-scatter.1

commit v3 on v2

--- a/solution.py
+++ b/solution.py
@@ -19,7 +19,11 @@
 LOW = -1e30
 LOG2E = 1.4426950408889634
 HIGH = lax.Precision.HIGHEST
+HALF = HP // 2
 STATE_ROWS = SN + 16
+Y_OFF = (0, 3, 1, 2)
+ROW_OF_GROUP = (0, 1, 99, 2)
+ROW_OF_SLOT = (0, 1, 3, 2)
 VMEM = pl.BlockSpec(memory_space=pltpu.VMEM)
 SMEM = pl.BlockSpec(memory_space=pltpu.SMEM)
 ANY = pl.BlockSpec(memory_space=pl.ANY)
@@ -51,16 +55,16 @@
     return jnp.dot(a, expand, precision=HIGH, preferred_element_type=jnp.float32)
 
 
-def ssd_kernel(len_ref, dl_ref, skip_ref, first_ref, x_ref, maps_ref, step_ref, y_ref, st_ref, fac_ref):
+def ssd_kernel(len_ref, dl_ref, skip_ref, first_ref, x_ref, maps_ref, step_ref, y_ref, keep_ref, send_ref, fac_ref):
     first = first_ref[0]
     ends = ends_of(len_ref)
     expand = spread()
-    head_lane = iota((1, HEADS), 1)
+    head_sub = iota((HEADS, 1), 0)
     wide_lane = iota((1, HP), 1) // (HP // HEADS)
-    rate = jnp.zeros((1, HEADS), jnp.float32)
+    rate = jnp.zeros((HEADS, 1), jnp.float32)
     skip = jnp.zeros((1, HP), jnp.float32)
     for h in range(HEADS):
-        rate = jnp.where(head_lane == h, dl_ref[h], rate)
+        rate = jnp.where(head_sub == h, dl_ref[h], rate)
         skip = jnp.where(wide_lane == h, skip_ref[h], skip)
     rate = -jnp.exp(rate)
     row = iota((BLOCK, 1), 0)
@@ -74,8 +78,10 @@
         base = first + n * BLOCK
         start_col = start_of(base + row, ends)
         last_start = start_of(base + (BLOCK - 1), ends)
-        cum = jnp.dot(tri, rate * step_ref[rows, :], precision=HIGH, preferred_element_type=jnp.float32)
-        cum_t = cum.T
+        cum_t = lax.dot_general(
+            rate * step_ref[:, rows], tri, (((1,), (1,)), ((), ())), precision=HIGH, preferred_element_type=jnp.float32
+        )
+        cum = cum_t.T
         write = maps_ref[rows, :SN]
         read = maps_ref[rows, SN:]
         prod = lax.dot_general(read, write, (((1,), (1,)), ((), ())), preferred_element_type=jnp.float32)
@@ -112,38 +118,74 @@
         state = new
         before = end[7:8, :]
     through = jnp.where(last_start < first, 1.0, 0.0) * widen(end, expand)[7:8, :]
-    st_ref[:SN, :] = state.astype(jnp.bfloat16)
-    store_through(st_ref, through)
-
-
-def store_through(ref, through):
+    core = (first // ROWS) % 2
+    left, right = slice(0, HALF), slice(HALF, HP)
+    for ref, wanted in ((keep_ref, 0), (send_ref, 1)):
+        store_run(
+            ref,
+            jnp.where(core == wanted, state[:, left], state[:, right]),
+            jnp.where(core == wanted, through[:, left], through[:, right]),
+        )
+
+
+def store_run(ref, state, through):
     high = through.astype(jnp.bfloat16).astype(jnp.float32)
     low = through - high
     sub = iota((16, 1), 0)
+    ref[:SN, :] = state.astype(jnp.bfloat16)
     ref[SN:, :] = jnp.where(sub == 0, high, jnp.where(sub == 1, low, 0.0)).astype(jnp.bfloat16)
 
 
-def through_of(ref):
+def load_run(ref):
     tail = ref[SN:, :].astype(jnp.float32)
-    return tail[0:1, :] + tail[1:2, :]
-
-
-def join_kernel(*refs):
-    out = refs[-1]
-    state = refs[0][:SN, :].astype(jnp.float32)
-    through = through_of(refs[0])
-    for ref in refs[1:-1]:
-        t = through_of(ref)
-        state = ref[:SN, :].astype(jnp.float32) + t * state
-        through = through * t
-    out[:SN, :] = state.astype(jnp.bfloat16)
-    store_through(out, through)
-
-
-def gate_kernel(y_ref, z_ref, read_ref, fac_ref, far_ref, near_ref, act_ref):
-    state = near_ref[:SN, :].astype(jnp.float32)
-    state = state + through_of(near_ref) * far_ref[:SN, :].astype(jnp.float32)
-    reads = jnp.dot(read_ref[...], state.astype(jnp.bfloat16), preferred_element_type=jnp.float32)
+    return ref[:SN, :].astype(jnp.float32), tail[0:1, :] + tail[1:2, :]
+
+
+def pick(cond, one, other):
+    return jnp.where(cond, one[0], other[0]), jnp.where(cond, one[1], other[1])
+
+
+def after(earlier, later):
+    return later[0] + later[1] * earlier[0], earlier[1] * later[1]
+
+
+def chip_kernel(first_ref, mine_ref, other_ref, out_ref):
+    core = (first_ref[0] // ROWS) % 2
+    mine, other = load_run(mine_ref), load_run(other_ref)
+    store_run(out_ref, *after(pick(core == 0, mine, other), pick(core == 0, other, mine)))
+
+
+def row_kernel(first_ref, mine_ref, below_ref, above_ref, across_ref, prefix_ref, total_ref):
+    y = (first_ref[0] // (2 * ROWS)) % 4
+    by_distance = [load_run(ref) for ref in (mine_ref, below_ref, across_ref, above_ref)]
+    run = (jnp.zeros((SN, HALF), jnp.float32), jnp.ones((1, HALF), jnp.float32))
+    prefix = run
+    for place in range(4):
+        distance = (y - place) % 4
+        piece = by_distance[0]
+        for d in range(1, 4):
+            piece = pick(distance == d, by_distance[d], piece)
+        prefix = pick(y == place, run, prefix)
+        run = after(run, piece)
+    store_run(prefix_ref, *prefix)
+    store_run(total_ref, *run)
+
+
+def carry_kernel(first_ref, row3_ref, row2_ref, row1_ref, prefix_ref, mine_ref, other_ref, keep_ref, send_ref):
+    core = (first_ref[0] // ROWS) % 2
+    run = load_run(row3_ref)
+    for ref in (row2_ref, row1_ref, prefix_ref):
+        run = after(run, load_run(ref))
+    behind = after(run, pick(core == 0, load_run(mine_ref), load_run(other_ref)))
+    keep_ref[...] = jnp.where(core == 0, run[0], behind[0]).astype(jnp.bfloat16)
+    send_ref[...] = jnp.where(core == 0, behind[0], run[0]).astype(jnp.bfloat16)
+
+
+def gate_kernel(first_ref, y_ref, z_ref, maps_ref, fac_ref, keep_ref, got_ref, act_ref):
+    core = (first_ref[0] // ROWS) % 2
+    keep, got = keep_ref[...], got_ref[...]
+    state = jnp.concatenate([jnp.where(core == 0, keep, got), jnp.where(core == 0, got, keep)], axis=1)
+    reads = jnp.dot(maps_ref[:, SN:], state, preferred_element_type=jnp.float32)
     y = y_ref[...] + reads * widen(fac_ref[...], spread())
     z = z_ref[...].astype(jnp.float32)
     act_ref[...] = (y * (z / (1.0 + jnp.exp(-z)))).astype(jnp.bfloat16)
@@ -154,7 +196,14 @@
     first_ref,
     q_ref,
     act_ref,
-    kv_hbm,
+    g0,
+    g1,
+    g2,
+    g3,
+    h0,
+    h1,
+    h2,
+    h3,
     wa_hbm,
     ws_hbm,
     o_hbm,
@@ -165,6 +214,7 @@
     w_scr,
     in_scr,
     o_scr,
+    ids,
     kv_sem,
     w_sem,
     o_sem,
@@ -174,16 +224,36 @@
     mine = first // CHUNK
     low = start_of(first, ends) // CHUNK
     last_start = start_of(first + ROWS - 1, ends)
-    count = mine - low + 1
+    x, y, core = mine // 8, (mine // 2) % 4, mine % 2
+
+    def kv_copy(src, slot, i):
+        return pltpu.make_async_copy(src.at[pl.ds(slot * CHUNK, CHUNK)], kv_scr.at[i], kv_sem.at[i])
+
+    ids[0] = mine
+    kv_copy(g0, 0, 0).start()
+    count = jnp.int32(1)
+    for which, group in enumerate((g0, g1, g2, g3, h0, h1, h2, h3)):
+        odd = (core + which // 4) % 2 == 1
+        for slot in range(4):
+            if which == 0 and slot == 0:
+                continue
+            even_x = x - ROW_OF_GROUP[which % 4]
+            odd_x = x - ROW_OF_SLOT[slot]
+            row = jnp.where(odd, odd_x, even_x)
+            place = jnp.where(odd, (y + Y_OFF[which % 4]) % 4, (y + Y_OFF[slot]) % 4)
+            block = row * 8 + place * 2 + odd.astype(jnp.int32)
+            needed = (row >= 0) & (block >= low) & (block < mine)
+
+            @pl.when(needed)
+            def _(group=group, slot=slot, block=block, count=count):
+                ids[count] = block
+                kv_copy(group, slot, count).start()
+
+            count = count + needed.astype(jnp.int32)
 
     def chunk_of(i):
-        return jnp.where(i == 0, mine, low + i - 1)
-
-    def kv_copy(i):
-        rows = pl.ds(pl.multiple_of(chunk_of(i) * CHUNK, CHUNK), CHUNK)
-        return pltpu.make_async_copy(kv_hbm.at[rows], kv_scr.at[i], kv_sem.at[i])
-
-    lax.fori_loop(0, count, lambda i, _: (kv_copy(i).start(), 0)[1], 0)
+        return ids[i]
+
     weights = [
         pltpu.make_async_copy(wa_hbm, w_scr.at[pl.ds(0, 2 * HD)], w_sem.at[0]),
         pltpu.make_async_copy(ws_hbm, w_scr.at[pl.ds(2 * HD, HP)], w_sem.at[1]),
@@ -235,7 +305,7 @@
     def over_chunks(step, wait):
         def one_chunk(i, _):
             if wait:
-                kv_copy(i).wait()
+                kv_copy(g0, 0, i).wait()
             masked = (i == 0) | (chunk_of(i) * CHUNK < last_start)
             pl.when(masked)(lambda: step(i, True))
             pl.when(jnp.logical_not(masked))(lambda: step(i, False))
@@ -277,19 +347,38 @@
     return pltpu.CompilerParams(vmem_limit_bytes=56 * 2**20, **more)
 
 
-def shifted(block, distance):
-    n = lax.axis_size("pack")
-    return lax.ppermute(block, "pack", [(i, i + distance) for i in range(n - distance)])
-
-
-def join(*runs):
+def moved(block, route0, route1):
+    pairs = []
+    for x in range(4):
+        for y in range(4):
+            for core, route in enumerate((route0, route1)):
+                to = route(x, y)
+                if to is not None:
+                    pairs.append((x * 8 + y * 2 + core, to[0] * 8 + to[1] * 2 + core))
+    return lax.ppermute(block, "pack", pairs)
+
+
+def along_x(distance):
+    return lambda x, y: (x + distance, y) if x + distance < 4 else None
+
+
+def along_y(distance):
+    return lambda x, y: (x, (y + distance) % 4)
+
+
+def swapped(block):
+    return lax.ppermute(block, "pack", [(i, i ^ 1) for i in range(32)])
+
+
+def call(kernel, shapes, ins, *args):
     return pl.pallas_call(
-        join_kernel,
-        out_shape=jax.ShapeDtypeStruct((STATE_ROWS, HP), jnp.bfloat16),
-        in_specs=[VMEM] * len(runs),
-        out_specs=VMEM,
+        kernel,
+        out_shape=tuple(jax.ShapeDtypeStruct(shape, jnp.bfloat16) for shape in shapes),
+        in_specs=[SMEM] + [VMEM] * ins,
+        out_specs=(VMEM,) * len(shapes),
         compiler_params=big(),
-    )(*runs)
+        cost_estimate=pl.CostEstimate(flops=10**6, bytes_accessed=10**6, transcendentals=0),
+    )(*args)
 
 
 def local(
@@ -306,48 +395,59 @@
     lengths,
 ):
     first = jnp.reshape(lax.axis_index("pack") * ROWS, (1,)).astype(jnp.int32)
-    kv = lax.all_gather(keys_values.reshape(ROWS, 2 * HD), "pack", axis=0, tiled=True)
-
-    y_local, summary, fac = pl.pallas_call(
+    kv = keys_values.reshape(ROWS, 2 * HD)
+    nowhere = lambda x, y: None
+    below = moved(kv, along_y(1), along_x(1))
+    above = moved(kv, along_y(3), along_x(3))
+    across = moved(kv, along_y(2), along_x(2))
+
+    y_local, run_keep, run_send, fac = pl.pallas_call(
         ssd_kernel,
         out_shape=(
             jax.ShapeDtypeStruct((ROWS, HP), jnp.float32),
-            jax.ShapeDtypeStruct((STATE_ROWS, HP), jnp.bfloat16),
+            jax.ShapeDtypeStruct((STATE_ROWS, HALF), jnp.bfloat16),
+            jax.ShapeDtypeStruct((STATE_ROWS, HALF), jnp.bfloat16),
             jax.ShapeDtypeStruct((ROWS, HEADS), jnp.float32),
         ),
         in_specs=[SMEM] * 4 + [VMEM] * 3,
-        out_specs=(VMEM, VMEM, VMEM),
+        out_specs=(VMEM, VMEM, VMEM, VMEM),
         compiler_params=big(),
         cost_estimate=pl.CostEstimate(flops=10**9, bytes_accessed=4 * 10**6, transcendentals=10**6),
         name="ssd_local",
-    )(lengths, decay_log, skip_gain, first, ssm_values, ssm_maps, step_size)
-
-    three = join(shifted(summary, 3), shifted(summary, 2), shifted(summary, 1))
-    nine = join(shifted(three, 6), shifted(three, 3), three)
-    far = shifted(nine, 9)
-
+    )(lengths, decay_log, skip_gain, first, ssm_values, ssm_maps, step_size.T)
+
+    below, above, across = lax.optimization_barrier((below, above, across, fac))[:3]
+    group = jnp.concatenate([kv, below, above, across], axis=0)
+    groups = [
+        group,
+        moved(group, along_x(1), along_y(1)),
+        moved(group, nowhere, along_y(3)),
+        moved(group, along_x(2), along_y(2)),
+    ]
+    run = (STATE_ROWS, HALF)
+    run_got = swapped(run_send)
+    (chip,) = call(chip_kernel, [run], 2, first, run_keep, run_got)
+    chips = [moved(chip, along_y(d), along_y(d)) for d in (1, 3, 2)]
+    prefix, total = call(row_kernel, [run, run], 4, first, chip, *chips)
+    rows = [moved(total, along_x(d), along_x(d)) for d in (3, 2, 1)]
+    groups = [groups[0], *lax.optimization_barrier((*groups[1:], *rows))[:3]]
+    groups = groups + [swapped(g) for g in groups]
+    keep, send = call(carry_kernel, [(SN, HALF)] * 2, 6, first, *rows, prefix, run_keep, run_got)
+    got = swapped(send)
     act = pl.pallas_call(
         gate_kernel,
         out_shape=jax.ShapeDtypeStruct((ROWS, HP), jnp.bfloat16),
-        grid=(1,),
-        in_specs=[
-            pl.BlockSpec((ROWS, HP), lambda i: (0, 0)),
-            pl.BlockSpec((ROWS, HP), lambda i: (0, 0)),
-            pl.BlockSpec((ROWS, SN), lambda i: (0, 1)),
-            pl.BlockSpec((ROWS, HEADS), lambda i: (0, 0)),
-            pl.BlockSpec((STATE_ROWS, HP), lambda i: (0, 0)),
-            pl.BlockSpec((STATE_ROWS, HP), lambda i: (0, 0)),
-        ],
-        out_specs=pl.BlockSpec((ROWS, HP), lambda i: (0, 0)),
+        in_specs=[SMEM] + [VMEM] * 6,
+        out_specs=VMEM,
         compiler_params=big(),
         cost_estimate=pl.CostEstimate(flops=10**8, bytes_accessed=3 * 10**6, transcendentals=3 * 10**5),
         name="gate",
-    )(y_local, ssm_gates, ssm_maps, fac, far, nine)
+    )(first, y_local, ssm_gates, ssm_maps, fac, keep, got)
 
     terms = pl.pallas_call(
         mix_kernel,
         out_shape=jax.ShapeDtypeStruct((ROWS, DM), jnp.bfloat16),
-        in_specs=[SMEM] * 2 + [VMEM] * 2 + [ANY] * 3,
+        in_specs=[SMEM] * 2 + [VMEM] * 2 + [ANY] * 10,
         out_specs=ANY,
         scratch_shapes=[
             pltpu.VMEM((2 * ROWS, 2 * HD), jnp.bfloat16),
@@ -357,6 +457,7 @@
             pltpu.VMEM((2 * HD + HP, DM), jnp.bfloat16),
             pltpu.VMEM((ROWS, 2 * HD + HP), jnp.bfloat16),
             pltpu.VMEM((ROWS, DM), jnp.bfloat16),
+            pltpu.SMEM((SLOTS,), jnp.int32),
             pltpu.SemaphoreType.DMA((SLOTS,)),
             pltpu.SemaphoreType.DMA((2,)),
             pltpu.SemaphoreType.DMA((DM // COLS,)),
@@ -364,7 +465,7 @@
         compiler_params=big(),
         cost_estimate=pl.CostEstimate(flops=9 * 10**9, bytes_accessed=25 * 10**6, transcendentals=9 * 10**6),
         name="mix",
-    )(lengths, first, queries, act, kv, attn_out_weight, ssd_out_weight)
+    )(lengths, first, queries, act, *groups, attn_out_weight, ssd_out_weight)
     return lax.psum_scatter(terms, "tp", scatter_dimension=0, tiled=True)
 
 

time: 204 us -> 205 us (level); the launches traced: 206 us -> 203 us
  waiting for transfers between devices: 137 us -> 111 us
  starting transfers between devices: 26 us -> 47.1 us
    ppermute x6 -> x18, starting transfers between devices: 26 us -> 47.1 us  [the longest x12 28.3 us: moved(): return lax.ppermute(block, 'pack', pairs)]
    ppermute x6 -> x18, waiting for transfers between devices: 33.6 us -> 16.3 us  [the longest x12 12.6 us: moved(): return lax.ppermute(block, 'pack', pairs)]
    reduce_scatter x1, waiting for transfers between devices: 102 us -> 94.3 us  [local(): return lax.psum_scatter(terms, 'tp', scatter_dimension=0, tiled=True)]
    pallas_call x2 -> x3, Pallas kernels: 4.08 us -> 5.81 us  [call(): pl.pallas_call(kernel, out_shape=tuple((jax.ShapeDtypeStruct(shape, jnp.b...]
  transfers between devices with their start and end apart: 8 -> 19, of which waited for: 5 -> 7; matrix products, arithmetic and copies ran while one was open for 1% -> 0% of each run, Pallas kernels for 7% -> 8%
where the time goes in v3:
time: 205 us; the launch traced here: 203 us
  waiting for transfers between devices  111 us (54%)
  starting transfers between devices  47.1 us (23%)
  Pallas kernels  27.9 us (14%)
  between operations  13.7 us (7%)
  local copies, waits for them, and re-layouts  3.7 us (2%)
    reduce_scatter x1, waiting for transfers between devices, local(): return lax.psum_scatter(terms, 'tp', scatter_dimension=0, tiled=True)  94.3 us
    ppermute x12, starting transfers between devices, moved(): return lax.ppermute(block, 'pack', pairs)  28.3 us
    ppermute x6, starting transfers between devices, swapped(): return lax.ppermute(block, 'pack', [(i, i ^ 1) for i in range(32)])  18.9 us
    ppermute x12, waiting for transfers between devices, moved(): return lax.ppermute(block, 'pack', pairs)  12.6 us
    pallas_call x1, Pallas kernels, local(): pl.pallas_call(mix_kernel, out_shape=jax.ShapeDtypeStruct((ROWS, DM), jnp...  12.1 us
    pallas_call x1, Pallas kernels, local(): pl.pallas_call(ssd_kernel, out_shape=(jax.ShapeDtypeStruct((ROWS, HP), jn...  6.23 us
    pallas_call x3, Pallas kernels, call(): pl.pallas_call(kernel, out_shape=tuple((jax.ShapeDtypeStruct(shape, jnp.b...  5.81 us
  transfers between devices with their start and end apart: 19, of which 7 were waited for; matrix products, arithmetic and copies ran while one was open for 0% of the time, Pallas kernels for 8%

profile of v3, /device:TPU:1, one launch (start us, length us, event | category | flops | bytes accessed | tf_op | source)
XLA Modules:
  0.0 203.1 jit_solution(2848309259928422182)
XLA Ops:
  6.5 5.6 %collective-permute-start.10 = (bf16[512,256]{1,0:T(8,128)(2,1)}, bf16[512,256]{1,0:T(8,128)(2,1)S(1)}, u32[]{:S(2)}, u32[]{:S(2)}) collective-permute-start(bf16[512,256]{1,0:T(8,128)(2,1)} %bitcast.3), channel_id=1, source_target_pairs={{0,32},{8,136},{16,48},{24,152},{32,0},{40,168},{48,16},{56,184},{... | collective-permute-start | bytes 786440 | tf_op jit(solution)/shard_map/ppermute | solution.py:358
  12.2 1.3 collective-permute-start.9
  13.5 1.6 collective-permute-start.8
  15.1 6.2 %ssd_local.1 = (f32[512,512]{1,0:T(8,128)}, bf16[272,256]{1,0:T(8,128)(2,1)}, bf16[272,256]{1,0:T(8,128)(2,1)}, f32[512,8]{1,0:T(8,128)}) custom-call(s32[4]{0:T(128)} %len_ref.3, f32[8]{0:T(128)} %dl_ref.1, f32[8]{0:T(128)} %skip_ref.1, s32[1]{0:T(128)} %bitcast.first_ref, bf16[512,512]{1,0:T(8,128)(2,1)} %x_ref.1, bf16[512,512]{1,0:T(8,128)(2,1)} %maps_ref.3, ...), custom_call_target="tpu_custom_call" | custom-call | flops 1000000000 | bytes 4000000 | tf_op jit(solution)/shard_map/ssd_local/pallas_call | solution.py:404
  21.5 4.8 %collective-permute-start.13 = (bf16[2048,256]{1,0:T(8,128)(2,1)S(1)}, bf16[2048,256]{1,0:T(8,128)(2,1)S(1)}, u32[]{:S(2)}, u32[]{:S(2)}) collective-permute-start(bf16[2048,256]{1,0:T(8,128)(2,1)S(1)} %pad_maximum_fusion.g0), channel_id=1, source_target_pairs={{0,128},{8,40},{16,144},{24,56},{32,160},{40,8},{48,176},{56,24},{... | collective-permute-start | bytes 3145736 | tf_op jit(solution)/shard_map/ppermute | solution.py:358
  26.3 2.7 %collective-permute-start.12 = (bf16[2048,256]{1,0:T(8,128)(2,1)S(1)}, bf16[2048,256]{1,0:T(8,128)(2,1)S(1)}, u32[]{:S(2)}, u32[]{:S(2)}) collective-permute-start(bf16[2048,256]{1,0:T(8,128)(2,1)S(1)} %pad_maximum_fusion.g0), channel_id=1, source_target_pairs={{8,56},{24,8},{40,24},{56,40},{72,120},{88,72},{104,88},{120,104},... | collective-permute-start | bytes 3145736 | tf_op jit(solution)/shard_map/ppermute | solution.py:358
  29.0 2.6 %collective-permute-start.11 = (bf16[2048,256]{1,0:T(8,128)(2,1)S(1)}, bf16[2048,256]{1,0:T(8,128)(2,1)S(1)}, u32[]{:S(2)}, u32[]{:S(2)}) collective-permute-start(bf16[2048,256]{1,0:T(8,128)(2,1)S(1)} %pad_maximum_fusion.g0), channel_id=1, source_target_pairs={{0,64},{8,24},{16,80},{24,40},{32,96},{40,56},{48,112},{56,8},{64,... | collective-permute-start | bytes 3145736 | tf_op jit(solution)/shard_map/ppermute | solution.py:358
  31.6 14.1 %collective-permute-start = (bf16[272,256]{1,0:T(8,128)(2,1)S(1)}, bf16[272,256]{1,0:T(8,128)(2,1)S(1)}, u32[]{:S(2)}, u32[]{:S(2)}) collective-permute-start(bf16[272,256]{1,0:T(8,128)(2,1)S(1)} %copy-done.16), channel_id=1, source_target_pairs={{0,8},{8,0},{16,24},{24,16},{32,40},{40,32},{48,56},{56,48},{64,72... | collective-permute-start | bytes 417800 | tf_op jit(solution)/shard_map/ppermute | solution.py:370
  45.7 1.0 collective-permute-done.other_ref
  47.4 1.7 shard_map.109.mine_ref
  49.1 6.6 %collective-permute-done.3.across_ref = bf16[272,256]{1,0:T(8,128)(2,1)S(1)} collective-permute-done((bf16[272,256]{1,0:T(8,128)(2,1)}, bf16[272,256]{1,0:T(8,128)(2,1)S(1)}, u32[]{:S(2)}, u32[]{:S(2)}) %collective-permute-start.3) | collective-permute-done | bytes 139296 | tf_op jit(solution)/shard_map/ppermute | solution.py:358
  56.4 4.6 %collective-permute-done.1.below_ref = bf16[272,256]{1,0:T(8,128)(2,1)S(1)} collective-permute-done((bf16[272,256]{1,0:T(8,128)(2,1)}, bf16[272,256]{1,0:T(8,128)(2,1)S(1)}, u32[]{:S(2)}, u32[]{:S(2)}) %collective-permute-start.1) | collective-permute-done | bytes 139296 | tf_op jit(solution)/shard_map/ppermute | solution.py:358
  61.7 2.0 %shard_map.110 = (bf16[272,256]{1,0:T(8,128)(2,1)}, bf16[272,256]{1,0:T(8,128)(2,1)}) custom-call(s32[1]{0:T(128)} %bitcast.first_ref, bf16[272,256]{1,0:T(8,128)(2,1)} %shard_map.109.mine_ref, bf16[272,256]{1,0:T(8,128)(2,1)} %copy-done.8, bf16[272,256]{1,0:T(8,128)(2,1)} %copy-done.7, bf16[272,256]{1,0:T(8,128)(2,1)} %copy-done.6), custom_call_target="tpu_custom_call" | custom-call | flops 1000000 | bytes 1000000 | tf_op jit(solution)/shard_map/pallas_call | solution.py:374
  63.7 1.6 collective-permute-start.6
  65.3 4.2 %collective-permute-start.5 = (bf16[272,256]{1,0:T(8,128)(2,1)}, bf16[272,256]{1,0:T(8,128)(2,1)S(1)}, u32[]{:S(2)}, u32[]{:S(2)}) collective-permute-start(bf16[272,256]{1,0:T(8,128)(2,1)} %get-tuple-element.23), channel_id=1, source_target_pairs={{0,128},{8,136},{16,144},{24,152},{32,160},{40,168},{48,176},{56,1... | collective-permute-start | bytes 417800 | tf_op jit(solution)/shard_map/ppermute | solution.py:358
  69.5 3.8 %collective-permute-start.4 = (bf16[272,256]{1,0:T(8,128)(2,1)}, bf16[272,256]{1,0:T(8,128)(2,1)S(1)}, u32[]{:S(2)}, u32[]{:S(2)}) collective-permute-start(bf16[272,256]{1,0:T(8,128)(2,1)} %get-tuple-element.23), channel_id=1, source_target_pairs={{0,192},{8,200},{16,208},{24,216},{32,224},{40,232},{48,240},{56,2... | collective-permute-start | bytes 417800 | tf_op jit(solution)/shard_map/ppermute | solution.py:358
  73.4 1.6 collective-permute-start.14
  75.7 2.2 %collective-permute-start.15 = (bf16[2048,256]{1,0:T(8,128)(2,1)S(1)}, bf16[2048,256]{1,0:T(8,128)(2,1)S(1)}, u32[]{:S(2)}, u32[]{:S(2)}) collective-permute-start(bf16[2048,256]{1,0:T(8,128)(2,1)S(1)} %collective-permute-done.11.g1), channel_id=1, source_target_pairs={{0,8},{8,0},{16,24},{24,16},{32,40},{40,32},{48,56},{56,48},{64,72... | collective-permute-start | bytes 3145736 | tf_op jit(solution)/shard_map/ppermute | solution.py:370
  78.4 2.1 %shard_map.111 = (bf16[256,256]{1,0:T(8,128)(2,1)}, bf16[256,256]{1,0:T(8,128)(2,1)}) custom-call(s32[1]{0:T(128)} %bitcast.first_ref, bf16[272,256]{1,0:T(8,128)(2,1)} %copy-done.5, bf16[272,256]{1,0:T(8,128)(2,1)} %copy-done.4, bf16[272,256]{1,0:T(8,128)(2,1)} %copy-done.3, bf16[272,256]{1,0:T(8,128)(2,1)} %get-tuple-element.24.prefix_ref, ...), custom_call_target="tpu_custom_call" | custom-call | flops 1000000 | bytes 1000000 | tf_op jit(solution)/shard_map/pallas_call | solution.py:374
  81.0 2.6 %collective-permute-done.7.got_ref = bf16[256,256]{1,0:T(8,128)(2,1)S(1)} collective-permute-done((bf16[256,256]{1,0:T(8,128)(2,1)}, bf16[256,256]{1,0:T(8,128)(2,1)S(1)}, u32[]{:S(2)}, u32[]{:S(2)}) %collective-permute-start.7) | collective-permute-done | bytes 131104 | tf_op jit(solution)/shard_map/ppermute | solution.py:370
  84.3 3.7 %gate.1.act_ref = bf16[512,512]{1,0:T(8,128)(2,1)} custom-call(s32[1]{0:T(128)} %bitcast.first_ref, f32[512,512]{1,0:T(8,128)} %get-tuple-element.19.y_ref, bf16[512,512]{1,0:T(8,128)(2,1)} %z_ref.1, bf16[512,512]{1,0:T(8,128)(2,1)} %maps_ref.3, f32[512,8]{1,0:T(8,128)} %get-tuple-element.20.fac_ref, bf16[256,256]{1,0:T(8,128)(2,1)} %get-tuple-element.25.keep_ref, ...), custom_call_target="tpu_custom_call" | custom-call | flops 100000000 | bytes 3000000 | tf_op jit(solution)/shard_map/gate/pallas_call | solution.py:437
  88.1 0.9 copy-done.13
  89.8 12.1 %mix.1 = bf16[512,5120]{1,0:T(8,128)(2,1)} custom-call(s32[4]{0:T(128)} %len_ref.3, s32[1]{0:T(128)} %bitcast.first_ref, bf16[512,256]{1,0:T(8,128)(2,1)} %q_ref.1, bf16[512,512]{1,0:T(8,128)(2,1)} %gate.1.act_ref, bf16[2048,256]{1,0:T(8,128)(2,1)} %copy-done, bf16[2048,256]{1,0:T(8,128)(2,1)} %copy-done.12, bf16[2048,256]{1,0:T(8,128)(2,1)} %copy-done.11, ...), custom_call_target="tpu_custom_call" | custom-call | flops 8999999488 | bytes 25000000 | tf_op jit(solution)/shard_map/mix/pallas_call | solution.py:447
  101.9 94.3 %reduce-scatter.2.cloned.1.call-done = bf16[64,5120]{1,0:T(8,128)(2,1)} async-done(((bf16[512,5120]{1,0:T(8,128)(2,1)}), bf16[64,5120]{1,0:T(8,128)(2,1)}) %reduce-scatter.2.cloned.1.call-update) | async-done | bytes 655376 | tf_op jit(solution)/shard_map/reduce_scatter | solution.py:469
  (56 shorter events, 5.4 us)
Async XLA Ops:
  6.5 14.8 %copy-start.2 = (bf16[512,1,256]{2,0,1:T(8,128)(2,1)S(1)}, bf16[512,1,256]{2,0,1:T(8,128)(2,1)}, u32[]{:S(2)}) copy-start(bf16[512,1,256]{2,0,1:T(8,128)(2,1)} %param.12) | copy-start | bytes 786436
  6.5 189.7 %reduce-scatter.2.cloned.1.call-start = ((), (), s32[]{:S(2)}) async-start(), calls=%async_computation.1 | async-start | bytes 5898240 | tf_op jit(solution)/shard_map/reduce_scatter | solution.py:469
  6.5 14.8 %collective-permute-start.10 = (bf16[512,256]{1,0:T(8,128)(2,1)}, bf16[512,256]{1,0:T(8,128)(2,1)S(1)}, u32[]{:S(2)}, u32[]{:S(2)}) collective-permute-start(bf16[512,256]{1,0:T(8,128)(2,1)} %bitcast.3), channel_id=1, source_target_pairs={{0,32},{8,136},{16,48},{24,152},{32,0},{40,168},{48,16},{56,184},{... | collective-permute-start | bytes 786440 | tf_op jit(solution)/shard_map/ppermute | solution.py:358
  12.2 9.2 %collective-permute-start.9 = (bf16[512,256]{1,0:T(8,128)(2,1)}, bf16[512,256]{1,0:T(8,128)(2,1)S(1)}, u32[]{:S(2)}, u32[]{:S(2)}) collective-permute-start(bf16[512,256]{1,0:T(8,128)(2,1)} %bitcast.4), channel_id=1, source_target_pairs={{0,48},{8,200},{16,0},{24,216},{32,16},{40,232},{48,32},{56,248},{... | collective-permute-start | bytes 786440 | tf_op jit(solution)/shard_map/ppermute | solution.py:358
  13.5 7.9 %collective-permute-start.8 = (bf16[512,256]{1,0:T(8,128)(2,1)}, bf16[512,256]{1,0:T(8,128)(2,1)S(1)}, u32[]{:S(2)}, u32[]{:S(2)}) collective-permute-start(bf16[512,256]{1,0:T(8,128)(2,1)} %bitcast.5), channel_id=1, source_target_pairs={{0,16},{8,72},{16,32},{24,88},{32,48},{40,104},{48,0},{56,120},{64... | collective-permute-start | bytes 786440 | tf_op jit(solution)/shard_map/ppermute | solution.py:358
  21.4 66.6 %copy-start = (bf16[2048,256]{1,0:T(8,128)(2,1)}, bf16[2048,256]{1,0:T(8,128)(2,1)S(1)}, u32[]{:S(2)}) copy-start(bf16[2048,256]{1,0:T(8,128)(2,1)S(1)} %pad_maximum_fusion.g0) | copy-start | bytes 3145732
  21.5 54.3 %collective-permute-start.13 = (bf16[2048,256]{1,0:T(8,128)(2,1)S(1)}, bf16[2048,256]{1,0:T(8,128)(2,1)S(1)}, u32[]{:S(2)}, u32[]{:S(2)}) collective-permute-start(bf16[2048,256]{1,0:T(8,128)(2,1)S(1)} %pad_maximum_fusion.g0), channel_id=1, source_target_pairs={{0,128},{8,40},{16,144},{24,56},{32,160},{40,8},{48,176},{56,24},{... | collective-permute-start | bytes 3145736 | tf_op jit(solution)/shard_map/ppermute | solution.py:358
  26.3 49.4 %collective-permute-start.12 = (bf16[2048,256]{1,0:T(8,128)(2,1)S(1)}, bf16[2048,256]{1,0:T(8,128)(2,1)S(1)}, u32[]{:S(2)}, u32[]{:S(2)}) collective-permute-start(bf16[2048,256]{1,0:T(8,128)(2,1)S(1)} %pad_maximum_fusion.g0), channel_id=1, source_target_pairs={{8,56},{24,8},{40,24},{56,40},{72,120},{88,72},{104,88},{120,104},... | collective-permute-start | bytes 3145736 | tf_op jit(solution)/shard_map/ppermute | solution.py:358
  29.0 46.7 %collective-permute-start.11 = (bf16[2048,256]{1,0:T(8,128)(2,1)S(1)}, bf16[2048,256]{1,0:T(8,128)(2,1)S(1)}, u32[]{:S(2)}, u32[]{:S(2)}) collective-permute-start(bf16[2048,256]{1,0:T(8,128)(2,1)S(1)} %pad_maximum_fusion.g0), channel_id=1, source_target_pairs={{0,64},{8,24},{16,80},{24,40},{32,96},{40,56},{48,112},{56,8},{64,... | collective-permute-start | bytes 3145736 | tf_op jit(solution)/shard_map/ppermute | solution.py:358
  31.6 15.1 %collective-permute-start = (bf16[272,256]{1,0:T(8,128)(2,1)S(1)}, bf16[272,256]{1,0:T(8,128)(2,1)S(1)}, u32[]{:S(2)}, u32[]{:S(2)}) collective-permute-start(bf16[272,256]{1,0:T(8,128)(2,1)S(1)} %copy-done.16), channel_id=1, source_target_pairs={{0,8},{8,0},{16,24},{24,16},{32,40},{40,32},{48,56},{56,48},{64,72... | collective-permute-start | bytes 417800 | tf_op jit(solution)/shard_map/ppermute | solution.py:370
  49.1 6.6 %collective-permute-start.3 = (bf16[272,256]{1,0:T(8,128)(2,1)}, bf16[272,256]{1,0:T(8,128)(2,1)S(1)}, u32[]{:S(2)}, u32[]{:S(2)}) collective-permute-start(bf16[272,256]{1,0:T(8,128)(2,1)} %shard_map.109.mine_ref), channel_id=1, source_target_pairs={{0,32},{8,40},{16,48},{24,56},{32,0},{40,8},{48,16},{56,24},{64,96... | collective-permute-start | bytes 417800 | tf_op jit(solution)/shard_map/ppermute | solution.py:358
  49.1 7.4 %collective-permute-start.2 = (bf16[272,256]{1,0:T(8,128)(2,1)}, bf16[272,256]{1,0:T(8,128)(2,1)S(1)}, u32[]{:S(2)}, u32[]{:S(2)}) collective-permute-start(bf16[272,256]{1,0:T(8,128)(2,1)} %shard_map.109.mine_ref), channel_id=1, source_target_pairs={{0,48},{8,56},{16,0},{24,8},{32,16},{40,24},{48,32},{56,40},{64,11... | collective-permute-start | bytes 417800 | tf_op jit(solution)/shard_map/ppermute | solution.py:358
  55.7 5.3 %collective-permute-start.1 = (bf16[272,256]{1,0:T(8,128)(2,1)}, bf16[272,256]{1,0:T(8,128)(2,1)S(1)}, u32[]{:S(2)}, u32[]{:S(2)}) collective-permute-start(bf16[272,256]{1,0:T(8,128)(2,1)} %shard_map.109.mine_ref), channel_id=1, source_target_pairs={{0,16},{8,24},{16,32},{24,40},{32,48},{40,56},{48,0},{56,8},{64,80... | collective-permute-start | bytes 417800 | tf_op jit(solution)/shard_map/ppermute | solution.py:358
  63.7 5.8 %collective-permute-start.6 = (bf16[272,256]{1,0:T(8,128)(2,1)}, bf16[272,256]{1,0:T(8,128)(2,1)S(1)}, u32[]{:S(2)}, u32[]{:S(2)}) collective-permute-start(bf16[272,256]{1,0:T(8,128)(2,1)} %get-tuple-element.23), channel_id=1, source_target_pairs={{0,64},{8,72},{16,80},{24,88},{32,96},{40,104},{48,112},{56,120},{... | collective-permute-start | bytes 417800 | tf_op jit(solution)/shard_map/ppermute | solution.py:358
  65.3 8.1 %collective-permute-start.5 = (bf16[272,256]{1,0:T(8,128)(2,1)}, bf16[272,256]{1,0:T(8,128)(2,1)S(1)}, u32[]{:S(2)}, u32[]{:S(2)}) collective-permute-start(bf16[272,256]{1,0:T(8,128)(2,1)} %get-tuple-element.23), channel_id=1, source_target_pairs={{0,128},{8,136},{16,144},{24,152},{32,160},{40,168},{48,176},{56,1... | collective-permute-start | bytes 417800 | tf_op jit(solution)/shard_map/ppermute | solution.py:358
  69.5 6.1 %collective-permute-start.4 = (bf16[272,256]{1,0:T(8,128)(2,1)}, bf16[272,256]{1,0:T(8,128)(2,1)S(1)}, u32[]{:S(2)}, u32[]{:S(2)}) collective-permute-start(bf16[272,256]{1,0:T(8,128)(2,1)} %get-tuple-element.23), channel_id=1, source_target_pairs={{0,192},{8,200},{16,208},{24,216},{32,224},{40,232},{48,240},{56,2... | collective-permute-start | bytes 417800 | tf_op jit(solution)/shard_map/ppermute | solution.py:358
  73.4 14.6 %collective-permute-start.14 = (bf16[2048,256]{1,0:T(8,128)(2,1)S(1)}, bf16[2048,256]{1,0:T(8,128)(2,1)S(1)}, u32[]{:S(2)}, u32[]{:S(2)}) collective-permute-start(bf16[2048,256]{1,0:T(8,128)(2,1)S(1)} %pad_maximum_fusion.g0), channel_id=1, source_target_pairs={{0,8},{8,0},{16,24},{24,16},{32,40},{40,32},{48,56},{56,48},{64,72... | collective-permute-start | bytes 3145736 | tf_op jit(solution)/shard_map/ppermute | solution.py:370
  75.7 12.4 %copy-start.10 = (bf16[2048,256]{1,0:T(8,128)(2,1)}, bf16[2048,256]{1,0:T(8,128)(2,1)S(1)}, u32[]{:S(2)}) copy-start(bf16[2048,256]{1,0:T(8,128)(2,1)S(1)} %collective-permute-done.13.g3) | copy-start | bytes 3145732
  75.7 12.4 %copy-start.11 = (bf16[2048,256]{1,0:T(8,128)(2,1)}, bf16[2048,256]{1,0:T(8,128)(2,1)S(1)}, u32[]{:S(2)}) copy-start(bf16[2048,256]{1,0:T(8,128)(2,1)S(1)} %collective-permute-done.12.g2) | copy-start | bytes 3145732
  75.7 12.4 %copy-start.12 = (bf16[2048,256]{1,0:T(8,128)(2,1)}, bf16[2048,256]{1,0:T(8,128)(2,1)S(1)}, u32[]{:S(2)}) copy-start(bf16[2048,256]{1,0:T(8,128)(2,1)S(1)} %collective-permute-done.11.g1) | copy-start | bytes 3145732
  75.7 12.3 %collective-permute-start.15 = (bf16[2048,256]{1,0:T(8,128)(2,1)S(1)}, bf16[2048,256]{1,0:T(8,128)(2,1)S(1)}, u32[]{:S(2)}, u32[]{:S(2)}) collective-permute-start(bf16[2048,256]{1,0:T(8,128)(2,1)S(1)} %collective-permute-done.11.g1), channel_id=1, source_target_pairs={{0,8},{8,0},{16,24},{24,16},{32,40},{40,32},{48,56},{56,48},{64,72... | collective-permute-start | bytes 3145736 | tf_op jit(solution)/shard_map/ppermute | solution.py:370
  77.9 10.1 %collective-permute-start.16 = (bf16[2048,256]{1,0:T(8,128)(2,1)S(1)}, bf16[2048,256]{1,0:T(8,128)(2,1)S(1)}, u32[]{:S(2)}, u32[]{:S(2)}) collective-permute-start(bf16[2048,256]{1,0:T(8,128)(2,1)S(1)} %collective-permute-done.12.g2), channel_id=1, source_target_pairs={{0,8},{8,0},{16,24},{24,16},{32,40},{40,32},{48,56},{56,48},{64,72... | collective-permute-start | bytes 3145736 | tf_op jit(solution)/shard_map/ppermute | solution.py:370
  78.0 10.1 %collective-permute-start.17 = (bf16[2048,256]{1,0:T(8,128)(2,1)S(1)}, bf16[2048,256]{1,0:T(8,128)(2,1)}, u32[]{:S(2)}, u32[]{:S(2)}) collective-permute-start(bf16[2048,256]{1,0:T(8,128)(2,1)S(1)} %collective-permute-done.13.g3), channel_id=1, source_target_pairs={{0,8},{8,0},{16,24},{24,16},{32,40},{40,32},{48,56},{56,48},{64,72... | collective-permute-start | bytes 3145736 | tf_op jit(solution)/shard_map/ppermute | solution.py:370
  80.5 3.1 %collective-permute-start.7 = (bf16[256,256]{1,0:T(8,128)(2,1)}, bf16[256,256]{1,0:T(8,128)(2,1)S(1)}, u32[]{:S(2)}, u32[]{:S(2)}) collective-permute-start(bf16[256,256]{1,0:T(8,128)(2,1)} %get-tuple-element.26), channel_id=1, source_target_pairs={{0,8},{8,0},{16,24},{24,16},{32,40},{40,32},{48,56},{56,48},{64,72... | collective-permute-start | bytes 393224 | tf_op jit(solution)/shard_map/ppermute | solution.py:370
  (12 other events, 42.9 us)
Sparse Core Ops, SparseCore 0:
  102.0 94.1 reduce-scatter.1

commit v4 on v3

--- a/solution.py
+++ b/solution.py
@@ -21,9 +21,6 @@
 HIGH = lax.Precision.HIGHEST
 HALF = HP // 2
 STATE_ROWS = SN + 16
-Y_OFF = (0, 3, 1, 2)
-ROW_OF_GROUP = (0, 1, 99, 2)
-ROW_OF_SLOT = (0, 1, 3, 2)
 VMEM = pl.BlockSpec(memory_space=pltpu.VMEM)
 SMEM = pl.BlockSpec(memory_space=pltpu.SMEM)
 ANY = pl.BlockSpec(memory_space=pl.ANY)
@@ -191,138 +188,146 @@
     act_ref[...] = (y * (z / (1.0 + jnp.exp(-z)))).astype(jnp.bfloat16)
 
 
+class Attention:
+    def __init__(self, len_ref, first_ref, q_ref, fetched, other, q_scr, kv_scr, kv_sem):
+        self.first = first_ref[0]
+        self.ends = ends_of(len_ref)
+        self.mine = self.first // CHUNK
+        self.low = start_of(self.first, self.ends) // CHUNK
+        self.last_start = start_of(self.first + ROWS - 1, self.ends)
+        self.arrays = (fetched, other)
+        self.q_scr, self.kv_scr, self.kv_sem = q_scr, kv_scr, kv_sem
+        for g in range(2):
+            rows = slice(g * ROWS, (g + 1) * ROWS)
+            scaled = q_ref[:, g * HD : (g + 1) * HD].astype(jnp.float32) * (LOG2E * HD**-0.5)
+            high = scaled.astype(jnp.bfloat16)
+            q_scr[rows, :HD] = high
+            q_scr[rows, HD:] = (scaled - high.astype(jnp.float32)).astype(jnp.bfloat16)
+
+    def count(self, far):
+        return (self.mine - far - self.low) // 2 + 1
+
+    def block(self, far, i):
+        return self.mine - far - 2 * i
+
+    def copy(self, far, i):
+        block = self.block(far, i)
+        x, y, core = block // 8, (block // 2) % 4, block % 2
+        slot = jnp.where(core == 0, x * 4 + y, y * 4 + x)
+        rows = pl.ds(pl.multiple_of(slot * CHUNK, CHUNK), CHUNK)
+        to = far * (SLOTS // 2) + i
+        return pltpu.make_async_copy(self.arrays[far].at[rows], self.kv_scr.at[to], self.kv_sem.at[to])
+
+    def fetch(self, far):
+        lax.fori_loop(0, self.count(far), lambda i, _: (self.copy(far, i).start(), 0)[1], 0)
+
+    def scores(self, far, i, rows, masked):
+        k = self.kv_scr[far * (SLOTS // 2) + i, :, :HD]
+        s = lax.dot_general(
+            self.q_scr[rows, :],
+            jnp.concatenate([k, k], axis=1),
+            (((1,), (1,)), ((), ())),
+            preferred_element_type=jnp.float32,
+        )
+        if masked:
+            pos = self.first + rows.start % ROWS + iota((rows.stop - rows.start, 1), 0)
+            key = self.block(far, i) * CHUNK + iota((1, CHUNK), 1)
+            s = jnp.where((key >= start_of(pos, self.ends)) & (key <= pos), s, LOW)
+        return s
+
+    def values(self, far, i):
+        return jnp.concatenate([self.kv_scr[far * (SLOTS // 2) + i, :, HD:], jnp.ones((CHUNK, HD), jnp.bfloat16)], axis=1)
+
+    def over_chunks(self, far, step, wait):
+        def one_chunk(i, _):
+            if wait:
+                self.copy(far, i).wait()
+            block = self.block(far, i)
+            masked = (block == self.mine) | (block * CHUNK < self.last_start)
+            pl.when(masked)(lambda: step(far, i, True))
+            pl.when(jnp.logical_not(masked))(lambda: step(far, i, False))
+            return 0
+
+        lax.fori_loop(0, self.count(far), one_chunk, 0)
+
+    def add(self, far, acc):
+        def step(far, i, masked):
+            v = self.values(far, i)
+            for r in range(2 * ROWS // TILE):
+                rows = slice(r * TILE, (r + 1) * TILE)
+                p = jnp.exp2(self.scores(far, i, rows, masked)).astype(jnp.bfloat16)
+                acc[rows, :] += jnp.dot(p, v, preferred_element_type=jnp.float32)
+
+        self.over_chunks(far, step, True)
+
+    def add_shifted(self, far, acc, m_scr):
+        def step(far, i, masked):
+            v = self.values(far, i)
+            for r in range(2 * ROWS // TILE):
+                rows = slice(r * TILE, (r + 1) * TILE)
+                s = self.scores(far, i, rows, masked)
+                old = m_scr[rows, :]
+                m = jnp.maximum(old, jnp.max(s, axis=1, keepdims=True))
+                alpha = jnp.exp2(old - m)
+                p = jnp.exp2(s - jnp.concatenate([m] * (CHUNK // 128), axis=1)).astype(jnp.bfloat16)
+                out = jnp.dot(p, v, preferred_element_type=jnp.float32)
+                acc[rows, :] = acc[rows, :] * jnp.concatenate([alpha, alpha], axis=1) + out
+                m_scr[rows, :] = m
+
+        self.over_chunks(far, step, False)
+
+
+def part_kernel(len_ref, first_ref, q_ref, fetched, acc_ref, q_scr, kv_scr, kv_sem):
+    attention = Attention(len_ref, first_ref, q_ref, fetched, None, q_scr, kv_scr, kv_sem)
+    attention.fetch(0)
+    acc_ref[...] = jnp.zeros_like(acc_ref)
+    attention.add(0, acc_ref)
+
+
 def mix_kernel(
     len_ref,
     first_ref,
     q_ref,
     act_ref,
-    g0,
-    g1,
-    g2,
-    g3,
-    h0,
-    h1,
-    h2,
-    h3,
+    acc_ref,
+    fetched,
+    other,
     wa_hbm,
     ws_hbm,
     o_hbm,
     q_scr,
     kv_scr,
+    kv_sem,
     acc_scr,
     m_scr,
     w_scr,
     in_scr,
     o_scr,
-    ids,
-    kv_sem,
     w_sem,
     o_sem,
 ):
-    first = first_ref[0]
-    ends = ends_of(len_ref)
-    mine = first // CHUNK
-    low = start_of(first, ends) // CHUNK
-    last_start = start_of(first + ROWS - 1, ends)
-    x, y, core = mine // 8, (mine // 2) % 4, mine % 2
-
-    def kv_copy(src, slot, i):
-        return pltpu.make_async_copy(src.at[pl.ds(slot * CHUNK, CHUNK)], kv_scr.at[i], kv_sem.at[i])
-
-    ids[0] = mine
-    kv_copy(g0, 0, 0).start()
-    count = jnp.int32(1)
-    for which, group in enumerate((g0, g1, g2, g3, h0, h1, h2, h3)):
-        odd = (core + which // 4) % 2 == 1
-        for slot in range(4):
-            if which == 0 and slot == 0:
-                continue
-            even_x = x - ROW_OF_GROUP[which % 4]
-            odd_x = x - ROW_OF_SLOT[slot]
-            row = jnp.where(odd, odd_x, even_x)
-            place = jnp.where(odd, (y + Y_OFF[which % 4]) % 4, (y + Y_OFF[slot]) % 4)
-            block = row * 8 + place * 2 + odd.astype(jnp.int32)
-            needed = (row >= 0) & (block >= low) & (block < mine)
-
-            @pl.when(needed)
-            def _(group=group, slot=slot, block=block, count=count):
-                ids[count] = block
-                kv_copy(group, slot, count).start()
-
-            count = count + needed.astype(jnp.int32)
-
-    def chunk_of(i):
-        return ids[i]
-
+    attention = Attention(len_ref, first_ref, q_ref, fetched, other, q_scr, kv_scr, kv_sem)
+    attention.fetch(1)
     weights = [
         pltpu.make_async_copy(wa_hbm, w_scr.at[pl.ds(0, 2 * HD)], w_sem.at[0]),
         pltpu.make_async_copy(ws_hbm, w_scr.at[pl.ds(2 * HD, HP)], w_sem.at[1]),
     ]
     for copy in weights:
         copy.start()
-    for g in range(2):
-        rows = slice(g * ROWS, (g + 1) * ROWS)
-        scaled = q_ref[:, g * HD : (g + 1) * HD].astype(jnp.float32) * (LOG2E * HD**-0.5)
-        high = scaled.astype(jnp.bfloat16)
-        q_scr[rows, :HD] = high
-        q_scr[rows, HD:] = (scaled - high.astype(jnp.float32)).astype(jnp.bfloat16)
-    one = jnp.ones((CHUNK, HD), jnp.bfloat16)
-
-    def scores(i, rows, masked):
-        k = kv_scr[i, :, :HD]
-        s = lax.dot_general(
-            q_scr[rows, :],
-            jnp.concatenate([k, k], axis=1),
-            (((1,), (1,)), ((), ())),
-            preferred_element_type=jnp.float32,
-        )
-        if masked:
-            pos = first + rows.start % ROWS + iota((rows.stop - rows.start, 1), 0)
-            key = chunk_of(i) * CHUNK + iota((1, CHUNK), 1)
-            s = jnp.where((key >= start_of(pos, ends)) & (key <= pos), s, LOW)
-        return s
-
-    def plain(i, masked):
-        v = jnp.concatenate([kv_scr[i, :, HD:], one], axis=1)
-        for r in range(2 * ROWS // TILE):
-            rows = slice(r * TILE, (r + 1) * TILE)
-            p = jnp.exp2(scores(i, rows, masked)).astype(jnp.bfloat16)
-            acc_scr[rows, :] += jnp.dot(p, v, preferred_element_type=jnp.float32)
-
-    def guarded(i, masked):
-        v = jnp.concatenate([kv_scr[i, :, HD:], one], axis=1)
-        for r in range(2 * ROWS // TILE):
-            rows = slice(r * TILE, (r + 1) * TILE)
-            s = scores(i, rows, masked)
-            old = m_scr[rows, :]
-            m = jnp.maximum(old, jnp.max(s, axis=1, keepdims=True))
-            alpha = jnp.exp2(old - m)
-            p = jnp.exp2(s - jnp.concatenate([m] * (CHUNK // 128), axis=1)).astype(jnp.bfloat16)
-            out = jnp.dot(p, v, preferred_element_type=jnp.float32)
-            acc_scr[rows, :] = acc_scr[rows, :] * jnp.concatenate([alpha, alpha], axis=1) + out
-            m_scr[rows, :] = m
-
-    def over_chunks(step, wait):
-        def one_chunk(i, _):
-            if wait:
-                kv_copy(g0, 0, i).wait()
-            masked = (i == 0) | (chunk_of(i) * CHUNK < last_start)
-            pl.when(masked)(lambda: step(i, True))
-            pl.when(jnp.logical_not(masked))(lambda: step(i, False))
-            return 0
-
-        lax.fori_loop(0, count, one_chunk, 0)
-
-    acc_scr[...] = jnp.zeros_like(acc_scr)
-    over_chunks(plain, True)
+
+    acc_scr[...] = acc_ref[...]
+    attention.add(1, acc_scr)
     total = acc_scr[:, HD:]
     fine = (jnp.min(total) > 2.0**-60) & (jnp.max(total) < 2.0**110)
 
     @pl.when(jnp.logical_not(fine))
     def _():
+        attention.fetch(0)
+        lax.fori_loop(0, attention.count(0), lambda i, _: (attention.copy(0, i).wait(), 0)[1], 0)
         acc_scr[...] = jnp.zeros_like(acc_scr)
         m_scr[...] = jnp.full(m_scr.shape, LOW, jnp.float32)
-        over_chunks(guarded, False)
+        attention.add_shifted(0, acc_scr, m_scr)
+        attention.add_shifted(1, acc_scr, m_scr)
 
     for g in range(2):
         rows = slice(g * ROWS, (g + 1) * ROWS)
@@ -356,6 +361,12 @@
                 if to is not None:
                     pairs.append((x * 8 + y * 2 + core, to[0] * 8 + to[1] * 2 + core))
     return lax.ppermute(block, "pack", pairs)
+
+
+def lines(stage):
+    rows = [[x * 8 + y * 2 + stage for y in range(4)] for x in range(4)]
+    columns = [[x * 8 + y * 2 + 1 - stage for x in range(4)] for y in range(4)]
+    return rows + columns
 
 
 def along_x(distance):
@@ -397,10 +408,7 @@
     first = jnp.reshape(lax.axis_index("pack") * ROWS, (1,)).astype(jnp.int32)
     kv = keys_values.reshape(ROWS, 2 * HD)
     nowhere = lambda x, y: None
-    below = moved(kv, along_y(1), along_x(1))
-    above = moved(kv, along_y(3), along_x(3))
-    across = moved(kv, along_y(2), along_x(2))
-
+    first_stage = lax.all_gather(kv, "pack", axis=0, tiled=True, axis_index_groups=lines(0))
     y_local, run_keep, run_send, fac = pl.pallas_call(
         ssd_kernel,
         out_shape=(
@@ -416,22 +424,14 @@
         name="ssd_local",
     )(lengths, decay_log, skip_gain, first, ssm_values, ssm_maps, step_size.T)
 
-    below, above, across = lax.optimization_barrier((below, above, across, fac))[:3]
-    group = jnp.concatenate([kv, below, above, across], axis=0)
-    groups = [
-        group,
-        moved(group, along_x(1), along_y(1)),
-        moved(group, nowhere, along_y(3)),
-        moved(group, along_x(2), along_y(2)),
-    ]
     run = (STATE_ROWS, HALF)
     run_got = swapped(run_send)
     (chip,) = call(chip_kernel, [run], 2, first, run_keep, run_got)
+    first_stage = lax.optimization_barrier((first_stage, chip))[0]
+    fetched = lax.all_gather(first_stage, "pack", axis=0, tiled=True, axis_index_groups=lines(1))
     chips = [moved(chip, along_y(d), along_y(d)) for d in (1, 3, 2)]
     prefix, total = call(row_kernel, [run, run], 4, first, chip, *chips)
     rows = [moved(total, along_x(d), along_x(d)) for d in (3, 2, 1)]
-    groups = [groups[0], *lax.optimization_barrier((*groups[1:], *rows))[:3]]
-    groups = groups + [swapped(g) for g in groups]
     keep, send = call(carry_kernel, [(SN, HALF)] * 2, 6, first, *rows, prefix, run_keep, run_got)
     got = swapped(send)
     act = pl.pallas_call(
@@ -444,28 +444,43 @@
         name="gate",
     )(first, y_local, ssm_gates, ssm_maps, fac, keep, got)
 
+    fetched = lax.optimization_barrier((fetched, act))[0]
+    other = swapped(fetched)
+    scores_scratch = [
+        pltpu.VMEM((2 * ROWS, 2 * HD), jnp.bfloat16),
+        pltpu.VMEM((SLOTS, CHUNK, 2 * HD), jnp.bfloat16),
+        pltpu.SemaphoreType.DMA((SLOTS,)),
+    ]
+    partial = pl.pallas_call(
+        part_kernel,
+        out_shape=jax.ShapeDtypeStruct((2 * ROWS, 2 * HD), jnp.float32),
+        in_specs=[SMEM] * 2 + [VMEM, ANY],
+        out_specs=VMEM,
+        scratch_shapes=scores_scratch,
+        compiler_params=big(),
+        cost_estimate=pl.CostEstimate(flops=9 * 10**9, bytes_accessed=5 * 10**6, transcendentals=5 * 10**6),
+        name="part",
+    )(lengths, first, queries, fetched)
+
     terms = pl.pallas_call(
         mix_kernel,
         out_shape=jax.ShapeDtypeStruct((ROWS, DM), jnp.bfloat16),
-        in_specs=[SMEM] * 2 + [VMEM] * 2 + [ANY] * 10,
+        in_specs=[SMEM] * 2 + [VMEM] * 3 + [ANY] * 4,
         out_specs=ANY,
-        scratch_shapes=[
-            pltpu.VMEM((2 * ROWS, 2 * HD), jnp.bfloat16),
-            pltpu.VMEM((SLOTS, CHUNK, 2 * HD), jnp.bfloat16),
+        scratch_shapes=scores_scratch
+        + [
             pltpu.VMEM((2 * ROWS, 2 * HD), jnp.float32),
             pltpu.VMEM((2 * ROWS, HD), jnp.float32),
             pltpu.VMEM((2 * HD + HP, DM), jnp.bfloat16),
             pltpu.VMEM((ROWS, 2 * HD + HP), jnp.bfloat16),
             pltpu.VMEM((ROWS, DM), jnp.bfloat16),
-            pltpu.SMEM((SLOTS,), jnp.int32),
-            pltpu.SemaphoreType.DMA((SLOTS,)),
             pltpu.SemaphoreType.DMA((2,)),
             pltpu.SemaphoreType.DMA((DM // COLS,)),
         ],
         compiler_params=big(),
         cost_estimate=pl.CostEstimate(flops=9 * 10**9, bytes_accessed=25 * 10**6, transcendentals=9 * 10**6),
         name="mix",
-    )(lengths, first, queries, act, *groups, attn_out_weight, ssd_out_weight)
+    )(lengths, first, queries, act, partial, fetched, other, attn_out_weight, ssd_out_weight)
     return lax.psum_scatter(terms, "tp", scatter_dimension=0, tiled=True)
 
 

time: 205 us -> 200 us (0.976); the launches traced: 203 us -> 203 us
  starting transfers between devices: 47.1 us -> 20.3 us
  waiting for transfers between devices: 111 us -> 132 us
  Pallas kernels: 27.9 us -> 33.1 us
    ppermute x12 -> x6, starting transfers between devices: 28.3 us -> 10.7 us  [moved(): return lax.ppermute(block, 'pack', pairs)]
    all_gather x0 -> x2, waiting for transfers between devices: none -> 17.2 us  [the longest x1 16.3 us: local(): lax.all_gather(kv, 'pack', axis=0, tiled=True, axis_index_groups=lines(0))]
    ppermute x6 -> x3, starting transfers between devices: 18.9 us -> 9.59 us  [swapped(): return lax.ppermute(block, 'pack', [(i, i ^ 1) for i in range(32)])]
    pallas_call x0 -> x1, Pallas kernels: none -> 4.06 us  [local(): pl.pallas_call(part_kernel, out_shape=jax.ShapeDtypeStruct((2 * ROWS, 2 *...]
    ppermute x6 -> x3, waiting for transfers between devices: 3.62 us -> 5.33 us  [swapped(): return lax.ppermute(block, 'pack', [(i, i ^ 1) for i in range(32)])]
    unnamed x34 -> x18, local copies, waits for them, and re-layouts: 3.7 us -> 4.75 us
    ppermute x12 -> x6, waiting for transfers between devices: 12.6 us -> 12.9 us  [moved(): return lax.ppermute(block, 'pack', pairs)]
  transfers between devices with their start and end apart: 19 -> 12, of which waited for: 7 -> 11; matrix products, arithmetic and copies ran while one was open for 0% -> 0% of each run, Pallas kernels for 8% -> 10%
where the time goes in v4:
time: 200 us; the launch traced here: 203 us
  waiting for transfers between devices  132 us (66%)
  Pallas kernels  33.1 us (17%)
  starting transfers between devices  20.3 us (10%)
  between operations  13.2 us (7%)
  local copies, waits for them, and re-layouts  4.75 us (2%)
    reduce_scatter x1, waiting for transfers between devices, local(): return lax.psum_scatter(terms, 'tp', scatter_dimension=0, tiled=True)  95.8 us
    all_gather x1, waiting for transfers between devices, local(): lax.all_gather(kv, 'pack', axis=0, tiled=True, axis_index_groups=lines(0))  16.3 us
    pallas_call x1, Pallas kernels, local(): pl.pallas_call(mix_kernel, out_shape=jax.ShapeDtypeStruct((ROWS, DM), jnp...  13.2 us
    ppermute x6, waiting for transfers between devices, moved(): return lax.ppermute(block, 'pack', pairs)  12.9 us
    ppermute x6, starting transfers between devices, moved(): return lax.ppermute(block, 'pack', pairs)  10.7 us
    ppermute x3, starting transfers between devices, swapped(): return lax.ppermute(block, 'pack', [(i, i ^ 1) for i in range(32)])  9.59 us
    pallas_call x1, Pallas kernels, local(): pl.pallas_call(ssd_kernel, out_shape=(jax.ShapeDtypeStruct((ROWS, HP), jn...  6.22 us
    pallas_call x3, Pallas kernels, call(): pl.pallas_call(kernel, out_shape=tuple((jax.ShapeDtypeStruct(shape, jnp.b...  5.87 us
  transfers between devices with their start and end apart: 12, of which 11 were waited for; matrix products, arithmetic and copies ran while one was open for 0% of the time, Pallas kernels for 10%

profile of v4, /device:TPU:1, one launch (start us, length us, event | category | flops | bytes accessed | tf_op | source)
XLA Modules:
  0.0 203.4 jit_solution(2614585605053156471)
XLA Ops:
  7.3 6.2 %ssd_local.1 = (f32[512,512]{1,0:T(8,128)}, bf16[272,256]{1,0:T(8,128)(2,1)}, bf16[272,256]{1,0:T(8,128)(2,1)}, f32[512,8]{1,0:T(8,128)}) custom-call(s32[4]{0:T(128)} %len_ref.5, f32[8]{0:T(128)} %dl_ref.1, f32[8]{0:T(128)} %skip_ref.1, s32[1]{0:T(128)} %bitcast.first_ref, bf16[512,512]{1,0:T(8,128)(2,1)} %x_ref.1, bf16[512,512]{1,0:T(8,128)(2,1)} %maps_ref.3, ...), custom_call_target="tpu_custom_call" | custom-call | flops 1000000000 | bytes 4000000 | tf_op jit(solution)/shard_map/ssd_local/pallas_call | solution.py:412
  13.5 3.2 %collective-permute-start = (bf16[272,256]{1,0:T(8,128)(2,1)}, bf16[272,256]{1,0:T(8,128)(2,1)S(1)}, u32[]{:S(2)}, u32[]{:S(2)}) collective-permute-start(bf16[272,256]{1,0:T(8,128)(2,1)} %get-tuple-element.18), channel_id=1, source_target_pairs={{0,8},{8,0},{16,24},{24,16},{32,40},{40,32},{48,56},{56,48},{64,72... | collective-permute-start | bytes 417800 | tf_op jit(solution)/shard_map/ppermute | solution.py:381
  16.8 1.2 collective-permute-done.other_ref
  18.6 1.7 shard_map.109.mine_ref
  20.3 16.3 %all-gather.6.cloned.1.call-done = bf16[2048,1,256]{2,0,1:T(8,128)(2,1)} async-done(((bf16[512,1,256]{2,0,1:T(8,128)(2,1)}), bf16[2048,1,256]{2,0,1:T(8,128)(2,1)}) %all-gather.6.cloned.1.call-update) | async-done | bytes 1048592 | tf_op jit(solution)/shard_map/all_gather | solution.py:411
  36.7 2.5 %collective-permute-start.3 = (bf16[272,256]{1,0:T(8,128)(2,1)}, bf16[272,256]{1,0:T(8,128)(2,1)S(1)}, u32[]{:S(2)}, u32[]{:S(2)}) collective-permute-start(bf16[272,256]{1,0:T(8,128)(2,1)} %shard_map.109.mine_ref), channel_id=1, source_target_pairs={{0,32},{8,40},{16,48},{24,56},{32,0},{40,8},{48,16},{56,24},{64,96... | collective-permute-start | bytes 417800 | tf_op jit(solution)/shard_map/ppermute | solution.py:363
  40.7 1.7 collective-permute-done.3.across_ref
  42.4 3.4 %collective-permute-done.2.above_ref = bf16[272,256]{1,0:T(8,128)(2,1)S(1)} collective-permute-done((bf16[272,256]{1,0:T(8,128)(2,1)}, bf16[272,256]{1,0:T(8,128)(2,1)S(1)}, u32[]{:S(2)}, u32[]{:S(2)}) %collective-permute-start.2) | collective-permute-done | bytes 139296 | tf_op jit(solution)/shard_map/ppermute | solution.py:363
  45.8 2.0 collective-permute-done.1.below_ref
  48.5 2.1 %shard_map.110 = (bf16[272,256]{1,0:T(8,128)(2,1)}, bf16[272,256]{1,0:T(8,128)(2,1)}) custom-call(s32[1]{0:T(128)} %bitcast.first_ref, bf16[272,256]{1,0:T(8,128)(2,1)} %shard_map.109.mine_ref, bf16[272,256]{1,0:T(8,128)(2,1)} %copy-done.6, bf16[272,256]{1,0:T(8,128)(2,1)} %copy-done.5, bf16[272,256]{1,0:T(8,128)(2,1)} %copy-done.3), custom_call_target="tpu_custom_call" | custom-call | flops 1000000 | bytes 1000000 | tf_op jit(solution)/shard_map/pallas_call | solution.py:385
  50.5 1.3 collective-permute-start.6
  51.8 4.1 %collective-permute-start.5 = (bf16[272,256]{1,0:T(8,128)(2,1)}, bf16[272,256]{1,0:T(8,128)(2,1)S(1)}, u32[]{:S(2)}, u32[]{:S(2)}) collective-permute-start(bf16[272,256]{1,0:T(8,128)(2,1)} %get-tuple-element.19), channel_id=1, source_target_pairs={{0,128},{8,136},{16,144},{24,152},{32,160},{40,168},{48,176},{56,1... | collective-permute-start | bytes 417800 | tf_op jit(solution)/shard_map/ppermute | solution.py:363
  55.9 1.3 collective-permute-start.4
  57.3 3.5 %collective-permute-done.5.row2_ref = bf16[272,256]{1,0:T(8,128)(2,1)S(1)} collective-permute-done((bf16[272,256]{1,0:T(8,128)(2,1)}, bf16[272,256]{1,0:T(8,128)(2,1)S(1)}, u32[]{:S(2)}, u32[]{:S(2)}) %collective-permute-start.5) | collective-permute-done | bytes 139296 | tf_op jit(solution)/shard_map/ppermute | solution.py:363
  60.7 2.3 %collective-permute-done.4.row3_ref = bf16[272,256]{1,0:T(8,128)(2,1)S(1)} collective-permute-done((bf16[272,256]{1,0:T(8,128)(2,1)}, bf16[272,256]{1,0:T(8,128)(2,1)S(1)}, u32[]{:S(2)}, u32[]{:S(2)}) %collective-permute-start.4) | collective-permute-done | bytes 139296 | tf_op jit(solution)/shard_map/ppermute | solution.py:363
  63.7 2.1 %shard_map.111 = (bf16[256,256]{1,0:T(8,128)(2,1)}, bf16[256,256]{1,0:T(8,128)(2,1)}) custom-call(s32[1]{0:T(128)} %bitcast.first_ref, bf16[272,256]{1,0:T(8,128)(2,1)} %copy-done.4, bf16[272,256]{1,0:T(8,128)(2,1)} %copy-done.2, bf16[272,256]{1,0:T(8,128)(2,1)} %copy-done.1, bf16[272,256]{1,0:T(8,128)(2,1)} %get-tuple-element.20.prefix_ref, ...), custom_call_target="tpu_custom_call" | custom-call | flops 1000000 | bytes 1000000 | tf_op jit(solution)/shard_map/pallas_call | solution.py:385
  65.8 2.3 %collective-permute-start.7 = (bf16[256,256]{1,0:T(8,128)(2,1)}, bf16[256,256]{1,0:T(8,128)(2,1)S(1)}, u32[]{:S(2)}, u32[]{:S(2)}) collective-permute-start(bf16[256,256]{1,0:T(8,128)(2,1)} %get-tuple-element.22), channel_id=1, source_target_pairs={{0,8},{8,0},{16,24},{24,16},{32,40},{40,32},{48,56},{56,48},{64,72... | collective-permute-start | bytes 393224 | tf_op jit(solution)/shard_map/ppermute | solution.py:381
  70.0 3.8 %gate.1.act_ref = bf16[512,512]{1,0:T(8,128)(2,1)} custom-call(s32[1]{0:T(128)} %bitcast.first_ref, f32[512,512]{1,0:T(8,128)} %get-tuple-element.15.y_ref, bf16[512,512]{1,0:T(8,128)(2,1)} %z_ref.1, bf16[512,512]{1,0:T(8,128)(2,1)} %maps_ref.3, f32[512,8]{1,0:T(8,128)} %get-tuple-element.16.fac_ref, bf16[256,256]{1,0:T(8,128)(2,1)} %get-tuple-element.21.keep_ref, ...), custom_call_target="tpu_custom_call" | custom-call | flops 100000000 | bytes 3000000 | tf_op jit(solution)/shard_map/gate/pallas_call | solution.py:437
  74.6 4.1 %collective-permute-start.8 = (bf16[8192,256]{1,0:T(8,128)(2,1)}, bf16[8192,256]{1,0:T(8,128)(2,1)S(1)}, u32[]{:S(2)}, u32[]{:S(2)}) collective-permute-start(bf16[8192,256]{1,0:T(8,128)(2,1)} %all-gather.4.cloned.1.call-done.fetched), channel_id=1, source_target_pairs={{0,8},{8,0},{16,24},{24,16},{32,40},{40,32},{48,56},{56,48},{64,72... | collective-permute-start | bytes 12582920 | tf_op jit(solution)/shard_map/ppermute | solution.py:381
  78.7 4.1 %part.1.acc_ref = f32[1024,256]{1,0:T(8,128)} custom-call(s32[4]{0:T(128)} %len_ref.5, s32[1]{0:T(128)} %bitcast.first_ref, bf16[512,256]{1,0:T(8,128)(2,1)} %q_ref.3, bf16[8192,256]{1,0:T(8,128)(2,1)} %all-gather.4.cloned.1.call-done.fetched), custom_call_target="tpu_custom_call" | custom-call | flops 8999999488 | bytes 5000000 | tf_op jit(solution)/shard_map/part/pallas_call | solution.py:454
  82.8 2.9 %collective-permute-done.8.other = bf16[8192,256]{1,0:T(8,128)(2,1)S(1)} collective-permute-done((bf16[8192,256]{1,0:T(8,128)(2,1)}, bf16[8192,256]{1,0:T(8,128)(2,1)S(1)}, u32[]{:S(2)}, u32[]{:S(2)}) %collective-permute-start.8) | collective-permute-done | bytes 4194336 | tf_op jit(solution)/shard_map/ppermute | solution.py:381
  85.7 2.1 %copy-done.8 = bf16[8192,256]{1,0:T(8,128)(2,1)} copy-done((bf16[8192,256]{1,0:T(8,128)(2,1)}, bf16[8192,256]{1,0:T(8,128)(2,1)S(1)}, u32[]{:S(2)}) %copy-start.8) | copy-done | bytes 4194328
  87.8 13.2 %mix.1 = bf16[512,5120]{1,0:T(8,128)(2,1)} custom-call(s32[4]{0:T(128)} %len_ref.5, s32[1]{0:T(128)} %bitcast.first_ref, bf16[512,256]{1,0:T(8,128)(2,1)} %q_ref.3, bf16[512,512]{1,0:T(8,128)(2,1)} %gate.1.act_ref, f32[1024,256]{1,0:T(8,128)} %part.1.acc_ref, bf16[8192,256]{1,0:T(8,128)(2,1)} %all-gather.4.cloned.1.call-done.fetched, ...), custom_call_target="tpu_custom_call" | custom-call | flops 8999999488 | bytes 25000000 | tf_op jit(solution)/shard_map/mix/pallas_call | solution.py:465
  101.0 95.8 %reduce-scatter.2.cloned.1.call-done = bf16[64,5120]{1,0:T(8,128)(2,1)} async-done(((bf16[512,5120]{1,0:T(8,128)(2,1)}), bf16[64,5120]{1,0:T(8,128)(2,1)}) %reduce-scatter.2.cloned.1.call-update) | async-done | bytes 655376 | tf_op jit(solution)/shard_map/reduce_scatter | solution.py:484
  (28 shorter events, 7.0 us)
Async XLA Ops:
  6.5 30.1 %all-gather.6.cloned.1.call-start = ((), (), s32[]{:S(2)}) async-start(), calls=%async_computation.3 | async-start | bytes 1310720 | tf_op jit(solution)/shard_map/all_gather | solution.py:411
  7.3 67.4 %all-gather.4.cloned.1.call-start = ((), (), s32[]{:S(2)}) async-start(), calls=%async_computation.1 | async-start | bytes 5242880 | tf_op jit(solution)/shard_map/all_gather | solution.py:431
  13.5 4.4 %collective-permute-start = (bf16[272,256]{1,0:T(8,128)(2,1)}, bf16[272,256]{1,0:T(8,128)(2,1)S(1)}, u32[]{:S(2)}, u32[]{:S(2)}) collective-permute-start(bf16[272,256]{1,0:T(8,128)(2,1)} %get-tuple-element.18), channel_id=1, source_target_pairs={{0,8},{8,0},{16,24},{24,16},{32,40},{40,32},{48,56},{56,48},{64,72... | collective-permute-start | bytes 417800 | tf_op jit(solution)/shard_map/ppermute | solution.py:381
  18.0 0.7 copy-start
  36.7 160.2 %reduce-scatter.2.cloned.1.call-start = ((), (), s32[]{:S(2)}) async-start(), calls=%async_computation.2 | async-start | bytes 5898240 | tf_op jit(solution)/shard_map/reduce_scatter | solution.py:484
  36.7 5.7 %collective-permute-start.3 = (bf16[272,256]{1,0:T(8,128)(2,1)}, bf16[272,256]{1,0:T(8,128)(2,1)S(1)}, u32[]{:S(2)}, u32[]{:S(2)}) collective-permute-start(bf16[272,256]{1,0:T(8,128)(2,1)} %shard_map.109.mine_ref), channel_id=1, source_target_pairs={{0,32},{8,40},{16,48},{24,56},{32,0},{40,8},{48,16},{56,24},{64,96... | collective-permute-start | bytes 417800 | tf_op jit(solution)/shard_map/ppermute | solution.py:363
  39.2 6.6 %collective-permute-start.2 = (bf16[272,256]{1,0:T(8,128)(2,1)}, bf16[272,256]{1,0:T(8,128)(2,1)S(1)}, u32[]{:S(2)}, u32[]{:S(2)}) collective-permute-start(bf16[272,256]{1,0:T(8,128)(2,1)} %shard_map.109.mine_ref), channel_id=1, source_target_pairs={{0,48},{8,56},{16,0},{24,8},{32,16},{40,24},{48,32},{56,40},{64,11... | collective-permute-start | bytes 417800 | tf_op jit(solution)/shard_map/ppermute | solution.py:363
  40.1 7.7 %collective-permute-start.1 = (bf16[272,256]{1,0:T(8,128)(2,1)}, bf16[272,256]{1,0:T(8,128)(2,1)S(1)}, u32[]{:S(2)}, u32[]{:S(2)}) collective-permute-start(bf16[272,256]{1,0:T(8,128)(2,1)} %shard_map.109.mine_ref), channel_id=1, source_target_pairs={{0,16},{8,24},{16,32},{24,40},{32,48},{40,56},{48,0},{56,8},{64,80... | collective-permute-start | bytes 417800 | tf_op jit(solution)/shard_map/ppermute | solution.py:363
  42.4 5.4 %copy-start.3 = (bf16[272,256]{1,0:T(8,128)(2,1)}, bf16[272,256]{1,0:T(8,128)(2,1)S(1)}, u32[]{:S(2)}) copy-start(bf16[272,256]{1,0:T(8,128)(2,1)S(1)} %collective-permute-done.3.across_ref) | copy-start | bytes 417796
  45.8 2.0 copy-start.5
  47.8 0.7 copy-start.6
  50.5 6.7 %collective-permute-start.6 = (bf16[272,256]{1,0:T(8,128)(2,1)}, bf16[272,256]{1,0:T(8,128)(2,1)S(1)}, u32[]{:S(2)}, u32[]{:S(2)}) collective-permute-start(bf16[272,256]{1,0:T(8,128)(2,1)} %get-tuple-element.19), channel_id=1, source_target_pairs={{0,64},{8,72},{16,80},{24,88},{32,96},{40,104},{48,112},{56,120},{... | collective-permute-start | bytes 417800 | tf_op jit(solution)/shard_map/ppermute | solution.py:363
  51.8 8.9 %collective-permute-start.5 = (bf16[272,256]{1,0:T(8,128)(2,1)}, bf16[272,256]{1,0:T(8,128)(2,1)S(1)}, u32[]{:S(2)}, u32[]{:S(2)}) collective-permute-start(bf16[272,256]{1,0:T(8,128)(2,1)} %get-tuple-element.19), channel_id=1, source_target_pairs={{0,128},{8,136},{16,144},{24,152},{32,160},{40,168},{48,176},{56,1... | collective-permute-start | bytes 417800 | tf_op jit(solution)/shard_map/ppermute | solution.py:363
  55.9 7.1 %collective-permute-start.4 = (bf16[272,256]{1,0:T(8,128)(2,1)}, bf16[272,256]{1,0:T(8,128)(2,1)S(1)}, u32[]{:S(2)}, u32[]{:S(2)}) collective-permute-start(bf16[272,256]{1,0:T(8,128)(2,1)} %get-tuple-element.19), channel_id=1, source_target_pairs={{0,192},{8,200},{16,208},{24,216},{32,224},{40,232},{48,240},{56,2... | collective-permute-start | bytes 417800 | tf_op jit(solution)/shard_map/ppermute | solution.py:363
  57.3 5.8 %copy-start.1 = (bf16[272,256]{1,0:T(8,128)(2,1)}, bf16[272,256]{1,0:T(8,128)(2,1)S(1)}, u32[]{:S(2)}) copy-start(bf16[272,256]{1,0:T(8,128)(2,1)S(1)} %collective-permute-done.6.row1_ref) | copy-start | bytes 417796
  60.7 2.3 %copy-start.2 = (bf16[272,256]{1,0:T(8,128)(2,1)}, bf16[272,256]{1,0:T(8,128)(2,1)S(1)}, u32[]{:S(2)}) copy-start(bf16[272,256]{1,0:T(8,128)(2,1)S(1)} %collective-permute-done.5.row2_ref) | copy-start | bytes 417796
  63.0 0.7 copy-start.4
  65.8 3.5 %collective-permute-start.7 = (bf16[256,256]{1,0:T(8,128)(2,1)}, bf16[256,256]{1,0:T(8,128)(2,1)S(1)}, u32[]{:S(2)}, u32[]{:S(2)}) collective-permute-start(bf16[256,256]{1,0:T(8,128)(2,1)} %get-tuple-element.22), channel_id=1, source_target_pairs={{0,8},{8,0},{16,24},{24,16},{32,40},{40,32},{48,56},{56,48},{64,72... | collective-permute-start | bytes 393224 | tf_op jit(solution)/shard_map/ppermute | solution.py:381
  69.3 0.7 copy-start.7
  74.6 11.1 %collective-permute-start.8 = (bf16[8192,256]{1,0:T(8,128)(2,1)}, bf16[8192,256]{1,0:T(8,128)(2,1)S(1)}, u32[]{:S(2)}, u32[]{:S(2)}) collective-permute-start(bf16[8192,256]{1,0:T(8,128)(2,1)} %all-gather.4.cloned.1.call-done.fetched), channel_id=1, source_target_pairs={{0,8},{8,0},{16,24},{24,16},{32,40},{40,32},{48,56},{56,48},{64,72... | collective-permute-start | bytes 12582920 | tf_op jit(solution)/shard_map/ppermute | solution.py:381
  85.7 2.1 %copy-start.8 = (bf16[8192,256]{1,0:T(8,128)(2,1)}, bf16[8192,256]{1,0:T(8,128)(2,1)S(1)}, u32[]{:S(2)}) copy-start(bf16[8192,256]{1,0:T(8,128)(2,1)S(1)} %collective-permute-done.8.other) | copy-start | bytes 12582916
Sparse Core Ops, SparseCore 0:
  9.2 27.4 all-gather.5
  38.4 36.1 all-gather.3
  101.2 95.6 reduce-scatter.1

commit v5 on v4

--- a/solution.py
+++ b/solution.py
@@ -189,13 +189,14 @@
 
 
 class Attention:
-    def __init__(self, len_ref, first_ref, q_ref, fetched, other, q_scr, kv_scr, kv_sem):
+    def __init__(self, len_ref, first_ref, q_ref, fetched, other, q_scr, kv_scr, kv_sem, near_only=False):
         self.first = first_ref[0]
         self.ends = ends_of(len_ref)
         self.mine = self.first // CHUNK
         self.low = start_of(self.first, self.ends) // CHUNK
         self.last_start = start_of(self.first + ROWS - 1, self.ends)
         self.arrays = (fetched, other)
+        self.near_only, self.every = near_only, False
         self.q_scr, self.kv_scr, self.kv_sem = q_scr, kv_scr, kv_sem
         for g in range(2):
             rows = slice(g * ROWS, (g + 1) * ROWS)
@@ -205,21 +206,52 @@
             q_scr[rows, HD:] = (scaled - high.astype(jnp.float32)).astype(jnp.bfloat16)
 
     def count(self, far):
-        return (self.mine - far - self.low) // 2 + 1
+        return 4 if self.near_only else (self.mine - far - self.low) // 2 + 1
 
     def block(self, far, i):
-        return self.mine - far - 2 * i
+        if not self.near_only:
+            return self.mine - far - 2 * i
+        core = self.mine % 2
+        step = jnp.where(core == far, 2, 8)
+        return self.mine + jnp.where(core == 0, far, -far) - step * i
+
+    def in_line(self, far, i):
+        block = self.block(far, i)
+        row = block // 8 == self.mine // 8
+        column = (block // 2) % 4 == (self.mine // 2) % 4
+        return jnp.where(block % 2 == 0, row, column)
+
+    def wanted(self, far, i):
+        block = self.block(far, i)
+        if self.near_only:
+            return (block >= self.low) & (block <= self.mine) & self.in_line(far, i)
+        return self.every | jnp.logical_not(self.in_line(far, i))
 
     def copy(self, far, i):
         block = self.block(far, i)
-        x, y, core = block // 8, (block // 2) % 4, block % 2
-        slot = jnp.where(core == 0, x * 4 + y, y * 4 + x)
+        x, y, even = block // 8, (block // 2) % 4, block % 2 == 0
+        my_x, my_y = self.mine // 8, (self.mine // 2) % 4
+        distance = jnp.where(even, (my_y - y) % 4, (my_x - x) % 4)
+        slot = distance ^ (distance >> 1)
+        if not self.near_only:
+            slot = slot + 4 * jnp.where(even, x, y)
         rows = pl.ds(pl.multiple_of(slot * CHUNK, CHUNK), CHUNK)
         to = far * (SLOTS // 2) + i
         return pltpu.make_async_copy(self.arrays[far].at[rows], self.kv_scr.at[to], self.kv_sem.at[to])
 
     def fetch(self, far):
-        lax.fori_loop(0, self.count(far), lambda i, _: (self.copy(far, i).start(), 0)[1], 0)
+        def one_chunk(i, _):
+            pl.when(self.wanted(far, i))(lambda: self.copy(far, i).start())
+            return 0
+
+        lax.fori_loop(0, self.count(far), one_chunk, 0)
+
+    def arrive(self, far):
+        def one_chunk(i, _):
+            pl.when(self.wanted(far, i))(lambda: self.copy(far, i).wait())
+            return 0
+
+        lax.fori_loop(0, self.count(far), one_chunk, 0)
 
     def scores(self, far, i, rows, masked):
         k = self.kv_scr[far * (SLOTS // 2) + i, :, :HD]
@@ -240,12 +272,13 @@
 
     def over_chunks(self, far, step, wait):
         def one_chunk(i, _):
+            wanted = self.wanted(far, i)
             if wait:
-                self.copy(far, i).wait()
+                pl.when(wanted)(lambda: self.copy(far, i).wait())
             block = self.block(far, i)
             masked = (block == self.mine) | (block * CHUNK < self.last_start)
-            pl.when(masked)(lambda: step(far, i, True))
-            pl.when(jnp.logical_not(masked))(lambda: step(far, i, False))
+            pl.when(wanted & masked)(lambda: step(far, i, True))
+            pl.when(wanted & jnp.logical_not(masked))(lambda: step(far, i, False))
             return 0
 
         lax.fori_loop(0, self.count(far), one_chunk, 0)
@@ -277,10 +310,19 @@
         self.over_chunks(far, step, False)
 
 
-def part_kernel(len_ref, first_ref, q_ref, fetched, acc_ref, q_scr, kv_scr, kv_sem):
+def line_kernel(len_ref, first_ref, q_ref, line, line_got, acc_ref, q_scr, kv_scr, kv_sem):
+    attention = Attention(len_ref, first_ref, q_ref, line, line_got, q_scr, kv_scr, kv_sem, near_only=True)
+    attention.fetch(0)
+    attention.fetch(1)
+    acc_ref[...] = jnp.zeros_like(acc_ref)
+    attention.add(0, acc_ref)
+    attention.add(1, acc_ref)
+
+
+def part_kernel(len_ref, first_ref, q_ref, before_ref, fetched, acc_ref, q_scr, kv_scr, kv_sem):
     attention = Attention(len_ref, first_ref, q_ref, fetched, None, q_scr, kv_scr, kv_sem)
     attention.fetch(0)
-    acc_ref[...] = jnp.zeros_like(acc_ref)
+    acc_ref[...] = before_ref[...]
     attention.add(0, acc_ref)
 
 
@@ -322,8 +364,10 @@
 
     @pl.when(jnp.logical_not(fine))
     def _():
-        attention.fetch(0)
-        lax.fori_loop(0, attention.count(0), lambda i, _: (attention.copy(0, i).wait(), 0)[1], 0)
+        attention.every = True
+        for far in range(2):
+            attention.fetch(far)
+            attention.arrive(far)
         acc_scr[...] = jnp.zeros_like(acc_scr)
         m_scr[...] = jnp.full(m_scr.shape, LOW, jnp.float32)
         attention.add_shifted(0, acc_scr, m_scr)
@@ -363,10 +407,10 @@
     return lax.ppermute(block, "pack", pairs)
 
 
-def lines(stage):
-    rows = [[x * 8 + y * 2 + stage for y in range(4)] for x in range(4)]
-    columns = [[x * 8 + y * 2 + 1 - stage for x in range(4)] for y in range(4)]
-    return rows + columns
+def lines():
+    columns = [[x * 8 + y * 2 for x in range(4)] for y in range(4)]
+    rows = [[x * 8 + y * 2 + 1 for y in range(4)] for x in range(4)]
+    return columns + rows
 
 
 def along_x(distance):
@@ -408,7 +452,9 @@
     first = jnp.reshape(lax.axis_index("pack") * ROWS, (1,)).astype(jnp.int32)
     kv = keys_values.reshape(ROWS, 2 * HD)
     nowhere = lambda x, y: None
-    first_stage = lax.all_gather(kv, "pack", axis=0, tiled=True, axis_index_groups=lines(0))
+    below = moved(kv, along_y(1), along_x(1))
+    above = moved(kv, along_y(3), along_x(3))
+    across = moved(kv, along_y(2), along_x(2))
     y_local, run_keep, run_send, fac = pl.pallas_call(
         ssd_kernel,
         out_shape=(
@@ -424,14 +470,35 @@
         name="ssd_local",
     )(lengths, decay_log, skip_gain, first, ssm_values, ssm_maps, step_size.T)
 
+    below, above, across = lax.optimization_barrier((below, above, across, fac))[:3]
+    line = jnp.concatenate([kv, below, above, across], axis=0)
+    fetched = lax.all_gather(line, "pack", axis=0, tiled=True, axis_index_groups=lines())
+    line_got = swapped(line)
+
     run = (STATE_ROWS, HALF)
     run_got = swapped(run_send)
     (chip,) = call(chip_kernel, [run], 2, first, run_keep, run_got)
-    first_stage = lax.optimization_barrier((first_stage, chip))[0]
-    fetched = lax.all_gather(first_stage, "pack", axis=0, tiled=True, axis_index_groups=lines(1))
     chips = [moved(chip, along_y(d), along_y(d)) for d in (1, 3, 2)]
     prefix, total = call(row_kernel, [run, run], 4, first, chip, *chips)
     rows = [moved(total, along_x(d), along_x(d)) for d in (3, 2, 1)]
+    line_got = lax.optimization_barrier((line_got, prefix))[0]
+    scores_scratch = [
+        pltpu.VMEM((2 * ROWS, 2 * HD), jnp.bfloat16),
+        pltpu.VMEM((SLOTS, CHUNK, 2 * HD), jnp.bfloat16),
+        pltpu.SemaphoreType.DMA((SLOTS,)),
+    ]
+    attention_out = jax.ShapeDtypeStruct((2 * ROWS, 2 * HD), jnp.float32)
+    near = pl.pallas_call(
+        line_kernel,
+        out_shape=attention_out,
+        in_specs=[SMEM] * 2 + [VMEM] + [ANY] * 2,
+        out_specs=VMEM,
+        scratch_shapes=scores_scratch,
+        compiler_params=big(),
+        cost_estimate=pl.CostEstimate(flops=4 * 10**9, bytes_accessed=5 * 10**6, transcendentals=5 * 10**6),
+        name="line",
+    )(lengths, first, queries, line, line_got)
+    rows = lax.optimization_barrier((*rows, near))[:3]
     keep, send = call(carry_kernel, [(SN, HALF)] * 2, 6, first, *rows, prefix, run_keep, run_got)
     got = swapped(send)
     act = pl.pallas_call(
@@ -446,21 +513,16 @@
 
     fetched = lax.optimization_barrier((fetched, act))[0]
     other = swapped(fetched)
-    scores_scratch = [
-        pltpu.VMEM((2 * ROWS, 2 * HD), jnp.bfloat16),
-        pltpu.VMEM((SLOTS, CHUNK, 2 * HD), jnp.bfloat16),
-        pltpu.SemaphoreType.DMA((SLOTS,)),
-    ]
     partial = pl.pallas_call(
         part_kernel,
-        out_shape=jax.ShapeDtypeStruct((2 * ROWS, 2 * HD), jnp.float32),
-        in_specs=[SMEM] * 2 + [VMEM, ANY],
+        out_shape=attention_out,
+        in_specs=[SMEM] * 2 + [VMEM] * 2 + [ANY],
         out_specs=VMEM,
         scratch_shapes=scores_scratch,
         compiler_params=big(),
         cost_estimate=pl.CostEstimate(flops=9 * 10**9, bytes_accessed=5 * 10**6, transcendentals=5 * 10**6),
         name="part",
-    )(lengths, first, queries, fetched)
+    )(lengths, first, queries, near, fetched)
 
     terms = pl.pallas_call(
         mix_kernel,

time: 200 us -> 191 us (0.955)
  waiting for transfers between devices: 132 us -> 108 us
  starting transfers between devices: 20.3 us -> 25.9 us
  Pallas kernels: 33.1 us -> 38 us
    all_gather x2 -> x1, waiting for transfers between devices: 17.2 us -> 0.01 us  [local(): lax.all_gather(line, 'pack', axis=0, tiled=True, axis_index_groups=lines())]
    ppermute x6 -> x9, starting transfers between devices: 10.7 us -> 20 us  [moved(): return lax.ppermute(block, 'pack', pairs)]
    ppermute x6 -> x9, waiting for transfers between devices: 12.9 us -> 7.15 us  [moved(): return lax.ppermute(block, 'pack', pairs)]
    pallas_call x1 -> x2, Pallas kernels: 4.06 us -> 7.93 us  [the longest x1 5.21 us: local(): pl.pallas_call(line_kernel, out_shape=attention_out, in_specs=[SMEM] * 2...]
    ppermute x3 -> x4, starting transfers between devices: 9.59 us -> 5.8 us  [swapped(): return lax.ppermute(block, 'pack', [(i, i ^ 1) for i in range(32)])]
    reduce_scatter x1, waiting for transfers between devices: 95.8 us -> 93.1 us  [local(): return lax.psum_scatter(terms, 'tp', scatter_dimension=0, tiled=True)]
    ppermute x3 -> x4, waiting for transfers between devices: 5.33 us -> 7.72 us  [swapped(): return lax.ppermute(block, 'pack', [(i, i ^ 1) for i in range(32)])]
    unnamed x18 -> x24, local copies, waits for them, and re-layouts: 4.75 us -> 6.34 us
  transfers between devices with their start and end apart: 12 -> 15, of which waited for: 11 -> 7; matrix products, arithmetic and copies ran while one was open for 0% -> 0% of each run, Pallas kernels for 10% -> 12%
where the time goes in v5:
time: 191 us; the launch traced here: 193 us
  waiting for transfers between devices  108 us (57%)
  Pallas kernels  38 us (20%)
  starting transfers between devices  25.9 us (14%)
  between operations  13.6 us (7%)
  local copies, waits for them, and re-layouts  6.34 us (3%)
    reduce_scatter x1, waiting for transfers between devices, local(): return lax.psum_scatter(terms, 'tp', scatter_dimension=0, tiled=True)  93.1 us
    ppermute x9, starting transfers between devices, moved(): return lax.ppermute(block, 'pack', pairs)  20 us
    pallas_call x1, Pallas kernels, local(): pl.pallas_call(mix_kernel, out_shape=jax.ShapeDtypeStruct((ROWS, DM), jnp...  14.3 us
    ppermute x4, waiting for transfers between devices, swapped(): return lax.ppermute(block, 'pack', [(i, i ^ 1) for i in range(32)])  7.72 us
    ppermute x9, waiting for transfers between devices, moved(): return lax.ppermute(block, 'pack', pairs)  7.15 us
    unnamed x24, local copies, waits for them, and re-layouts  6.34 us
    pallas_call x1, Pallas kernels, local(): pl.pallas_call(ssd_kernel, out_shape=(jax.ShapeDtypeStruct((ROWS, HP), jn...  6.22 us
    pallas_call x3, Pallas kernels, call(): pl.pallas_call(kernel, out_shape=tuple((jax.ShapeDtypeStruct(shape, jnp.b...  5.88 us
  transfers between devices with their start and end apart: 15, of which 7 were waited for; matrix products, arithmetic and copies ran while one was open for 0% of the time, Pallas kernels for 12%

profile of v5, /device:TPU:1, one launch (start us, length us, event | category | flops | bytes accessed | tf_op | source)
XLA Modules:
  0.0 192.8 jit_solution(15202153455034061219)
XLA Ops:
  6.5 5.6 %collective-permute-start.9 = (bf16[512,256]{1,0:T(8,128)(2,1)}, bf16[512,256]{1,0:T(8,128)(2,1)S(1)}, u32[]{:S(2)}, u32[]{:S(2)}) collective-permute-start(bf16[512,256]{1,0:T(8,128)(2,1)} %bitcast.3), channel_id=1, source_target_pairs={{0,32},{8,136},{16,48},{24,152},{32,0},{40,168},{48,16},{56,184},{... | collective-permute-start | bytes 786440 | tf_op jit(solution)/shard_map/ppermute | solution.py:407
  12.2 1.3 collective-permute-start.8
  13.5 1.6 collective-permute-start.7
  15.1 6.2 %ssd_local.1 = (f32[512,512]{1,0:T(8,128)}, bf16[272,256]{1,0:T(8,128)(2,1)}, bf16[272,256]{1,0:T(8,128)(2,1)}, f32[512,8]{1,0:T(8,128)}) custom-call(s32[4]{0:T(128)} %len_ref.7, f32[8]{0:T(128)} %dl_ref.1, f32[8]{0:T(128)} %skip_ref.1, s32[1]{0:T(128)} %bitcast.first_ref, bf16[512,512]{1,0:T(8,128)(2,1)} %x_ref.1, bf16[512,512]{1,0:T(8,128)(2,1)} %maps_ref.3, ...), custom_call_target="tpu_custom_call" | custom-call | flops 1000000000 | bytes 4000000 | tf_op jit(solution)/shard_map/ssd_local/pallas_call | solution.py:458
  22.5 4.7 %collective-permute-start.10 = (bf16[2048,256]{1,0:T(8,128)(2,1)}, bf16[2048,256]{1,0:T(8,128)(2,1)S(1)}, u32[]{:S(2)}, u32[]{:S(2)}) collective-permute-start(bf16[2048,256]{1,0:T(8,128)(2,1)} %pad_maximum_fusion.line), channel_id=1, source_target_pairs={{0,8},{8,0},{16,24},{24,16},{32,40},{40,32},{48,56},{56,48},{64,72... | collective-permute-start | bytes 3145736 | tf_op jit(solution)/shard_map/ppermute | solution.py:425
  27.3 2.2 %collective-permute-done.other_ref = bf16[272,256]{1,0:T(8,128)(2,1)S(1)} collective-permute-done((bf16[272,256]{1,0:T(8,128)(2,1)S(1)}, bf16[272,256]{1,0:T(8,128)(2,1)S(1)}, u32[]{:S(2)}, u32[]{:S(2)}) %collective-permute-start) | collective-permute-done | bytes 139296 | tf_op jit(solution)/shard_map/ppermute | solution.py:425
  30.2 1.7 shard_map.109.mine_ref
  31.9 1.3 collective-permute-start.3
  34.6 4.0 %collective-permute-done.3.across_ref = bf16[272,256]{1,0:T(8,128)(2,1)S(1)} collective-permute-done((bf16[272,256]{1,0:T(8,128)(2,1)}, bf16[272,256]{1,0:T(8,128)(2,1)S(1)}, u32[]{:S(2)}, u32[]{:S(2)}) %collective-permute-start.3) | collective-permute-done | bytes 139296 | tf_op jit(solution)/shard_map/ppermute | solution.py:407
  38.5 2.1 %collective-permute-done.2.above_ref = bf16[272,256]{1,0:T(8,128)(2,1)S(1)} collective-permute-done((bf16[272,256]{1,0:T(8,128)(2,1)}, bf16[272,256]{1,0:T(8,128)(2,1)S(1)}, u32[]{:S(2)}, u32[]{:S(2)}) %collective-permute-start.2) | collective-permute-done | bytes 139296 | tf_op jit(solution)/shard_map/ppermute | solution.py:407
  40.6 1.1 collective-permute-done.1.below_ref
  42.4 2.1 %shard_map.110 = (bf16[272,256]{1,0:T(8,128)(2,1)}, bf16[272,256]{1,0:T(8,128)(2,1)}) custom-call(s32[1]{0:T(128)} %bitcast.first_ref, bf16[272,256]{1,0:T(8,128)(2,1)} %shard_map.109.mine_ref, bf16[272,256]{1,0:T(8,128)(2,1)} %copy-done.7, bf16[272,256]{1,0:T(8,128)(2,1)} %copy-done.6, bf16[272,256]{1,0:T(8,128)(2,1)} %copy-done.5), custom_call_target="tpu_custom_call" | custom-call | flops 1000000 | bytes 1000000 | tf_op jit(solution)/shard_map/pallas_call | solution.py:429
  44.5 3.1 %collective-permute-start.6 = (bf16[272,256]{1,0:T(8,128)(2,1)}, bf16[272,256]{1,0:T(8,128)(2,1)S(1)}, u32[]{:S(2)}, u32[]{:S(2)}) collective-permute-start(bf16[272,256]{1,0:T(8,128)(2,1)} %get-tuple-element.25), channel_id=1, source_target_pairs={{0,64},{8,72},{16,80},{24,88},{32,96},{40,104},{48,112},{56,120},{... | collective-permute-start | bytes 417800 | tf_op jit(solution)/shard_map/ppermute | solution.py:407
  47.6 4.4 %collective-permute-start.5 = (bf16[272,256]{1,0:T(8,128)(2,1)}, bf16[272,256]{1,0:T(8,128)(2,1)S(1)}, u32[]{:S(2)}, u32[]{:S(2)}) collective-permute-start(bf16[272,256]{1,0:T(8,128)(2,1)} %get-tuple-element.25), channel_id=1, source_target_pairs={{0,128},{8,136},{16,144},{24,152},{32,160},{40,168},{48,176},{56,1... | collective-permute-start | bytes 417800 | tf_op jit(solution)/shard_map/ppermute | solution.py:407
  52.0 1.3 collective-permute-start.4
  54.2 5.2 %line.1.before_ref = f32[1024,256]{1,0:T(8,128)} custom-call(s32[4]{0:T(128)} %len_ref.7, s32[1]{0:T(128)} %bitcast.first_ref, bf16[512,256]{1,0:T(8,128)(2,1)} %q_ref.5, bf16[2048,256]{1,0:T(8,128)(2,1)} %pad_maximum_fusion.line, bf16[2048,256]{1,0:T(8,128)(2,1)} %copy-done.10), custom_call_target="tpu_custom_call" | custom-call | flops 4000000000 | bytes 5000000 | tf_op jit(solution)/shard_map/line/pallas_call | solution.py:491
  60.8 2.1 %shard_map.111 = (bf16[256,256]{1,0:T(8,128)(2,1)}, bf16[256,256]{1,0:T(8,128)(2,1)}) custom-call(s32[1]{0:T(128)} %bitcast.first_ref, bf16[272,256]{1,0:T(8,128)(2,1)} %copy-done.4, bf16[272,256]{1,0:T(8,128)(2,1)} %copy-done.3, bf16[272,256]{1,0:T(8,128)(2,1)} %copy-done.2, bf16[272,256]{1,0:T(8,128)(2,1)} %get-tuple-element.29.prefix_ref, ...), custom_call_target="tpu_custom_call" | custom-call | flops 1000000 | bytes 1000000 | tf_op jit(solution)/shard_map/pallas_call | solution.py:429
  63.6 1.2 collective-permute-done.11.got_ref
  65.4 3.7 %gate.1.act_ref = bf16[512,512]{1,0:T(8,128)(2,1)} custom-call(s32[1]{0:T(128)} %bitcast.first_ref, f32[512,512]{1,0:T(8,128)} %get-tuple-element.21.y_ref, bf16[512,512]{1,0:T(8,128)(2,1)} %z_ref.1, bf16[512,512]{1,0:T(8,128)(2,1)} %maps_ref.3, f32[512,8]{1,0:T(8,128)} %get-tuple-element.22.fac_ref, bf16[256,256]{1,0:T(8,128)(2,1)} %get-tuple-element.34.keep_ref, ...), custom_call_target="tpu_custom_call" | custom-call | flops 100000000 | bytes 3000000 | tf_op jit(solution)/shard_map/gate/pallas_call | solution.py:504
  69.5 2.7 %part.1.acc_ref = f32[1024,256]{1,0:T(8,128)} custom-call(s32[4]{0:T(128)} %len_ref.7, s32[1]{0:T(128)} %bitcast.first_ref, bf16[512,256]{1,0:T(8,128)(2,1)} %q_ref.5, f32[1024,256]{1,0:T(8,128)} %line.1.before_ref, bf16[8192,256]{1,0:T(8,128)(2,1)} %all-gather.2.cloned.1.call-done.fetched), custom_call_target="tpu_custom_call" | custom-call | flops 8999999488 | bytes 5000000 | tf_op jit(solution)/shard_map/part/pallas_call | solution.py:516
  72.3 4.3 %collective-permute-done.12.other = bf16[8192,256]{1,0:T(8,128)(2,1)S(1)} collective-permute-done((bf16[8192,256]{1,0:T(8,128)(2,1)}, bf16[8192,256]{1,0:T(8,128)(2,1)S(1)}, u32[]{:S(2)}, u32[]{:S(2)}) %collective-permute-start.12) | collective-permute-done | bytes 4194336 | tf_op jit(solution)/shard_map/ppermute | solution.py:425
  76.5 2.1 %copy-done.9 = bf16[8192,256]{1,0:T(8,128)(2,1)} copy-done((bf16[8192,256]{1,0:T(8,128)(2,1)}, bf16[8192,256]{1,0:T(8,128)(2,1)S(1)}, u32[]{:S(2)}) %copy-start.9) | copy-done | bytes 4194328
  78.6 14.3 %mix.1 = bf16[512,5120]{1,0:T(8,128)(2,1)} custom-call(s32[4]{0:T(128)} %len_ref.7, s32[1]{0:T(128)} %bitcast.first_ref, bf16[512,256]{1,0:T(8,128)(2,1)} %q_ref.5, bf16[512,512]{1,0:T(8,128)(2,1)} %gate.1.act_ref, f32[1024,256]{1,0:T(8,128)} %part.1.acc_ref, bf16[8192,256]{1,0:T(8,128)(2,1)} %all-gather.2.cloned.1.call-done.fetched, ...), custom_call_target="tpu_custom_call" | custom-call | flops 8999999488 | bytes 25000000 | tf_op jit(solution)/shard_map/mix/pallas_call | solution.py:527
  92.9 93.1 %reduce-scatter.2.cloned.1.call-done = bf16[64,5120]{1,0:T(8,128)(2,1)} async-done(((bf16[512,5120]{1,0:T(8,128)(2,1)}), bf16[64,5120]{1,0:T(8,128)(2,1)}) %reduce-scatter.2.cloned.1.call-update) | async-done | bytes 655376 | tf_op jit(solution)/shard_map/reduce_scatter | solution.py:546
  (41 shorter events, 8.0 us)
Async XLA Ops:
  6.5 14.8 %copy-start.1 = (bf16[512,1,256]{2,0,1:T(8,128)(2,1)S(1)}, bf16[512,1,256]{2,0,1:T(8,128)(2,1)}, u32[]{:S(2)}) copy-start(bf16[512,1,256]{2,0,1:T(8,128)(2,1)} %param.12) | copy-start | bytes 786436
  6.5 62.6 %all-gather.2.cloned.1.call-start = ((), (), s32[]{:S(2)}) async-start(), calls=%async_computation.1 | async-start | bytes 5242880 | tf_op jit(solution)/shard_map/all_gather | solution.py:475
  6.5 14.8 %collective-permute-start.9 = (bf16[512,256]{1,0:T(8,128)(2,1)}, bf16[512,256]{1,0:T(8,128)(2,1)S(1)}, u32[]{:S(2)}, u32[]{:S(2)}) collective-permute-start(bf16[512,256]{1,0:T(8,128)(2,1)} %bitcast.3), channel_id=1, source_target_pairs={{0,32},{8,136},{16,48},{24,152},{32,0},{40,168},{48,16},{56,184},{... | collective-permute-start | bytes 786440 | tf_op jit(solution)/shard_map/ppermute | solution.py:407
  12.2 9.2 %collective-permute-start.8 = (bf16[512,256]{1,0:T(8,128)(2,1)}, bf16[512,256]{1,0:T(8,128)(2,1)S(1)}, u32[]{:S(2)}, u32[]{:S(2)}) collective-permute-start(bf16[512,256]{1,0:T(8,128)(2,1)} %bitcast.4), channel_id=1, source_target_pairs={{0,48},{8,200},{16,0},{24,216},{32,16},{40,232},{48,32},{56,248},{... | collective-permute-start | bytes 786440 | tf_op jit(solution)/shard_map/ppermute | solution.py:407
  13.5 7.9 %collective-permute-start.7 = (bf16[512,256]{1,0:T(8,128)(2,1)}, bf16[512,256]{1,0:T(8,128)(2,1)S(1)}, u32[]{:S(2)}, u32[]{:S(2)}) collective-permute-start(bf16[512,256]{1,0:T(8,128)(2,1)} %bitcast.5), channel_id=1, source_target_pairs={{0,16},{8,72},{16,32},{24,88},{32,48},{40,104},{48,0},{56,120},{64... | collective-permute-start | bytes 786440 | tf_op jit(solution)/shard_map/ppermute | solution.py:407
  21.3 5.8 %copy-start.11 = (bf16[272,256]{1,0:T(8,128)(2,1)S(1)}, bf16[272,256]{1,0:T(8,128)(2,1)}, u32[]{:S(2)}) copy-start(bf16[272,256]{1,0:T(8,128)(2,1)} %get-tuple-element.24) | copy-start | bytes 417796
  22.4 163.6 %reduce-scatter.2.cloned.1.call-start = ((), (), s32[]{:S(2)}) async-start(), calls=%async_computation.2 | async-start | bytes 5898240 | tf_op jit(solution)/shard_map/reduce_scatter | solution.py:546
  22.5 30.8 %collective-permute-start.10 = (bf16[2048,256]{1,0:T(8,128)(2,1)}, bf16[2048,256]{1,0:T(8,128)(2,1)S(1)}, u32[]{:S(2)}, u32[]{:S(2)}) collective-permute-start(bf16[2048,256]{1,0:T(8,128)(2,1)} %pad_maximum_fusion.line), channel_id=1, source_target_pairs={{0,8},{8,0},{16,24},{24,16},{32,40},{40,32},{48,56},{56,48},{64,72... | collective-permute-start | bytes 3145736 | tf_op jit(solution)/shard_map/ppermute | solution.py:425
  27.1 2.4 %collective-permute-start = (bf16[272,256]{1,0:T(8,128)(2,1)S(1)}, bf16[272,256]{1,0:T(8,128)(2,1)S(1)}, u32[]{:S(2)}, u32[]{:S(2)}) collective-permute-start(bf16[272,256]{1,0:T(8,128)(2,1)S(1)} %copy-done.11), channel_id=1, source_target_pairs={{0,8},{8,0},{16,24},{24,16},{32,40},{40,32},{48,56},{56,48},{64,72... | collective-permute-start | bytes 417800 | tf_op jit(solution)/shard_map/ppermute | solution.py:425
  31.9 6.7 %collective-permute-start.3 = (bf16[272,256]{1,0:T(8,128)(2,1)}, bf16[272,256]{1,0:T(8,128)(2,1)S(1)}, u32[]{:S(2)}, u32[]{:S(2)}) collective-permute-start(bf16[272,256]{1,0:T(8,128)(2,1)} %shard_map.109.mine_ref), channel_id=1, source_target_pairs={{0,32},{8,40},{16,48},{24,56},{32,0},{40,8},{48,16},{56,24},{64,96... | collective-permute-start | bytes 417800 | tf_op jit(solution)/shard_map/ppermute | solution.py:407
  33.1 7.5 %collective-permute-start.2 = (bf16[272,256]{1,0:T(8,128)(2,1)}, bf16[272,256]{1,0:T(8,128)(2,1)S(1)}, u32[]{:S(2)}, u32[]{:S(2)}) collective-permute-start(bf16[272,256]{1,0:T(8,128)(2,1)} %shard_map.109.mine_ref), channel_id=1, source_target_pairs={{0,48},{8,56},{16,0},{24,8},{32,16},{40,24},{48,32},{56,40},{64,11... | collective-permute-start | bytes 417800 | tf_op jit(solution)/shard_map/ppermute | solution.py:407
  34.1 7.6 %collective-permute-start.1 = (bf16[272,256]{1,0:T(8,128)(2,1)}, bf16[272,256]{1,0:T(8,128)(2,1)S(1)}, u32[]{:S(2)}, u32[]{:S(2)}) collective-permute-start(bf16[272,256]{1,0:T(8,128)(2,1)} %shard_map.109.mine_ref), channel_id=1, source_target_pairs={{0,16},{8,24},{16,32},{24,40},{32,48},{40,56},{48,0},{56,8},{64,80... | collective-permute-start | bytes 417800 | tf_op jit(solution)/shard_map/ppermute | solution.py:407
  38.5 3.2 %copy-start.5 = (bf16[272,256]{1,0:T(8,128)(2,1)}, bf16[272,256]{1,0:T(8,128)(2,1)S(1)}, u32[]{:S(2)}) copy-start(bf16[272,256]{1,0:T(8,128)(2,1)S(1)} %collective-permute-done.3.across_ref) | copy-start | bytes 417796
  40.6 1.1 copy-start.6
  41.7 0.7 copy-start.7
  44.5 15.0 %collective-permute-start.6 = (bf16[272,256]{1,0:T(8,128)(2,1)}, bf16[272,256]{1,0:T(8,128)(2,1)S(1)}, u32[]{:S(2)}, u32[]{:S(2)}) collective-permute-start(bf16[272,256]{1,0:T(8,128)(2,1)} %get-tuple-element.25), channel_id=1, source_target_pairs={{0,64},{8,72},{16,80},{24,88},{32,96},{40,104},{48,112},{56,120},{... | collective-permute-start | bytes 417800 | tf_op jit(solution)/shard_map/ppermute | solution.py:407
  47.6 11.9 %collective-permute-start.5 = (bf16[272,256]{1,0:T(8,128)(2,1)}, bf16[272,256]{1,0:T(8,128)(2,1)S(1)}, u32[]{:S(2)}, u32[]{:S(2)}) collective-permute-start(bf16[272,256]{1,0:T(8,128)(2,1)} %get-tuple-element.25), channel_id=1, source_target_pairs={{0,128},{8,136},{16,144},{24,152},{32,160},{40,168},{48,176},{56,1... | collective-permute-start | bytes 417800 | tf_op jit(solution)/shard_map/ppermute | solution.py:407
  52.0 7.6 %collective-permute-start.4 = (bf16[272,256]{1,0:T(8,128)(2,1)}, bf16[272,256]{1,0:T(8,128)(2,1)S(1)}, u32[]{:S(2)}, u32[]{:S(2)}) collective-permute-start(bf16[272,256]{1,0:T(8,128)(2,1)} %get-tuple-element.25), channel_id=1, source_target_pairs={{0,192},{8,200},{16,208},{24,216},{32,224},{40,232},{48,240},{56,2... | collective-permute-start | bytes 417800 | tf_op jit(solution)/shard_map/ppermute | solution.py:407
  53.3 1.0 copy-start.10
  59.5 0.7 copy-start.2
  59.5 0.7 copy-start.3
  62.9 1.9 collective-permute-start.11
  69.2 7.4 %collective-permute-start.12 = (bf16[8192,256]{1,0:T(8,128)(2,1)}, bf16[8192,256]{1,0:T(8,128)(2,1)S(1)}, u32[]{:S(2)}, u32[]{:S(2)}) collective-permute-start(bf16[8192,256]{1,0:T(8,128)(2,1)} %all-gather.2.cloned.1.call-done.fetched), channel_id=1, source_target_pairs={{0,8},{8,0},{16,24},{24,16},{32,40},{40,32},{48,56},{56,48},{64,72... | collective-permute-start | bytes 12582920 | tf_op jit(solution)/shard_map/ppermute | solution.py:425
  76.5 2.1 %copy-start.9 = (bf16[8192,256]{1,0:T(8,128)(2,1)}, bf16[8192,256]{1,0:T(8,128)(2,1)S(1)}, u32[]{:S(2)}) copy-start(bf16[8192,256]{1,0:T(8,128)(2,1)S(1)} %collective-permute-done.12.other) | copy-start | bytes 12582916
  (3 other events, 2.0 us)
Sparse Core Ops, SparseCore 0:
  22.5 39.6 all-gather.1
  93.0 92.9 reduce-scatter.1

commit v6 on v4

--- a/solution.py
+++ b/solution.py
@@ -19,6 +19,7 @@
 LOW = -1e30
 LOG2E = 1.4426950408889634
 HIGH = lax.Precision.HIGHEST
+LIMIT = 62 * 2**20
 HALF = HP // 2
 STATE_ROWS = SN + 16
 VMEM = pl.BlockSpec(memory_space=pltpu.VMEM)
@@ -178,51 +179,91 @@
     send_ref[...] = jnp.where(core == 0, behind[0], run[0]).astype(jnp.bfloat16)
 
 
-def gate_kernel(first_ref, y_ref, z_ref, maps_ref, fac_ref, keep_ref, got_ref, act_ref):
+def gate_kernel(first_ref, y_ref, z_ref, read_ref, fac_ref, keep_ref, got_ref, act_ref):
     core = (first_ref[0] // ROWS) % 2
     keep, got = keep_ref[...], got_ref[...]
     state = jnp.concatenate([jnp.where(core == 0, keep, got), jnp.where(core == 0, got, keep)], axis=1)
-    reads = jnp.dot(maps_ref[:, SN:], state, preferred_element_type=jnp.float32)
+    reads = jnp.dot(read_ref[...], state, preferred_element_type=jnp.float32)
     y = y_ref[...] + reads * widen(fac_ref[...], spread())
     z = z_ref[...].astype(jnp.float32)
     act_ref[...] = (y * (z / (1.0 + jnp.exp(-z)))).astype(jnp.bfloat16)
 
 
 class Attention:
-    def __init__(self, len_ref, first_ref, q_ref, fetched, other, q_scr, kv_scr, kv_sem):
+    def __init__(self, len_ref, first_ref, fetched, other, q_scr, kv_scr, ids, kv_sem, near_only=False):
         self.first = first_ref[0]
         self.ends = ends_of(len_ref)
         self.mine = self.first // CHUNK
         self.low = start_of(self.first, self.ends) // CHUNK
         self.last_start = start_of(self.first + ROWS - 1, self.ends)
         self.arrays = (fetched, other)
-        self.q_scr, self.kv_scr, self.kv_sem = q_scr, kv_scr, kv_sem
-        for g in range(2):
-            rows = slice(g * ROWS, (g + 1) * ROWS)
-            scaled = q_ref[:, g * HD : (g + 1) * HD].astype(jnp.float32) * (LOG2E * HD**-0.5)
-            high = scaled.astype(jnp.bfloat16)
-            q_scr[rows, :HD] = high
-            q_scr[rows, HD:] = (scaled - high.astype(jnp.float32)).astype(jnp.bfloat16)
+        self.near_only = near_only
+        self.q_scr, self.kv_scr, self.ids, self.kv_sem = q_scr, kv_scr, ids, kv_sem
 
     def count(self, far):
-        return (self.mine - far - self.low) // 2 + 1
+        return 4 if self.near_only else (self.mine - far - self.low) // 2 + 1
 
     def block(self, far, i):
-        return self.mine - far - 2 * i
-
-    def copy(self, far, i):
-        block = self.block(far, i)
-        x, y, core = block // 8, (block // 2) % 4, block % 2
-        slot = jnp.where(core == 0, x * 4 + y, y * 4 + x)
-        rows = pl.ds(pl.multiple_of(slot * CHUNK, CHUNK), CHUNK)
-        to = far * (SLOTS // 2) + i
-        return pltpu.make_async_copy(self.arrays[far].at[rows], self.kv_scr.at[to], self.kv_sem.at[to])
-
-    def fetch(self, far):
-        lax.fori_loop(0, self.count(far), lambda i, _: (self.copy(far, i).start(), 0)[1], 0)
-
-    def scores(self, far, i, rows, masked):
-        k = self.kv_scr[far * (SLOTS // 2) + i, :, :HD]
+        if not self.near_only:
+            return self.mine - far - 2 * i
+        core = self.mine % 2
+        step = jnp.where(core == far, 2, 8)
+        return self.mine + jnp.where(core == 0, far, -far) - step * i
+
+    def in_line(self, block):
+        row = block // 8 == self.mine // 8
+        column = (block // 2) % 4 == (self.mine // 2) % 4
+        return jnp.where(block % 2 == 0, row, column)
+
+    def place(self, block):
+        x, y, even = block // 8, (block // 2) % 4, block % 2 == 0
+        my_x, my_y = self.mine // 8, (self.mine // 2) % 4
+        distance = jnp.where(even, (my_y - y) % 4, (my_x - x) % 4)
+        place = distance ^ (distance >> 1)
+        if not self.near_only:
+            place = place + 4 * jnp.where(even, x, y)
+        return place
+
+    def copy(self, far, place, slot):
+        rows = pl.ds(pl.multiple_of(place * CHUNK, CHUNK), CHUNK)
+        to = pl.ds(pl.multiple_of(slot * CHUNK, CHUNK), CHUNK)
+        return pltpu.make_async_copy(self.arrays[far].at[rows], self.kv_scr.at[to], self.kv_sem.at[slot])
+
+    def fetch(self, fars, every=False):
+        def one_chunk(far, i, carry):
+            plain, masked = carry
+            block = self.block(far, i)
+            if self.near_only:
+                wanted = (block >= self.low) & (block <= self.mine) & self.in_line(block)
+            elif every:
+                wanted = block >= self.low
+            else:
+                wanted = jnp.logical_not(self.in_line(block))
+            mask = (block == self.mine) | (block * CHUNK < self.last_start)
+            slot = jnp.where(mask, SLOTS - 1 - masked, plain)
+
+            @pl.when(wanted)
+            def _():
+                self.ids[slot] = block
+                self.copy(far, self.place(block), slot).start()
+
+            new = wanted.astype(jnp.int32)
+            return plain + jnp.where(mask, 0, new), masked + jnp.where(mask, new, 0)
+
+        carry = (jnp.int32(0), jnp.int32(0))
+        for far in fars:
+            carry = lax.fori_loop(0, self.count(far), lambda i, c, far=far: one_chunk(far, i, c), carry)
+        self.plain, self.masked = carry
+
+    def wait(self, slot):
+        self.copy(0, 0, slot).wait()
+
+    def keys(self, slot, chunks):
+        return pl.ds(pl.multiple_of(slot * CHUNK, CHUNK), chunks * CHUNK)
+
+    def scores(self, slot, chunks, r, masked):
+        rows = slice(r * TILE, (r + 1) * TILE)
+        k = self.kv_scr[self.keys(slot, chunks), :HD]
         s = lax.dot_general(
             self.q_scr[rows, :],
             jnp.concatenate([k, k], axis=1),
@@ -230,42 +271,53 @@
             preferred_element_type=jnp.float32,
         )
         if masked:
-            pos = self.first + rows.start % ROWS + iota((rows.stop - rows.start, 1), 0)
-            key = self.block(far, i) * CHUNK + iota((1, CHUNK), 1)
+            pos = self.first + rows.start % ROWS + iota((TILE, 1), 0)
+            key = self.ids[slot] * CHUNK + iota((1, CHUNK), 1)
             s = jnp.where((key >= start_of(pos, self.ends)) & (key <= pos), s, LOW)
         return s
 
-    def values(self, far, i):
-        return jnp.concatenate([self.kv_scr[far * (SLOTS // 2) + i, :, HD:], jnp.ones((CHUNK, HD), jnp.bfloat16)], axis=1)
-
-    def over_chunks(self, far, step, wait):
-        def one_chunk(i, _):
-            if wait:
-                self.copy(far, i).wait()
-            block = self.block(far, i)
-            masked = (block == self.mine) | (block * CHUNK < self.last_start)
-            pl.when(masked)(lambda: step(far, i, True))
-            pl.when(jnp.logical_not(masked))(lambda: step(far, i, False))
+    def values(self, slot, chunks):
+        v = self.kv_scr[self.keys(slot, chunks), HD:]
+        return jnp.concatenate([v, jnp.ones((chunks * CHUNK, HD), jnp.bfloat16)], axis=1)
+
+    def step(self, acc, slot, chunks, masked):
+        v = self.values(slot, chunks)
+        tiles = 2 * ROWS // TILE
+        s = self.scores(slot, chunks, 0, masked)
+        for r in range(tiles):
+            following = self.scores(slot, chunks, r + 1, masked) if r + 1 < tiles else None
+            p = jnp.exp2(s).astype(jnp.bfloat16)
+            acc[r * TILE : (r + 1) * TILE, :] += jnp.dot(p, v, preferred_element_type=jnp.float32)
+            s = following
+
+    def add(self, acc):
+        def one_masked(j, _):
+            self.wait(SLOTS - 1 - j)
+            self.step(acc, SLOTS - 1 - j, 1, True)
             return 0
 
-        lax.fori_loop(0, self.count(far), one_chunk, 0)
-
-    def add(self, far, acc):
-        def step(far, i, masked):
-            v = self.values(far, i)
+        def two_plain(j, _):
+            self.wait(2 * j)
+            self.wait(2 * j + 1)
+            self.step(acc, 2 * j, 2, False)
+            return 0
+
+        lax.fori_loop(0, self.masked, one_masked, 0)
+        lax.fori_loop(0, self.plain // 2, two_plain, 0)
+
+        @pl.when(self.plain % 2 == 1)
+        def _():
+            self.wait(self.plain - 1)
+            self.step(acc, self.plain - 1, 1, False)
+
+    def add_shifted(self, acc, m_scr):
+        def one_chunk(j, _):
+            slot = jnp.where(j < self.plain, j, SLOTS - 1 - (j - self.plain))
+            self.wait(slot)
+            v = self.values(slot, 1)
             for r in range(2 * ROWS // TILE):
                 rows = slice(r * TILE, (r + 1) * TILE)
-                p = jnp.exp2(self.scores(far, i, rows, masked)).astype(jnp.bfloat16)
-                acc[rows, :] += jnp.dot(p, v, preferred_element_type=jnp.float32)
-
-        self.over_chunks(far, step, True)
-
-    def add_shifted(self, far, acc, m_scr):
-        def step(far, i, masked):
-            v = self.values(far, i)
-            for r in range(2 * ROWS // TILE):
-                rows = slice(r * TILE, (r + 1) * TILE)
-                s = self.scores(far, i, rows, masked)
+                s = self.scores(slot, 1, r, True)
                 old = m_scr[rows, :]
                 m = jnp.maximum(old, jnp.max(s, axis=1, keepdims=True))
                 alpha = jnp.exp2(old - m)
@@ -273,68 +325,102 @@
                 out = jnp.dot(p, v, preferred_element_type=jnp.float32)
                 acc[rows, :] = acc[rows, :] * jnp.concatenate([alpha, alpha], axis=1) + out
                 m_scr[rows, :] = m
-
-        self.over_chunks(far, step, False)
-
-
-def part_kernel(len_ref, first_ref, q_ref, fetched, acc_ref, q_scr, kv_scr, kv_sem):
-    attention = Attention(len_ref, first_ref, q_ref, fetched, None, q_scr, kv_scr, kv_sem)
-    attention.fetch(0)
+            return 0
+
+        lax.fori_loop(0, self.plain + self.masked, one_chunk, 0)
+
+
+def own_line_kernel(len_ref, first_ref, q_ref, line, acc_ref, split_ref, kv_scr, ids, kv_sem):
+    attention = Attention(len_ref, first_ref, line, None, split_ref, kv_scr, ids, kv_sem, near_only=True)
+    attention.fetch((0,))
+    for g in range(2):
+        rows = slice(g * ROWS, (g + 1) * ROWS)
+        scaled = q_ref[:, g * HD : (g + 1) * HD].astype(jnp.float32) * (LOG2E * HD**-0.5)
+        high = scaled.astype(jnp.bfloat16)
+        split_ref[rows, :HD] = high
+        split_ref[rows, HD:] = (scaled - high.astype(jnp.float32)).astype(jnp.bfloat16)
     acc_ref[...] = jnp.zeros_like(acc_ref)
-    attention.add(0, acc_ref)
+    attention.add(acc_ref)
+
+
+def other_line_kernel(len_ref, first_ref, split_ref, before_ref, line_got, acc_ref, kv_scr, ids, kv_sem):
+    attention = Attention(len_ref, first_ref, line_got, line_got, split_ref, kv_scr, ids, kv_sem, near_only=True)
+    attention.fetch((1,))
+    acc_ref[...] = before_ref[...]
+    attention.add(acc_ref)
+
+
+def part_kernel(len_ref, first_ref, split_ref, before_ref, fetched, acc_ref, kv_scr, ids, kv_sem):
+    attention = Attention(len_ref, first_ref, fetched, None, split_ref, kv_scr, ids, kv_sem)
+    attention.fetch((0,))
+    acc_ref[...] = before_ref[...]
+    attention.add(acc_ref)
 
 
 def mix_kernel(
     len_ref,
     first_ref,
-    q_ref,
-    act_ref,
-    acc_ref,
+    split_hbm,
+    act_hbm,
+    before_hbm,
     fetched,
     other,
     wa_hbm,
     ws_hbm,
     o_hbm,
+    kv_scr,
+    ids,
+    kv_sem,
     q_scr,
-    kv_scr,
-    kv_sem,
     acc_scr,
     m_scr,
     w_scr,
     in_scr,
     o_scr,
+    in_sem,
     w_sem,
     o_sem,
 ):
-    attention = Attention(len_ref, first_ref, q_ref, fetched, other, q_scr, kv_scr, kv_sem)
-    attention.fetch(1)
-    weights = [
-        pltpu.make_async_copy(wa_hbm, w_scr.at[pl.ds(0, 2 * HD)], w_sem.at[0]),
-        pltpu.make_async_copy(ws_hbm, w_scr.at[pl.ds(2 * HD, HP)], w_sem.at[1]),
+    attention = Attention(len_ref, first_ref, fetched, other, q_scr, kv_scr, ids, kv_sem)
+    inputs = [
+        pltpu.make_async_copy(split_hbm, q_scr, in_sem.at[0]),
+        pltpu.make_async_copy(before_hbm, acc_scr, in_sem.at[1]),
+        pltpu.make_async_copy(act_hbm, in_scr.at[:, pl.ds(2 * HD, HP)], in_sem.at[2]),
     ]
-    for copy in weights:
+    for copy in inputs[:2]:
         copy.start()
-
-    acc_scr[...] = acc_ref[...]
-    attention.add(1, acc_scr)
+    attention.fetch((1,))
+    weights = []
+    for i in range(DM // COLS):
+        cols = pl.ds(i * COLS, COLS)
+        weights.append(
+            (
+                pltpu.make_async_copy(wa_hbm.at[:, cols], w_scr.at[pl.ds(0, 2 * HD), cols], w_sem.at[2 * i]),
+                pltpu.make_async_copy(ws_hbm.at[:, cols], w_scr.at[pl.ds(2 * HD, HP), cols], w_sem.at[2 * i + 1]),
+            )
+        )
+    inputs[2].start()
+    for pair in weights:
+        for copy in pair:
+            copy.start()
+    for copy in inputs[:2]:
+        copy.wait()
+
+    attention.add(acc_scr)
     total = acc_scr[:, HD:]
     fine = (jnp.min(total) > 2.0**-60) & (jnp.max(total) < 2.0**110)
 
     @pl.when(jnp.logical_not(fine))
     def _():
-        attention.fetch(0)
-        lax.fori_loop(0, attention.count(0), lambda i, _: (attention.copy(0, i).wait(), 0)[1], 0)
+        attention.fetch((0, 1), every=True)
         acc_scr[...] = jnp.zeros_like(acc_scr)
         m_scr[...] = jnp.full(m_scr.shape, LOW, jnp.float32)
-        attention.add_shifted(0, acc_scr, m_scr)
-        attention.add_shifted(1, acc_scr, m_scr)
+        attention.add_shifted(acc_scr, m_scr)
 
     for g in range(2):
         rows = slice(g * ROWS, (g + 1) * ROWS)
         in_scr[:, g * HD : (g + 1) * HD] = (acc_scr[rows, :HD] / acc_scr[rows, HD:]).astype(jnp.bfloat16)
-    in_scr[:, 2 * HD :] = act_ref[...]
-    for copy in weights:
-        copy.wait()
+    inputs[2].wait()
 
     def out_copy(i):
         cols = pl.ds(i * COLS, COLS)
@@ -342,6 +428,8 @@
 
     for i in range(DM // COLS):
         cols = slice(i * COLS, (i + 1) * COLS)
+        for copy in weights[i]:
+            copy.wait()
         o_scr[:, cols] = jnp.dot(in_scr[...], w_scr[:, cols], preferred_element_type=jnp.float32).astype(jnp.bfloat16)
         out_copy(i).start()
     for i in range(DM // COLS):
@@ -349,7 +437,7 @@
 
 
 def big(**more):
-    return pltpu.CompilerParams(vmem_limit_bytes=56 * 2**20, **more)
+    return pltpu.CompilerParams(vmem_limit_bytes=LIMIT, **more)
 
 
 def moved(block, route0, route1):
@@ -363,10 +451,10 @@
     return lax.ppermute(block, "pack", pairs)
 
 
-def lines(stage):
-    rows = [[x * 8 + y * 2 + stage for y in range(4)] for x in range(4)]
-    columns = [[x * 8 + y * 2 + 1 - stage for x in range(4)] for y in range(4)]
-    return rows + columns
+def lines():
+    columns = [[x * 8 + y * 2 for x in range(4)] for y in range(4)]
+    rows = [[x * 8 + y * 2 + 1 for y in range(4)] for x in range(4)]
+    return columns + rows
 
 
 def along_x(distance):
@@ -408,7 +496,9 @@
     first = jnp.reshape(lax.axis_index("pack") * ROWS, (1,)).astype(jnp.int32)
     kv = keys_values.reshape(ROWS, 2 * HD)
     nowhere = lambda x, y: None
-    first_stage = lax.all_gather(kv, "pack", axis=0, tiled=True, axis_index_groups=lines(0))
+    below = moved(kv, along_y(1), along_x(1))
+    above = moved(kv, along_y(3), along_x(3))
+    across = moved(kv, along_y(2), along_x(2))
     y_local, run_keep, run_send, fac = pl.pallas_call(
         ssd_kernel,
         out_shape=(
@@ -424,21 +514,60 @@
         name="ssd_local",
     )(lengths, decay_log, skip_gain, first, ssm_values, ssm_maps, step_size.T)
 
+    below, above, across = lax.optimization_barrier((below, above, across, fac))[:3]
+    line = jnp.concatenate([kv, below, above, across], axis=0)
+    fetched = lax.all_gather(line, "pack", axis=0, tiled=True, axis_index_groups=lines())
+    line_got = swapped(line)
+
     run = (STATE_ROWS, HALF)
     run_got = swapped(run_send)
     (chip,) = call(chip_kernel, [run], 2, first, run_keep, run_got)
-    first_stage = lax.optimization_barrier((first_stage, chip))[0]
-    fetched = lax.all_gather(first_stage, "pack", axis=0, tiled=True, axis_index_groups=lines(1))
     chips = [moved(chip, along_y(d), along_y(d)) for d in (1, 3, 2)]
+    chunks_scratch = [
+        pltpu.VMEM((SLOTS * CHUNK, 2 * HD), jnp.bfloat16),
+        pltpu.SMEM((SLOTS,), jnp.int32),
+        pltpu.SemaphoreType.DMA((SLOTS,)),
+    ]
+    sums = jax.ShapeDtypeStruct((2 * ROWS, 2 * HD), jnp.float32)
+    split = jax.ShapeDtypeStruct((2 * ROWS, 2 * HD), jnp.bfloat16)
+
+    def attend(kernel, name, shapes, vmem, *args):
+        out = pl.pallas_call(
+            kernel,
+            out_shape=shapes,
+            in_specs=[SMEM] * 2 + [VMEM] * vmem + [ANY],
+            out_specs=(VMEM,) * len(shapes),
+            scratch_shapes=chunks_scratch,
+            compiler_params=big(),
+            cost_estimate=pl.CostEstimate(flops=3 * 10**9, bytes_accessed=5 * 10**6, transcendentals=5 * 10**6),
+            name=name,
+        )(lengths, first, *args)
+        return out
+
+    line = lax.optimization_barrier((line, chip))[0]
+    acc, queries_split = attend(own_line_kernel, "own_line", (sums, split), 1, queries, line)
+    chips = lax.optimization_barrier((*chips, acc))[:3]
     prefix, total = call(row_kernel, [run, run], 4, first, chip, *chips)
     rows = [moved(total, along_x(d), along_x(d)) for d in (3, 2, 1)]
+    line_got = lax.optimization_barrier((line_got, prefix))[0]
+    (acc,) = attend(other_line_kernel, "other_line", (sums,), 2, queries_split, acc, line_got)
+    rows = lax.optimization_barrier((*rows, acc))[:3]
     keep, send = call(carry_kernel, [(SN, HALF)] * 2, 6, first, *rows, prefix, run_keep, run_got)
     got = swapped(send)
     act = pl.pallas_call(
         gate_kernel,
         out_shape=jax.ShapeDtypeStruct((ROWS, HP), jnp.bfloat16),
-        in_specs=[SMEM] + [VMEM] * 6,
-        out_specs=VMEM,
+        grid=(2,),
+        in_specs=[
+            SMEM,
+            pl.BlockSpec((ROWS // 2, HP), lambda i: (i, 0)),
+            pl.BlockSpec((ROWS // 2, HP), lambda i: (i, 0)),
+            pl.BlockSpec((ROWS // 2, SN), lambda i: (i, 1)),
+            pl.BlockSpec((ROWS // 2, HEADS), lambda i: (i, 0)),
+            pl.BlockSpec((SN, HALF), lambda i: (0, 0)),
+            pl.BlockSpec((SN, HALF), lambda i: (0, 0)),
+        ],
+        out_specs=pl.BlockSpec((ROWS // 2, HP), lambda i: (i, 0)),
         compiler_params=big(),
         cost_estimate=pl.CostEstimate(flops=10**8, bytes_accessed=3 * 10**6, transcendentals=3 * 10**5),
         name="gate",
@@ -446,41 +575,29 @@
 
     fetched = lax.optimization_barrier((fetched, act))[0]
     other = swapped(fetched)
-    scores_scratch = [
-        pltpu.VMEM((2 * ROWS, 2 * HD), jnp.bfloat16),
-        pltpu.VMEM((SLOTS, CHUNK, 2 * HD), jnp.bfloat16),
-        pltpu.SemaphoreType.DMA((SLOTS,)),
-    ]
-    partial = pl.pallas_call(
-        part_kernel,
-        out_shape=jax.ShapeDtypeStruct((2 * ROWS, 2 * HD), jnp.float32),
-        in_specs=[SMEM] * 2 + [VMEM, ANY],
-        out_specs=VMEM,
-        scratch_shapes=scores_scratch,
-        compiler_params=big(),
-        cost_estimate=pl.CostEstimate(flops=9 * 10**9, bytes_accessed=5 * 10**6, transcendentals=5 * 10**6),
-        name="part",
-    )(lengths, first, queries, fetched)
+    (acc,) = attend(part_kernel, "part", (sums,), 2, queries_split, acc, fetched)
 
     terms = pl.pallas_call(
         mix_kernel,
         out_shape=jax.ShapeDtypeStruct((ROWS, DM), jnp.bfloat16),
-        in_specs=[SMEM] * 2 + [VMEM] * 3 + [ANY] * 4,
+        in_specs=[SMEM] * 2 + [ANY] * 7,
         out_specs=ANY,
-        scratch_shapes=scores_scratch
+        scratch_shapes=chunks_scratch
         + [
+            pltpu.VMEM((2 * ROWS, 2 * HD), jnp.bfloat16),
             pltpu.VMEM((2 * ROWS, 2 * HD), jnp.float32),
             pltpu.VMEM((2 * ROWS, HD), jnp.float32),
             pltpu.VMEM((2 * HD + HP, DM), jnp.bfloat16),
             pltpu.VMEM((ROWS, 2 * HD + HP), jnp.bfloat16),
             pltpu.VMEM((ROWS, DM), jnp.bfloat16),
-            pltpu.SemaphoreType.DMA((2,)),
+            pltpu.SemaphoreType.DMA((3,)),
+            pltpu.SemaphoreType.DMA((2 * (DM // COLS),)),
             pltpu.SemaphoreType.DMA((DM // COLS,)),
         ],
         compiler_params=big(),
         cost_estimate=pl.CostEstimate(flops=9 * 10**9, bytes_accessed=25 * 10**6, transcendentals=9 * 10**6),
         name="mix",
-    )(lengths, first, queries, act, partial, fetched, other, attn_out_weight, ssd_out_weight)
+    )(lengths, first, queries_split, act, acc, fetched, other, attn_out_weight, ssd_out_weight)
     return lax.psum_scatter(terms, "tp", scatter_dimension=0, tiled=True)
 
 

time: 200 us -> 184 us (0.920); the launches traced: 203 us -> 183 us
  waiting for transfers between devices: 132 us -> 97.7 us
  Pallas kernels: 33.1 us -> 41.1 us
  starting transfers between devices: 20.3 us -> 26.3 us
    all_gather x2 -> x1, waiting for transfers between devices: 17.2 us -> 0.01 us  [local(): lax.all_gather(line, 'pack', axis=0, tiled=True, axis_index_groups=lines())]
    reduce_scatter x1, waiting for transfers between devices: 95.8 us -> 85.9 us  [local(): return lax.psum_scatter(terms, 'tp', scatter_dimension=0, tiled=True)]
    ppermute x6 -> x9, starting transfers between devices: 10.7 us -> 20 us  [moved(): return lax.ppermute(block, 'pack', pairs)]
    ppermute x6 -> x9, waiting for transfers between devices: 12.9 us -> 3.81 us  [moved(): return lax.ppermute(block, 'pack', pairs)]
    pallas_call x1 -> x3, Pallas kernels: 4.06 us -> 11.1 us  [attend(): pl.pallas_call(kernel, out_shape=shapes, in_specs=[SMEM] * 2 + [VMEM] * v...]
    ppermute x3 -> x4, starting transfers between devices: 9.59 us -> 6.2 us  [swapped(): return lax.ppermute(block, 'pack', [(i, i ^ 1) for i in range(32)])]
    ppermute x3 -> x4, waiting for transfers between devices: 5.33 us -> 7.89 us  [swapped(): return lax.ppermute(block, 'pack', [(i, i ^ 1) for i in range(32)])]
    unnamed x18 -> x22, local copies, waits for them, and re-layouts: 4.75 us -> 3.62 us
  transfers between devices with their start and end apart: 12 -> 15, of which waited for: 11 -> 7; matrix products, arithmetic and copies ran while one was open for 0% -> 0% of each run, Pallas kernels for 10% -> 15%
where the time goes in v6:
time: 184 us; the launch traced here: 183 us
  waiting for transfers between devices  97.7 us (53%)
  Pallas kernels  41.1 us (22%)
  starting transfers between devices  26.3 us (14%)
  between operations  13.6 us (7%)
  local copies, waits for them, and re-layouts  3.62 us (2%)
    reduce_scatter x1, waiting for transfers between devices, local(): return lax.psum_scatter(terms, 'tp', scatter_dimension=0, tiled=True)  85.9 us
    ppermute x9, starting transfers between devices, moved(): return lax.ppermute(block, 'pack', pairs)  20 us
    pallas_call x1, Pallas kernels, local(): pl.pallas_call(mix_kernel, out_shape=jax.ShapeDtypeStruct((ROWS, DM), jnp...  14.4 us
    pallas_call x3, Pallas kernels, attend(): pl.pallas_call(kernel, out_shape=shapes, in_specs=[SMEM] * 2 + [VMEM] * v...  11.1 us
    ppermute x4, waiting for transfers between devices, swapped(): return lax.ppermute(block, 'pack', [(i, i ^ 1) for i in range(32)])  7.89 us
    pallas_call x1, Pallas kernels, local(): pl.pallas_call(ssd_kernel, out_shape=(jax.ShapeDtypeStruct((ROWS, HP), jn...  6.22 us
    ppermute x4, starting transfers between devices, swapped(): return lax.ppermute(block, 'pack', [(i, i ^ 1) for i in range(32)])  6.2 us
    pallas_call x3, Pallas kernels, call(): pl.pallas_call(kernel, out_shape=tuple((jax.ShapeDtypeStruct(shape, jnp.b...  5.89 us
  transfers between devices with their start and end apart: 15, of which 7 were waited for; matrix products, arithmetic and copies ran while one was open for 0% of the time, Pallas kernels for 15%

profile of v6, /device:TPU:1, one launch (start us, length us, event | category | flops | bytes accessed | tf_op | source)
XLA Modules:
  0.0 183.3 jit_solution(1943683756790141491)
XLA Ops:
  6.5 5.6 %collective-permute-start.2 = (bf16[512,256]{1,0:T(8,128)(2,1)}, bf16[512,256]{1,0:T(8,128)(2,1)S(1)}, u32[]{:S(2)}, u32[]{:S(2)}) collective-permute-start(bf16[512,256]{1,0:T(8,128)(2,1)} %bitcast.3), channel_id=1, source_target_pairs={{0,32},{8,136},{16,48},{24,152},{32,0},{40,168},{48,16},{56,184},{... | collective-permute-start | bytes 786440 | tf_op jit(solution)/shard_map/ppermute | solution.py:451
  12.2 1.3 collective-permute-start.1
  13.5 1.6 collective-permute-start
  15.1 6.2 %ssd_local.1 = (f32[512,512]{1,0:T(8,128)}, bf16[272,256]{1,0:T(8,128)(2,1)}, bf16[272,256]{1,0:T(8,128)(2,1)}, f32[512,8]{1,0:T(8,128)}) custom-call(s32[4]{0:T(128)} %len_ref.9, f32[8]{0:T(128)} %dl_ref.1, f32[8]{0:T(128)} %skip_ref.1, s32[1]{0:T(128)} %bitcast.first_ref, bf16[512,512]{1,0:T(8,128)(2,1)} %x_ref.1, bf16[512,512]{1,0:T(8,128)(2,1)} %read_ref.1, ...), custom_call_target="tpu_custom_call" | custom-call | flops 1000000000 | bytes 4000000 | tf_op jit(solution)/shard_map/ssd_local/pallas_call | solution.py:502
  22.5 4.7 %collective-permute-start.10 = (bf16[2048,256]{1,0:T(8,128)(2,1)}, bf16[2048,256]{1,0:T(8,128)(2,1)S(1)}, u32[]{:S(2)}, u32[]{:S(2)}) collective-permute-start(bf16[2048,256]{1,0:T(8,128)(2,1)} %pad_maximum_fusion.line), channel_id=1, source_target_pairs={{0,8},{8,0},{16,24},{24,16},{32,40},{40,32},{48,56},{56,48},{64,72... | collective-permute-start | bytes 3145736 | tf_op jit(solution)/shard_map/ppermute | solution.py:469
  27.3 2.2 %collective-permute-done.3.other_ref = bf16[272,256]{1,0:T(8,128)(2,1)S(1)} collective-permute-done((bf16[272,256]{1,0:T(8,128)(2,1)S(1)}, bf16[272,256]{1,0:T(8,128)(2,1)S(1)}, u32[]{:S(2)}, u32[]{:S(2)}) %collective-permute-start.3) | collective-permute-done | bytes 139296 | tf_op jit(solution)/shard_map/ppermute | solution.py:469
  30.2 1.7 shard_map.109.mine_ref
  31.9 1.3 collective-permute-start.6
  34.6 4.1 %own_line.1 = (f32[1024,256]{1,0:T(8,128)}, bf16[1024,256]{1,0:T(8,128)(2,1)}) custom-call(s32[4]{0:T(128)} %len_ref.9, s32[1]{0:T(128)} %bitcast.first_ref, bf16[512,256]{1,0:T(8,128)(2,1)} %q_ref.1, bf16[2048,256]{1,0:T(8,128)(2,1)} %pad_maximum_fusion.line), custom_call_target="tpu_custom_call" | custom-call | flops 3000000000 | bytes 5000000 | tf_op jit(solution)/shard_map/own_line/pallas_call | solution.py:535
  38.7 1.9 %collective-permute-done.5.above_ref = bf16[272,256]{1,0:T(8,128)(2,1)S(1)} collective-permute-done((bf16[272,256]{1,0:T(8,128)(2,1)}, bf16[272,256]{1,0:T(8,128)(2,1)S(1)}, u32[]{:S(2)}, u32[]{:S(2)}) %collective-permute-start.5) | collective-permute-done | bytes 139296 | tf_op jit(solution)/shard_map/ppermute | solution.py:451
  40.6 1.1 collective-permute-done.4.below_ref
  42.3 2.1 %shard_map.110 = (bf16[272,256]{1,0:T(8,128)(2,1)}, bf16[272,256]{1,0:T(8,128)(2,1)}) custom-call(s32[1]{0:T(128)} %bitcast.first_ref, bf16[272,256]{1,0:T(8,128)(2,1)} %shard_map.109.mine_ref, bf16[272,256]{1,0:T(8,128)(2,1)} %copy-done.7, bf16[272,256]{1,0:T(8,128)(2,1)} %copy-done.6, bf16[272,256]{1,0:T(8,128)(2,1)} %copy-done.5), custom_call_target="tpu_custom_call" | custom-call | flops 1000000 | bytes 1000000 | tf_op jit(solution)/shard_map/pallas_call | solution.py:473
  44.5 3.1 %collective-permute-start.9 = (bf16[272,256]{1,0:T(8,128)(2,1)}, bf16[272,256]{1,0:T(8,128)(2,1)S(1)}, u32[]{:S(2)}, u32[]{:S(2)}) collective-permute-start(bf16[272,256]{1,0:T(8,128)(2,1)} %get-tuple-element.40), channel_id=1, source_target_pairs={{0,64},{8,72},{16,80},{24,88},{32,96},{40,104},{48,112},{56,120},{... | collective-permute-start | bytes 417800 | tf_op jit(solution)/shard_map/ppermute | solution.py:451
  47.6 4.4 %collective-permute-start.8 = (bf16[272,256]{1,0:T(8,128)(2,1)}, bf16[272,256]{1,0:T(8,128)(2,1)S(1)}, u32[]{:S(2)}, u32[]{:S(2)}) collective-permute-start(bf16[272,256]{1,0:T(8,128)(2,1)} %get-tuple-element.40), channel_id=1, source_target_pairs={{0,128},{8,136},{16,144},{24,152},{32,160},{40,168},{48,176},{56,1... | collective-permute-start | bytes 417800 | tf_op jit(solution)/shard_map/ppermute | solution.py:451
  52.0 1.3 collective-permute-start.7
  54.3 4.3 %other_line.1.before_ref = f32[1024,256]{1,0:T(8,128)} custom-call(s32[4]{0:T(128)} %len_ref.9, s32[1]{0:T(128)} %bitcast.first_ref, bf16[1024,256]{1,0:T(8,128)(2,1)} %get-tuple-element.34.split_ref.split_hbm, f32[1024,256]{1,0:T(8,128)} %get-tuple-element.36.before_ref, bf16[2048,256]{1,0:T(8,128)(2,1)} %copy-done.9), custom_call_target="tpu_custom_call" | custom-call | flops 3000000000 | bytes 5000000 | tf_op jit(solution)/shard_map/other_line/pallas_call | solution.py:535
  60.2 2.1 %shard_map.111 = (bf16[256,256]{1,0:T(8,128)(2,1)}, bf16[256,256]{1,0:T(8,128)(2,1)}) custom-call(s32[1]{0:T(128)} %bitcast.first_ref, bf16[272,256]{1,0:T(8,128)(2,1)} %copy-done.4, bf16[272,256]{1,0:T(8,128)(2,1)} %copy-done.3, bf16[272,256]{1,0:T(8,128)(2,1)} %copy-done.2, bf16[272,256]{1,0:T(8,128)(2,1)} %get-tuple-element.41.prefix_ref, ...), custom_call_target="tpu_custom_call" | custom-call | flops 1000000 | bytes 1000000 | tf_op jit(solution)/shard_map/pallas_call | solution.py:473
  62.3 1.1 collective-permute-start.11
  63.3 1.2 collective-permute-done.11.got_ref
  65.2 3.5 %gate.1.act_hbm = bf16[512,512]{1,0:T(8,128)(2,1)} custom-call(s32[1]{0:T(128)} %bitcast.first_ref, f32[512,512]{1,0:T(8,128)} %get-tuple-element.35.y_ref, bf16[512,512]{1,0:T(8,128)(2,1)} %z_ref.1, bf16[512,512]{1,0:T(8,128)(2,1)} %read_ref.1, f32[512,8]{1,0:T(8,128)} %get-tuple-element.27.fac_ref, bf16[256,256]{1,0:T(8,128)(2,1)} %get-tuple-element.46.keep_ref, ...), custom_call_target="tpu_custom_call" | custom-call | flops 100000000 | bytes 3000000 | tf_op jit(solution)/shard_map/gate/pallas_call | solution.py:557
  69.0 2.7 %part.1.before_hbm = f32[1024,256]{1,0:T(8,128)} custom-call(s32[4]{0:T(128)} %len_ref.9, s32[1]{0:T(128)} %bitcast.first_ref, bf16[1024,256]{1,0:T(8,128)(2,1)} %get-tuple-element.34.split_ref.split_hbm, f32[1024,256]{1,0:T(8,128)} %other_line.1.before_ref, bf16[8192,256]{1,0:T(8,128)(2,1)} %all-gather.2.cloned.1.call-done.fetched), custom_call_target="tpu_custom_call" | custom-call | flops 3000000000 | bytes 5000000 | tf_op jit(solution)/shard_map/part/pallas_call | solution.py:535
  71.7 4.4 %collective-permute-done.12.other = bf16[8192,256]{1,0:T(8,128)(2,1)} collective-permute-done((bf16[8192,256]{1,0:T(8,128)(2,1)}, bf16[8192,256]{1,0:T(8,128)(2,1)}, u32[]{:S(2)}, u32[]{:S(2)}) %collective-permute-start.12) | collective-permute-done | bytes 4194336 | tf_op jit(solution)/shard_map/ppermute | solution.py:469
  76.2 14.4 %mix.1 = bf16[512,5120]{1,0:T(8,128)(2,1)} custom-call(s32[4]{0:T(128)} %len_ref.9, s32[1]{0:T(128)} %bitcast.first_ref, bf16[1024,256]{1,0:T(8,128)(2,1)} %get-tuple-element.34.split_ref.split_hbm, bf16[512,512]{1,0:T(8,128)(2,1)} %gate.1.act_hbm, f32[1024,256]{1,0:T(8,128)} %part.1.before_hbm, bf16[8192,256]{1,0:T(8,128)(2,1)} %all-gather.2.cloned.1.call-done.fetched, ...), custom_call_target="tpu_custom_call" | custom-call | flops 8999999488 | bytes 25000000 | tf_op jit(solution)/shard_map/mix/pallas_call | solution.py:580
  90.6 85.9 %reduce-scatter.2.cloned.1.call-done = bf16[64,5120]{1,0:T(8,128)(2,1)} async-done(((bf16[512,5120]{1,0:T(8,128)(2,1)}), bf16[64,5120]{1,0:T(8,128)(2,1)}) %reduce-scatter.2.cloned.1.call-update) | async-done | bytes 655376 | tf_op jit(solution)/shard_map/reduce_scatter | solution.py:601
  (40 shorter events, 7.6 us)
Async XLA Ops:
  6.5 14.8 %copy-start.1 = (bf16[512,1,256]{2,0,1:T(8,128)(2,1)S(1)}, bf16[512,1,256]{2,0,1:T(8,128)(2,1)}, u32[]{:S(2)}) copy-start(bf16[512,1,256]{2,0,1:T(8,128)(2,1)} %param.12) | copy-start | bytes 786436
  6.5 62.1 %all-gather.2.cloned.1.call-start = ((), (), s32[]{:S(2)}) async-start(), calls=%async_computation.1 | async-start | bytes 5242880 | tf_op jit(solution)/shard_map/all_gather | solution.py:519
  6.5 14.8 %collective-permute-start.2 = (bf16[512,256]{1,0:T(8,128)(2,1)}, bf16[512,256]{1,0:T(8,128)(2,1)S(1)}, u32[]{:S(2)}, u32[]{:S(2)}) collective-permute-start(bf16[512,256]{1,0:T(8,128)(2,1)} %bitcast.3), channel_id=1, source_target_pairs={{0,32},{8,136},{16,48},{24,152},{32,0},{40,168},{48,16},{56,184},{... | collective-permute-start | bytes 786440 | tf_op jit(solution)/shard_map/ppermute | solution.py:451
  12.2 9.2 %collective-permute-start.1 = (bf16[512,256]{1,0:T(8,128)(2,1)}, bf16[512,256]{1,0:T(8,128)(2,1)S(1)}, u32[]{:S(2)}, u32[]{:S(2)}) collective-permute-start(bf16[512,256]{1,0:T(8,128)(2,1)} %bitcast.4), channel_id=1, source_target_pairs={{0,48},{8,200},{16,0},{24,216},{32,16},{40,232},{48,32},{56,248},{... | collective-permute-start | bytes 786440 | tf_op jit(solution)/shard_map/ppermute | solution.py:451
  13.5 7.9 %collective-permute-start = (bf16[512,256]{1,0:T(8,128)(2,1)}, bf16[512,256]{1,0:T(8,128)(2,1)S(1)}, u32[]{:S(2)}, u32[]{:S(2)}) collective-permute-start(bf16[512,256]{1,0:T(8,128)(2,1)} %bitcast.5), channel_id=1, source_target_pairs={{0,16},{8,72},{16,32},{24,88},{32,48},{40,104},{48,0},{56,120},{64... | collective-permute-start | bytes 786440 | tf_op jit(solution)/shard_map/ppermute | solution.py:451
  21.3 5.8 %copy-start.10 = (bf16[272,256]{1,0:T(8,128)(2,1)S(1)}, bf16[272,256]{1,0:T(8,128)(2,1)}, u32[]{:S(2)}) copy-start(bf16[272,256]{1,0:T(8,128)(2,1)} %get-tuple-element.32) | copy-start | bytes 417796
  22.4 154.1 %reduce-scatter.2.cloned.1.call-start = ((), (), s32[]{:S(2)}) async-start(), calls=%async_computation.2 | async-start | bytes 5898240 | tf_op jit(solution)/shard_map/reduce_scatter | solution.py:601
  22.5 30.8 %collective-permute-start.10 = (bf16[2048,256]{1,0:T(8,128)(2,1)}, bf16[2048,256]{1,0:T(8,128)(2,1)S(1)}, u32[]{:S(2)}, u32[]{:S(2)}) collective-permute-start(bf16[2048,256]{1,0:T(8,128)(2,1)} %pad_maximum_fusion.line), channel_id=1, source_target_pairs={{0,8},{8,0},{16,24},{24,16},{32,40},{40,32},{48,56},{56,48},{64,72... | collective-permute-start | bytes 3145736 | tf_op jit(solution)/shard_map/ppermute | solution.py:469
  27.1 2.4 %collective-permute-start.3 = (bf16[272,256]{1,0:T(8,128)(2,1)S(1)}, bf16[272,256]{1,0:T(8,128)(2,1)S(1)}, u32[]{:S(2)}, u32[]{:S(2)}) collective-permute-start(bf16[272,256]{1,0:T(8,128)(2,1)S(1)} %copy-done.10), channel_id=1, source_target_pairs={{0,8},{8,0},{16,24},{24,16},{32,40},{40,32},{48,56},{56,48},{64,72... | collective-permute-start | bytes 417800 | tf_op jit(solution)/shard_map/ppermute | solution.py:469
  29.5 0.7 copy-start
  31.9 6.9 %collective-permute-start.6 = (bf16[272,256]{1,0:T(8,128)(2,1)}, bf16[272,256]{1,0:T(8,128)(2,1)S(1)}, u32[]{:S(2)}, u32[]{:S(2)}) collective-permute-start(bf16[272,256]{1,0:T(8,128)(2,1)} %shard_map.109.mine_ref), channel_id=1, source_target_pairs={{0,32},{8,40},{16,48},{24,56},{32,0},{40,8},{48,16},{56,24},{64,96... | collective-permute-start | bytes 417800 | tf_op jit(solution)/shard_map/ppermute | solution.py:451
  33.1 7.5 %collective-permute-start.5 = (bf16[272,256]{1,0:T(8,128)(2,1)}, bf16[272,256]{1,0:T(8,128)(2,1)S(1)}, u32[]{:S(2)}, u32[]{:S(2)}) collective-permute-start(bf16[272,256]{1,0:T(8,128)(2,1)} %shard_map.109.mine_ref), channel_id=1, source_target_pairs={{0,48},{8,56},{16,0},{24,8},{32,16},{40,24},{48,32},{56,40},{64,11... | collective-permute-start | bytes 417800 | tf_op jit(solution)/shard_map/ppermute | solution.py:451
  34.1 7.6 %collective-permute-start.4 = (bf16[272,256]{1,0:T(8,128)(2,1)}, bf16[272,256]{1,0:T(8,128)(2,1)S(1)}, u32[]{:S(2)}, u32[]{:S(2)}) collective-permute-start(bf16[272,256]{1,0:T(8,128)(2,1)} %shard_map.109.mine_ref), channel_id=1, source_target_pairs={{0,16},{8,24},{16,32},{24,40},{32,48},{40,56},{48,0},{56,8},{64,80... | collective-permute-start | bytes 417800 | tf_op jit(solution)/shard_map/ppermute | solution.py:451
  38.7 3.0 %copy-start.5 = (bf16[272,256]{1,0:T(8,128)(2,1)}, bf16[272,256]{1,0:T(8,128)(2,1)S(1)}, u32[]{:S(2)}) copy-start(bf16[272,256]{1,0:T(8,128)(2,1)S(1)} %collective-permute-done.6.across_ref) | copy-start | bytes 417796
  40.6 1.1 copy-start.6
  44.5 14.2 %collective-permute-start.9 = (bf16[272,256]{1,0:T(8,128)(2,1)}, bf16[272,256]{1,0:T(8,128)(2,1)S(1)}, u32[]{:S(2)}, u32[]{:S(2)}) collective-permute-start(bf16[272,256]{1,0:T(8,128)(2,1)} %get-tuple-element.40), channel_id=1, source_target_pairs={{0,64},{8,72},{16,80},{24,88},{32,96},{40,104},{48,112},{56,120},{... | collective-permute-start | bytes 417800 | tf_op jit(solution)/shard_map/ppermute | solution.py:451
  47.6 11.1 %collective-permute-start.8 = (bf16[272,256]{1,0:T(8,128)(2,1)}, bf16[272,256]{1,0:T(8,128)(2,1)S(1)}, u32[]{:S(2)}, u32[]{:S(2)}) collective-permute-start(bf16[272,256]{1,0:T(8,128)(2,1)} %get-tuple-element.40), channel_id=1, source_target_pairs={{0,128},{8,136},{16,144},{24,152},{32,160},{40,168},{48,176},{56,1... | collective-permute-start | bytes 417800 | tf_op jit(solution)/shard_map/ppermute | solution.py:451
  52.0 7.6 %collective-permute-start.7 = (bf16[272,256]{1,0:T(8,128)(2,1)}, bf16[272,256]{1,0:T(8,128)(2,1)S(1)}, u32[]{:S(2)}, u32[]{:S(2)}) collective-permute-start(bf16[272,256]{1,0:T(8,128)(2,1)} %get-tuple-element.40), channel_id=1, source_target_pairs={{0,192},{8,200},{16,208},{24,216},{32,224},{40,232},{48,240},{56,2... | collective-permute-start | bytes 417800 | tf_op jit(solution)/shard_map/ppermute | solution.py:451
  53.3 1.0 copy-start.9
  58.6 0.9 copy-start.2
  58.7 0.9 copy-start.3
  59.5 0.7 copy-start.4
  62.3 2.3 %collective-permute-start.11 = (bf16[256,256]{1,0:T(8,128)(2,1)}, bf16[256,256]{1,0:T(8,128)(2,1)S(1)}, u32[]{:S(2)}, u32[]{:S(2)}) collective-permute-start(bf16[256,256]{1,0:T(8,128)(2,1)} %get-tuple-element.47), channel_id=1, source_target_pairs={{0,8},{8,0},{16,24},{24,16},{32,40},{40,32},{48,56},{56,48},{64,72... | collective-permute-start | bytes 393224 | tf_op jit(solution)/shard_map/ppermute | solution.py:469
  68.7 7.5 %collective-permute-start.12 = (bf16[8192,256]{1,0:T(8,128)(2,1)}, bf16[8192,256]{1,0:T(8,128)(2,1)}, u32[]{:S(2)}, u32[]{:S(2)}) collective-permute-start(bf16[8192,256]{1,0:T(8,128)(2,1)} %all-gather.2.cloned.1.call-done.fetched), channel_id=1, source_target_pairs={{0,8},{8,0},{16,24},{24,16},{32,40},{40,32},{48,56},{56,48},{64,72... | collective-permute-start | bytes 12582920 | tf_op jit(solution)/shard_map/ppermute | solution.py:469
  (2 other events, 1.3 us)
Sparse Core Ops, SparseCore 0:
  22.6 39.6 all-gather.1
  90.7 85.7 reduce-scatter.1

commit v7 on v6

--- a/solution.py
+++ b/solution.py
@@ -201,7 +201,7 @@
         self.q_scr, self.kv_scr, self.ids, self.kv_sem = q_scr, kv_scr, ids, kv_sem
 
     def count(self, far):
-        return 4 if self.near_only else (self.mine - far - self.low) // 2 + 1
+        return (self.mine - far - self.low) // 2 + 1
 
     def block(self, far, i):
         if not self.near_only:
@@ -215,19 +215,14 @@
         column = (block // 2) % 4 == (self.mine // 2) % 4
         return jnp.where(block % 2 == 0, row, column)
 
-    def place(self, block):
-        x, y, even = block // 8, (block // 2) % 4, block % 2 == 0
-        my_x, my_y = self.mine // 8, (self.mine // 2) % 4
-        distance = jnp.where(even, (my_y - y) % 4, (my_x - x) % 4)
-        place = distance ^ (distance >> 1)
-        if not self.near_only:
-            place = place + 4 * jnp.where(even, x, y)
-        return place
-
-    def copy(self, far, place, slot):
-        rows = pl.ds(pl.multiple_of(place * CHUNK, CHUNK), CHUNK)
+    def copy(self, far, i, slot):
+        if self.near_only:
+            source = self.arrays[far][i ^ (i >> 1)]
+        else:
+            chip = self.block(far, i) // 2
+            source = self.arrays[far].at[pl.ds(pl.multiple_of(chip * CHUNK, CHUNK), CHUNK)]
         to = pl.ds(pl.multiple_of(slot * CHUNK, CHUNK), CHUNK)
-        return pltpu.make_async_copy(self.arrays[far].at[rows], self.kv_scr.at[to], self.kv_sem.at[slot])
+        return pltpu.make_async_copy(source, self.kv_scr.at[to], self.kv_sem.at[slot])
 
     def fetch(self, fars, every=False):
         def one_chunk(far, i, carry):
@@ -245,18 +240,23 @@
             @pl.when(wanted)
             def _():
                 self.ids[slot] = block
-                self.copy(far, self.place(block), slot).start()
+                self.copy(far, i, slot).start()
 
             new = wanted.astype(jnp.int32)
             return plain + jnp.where(mask, 0, new), masked + jnp.where(mask, new, 0)
 
         carry = (jnp.int32(0), jnp.int32(0))
         for far in fars:
-            carry = lax.fori_loop(0, self.count(far), lambda i, c, far=far: one_chunk(far, i, c), carry)
+            if self.near_only:
+                for i in range(4):
+                    carry = one_chunk(far, i, carry)
+            else:
+                carry = lax.fori_loop(0, self.count(far), lambda i, c, far=far: one_chunk(far, i, c), carry)
         self.plain, self.masked = carry
 
     def wait(self, slot):
-        self.copy(0, 0, slot).wait()
+        to = self.kv_scr.at[self.keys(slot, 1)]
+        pltpu.make_async_copy(to, to, self.kv_sem.at[slot]).wait()
 
     def keys(self, slot, chunks):
         return pl.ds(pl.multiple_of(slot * CHUNK, CHUNK), chunks * CHUNK)
@@ -330,8 +330,20 @@
         lax.fori_loop(0, self.plain + self.masked, one_chunk, 0)
 
 
+def stack_kernel(kv, below, above, across, _, line, sem):
+    copies = [
+        pltpu.make_async_copy(piece, line.at[pl.ds(i * CHUNK, CHUNK)], sem.at[i])
+        for i, piece in enumerate((kv, below, above, across))
+    ]
+    for copy in copies:
+        copy.start()
+    for copy in copies:
+        copy.wait()
+
+
 def own_line_kernel(len_ref, first_ref, q_ref, line, acc_ref, split_ref, kv_scr, ids, kv_sem):
-    attention = Attention(len_ref, first_ref, line, None, split_ref, kv_scr, ids, kv_sem, near_only=True)
+    pieces = [line.at[pl.ds(i * CHUNK, CHUNK)] for i in range(4)]
+    attention = Attention(len_ref, first_ref, pieces, None, split_ref, kv_scr, ids, kv_sem, near_only=True)
     attention.fetch((0,))
     for g in range(2):
         rows = slice(g * ROWS, (g + 1) * ROWS)
@@ -344,7 +356,8 @@
 
 
 def other_line_kernel(len_ref, first_ref, split_ref, before_ref, line_got, acc_ref, kv_scr, ids, kv_sem):
-    attention = Attention(len_ref, first_ref, line_got, line_got, split_ref, kv_scr, ids, kv_sem, near_only=True)
+    pieces = [line_got.at[pl.ds(i * CHUNK, CHUNK)] for i in range(4)]
+    attention = Attention(len_ref, first_ref, None, pieces, split_ref, kv_scr, ids, kv_sem, near_only=True)
     attention.fetch((1,))
     acc_ref[...] = before_ref[...]
     attention.add(acc_ref)
@@ -451,10 +464,8 @@
     return lax.ppermute(block, "pack", pairs)
 
 
-def lines():
-    columns = [[x * 8 + y * 2 for x in range(4)] for y in range(4)]
-    rows = [[x * 8 + y * 2 + 1 for y in range(4)] for x in range(4)]
-    return columns + rows
+def parities():
+    return [list(range(core, 32, 2)) for core in range(2)]
 
 
 def along_x(distance):
@@ -496,9 +507,8 @@
     first = jnp.reshape(lax.axis_index("pack") * ROWS, (1,)).astype(jnp.int32)
     kv = keys_values.reshape(ROWS, 2 * HD)
     nowhere = lambda x, y: None
-    below = moved(kv, along_y(1), along_x(1))
-    above = moved(kv, along_y(3), along_x(3))
-    across = moved(kv, along_y(2), along_x(2))
+    fetched = lax.all_gather(kv, "pack", axis=0, tiled=True, axis_index_groups=parities())
+
     y_local, run_keep, run_send, fac = pl.pallas_call(
         ssd_kernel,
         out_shape=(
@@ -514,10 +524,10 @@
         name="ssd_local",
     )(lengths, decay_log, skip_gain, first, ssm_values, ssm_maps, step_size.T)
 
-    below, above, across = lax.optimization_barrier((below, above, across, fac))[:3]
-    line = jnp.concatenate([kv, below, above, across], axis=0)
-    fetched = lax.all_gather(line, "pack", axis=0, tiled=True, axis_index_groups=lines())
-    line_got = swapped(line)
+    kv = lax.optimization_barrier((kv, fac))[0]
+    below = moved(kv, along_y(1), along_x(1))
+    above = moved(kv, along_y(3), along_x(3))
+    across = moved(kv, along_y(2), along_x(2))
 
     run = (STATE_ROWS, HALF)
     run_got = swapped(run_send)
@@ -544,7 +554,16 @@
         )(lengths, first, *args)
         return out
 
-    line = lax.optimization_barrier((line, chip))[0]
+    line = pl.pallas_call(
+        stack_kernel,
+        out_shape=jax.ShapeDtypeStruct((4 * CHUNK, 2 * HD), jnp.bfloat16),
+        in_specs=[ANY] * 5,
+        out_specs=ANY,
+        scratch_shapes=[pltpu.SemaphoreType.DMA((4,))],
+        compiler_params=big(),
+        name="stack",
+    )(kv, below, above, across, chip)
+    line_got = swapped(line)
     acc, queries_split = attend(own_line_kernel, "own_line", (sums, split), 1, queries, line)
     chips = lax.optimization_barrier((*chips, acc))[:3]
     prefix, total = call(row_kernel, [run, run], 4, first, chip, *chips)

time: 184 us -> 217 us (1.18)
  Pallas kernels: 41.1 us -> 73.8 us
    pallas_call x0 -> x1, Pallas kernels: none -> 32.9 us  [local(): pl.pallas_call(stack_kernel, out_shape=jax.ShapeDtypeStruct((4 * CHUNK, 2...]
    unnamed x22 -> x24, local copies, waits for them, and re-layouts: 3.62 us -> 5.71 us
  transfers between devices with their start and end apart: 15 -> 15, of which waited for: 7 -> 7; matrix products, arithmetic and copies ran while one was open for 0% -> 0% of each run, Pallas kernels for 15% -> 27%
where the time goes in v7:
time: 217 us; the launch traced here: 218 us
  waiting for transfers between devices  96.6 us (45%)
  Pallas kernels  73.8 us (34%)
  starting transfers between devices  28.4 us (13%)
  between operations  13.6 us (6%)
  local copies, waits for them, and re-layouts  5.71 us (3%)
    reduce_scatter x1, waiting for transfers between devices, local(): return lax.psum_scatter(terms, 'tp', scatter_dimension=0, tiled=True)  84.1 us
    pallas_call x1, Pallas kernels, local(): pl.pallas_call(stack_kernel, out_shape=jax.ShapeDtypeStruct((4 * CHUNK, 2...  32.9 us
    ppermute x9, starting transfers between devices, moved(): return lax.ppermute(block, 'pack', pairs)  20.2 us
    pallas_call x1, Pallas kernels, local(): pl.pallas_call(mix_kernel, out_shape=jax.ShapeDtypeStruct((ROWS, DM), jnp...  14.3 us
    pallas_call x3, Pallas kernels, attend(): pl.pallas_call(kernel, out_shape=shapes, in_specs=[SMEM] * 2 + [VMEM] * v...  11.1 us
    ppermute x4, starting transfers between devices, swapped(): return lax.ppermute(block, 'pack', [(i, i ^ 1) for i in range(32)])  8.11 us
    ppermute x4, waiting for transfers between devices, swapped(): return lax.ppermute(block, 'pack', [(i, i ^ 1) for i in range(32)])  7.43 us
    pallas_call x1, Pallas kernels, local(): pl.pallas_call(ssd_kernel, out_shape=(jax.ShapeDtypeStruct((ROWS, HP), jn...  6.23 us
  transfers between devices with their start and end apart: 15, of which 7 were waited for; matrix products, arithmetic and copies ran while one was open for 0% of the time, Pallas kernels for 27%

profile of v7, /device:TPU:1, one launch (start us, length us, event | category | flops | bytes accessed | tf_op | source)
XLA Modules:
  0.0 218.0 jit_solution(12561857755381041802)
XLA Ops:
  7.3 6.2 %ssd_local.1 = (f32[512,512]{1,0:T(8,128)}, bf16[272,256]{1,0:T(8,128)(2,1)}, bf16[272,256]{1,0:T(8,128)(2,1)}, f32[512,8]{1,0:T(8,128)}) custom-call(s32[4]{0:T(128)} %len_ref.9, f32[8]{0:T(128)} %dl_ref.1, f32[8]{0:T(128)} %skip_ref.1, s32[1]{0:T(128)} %bitcast.first_ref, bf16[512,512]{1,0:T(8,128)(2,1)} %x_ref.1, bf16[512,512]{1,0:T(8,128)(2,1)} %read_ref.1, ...), custom_call_target="tpu_custom_call" | custom-call | flops 1000000000 | bytes 4000000 | tf_op jit(solution)/shard_map/ssd_local/pallas_call | solution.py:512
  13.5 5.5 %collective-permute-start.2 = (bf16[512,256]{1,0:T(8,128)(2,1)}, bf16[512,256]{1,0:T(8,128)(2,1)S(1)}, u32[]{:S(2)}, u32[]{:S(2)}) collective-permute-start(bf16[512,256]{1,0:T(8,128)(2,1)} %bitcast.4), channel_id=1, source_target_pairs={{0,32},{8,136},{16,48},{24,152},{32,0},{40,168},{48,16},{56,184},{... | collective-permute-start | bytes 786440 | tf_op jit(solution)/shard_map/ppermute | solution.py:464
  19.0 1.3 collective-permute-start.1
  20.3 1.6 collective-permute-start
  22.0 4.1 %collective-permute-start.3 = (bf16[272,256]{1,0:T(8,128)(2,1)}, bf16[272,256]{1,0:T(8,128)(2,1)S(1)}, u32[]{:S(2)}, u32[]{:S(2)}) collective-permute-start(bf16[272,256]{1,0:T(8,128)(2,1)} %get-tuple-element.27), channel_id=1, source_target_pairs={{0,8},{8,0},{16,24},{24,16},{32,40},{40,32},{48,56},{56,48},{64,72... | collective-permute-start | bytes 417800 | tf_op jit(solution)/shard_map/ppermute | solution.py:480
  26.1 1.2 collective-permute-done.3.other_ref
  27.9 1.7 shard_map.109._.mine_ref
  31.2 32.9 %stack.1.line = bf16[2048,256]{1,0:T(8,128)(2,1)} custom-call(bf16[512,256]{1,0:T(8,128)(2,1)} %bitcast.7, bf16[512,256]{1,0:T(8,128)(2,1)} %copy-done.3, bf16[512,256]{1,0:T(8,128)(2,1)} %copy-done.2, bf16[512,256]{1,0:T(8,128)(2,1)} %copy-done.1, bf16[272,256]{1,0:T(8,128)(2,1)} %shard_map.109._.mine_ref), custom_call_target="tpu_custom_call" | custom-call | tf_op jit(solution)/shard_map/stack/pallas_call | solution.py:557
  64.1 3.8 %collective-permute-start.10 = (bf16[2048,256]{1,0:T(8,128)(2,1)}, bf16[2048,256]{1,0:T(8,128)(2,1)S(1)}, u32[]{:S(2)}, u32[]{:S(2)}) collective-permute-start(bf16[2048,256]{1,0:T(8,128)(2,1)} %stack.1.line), channel_id=1, source_target_pairs={{0,8},{8,0},{16,24},{24,16},{32,40},{40,32},{48,56},{56,48},{64,72... | collective-permute-start | bytes 3145736 | tf_op jit(solution)/shard_map/ppermute | solution.py:480
  68.1 1.7 collective-permute-start.5
  69.8 4.1 %own_line.1 = (f32[1024,256]{1,0:T(8,128)}, bf16[1024,256]{1,0:T(8,128)(2,1)}) custom-call(s32[4]{0:T(128)} %len_ref.9, s32[1]{0:T(128)} %bitcast.first_ref, bf16[512,256]{1,0:T(8,128)(2,1)} %q_ref.1, bf16[2048,256]{1,0:T(8,128)(2,1)} %stack.1.line), custom_call_target="tpu_custom_call" | custom-call | flops 3000000000 | bytes 5000000 | tf_op jit(solution)/shard_map/own_line/pallas_call | solution.py:545
  75.5 2.7 %collective-permute-done.4.below_ref = bf16[272,256]{1,0:T(8,128)(2,1)S(1)} collective-permute-done((bf16[272,256]{1,0:T(8,128)(2,1)}, bf16[272,256]{1,0:T(8,128)(2,1)S(1)}, u32[]{:S(2)}, u32[]{:S(2)}) %collective-permute-start.4) | collective-permute-done | bytes 139296 | tf_op jit(solution)/shard_map/ppermute | solution.py:464
  78.9 2.0 shard_map.110
  80.9 3.5 %collective-permute-start.9 = (bf16[272,256]{1,0:T(8,128)(2,1)}, bf16[272,256]{1,0:T(8,128)(2,1)S(1)}, u32[]{:S(2)}, u32[]{:S(2)}) collective-permute-start(bf16[272,256]{1,0:T(8,128)(2,1)} %get-tuple-element.34), channel_id=1, source_target_pairs={{0,64},{8,72},{16,80},{24,88},{32,96},{40,104},{48,112},{56,120},{... | collective-permute-start | bytes 417800 | tf_op jit(solution)/shard_map/ppermute | solution.py:464
  84.4 5.1 %collective-permute-start.8 = (bf16[272,256]{1,0:T(8,128)(2,1)}, bf16[272,256]{1,0:T(8,128)(2,1)S(1)}, u32[]{:S(2)}, u32[]{:S(2)}) collective-permute-start(bf16[272,256]{1,0:T(8,128)(2,1)} %get-tuple-element.34), channel_id=1, source_target_pairs={{0,128},{8,136},{16,144},{24,152},{32,160},{40,168},{48,176},{56,1... | collective-permute-start | bytes 417800 | tf_op jit(solution)/shard_map/ppermute | solution.py:464
  89.5 1.3 collective-permute-start.7
  91.8 4.3 %other_line.1.before_ref = f32[1024,256]{1,0:T(8,128)} custom-call(s32[4]{0:T(128)} %len_ref.9, s32[1]{0:T(128)} %bitcast.first_ref, bf16[1024,256]{1,0:T(8,128)(2,1)} %get-tuple-element.28.split_ref.split_hbm, f32[1024,256]{1,0:T(8,128)} %get-tuple-element.30.before_ref, bf16[2048,256]{1,0:T(8,128)(2,1)} %copy-done.11), custom_call_target="tpu_custom_call" | custom-call | flops 3000000000 | bytes 5000000 | tf_op jit(solution)/shard_map/other_line/pallas_call | solution.py:545
  97.5 2.1 shard_map.111
  99.5 1.6 collective-permute-done.11.got_ref
  101.7 3.5 %gate.1.act_hbm = bf16[512,512]{1,0:T(8,128)(2,1)} custom-call(s32[1]{0:T(128)} %bitcast.first_ref, f32[512,512]{1,0:T(8,128)} %get-tuple-element.29.y_ref, bf16[512,512]{1,0:T(8,128)(2,1)} %z_ref.1, bf16[512,512]{1,0:T(8,128)(2,1)} %read_ref.1, f32[512,8]{1,0:T(8,128)} %get-tuple-element.24.fac_ref, bf16[256,256]{1,0:T(8,128)(2,1)} %get-tuple-element.40.keep_ref, ...), custom_call_target="tpu_custom_call" | custom-call | flops 100000000 | bytes 3000000 | tf_op jit(solution)/shard_map/gate/pallas_call | solution.py:576
  105.4 2.7 %part.1.before_hbm = f32[1024,256]{1,0:T(8,128)} custom-call(s32[4]{0:T(128)} %len_ref.9, s32[1]{0:T(128)} %bitcast.first_ref, bf16[1024,256]{1,0:T(8,128)(2,1)} %get-tuple-element.28.split_ref.split_hbm, f32[1024,256]{1,0:T(8,128)} %other_line.1.before_ref, bf16[8192,256]{1,0:T(8,128)(2,1)} %bitcast.9), custom_call_target="tpu_custom_call" | custom-call | flops 3000000000 | bytes 5000000 | tf_op jit(solution)/shard_map/part/pallas_call | solution.py:545
  108.1 4.7 %collective-permute-done.12.other = bf16[8192,256]{1,0:T(8,128)(2,1)} collective-permute-done((bf16[8192,256]{1,0:T(8,128)(2,1)}, bf16[8192,256]{1,0:T(8,128)(2,1)}, u32[]{:S(2)}, u32[]{:S(2)}) %collective-permute-start.12) | collective-permute-done | bytes 4194336 | tf_op jit(solution)/shard_map/ppermute | solution.py:480
  112.8 14.3 %mix.1 = bf16[512,5120]{1,0:T(8,128)(2,1)} custom-call(s32[4]{0:T(128)} %len_ref.9, s32[1]{0:T(128)} %bitcast.first_ref, bf16[1024,256]{1,0:T(8,128)(2,1)} %get-tuple-element.28.split_ref.split_hbm, bf16[512,512]{1,0:T(8,128)(2,1)} %gate.1.act_hbm, f32[1024,256]{1,0:T(8,128)} %part.1.before_hbm, bf16[8192,256]{1,0:T(8,128)(2,1)} %bitcast.10, ...), custom_call_target="tpu_custom_call" | custom-call | flops 8999999488 | bytes 25000000 | tf_op jit(solution)/shard_map/mix/pallas_call | solution.py:599
  127.1 84.1 %reduce-scatter.2.cloned.1.call-done = bf16[64,5120]{1,0:T(8,128)(2,1)} async-done(((bf16[512,5120]{1,0:T(8,128)(2,1)}), bf16[64,5120]{1,0:T(8,128)(2,1)}) %reduce-scatter.2.cloned.1.call-update) | async-done | bytes 655376 | tf_op jit(solution)/shard_map/reduce_scatter | solution.py:620
  (42 shorter events, 8.5 us)
Async XLA Ops:
  6.5 98.7 %all-gather.3.cloned.1.call-start = ((), (), s32[]{:S(2)}) async-start(), calls=%async_computation.2 | async-start | bytes 4456448 | tf_op jit(solution)/shard_map/all_gather | solution.py:510
  7.3 203.9 %reduce-scatter.2.cloned.1.call-start = ((), (), s32[]{:S(2)}) async-start(), calls=%async_computation.1 | async-start | bytes 5898240 | tf_op jit(solution)/shard_map/reduce_scatter | solution.py:620
  13.5 16.1 %collective-permute-start.2 = (bf16[512,256]{1,0:T(8,128)(2,1)}, bf16[512,256]{1,0:T(8,128)(2,1)S(1)}, u32[]{:S(2)}, u32[]{:S(2)}) collective-permute-start(bf16[512,256]{1,0:T(8,128)(2,1)} %bitcast.4), channel_id=1, source_target_pairs={{0,32},{8,136},{16,48},{24,152},{32,0},{40,168},{48,16},{56,184},{... | collective-permute-start | bytes 786440 | tf_op jit(solution)/shard_map/ppermute | solution.py:464
  19.0 10.6 %collective-permute-start.1 = (bf16[512,256]{1,0:T(8,128)(2,1)}, bf16[512,256]{1,0:T(8,128)(2,1)S(1)}, u32[]{:S(2)}, u32[]{:S(2)}) collective-permute-start(bf16[512,256]{1,0:T(8,128)(2,1)} %bitcast.5), channel_id=1, source_target_pairs={{0,48},{8,200},{16,0},{24,216},{32,16},{40,232},{48,32},{56,248},{... | collective-permute-start | bytes 786440 | tf_op jit(solution)/shard_map/ppermute | solution.py:464
  20.3 9.3 %collective-permute-start = (bf16[512,256]{1,0:T(8,128)(2,1)}, bf16[512,256]{1,0:T(8,128)(2,1)S(1)}, u32[]{:S(2)}, u32[]{:S(2)}) collective-permute-start(bf16[512,256]{1,0:T(8,128)(2,1)} %bitcast.6), channel_id=1, source_target_pairs={{0,16},{8,72},{16,32},{24,88},{32,48},{40,104},{48,0},{56,120},{64... | collective-permute-start | bytes 786440 | tf_op jit(solution)/shard_map/ppermute | solution.py:464
  22.0 5.3 %collective-permute-start.3 = (bf16[272,256]{1,0:T(8,128)(2,1)}, bf16[272,256]{1,0:T(8,128)(2,1)S(1)}, u32[]{:S(2)}, u32[]{:S(2)}) collective-permute-start(bf16[272,256]{1,0:T(8,128)(2,1)} %get-tuple-element.27), channel_id=1, source_target_pairs={{0,8},{8,0},{16,24},{24,16},{32,40},{40,32},{48,56},{56,48},{64,72... | collective-permute-start | bytes 417800 | tf_op jit(solution)/shard_map/ppermute | solution.py:480
  27.3 0.7 copy-start
  29.7 0.7 copy-start.1
  29.7 0.8 copy-start.2
  30.5 0.7 copy-start.3
  64.1 26.8 %collective-permute-start.10 = (bf16[2048,256]{1,0:T(8,128)(2,1)}, bf16[2048,256]{1,0:T(8,128)(2,1)S(1)}, u32[]{:S(2)}, u32[]{:S(2)}) collective-permute-start(bf16[2048,256]{1,0:T(8,128)(2,1)} %stack.1.line), channel_id=1, source_target_pairs={{0,8},{8,0},{16,24},{24,16},{32,40},{40,32},{48,56},{56,48},{64,72... | collective-permute-start | bytes 3145736 | tf_op jit(solution)/shard_map/ppermute | solution.py:480
  67.9 6.9 %collective-permute-start.6 = (bf16[272,256]{1,0:T(8,128)(2,1)}, bf16[272,256]{1,0:T(8,128)(2,1)S(1)}, u32[]{:S(2)}, u32[]{:S(2)}) collective-permute-start(bf16[272,256]{1,0:T(8,128)(2,1)} %shard_map.109._.mine_ref), channel_id=1, source_target_pairs={{0,32},{8,40},{16,48},{24,56},{32,0},{40,8},{48,16},{56,24},{64,96... | collective-permute-start | bytes 417800 | tf_op jit(solution)/shard_map/ppermute | solution.py:464
  68.1 7.4 %collective-permute-start.5 = (bf16[272,256]{1,0:T(8,128)(2,1)}, bf16[272,256]{1,0:T(8,128)(2,1)S(1)}, u32[]{:S(2)}, u32[]{:S(2)}) collective-permute-start(bf16[272,256]{1,0:T(8,128)(2,1)} %shard_map.109._.mine_ref), channel_id=1, source_target_pairs={{0,48},{8,56},{16,0},{24,8},{32,16},{40,24},{48,32},{56,40},{64,11... | collective-permute-start | bytes 417800 | tf_op jit(solution)/shard_map/ppermute | solution.py:464
  69.8 8.4 %collective-permute-start.4 = (bf16[272,256]{1,0:T(8,128)(2,1)}, bf16[272,256]{1,0:T(8,128)(2,1)S(1)}, u32[]{:S(2)}, u32[]{:S(2)}) collective-permute-start(bf16[272,256]{1,0:T(8,128)(2,1)} %shard_map.109._.mine_ref), channel_id=1, source_target_pairs={{0,16},{8,24},{16,32},{24,40},{32,48},{40,56},{48,0},{56,8},{64,80... | collective-permute-start | bytes 417800 | tf_op jit(solution)/shard_map/ppermute | solution.py:464
  74.9 3.4 %copy-start.7 = (bf16[272,256]{1,0:T(8,128)(2,1)}, bf16[272,256]{1,0:T(8,128)(2,1)S(1)}, u32[]{:S(2)}) copy-start(bf16[272,256]{1,0:T(8,128)(2,1)S(1)} %collective-permute-done.6.across_ref) | copy-start | bytes 417796
  75.5 2.7 %copy-start.8 = (bf16[272,256]{1,0:T(8,128)(2,1)}, bf16[272,256]{1,0:T(8,128)(2,1)S(1)}, u32[]{:S(2)}) copy-start(bf16[272,256]{1,0:T(8,128)(2,1)S(1)} %collective-permute-done.5.above_ref) | copy-start | bytes 417796
  78.2 0.7 copy-start.9
  80.9 15.2 %collective-permute-start.9 = (bf16[272,256]{1,0:T(8,128)(2,1)}, bf16[272,256]{1,0:T(8,128)(2,1)S(1)}, u32[]{:S(2)}, u32[]{:S(2)}) collective-permute-start(bf16[272,256]{1,0:T(8,128)(2,1)} %get-tuple-element.34), channel_id=1, source_target_pairs={{0,64},{8,72},{16,80},{24,88},{32,96},{40,104},{48,112},{56,120},{... | collective-permute-start | bytes 417800 | tf_op jit(solution)/shard_map/ppermute | solution.py:464
  84.4 11.7 %collective-permute-start.8 = (bf16[272,256]{1,0:T(8,128)(2,1)}, bf16[272,256]{1,0:T(8,128)(2,1)S(1)}, u32[]{:S(2)}, u32[]{:S(2)}) collective-permute-start(bf16[272,256]{1,0:T(8,128)(2,1)} %get-tuple-element.34), channel_id=1, source_target_pairs={{0,128},{8,136},{16,144},{24,152},{32,160},{40,168},{48,176},{56,1... | collective-permute-start | bytes 417800 | tf_op jit(solution)/shard_map/ppermute | solution.py:464
  89.5 6.6 %collective-permute-start.7 = (bf16[272,256]{1,0:T(8,128)(2,1)}, bf16[272,256]{1,0:T(8,128)(2,1)S(1)}, u32[]{:S(2)}, u32[]{:S(2)}) collective-permute-start(bf16[272,256]{1,0:T(8,128)(2,1)} %get-tuple-element.34), channel_id=1, source_target_pairs={{0,192},{8,200},{16,208},{24,216},{32,224},{40,232},{48,240},{56,2... | collective-permute-start | bytes 417800 | tf_op jit(solution)/shard_map/ppermute | solution.py:464
  90.8 1.0 copy-start.11
  96.1 0.7 copy-start.5
  99.5 1.6 collective-permute-start.11
  105.3 7.5 %collective-permute-start.12 = (bf16[8192,256]{1,0:T(8,128)(2,1)}, bf16[8192,256]{1,0:T(8,128)(2,1)}, u32[]{:S(2)}, u32[]{:S(2)}) collective-permute-start(bf16[8192,256]{1,0:T(8,128)(2,1)} %bitcast.8), channel_id=1, source_target_pairs={{0,8},{8,0},{16,24},{24,16},{32,40},{40,32},{48,56},{56,48},{64,72... | collective-permute-start | bytes 12582920 | tf_op jit(solution)/shard_map/ppermute | solution.py:480
  (3 other events, 1.9 us)
Sparse Core Ops, SparseCore 0:
  9.8 61.0 all-gather.2
  127.2 83.9 reduce-scatter.1

commit v8 on v6

--- a/solution.py
+++ b/solution.py
@@ -19,7 +19,7 @@
 LOW = -1e30
 LOG2E = 1.4426950408889634
 HIGH = lax.Precision.HIGHEST
-LIMIT = 62 * 2**20
+LIMIT = 64 * 2**20 - 2**16
 HALF = HP // 2
 STATE_ROWS = SN + 16
 VMEM = pl.BlockSpec(memory_space=pltpu.VMEM)
@@ -190,7 +190,7 @@
 
 
 class Attention:
-    def __init__(self, len_ref, first_ref, fetched, other, q_scr, kv_scr, ids, kv_sem, near_only=False):
+    def __init__(self, len_ref, first_ref, fetched, other, q_scr, kv_scr, ids, kinds, kv_sem, near_only=False):
         self.first = first_ref[0]
         self.ends = ends_of(len_ref)
         self.mine = self.first // CHUNK
@@ -198,7 +198,7 @@
         self.last_start = start_of(self.first + ROWS - 1, self.ends)
         self.arrays = (fetched, other)
         self.near_only = near_only
-        self.q_scr, self.kv_scr, self.ids, self.kv_sem = q_scr, kv_scr, ids, kv_sem
+        self.q_scr, self.kv_scr, self.ids, self.kinds, self.kv_sem = q_scr, kv_scr, ids, kinds, kv_sem
 
     def count(self, far):
         return 4 if self.near_only else (self.mine - far - self.low) // 2 + 1
@@ -245,6 +245,8 @@
             @pl.when(wanted)
             def _():
                 self.ids[slot] = block
+                inside = start_of(block * CHUNK + (CHUNK - 1), self.ends) > block * CHUNK
+                self.kinds[slot] = jnp.where((block == self.mine) | inside, 1, 0)
                 self.copy(far, self.place(block), slot).start()
 
             new = wanted.astype(jnp.int32)
@@ -280,20 +282,26 @@
         v = self.kv_scr[self.keys(slot, chunks), HD:]
         return jnp.concatenate([v, jnp.ones((chunks * CHUNK, HD), jnp.bfloat16)], axis=1)
 
-    def step(self, acc, slot, chunks, masked):
+    def step(self, acc, slot, chunks, masked, by_row=False):
         v = self.values(slot, chunks)
         tiles = 2 * ROWS // TILE
         s = self.scores(slot, chunks, 0, masked)
         for r in range(tiles):
             following = self.scores(slot, chunks, r + 1, masked) if r + 1 < tiles else None
             p = jnp.exp2(s).astype(jnp.bfloat16)
-            acc[r * TILE : (r + 1) * TILE, :] += jnp.dot(p, v, preferred_element_type=jnp.float32)
+            out = jnp.dot(p, v, preferred_element_type=jnp.float32)
+            if by_row:
+                pos = self.first + (r * TILE) % ROWS + iota((TILE, 1), 0)
+                out = jnp.where(start_of(pos, self.ends) <= self.ids[slot] * CHUNK, out, 0.0)
+            acc[r * TILE : (r + 1) * TILE, :] += out
             s = following
 
     def add(self, acc):
         def one_masked(j, _):
-            self.wait(SLOTS - 1 - j)
-            self.step(acc, SLOTS - 1 - j, 1, True)
+            slot = SLOTS - 1 - j
+            self.wait(slot)
+            pl.when(self.kinds[slot] == 0)(lambda: self.step(acc, slot, 1, False, by_row=True))
+            pl.when(self.kinds[slot] == 1)(lambda: self.step(acc, slot, 1, True))
             return 0
 
         def two_plain(j, _):
@@ -330,8 +338,8 @@
         lax.fori_loop(0, self.plain + self.masked, one_chunk, 0)
 
 
-def own_line_kernel(len_ref, first_ref, q_ref, line, acc_ref, split_ref, kv_scr, ids, kv_sem):
-    attention = Attention(len_ref, first_ref, line, None, split_ref, kv_scr, ids, kv_sem, near_only=True)
+def own_line_kernel(len_ref, first_ref, q_ref, line, acc_ref, split_ref, kv_scr, ids, kinds, kv_sem):
+    attention = Attention(len_ref, first_ref, line, None, split_ref, kv_scr, ids, kinds, kv_sem, near_only=True)
     attention.fetch((0,))
     for g in range(2):
         rows = slice(g * ROWS, (g + 1) * ROWS)
@@ -343,15 +351,15 @@
     attention.add(acc_ref)
 
 
-def other_line_kernel(len_ref, first_ref, split_ref, before_ref, line_got, acc_ref, kv_scr, ids, kv_sem):
-    attention = Attention(len_ref, first_ref, line_got, line_got, split_ref, kv_scr, ids, kv_sem, near_only=True)
+def other_line_kernel(len_ref, first_ref, split_ref, before_ref, line_got, acc_ref, kv_scr, ids, kinds, kv_sem):
+    attention = Attention(len_ref, first_ref, line_got, line_got, split_ref, kv_scr, ids, kinds, kv_sem, near_only=True)
     attention.fetch((1,))
     acc_ref[...] = before_ref[...]
     attention.add(acc_ref)
 
 
-def part_kernel(len_ref, first_ref, split_ref, before_ref, fetched, acc_ref, kv_scr, ids, kv_sem):
-    attention = Attention(len_ref, first_ref, fetched, None, split_ref, kv_scr, ids, kv_sem)
+def part_kernel(len_ref, first_ref, split_ref, before_ref, fetched, acc_ref, kv_scr, ids, kinds, kv_sem):
+    attention = Attention(len_ref, first_ref, fetched, None, split_ref, kv_scr, ids, kinds, kv_sem)
     attention.fetch((0,))
     acc_ref[...] = before_ref[...]
     attention.add(acc_ref)
@@ -370,6 +378,7 @@
     o_hbm,
     kv_scr,
     ids,
+    kinds,
     kv_sem,
     q_scr,
     acc_scr,
@@ -381,7 +390,7 @@
     w_sem,
     o_sem,
 ):
-    attention = Attention(len_ref, first_ref, fetched, other, q_scr, kv_scr, ids, kv_sem)
+    attention = Attention(len_ref, first_ref, fetched, other, q_scr, kv_scr, ids, kinds, kv_sem)
     inputs = [
         pltpu.make_async_copy(split_hbm, q_scr, in_sem.at[0]),
         pltpu.make_async_copy(before_hbm, acc_scr, in_sem.at[1]),
@@ -526,6 +535,7 @@
     chunks_scratch = [
         pltpu.VMEM((SLOTS * CHUNK, 2 * HD), jnp.bfloat16),
         pltpu.SMEM((SLOTS,), jnp.int32),
+        pltpu.SMEM((SLOTS,), jnp.int32),
         pltpu.SemaphoreType.DMA((SLOTS,)),
     ]
     sums = jax.ShapeDtypeStruct((2 * ROWS, 2 * HD), jnp.float32)

time: 184 us -> 185 us (level); the launches traced: 183 us -> 187 us
  waiting for transfers between devices: 97.7 us -> 103 us
  local copies, waits for them, and re-layouts: 3.62 us -> 0.01 us
    reduce_scatter x1, waiting for transfers between devices: 85.9 us -> 90.5 us  [local(): return lax.psum_scatter(terms, 'tp', scatter_dimension=0, tiled=True)]
    unnamed x22 -> x2, local copies, waits for them, and re-layouts: 3.62 us -> 0.01 us
    ppermute x9, starting transfers between devices: 20 us -> 23.2 us  [moved(): return lax.ppermute(block, 'pack', pairs)]
  transfers between devices with their start and end apart: 15 -> 15, of which waited for: 7 -> 7; matrix products, arithmetic and copies ran while one was open for 0% -> 0% of each run, Pallas kernels for 15% -> 14%
where the time goes in v8:
time: 185 us; the launch traced here: 187 us
  waiting for transfers between devices  103 us (56%)
  Pallas kernels  41.1 us (22%)
  starting transfers between devices  27.7 us (15%)
  between operations  13.5 us (7%)
  other arithmetic  2.28 us (1%)
    reduce_scatter x1, waiting for transfers between devices, local(): return lax.psum_scatter(terms, 'tp', scatter_dimension=0, tiled=True)  90.5 us
    ppermute x9, starting transfers between devices, moved(): return lax.ppermute(block, 'pack', pairs)  23.2 us
    pallas_call x1, Pallas kernels, local(): pl.pallas_call(mix_kernel, out_shape=jax.ShapeDtypeStruct((ROWS, DM), jnp...  14.4 us
    pallas_call x3, Pallas kernels, attend(): pl.pallas_call(kernel, out_shape=shapes, in_specs=[SMEM] * 2 + [VMEM] * v...  11.2 us
    ppermute x4, waiting for transfers between devices, swapped(): return lax.ppermute(block, 'pack', [(i, i ^ 1) for i in range(32)])  8.12 us
    pallas_call x1, Pallas kernels, local(): pl.pallas_call(ssd_kernel, out_shape=(jax.ShapeDtypeStruct((ROWS, HP), jn...  6.22 us
    pallas_call x3, Pallas kernels, call(): pl.pallas_call(kernel, out_shape=tuple((jax.ShapeDtypeStruct(shape, jnp.b...  5.84 us
    ppermute x4, starting transfers between devices, swapped(): return lax.ppermute(block, 'pack', [(i, i ^ 1) for i in range(32)])  4.41 us
  transfers between devices with their start and end apart: 15, of which 7 were waited for; matrix products, arithmetic and copies ran while one was open for 0% of the time, Pallas kernels for 14%

profile of v8, /device:TPU:1, one launch (start us, length us, event | category | flops | bytes accessed | tf_op | source)
XLA Modules:
  0.0 187.2 jit_solution(11556583848065870455)
XLA Ops:
  6.5 6.2 %collective-permute-start.2 = (bf16[512,256]{1,0:T(8,128)(2,1)}, bf16[512,256]{1,0:T(8,128)(2,1)}, u32[]{:S(2)}, u32[]{:S(2)}) collective-permute-start(bf16[512,256]{1,0:T(8,128)(2,1)} %bitcast.3), channel_id=1, source_target_pairs={{0,32},{8,136},{16,48},{24,152},{32,0},{40,168},{48,16},{56,184},{... | collective-permute-start | bytes 786440 | tf_op jit(solution)/shard_map/ppermute | solution.py:460
  12.7 2.0 %collective-permute-start.1 = (bf16[512,256]{1,0:T(8,128)(2,1)}, bf16[512,256]{1,0:T(8,128)(2,1)}, u32[]{:S(2)}, u32[]{:S(2)}) collective-permute-start(bf16[512,256]{1,0:T(8,128)(2,1)} %bitcast.4), channel_id=1, source_target_pairs={{0,48},{8,200},{16,0},{24,216},{32,16},{40,232},{48,32},{56,248},{... | collective-permute-start | bytes 786440 | tf_op jit(solution)/shard_map/ppermute | solution.py:460
  14.7 2.3 %collective-permute-start = (bf16[512,256]{1,0:T(8,128)(2,1)}, bf16[512,256]{1,0:T(8,128)(2,1)}, u32[]{:S(2)}, u32[]{:S(2)}) collective-permute-start(bf16[512,256]{1,0:T(8,128)(2,1)} %bitcast.5), channel_id=1, source_target_pairs={{0,16},{8,72},{16,32},{24,88},{32,48},{40,104},{48,0},{56,120},{64... | collective-permute-start | bytes 786440 | tf_op jit(solution)/shard_map/ppermute | solution.py:460
  17.0 6.2 %ssd_local.1 = (f32[512,512]{1,0:T(8,128)}, bf16[272,256]{1,0:T(8,128)(2,1)}, bf16[272,256]{1,0:T(8,128)(2,1)}, f32[512,8]{1,0:T(8,128)}) custom-call(s32[4]{0:T(128)} %len_ref.9, f32[8]{0:T(128)} %dl_ref.1, f32[8]{0:T(128)} %skip_ref.1, s32[1]{0:T(128)} %bitcast.first_ref, bf16[512,512]{1,0:T(8,128)(2,1)} %x_ref.1, bf16[512,512]{1,0:T(8,128)(2,1)} %read_ref.1, ...), custom_call_target="tpu_custom_call" | custom-call | flops 1000000000 | bytes 4000000 | tf_op jit(solution)/shard_map/ssd_local/pallas_call | solution.py:511
  23.3 2.3 %pad_maximum_fusion.line = bf16[2048,256]{1,0:T(8,128)(2,1)} fusion(bf16[512,256]{1,0:T(8,128)(2,1)} %collective-permute-done.2, bf16[512,256]{1,0:T(8,128)(2,1)} %collective-permute-done.1, bf16[512,256]{1,0:T(8,128)(2,1)} %collective-permute-done, bf16[512,256]{1,0:T(8,128)(2,1)} %bitcast.6), kind=kLoop, calls=%fused_computation | loop fusion | flops 4194304 | bytes 2097152 | tf_op jit(solution)/shard_map/concatenate | solution.py:527
  25.6 2.7 %collective-permute-start.10 = (bf16[2048,256]{1,0:T(8,128)(2,1)}, bf16[2048,256]{1,0:T(8,128)(2,1)}, u32[]{:S(2)}, u32[]{:S(2)}) collective-permute-start(bf16[2048,256]{1,0:T(8,128)(2,1)} %pad_maximum_fusion.line), channel_id=1, source_target_pairs={{0,8},{8,0},{16,24},{24,16},{32,40},{40,32},{48,56},{56,48},{64,72... | collective-permute-start | bytes 3145736 | tf_op jit(solution)/shard_map/ppermute | solution.py:478
  28.4 2.4 %collective-permute-done.3.other_ref = bf16[272,256]{1,0:T(8,128)(2,1)} collective-permute-done((bf16[272,256]{1,0:T(8,128)(2,1)S(1)}, bf16[272,256]{1,0:T(8,128)(2,1)}, u32[]{:S(2)}, u32[]{:S(2)}) %collective-permute-start.3) | collective-permute-done | bytes 139296 | tf_op jit(solution)/shard_map/ppermute | solution.py:478
  30.8 1.7 shard_map.109.mine_ref
  35.2 4.1 %own_line.1 = (f32[1024,256]{1,0:T(8,128)}, bf16[1024,256]{1,0:T(8,128)(2,1)}) custom-call(s32[4]{0:T(128)} %len_ref.9, s32[1]{0:T(128)} %bitcast.first_ref, bf16[512,256]{1,0:T(8,128)(2,1)} %q_ref.1, bf16[2048,256]{1,0:T(8,128)(2,1)} %pad_maximum_fusion.line), custom_call_target="tpu_custom_call" | custom-call | flops 3000000000 | bytes 5000000 | tf_op jit(solution)/shard_map/own_line/pallas_call | solution.py:545
  39.3 2.0 %collective-permute-done.5.above_ref = bf16[272,256]{1,0:T(8,128)(2,1)} collective-permute-done((bf16[272,256]{1,0:T(8,128)(2,1)}, bf16[272,256]{1,0:T(8,128)(2,1)}, u32[]{:S(2)}, u32[]{:S(2)}) %collective-permute-start.5) | collective-permute-done | bytes 139296 | tf_op jit(solution)/shard_map/ppermute | solution.py:460
  41.3 1.2 collective-permute-done.4.below_ref
  42.5 2.1 %shard_map.110 = (bf16[272,256]{1,0:T(8,128)(2,1)}, bf16[272,256]{1,0:T(8,128)(2,1)}) custom-call(s32[1]{0:T(128)} %bitcast.first_ref, bf16[272,256]{1,0:T(8,128)(2,1)} %shard_map.109.mine_ref, bf16[272,256]{1,0:T(8,128)(2,1)} %collective-permute-done.4.below_ref, bf16[272,256]{1,0:T(8,128)(2,1)} %collective-permute-done.5.above_ref, ...), custom_call_target="tpu_custom_call" | custom-call | flops 1000000 | bytes 1000000 | tf_op jit(solution)/shard_map/pallas_call | solution.py:482
  44.5 3.8 %collective-permute-start.9 = (bf16[272,256]{1,0:T(8,128)(2,1)}, bf16[272,256]{1,0:T(8,128)(2,1)}, u32[]{:S(2)}, u32[]{:S(2)}) collective-permute-start(bf16[272,256]{1,0:T(8,128)(2,1)} %get-tuple-element.40), channel_id=1, source_target_pairs={{0,64},{8,72},{16,80},{24,88},{32,96},{40,104},{48,112},{56,120},{... | collective-permute-start | bytes 417800 | tf_op jit(solution)/shard_map/ppermute | solution.py:460
  48.3 4.4 %collective-permute-start.8 = (bf16[272,256]{1,0:T(8,128)(2,1)}, bf16[272,256]{1,0:T(8,128)(2,1)}, u32[]{:S(2)}, u32[]{:S(2)}) collective-permute-start(bf16[272,256]{1,0:T(8,128)(2,1)} %get-tuple-element.40), channel_id=1, source_target_pairs={{0,128},{8,136},{16,144},{24,152},{32,160},{40,168},{48,176},{56,1... | collective-permute-start | bytes 417800 | tf_op jit(solution)/shard_map/ppermute | solution.py:460
  52.7 2.0 %collective-permute-start.7 = (bf16[272,256]{1,0:T(8,128)(2,1)}, bf16[272,256]{1,0:T(8,128)(2,1)}, u32[]{:S(2)}, u32[]{:S(2)}) collective-permute-start(bf16[272,256]{1,0:T(8,128)(2,1)} %get-tuple-element.40), channel_id=1, source_target_pairs={{0,192},{8,200},{16,208},{24,216},{32,224},{40,232},{48,240},{56,2... | collective-permute-start | bytes 417800 | tf_op jit(solution)/shard_map/ppermute | solution.py:460
  54.7 4.3 %other_line.1.before_ref = f32[1024,256]{1,0:T(8,128)} custom-call(s32[4]{0:T(128)} %len_ref.9, s32[1]{0:T(128)} %bitcast.first_ref, bf16[1024,256]{1,0:T(8,128)(2,1)} %get-tuple-element.34.split_ref.split_hbm, f32[1024,256]{1,0:T(8,128)} %get-tuple-element.36.before_ref, bf16[2048,256]{1,0:T(8,128)(2,1)} %collective-permute-done.10.line_got), custom_call_target="tpu_custom_call" | custom-call | flops 3000000000 | bytes 5000000 | tf_op jit(solution)/shard_map/other_line/pallas_call | solution.py:545
  59.8 2.1 %shard_map.111 = (bf16[256,256]{1,0:T(8,128)(2,1)}, bf16[256,256]{1,0:T(8,128)(2,1)}) custom-call(s32[1]{0:T(128)} %bitcast.first_ref, bf16[272,256]{1,0:T(8,128)(2,1)} %collective-permute-done.7.row3_ref, bf16[272,256]{1,0:T(8,128)(2,1)} %collective-permute-done.8.row2_ref, bf16[272,256]{1,0:T(8,128)(2,1)} %collective-permute-done.9.row1_ref, ...), custom_call_target="tpu_custom_call" | custom-call | flops 1000000 | bytes 1000000 | tf_op jit(solution)/shard_map/pallas_call | solution.py:482
  61.8 1.2 collective-permute-start.11
  63.1 1.3 collective-permute-done.11.got_ref
  64.4 3.5 %gate.1.act_hbm = bf16[512,512]{1,0:T(8,128)(2,1)} custom-call(s32[1]{0:T(128)} %bitcast.first_ref, f32[512,512]{1,0:T(8,128)} %get-tuple-element.35.y_ref, bf16[512,512]{1,0:T(8,128)(2,1)} %z_ref.1, bf16[512,512]{1,0:T(8,128)(2,1)} %read_ref.1, f32[512,8]{1,0:T(8,128)} %get-tuple-element.27.fac_ref, bf16[256,256]{1,0:T(8,128)(2,1)} %get-tuple-element.46.keep_ref, ...), custom_call_target="tpu_custom_call" | custom-call | flops 100000000 | bytes 3000000 | tf_op jit(solution)/shard_map/gate/pallas_call | solution.py:567
  68.3 2.7 %part.1.before_hbm = f32[1024,256]{1,0:T(8,128)} custom-call(s32[4]{0:T(128)} %len_ref.9, s32[1]{0:T(128)} %bitcast.first_ref, bf16[1024,256]{1,0:T(8,128)(2,1)} %get-tuple-element.34.split_ref.split_hbm, f32[1024,256]{1,0:T(8,128)} %other_line.1.before_ref, bf16[8192,256]{1,0:T(8,128)(2,1)} %all-gather.2.cloned.1.call-done.fetched), custom_call_target="tpu_custom_call" | custom-call | flops 3000000000 | bytes 5000000 | tf_op jit(solution)/shard_map/part/pallas_call | solution.py:545
  71.0 4.4 %collective-permute-done.12.other = bf16[8192,256]{1,0:T(8,128)(2,1)} collective-permute-done((bf16[8192,256]{1,0:T(8,128)(2,1)}, bf16[8192,256]{1,0:T(8,128)(2,1)}, u32[]{:S(2)}, u32[]{:S(2)}) %collective-permute-start.12) | collective-permute-done | bytes 4194336 | tf_op jit(solution)/shard_map/ppermute | solution.py:478
  75.4 14.4 %mix.1 = bf16[512,5120]{1,0:T(8,128)(2,1)} custom-call(s32[4]{0:T(128)} %len_ref.9, s32[1]{0:T(128)} %bitcast.first_ref, bf16[1024,256]{1,0:T(8,128)(2,1)} %get-tuple-element.34.split_ref.split_hbm, bf16[512,512]{1,0:T(8,128)(2,1)} %gate.1.act_hbm, f32[1024,256]{1,0:T(8,128)} %part.1.before_hbm, bf16[8192,256]{1,0:T(8,128)(2,1)} %all-gather.2.cloned.1.call-done.fetched, ...), custom_call_target="tpu_custom_call" | custom-call | flops 8999999488 | bytes 25000000 | tf_op jit(solution)/shard_map/mix/pallas_call | solution.py:590
  89.8 90.5 %reduce-scatter.2.cloned.1.call-done = bf16[64,5120]{1,0:T(8,128)(2,1)} async-done(((bf16[512,5120]{1,0:T(8,128)(2,1)}), bf16[64,5120]{1,0:T(8,128)(2,1)}) %reduce-scatter.2.cloned.1.call-update) | async-done | bytes 655376 | tf_op jit(solution)/shard_map/reduce_scatter | solution.py:611
  (20 shorter events, 4.0 us)
Async XLA Ops:
  6.5 61.4 %all-gather.2.cloned.1.call-start = ((), (), s32[]{:S(2)}) async-start(), calls=%async_computation.1 | async-start | bytes 5242880 | tf_op jit(solution)/shard_map/all_gather | solution.py:528
  6.5 16.7 %collective-permute-start.2 = (bf16[512,256]{1,0:T(8,128)(2,1)}, bf16[512,256]{1,0:T(8,128)(2,1)}, u32[]{:S(2)}, u32[]{:S(2)}) collective-permute-start(bf16[512,256]{1,0:T(8,128)(2,1)} %bitcast.3), channel_id=1, source_target_pairs={{0,32},{8,136},{16,48},{24,152},{32,0},{40,168},{48,16},{56,184},{... | collective-permute-start | bytes 786440 | tf_op jit(solution)/shard_map/ppermute | solution.py:460
  12.7 10.5 %collective-permute-start.1 = (bf16[512,256]{1,0:T(8,128)(2,1)}, bf16[512,256]{1,0:T(8,128)(2,1)}, u32[]{:S(2)}, u32[]{:S(2)}) collective-permute-start(bf16[512,256]{1,0:T(8,128)(2,1)} %bitcast.4), channel_id=1, source_target_pairs={{0,48},{8,200},{16,0},{24,216},{32,16},{40,232},{48,32},{56,248},{... | collective-permute-start | bytes 786440 | tf_op jit(solution)/shard_map/ppermute | solution.py:460
  14.7 8.5 %collective-permute-start = (bf16[512,256]{1,0:T(8,128)(2,1)}, bf16[512,256]{1,0:T(8,128)(2,1)}, u32[]{:S(2)}, u32[]{:S(2)}) collective-permute-start(bf16[512,256]{1,0:T(8,128)(2,1)} %bitcast.5), channel_id=1, source_target_pairs={{0,16},{8,72},{16,32},{24,88},{32,48},{40,104},{48,0},{56,120},{64... | collective-permute-start | bytes 786440 | tf_op jit(solution)/shard_map/ppermute | solution.py:460
  23.2 5.1 %copy-start = (bf16[272,256]{1,0:T(8,128)(2,1)S(1)}, bf16[272,256]{1,0:T(8,128)(2,1)}, u32[]{:S(2)}) copy-start(bf16[272,256]{1,0:T(8,128)(2,1)} %get-tuple-element.32) | copy-start | bytes 417796
  25.6 154.8 %reduce-scatter.2.cloned.1.call-start = ((), (), s32[]{:S(2)}) async-start(), calls=%async_computation.2 | async-start | bytes 5898240 | tf_op jit(solution)/shard_map/reduce_scatter | solution.py:611
  25.6 29.1 %collective-permute-start.10 = (bf16[2048,256]{1,0:T(8,128)(2,1)}, bf16[2048,256]{1,0:T(8,128)(2,1)}, u32[]{:S(2)}, u32[]{:S(2)}) collective-permute-start(bf16[2048,256]{1,0:T(8,128)(2,1)} %pad_maximum_fusion.line), channel_id=1, source_target_pairs={{0,8},{8,0},{16,24},{24,16},{32,40},{40,32},{48,56},{56,48},{64,72... | collective-permute-start | bytes 3145736 | tf_op jit(solution)/shard_map/ppermute | solution.py:478
  28.3 2.5 %collective-permute-start.3 = (bf16[272,256]{1,0:T(8,128)(2,1)S(1)}, bf16[272,256]{1,0:T(8,128)(2,1)}, u32[]{:S(2)}, u32[]{:S(2)}) collective-permute-start(bf16[272,256]{1,0:T(8,128)(2,1)S(1)} %copy-done), channel_id=1, source_target_pairs={{0,8},{8,0},{16,24},{24,16},{32,40},{40,32},{48,56},{56,48},{64,72... | collective-permute-start | bytes 417800 | tf_op jit(solution)/shard_map/ppermute | solution.py:478
  32.5 6.8 %collective-permute-start.6 = (bf16[272,256]{1,0:T(8,128)(2,1)}, bf16[272,256]{1,0:T(8,128)(2,1)}, u32[]{:S(2)}, u32[]{:S(2)}) collective-permute-start(bf16[272,256]{1,0:T(8,128)(2,1)} %shard_map.109.mine_ref), channel_id=1, source_target_pairs={{0,32},{8,40},{16,48},{24,56},{32,0},{40,8},{48,16},{56,24},{64,96... | collective-permute-start | bytes 417800 | tf_op jit(solution)/shard_map/ppermute | solution.py:460
  33.7 7.6 %collective-permute-start.5 = (bf16[272,256]{1,0:T(8,128)(2,1)}, bf16[272,256]{1,0:T(8,128)(2,1)}, u32[]{:S(2)}, u32[]{:S(2)}) collective-permute-start(bf16[272,256]{1,0:T(8,128)(2,1)} %shard_map.109.mine_ref), channel_id=1, source_target_pairs={{0,48},{8,56},{16,0},{24,8},{32,16},{40,24},{48,32},{56,40},{64,11... | collective-permute-start | bytes 417800 | tf_op jit(solution)/shard_map/ppermute | solution.py:460
  34.7 7.8 %collective-permute-start.4 = (bf16[272,256]{1,0:T(8,128)(2,1)}, bf16[272,256]{1,0:T(8,128)(2,1)}, u32[]{:S(2)}, u32[]{:S(2)}) collective-permute-start(bf16[272,256]{1,0:T(8,128)(2,1)} %shard_map.109.mine_ref), channel_id=1, source_target_pairs={{0,16},{8,24},{16,32},{24,40},{32,48},{40,56},{48,0},{56,8},{64,80... | collective-permute-start | bytes 417800 | tf_op jit(solution)/shard_map/ppermute | solution.py:460
  44.5 14.5 %collective-permute-start.9 = (bf16[272,256]{1,0:T(8,128)(2,1)}, bf16[272,256]{1,0:T(8,128)(2,1)}, u32[]{:S(2)}, u32[]{:S(2)}) collective-permute-start(bf16[272,256]{1,0:T(8,128)(2,1)} %get-tuple-element.40), channel_id=1, source_target_pairs={{0,64},{8,72},{16,80},{24,88},{32,96},{40,104},{48,112},{56,120},{... | collective-permute-start | bytes 417800 | tf_op jit(solution)/shard_map/ppermute | solution.py:460
  48.3 10.7 %collective-permute-start.8 = (bf16[272,256]{1,0:T(8,128)(2,1)}, bf16[272,256]{1,0:T(8,128)(2,1)}, u32[]{:S(2)}, u32[]{:S(2)}) collective-permute-start(bf16[272,256]{1,0:T(8,128)(2,1)} %get-tuple-element.40), channel_id=1, source_target_pairs={{0,128},{8,136},{16,144},{24,152},{32,160},{40,168},{48,176},{56,1... | collective-permute-start | bytes 417800 | tf_op jit(solution)/shard_map/ppermute | solution.py:460
  52.7 7.1 %collective-permute-start.7 = (bf16[272,256]{1,0:T(8,128)(2,1)}, bf16[272,256]{1,0:T(8,128)(2,1)}, u32[]{:S(2)}, u32[]{:S(2)}) collective-permute-start(bf16[272,256]{1,0:T(8,128)(2,1)} %get-tuple-element.40), channel_id=1, source_target_pairs={{0,192},{8,200},{16,208},{24,216},{32,224},{40,232},{48,240},{56,2... | collective-permute-start | bytes 417800 | tf_op jit(solution)/shard_map/ppermute | solution.py:460
  61.8 2.5 %collective-permute-start.11 = (bf16[256,256]{1,0:T(8,128)(2,1)}, bf16[256,256]{1,0:T(8,128)(2,1)}, u32[]{:S(2)}, u32[]{:S(2)}) collective-permute-start(bf16[256,256]{1,0:T(8,128)(2,1)} %get-tuple-element.47), channel_id=1, source_target_pairs={{0,8},{8,0},{16,24},{24,16},{32,40},{40,32},{48,56},{56,48},{64,72... | collective-permute-start | bytes 393224 | tf_op jit(solution)/shard_map/ppermute | solution.py:478
  67.9 7.5 %collective-permute-start.12 = (bf16[8192,256]{1,0:T(8,128)(2,1)}, bf16[8192,256]{1,0:T(8,128)(2,1)}, u32[]{:S(2)}, u32[]{:S(2)}) collective-permute-start(bf16[8192,256]{1,0:T(8,128)(2,1)} %all-gather.2.cloned.1.call-done.fetched), channel_id=1, source_target_pairs={{0,8},{8,0},{16,24},{24,16},{32,40},{40,32},{48,56},{56,48},{64,72... | collective-permute-start | bytes 12582920 | tf_op jit(solution)/shard_map/ppermute | solution.py:478
Sparse Core Ops, SparseCore 0:
  25.7 37.5 all-gather.1
  89.9 90.3 reduce-scatter.1

commit v9 on v8

--- a/solution.py
+++ b/solution.py
@@ -211,17 +211,17 @@
         return self.mine + jnp.where(core == 0, far, -far) - step * i
 
     def in_line(self, block):
-        row = block // 8 == self.mine // 8
+        row = self.mine // 2 - block // 2 <= 3
         column = (block // 2) % 4 == (self.mine // 2) % 4
         return jnp.where(block % 2 == 0, row, column)
 
     def place(self, block):
-        x, y, even = block // 8, (block // 2) % 4, block % 2 == 0
+        chip, even = block // 2, block % 2 == 0
         my_x, my_y = self.mine // 8, (self.mine // 2) % 4
-        distance = jnp.where(even, (my_y - y) % 4, (my_x - x) % 4)
+        distance = jnp.where(even, (my_y - chip) % 4, (my_x - chip // 4) % 4)
         place = distance ^ (distance >> 1)
         if not self.near_only:
-            place = place + 4 * jnp.where(even, x, y)
+            place = place + 4 * jnp.where(even, (chip + distance) // 4, chip % 4)
         return place
 
     def copy(self, far, place, slot):
@@ -234,7 +234,7 @@
             plain, masked = carry
             block = self.block(far, i)
             if self.near_only:
-                wanted = (block >= self.low) & (block <= self.mine) & self.in_line(block)
+                wanted = (block >= self.low) & (block <= self.mine)
             elif every:
                 wanted = block >= self.low
             else:
@@ -358,10 +358,19 @@
     attention.add(acc_ref)
 
 
-def part_kernel(len_ref, first_ref, split_ref, before_ref, fetched, acc_ref, kv_scr, ids, kinds, kv_sem):
-    attention = Attention(len_ref, first_ref, fetched, None, split_ref, kv_scr, ids, kinds, kv_sem)
+def part_kernel(
+    len_ref, first_ref, split_hbm, before_hbm, fetched, acc_ref, kv_scr, ids, kinds, kv_sem, q_scr, in_sem
+):
+    attention = Attention(len_ref, first_ref, fetched, None, q_scr, kv_scr, ids, kinds, kv_sem)
+    inputs = [
+        pltpu.make_async_copy(split_hbm, q_scr, in_sem.at[0]),
+        pltpu.make_async_copy(before_hbm, acc_ref, in_sem.at[1]),
+    ]
+    for copy in inputs:
+        copy.start()
     attention.fetch((0,))
-    acc_ref[...] = before_ref[...]
+    for copy in inputs:
+        copy.wait()
     attention.add(acc_ref)
 
 
@@ -408,12 +417,12 @@
                 pltpu.make_async_copy(ws_hbm.at[:, cols], w_scr.at[pl.ds(2 * HD, HP), cols], w_sem.at[2 * i + 1]),
             )
         )
+    for copy in inputs[:2]:
+        copy.wait()
     inputs[2].start()
     for pair in weights:
         for copy in pair:
             copy.start()
-    for copy in inputs[:2]:
-        copy.wait()
 
     attention.add(acc_scr)
     total = acc_scr[:, HD:]
@@ -445,8 +454,8 @@
         out_copy(i).wait()
 
 
-def big(**more):
-    return pltpu.CompilerParams(vmem_limit_bytes=LIMIT, **more)
+def big(limit=LIMIT):
+    return pltpu.CompilerParams(vmem_limit_bytes=limit)
 
 
 def moved(block, route0, route1):
@@ -468,6 +477,14 @@
 
 def along_x(distance):
     return lambda x, y: (x + distance, y) if x + distance < 4 else None
+
+
+def along_tokens(distance):
+    def to(x, y):
+        chip = 4 * x + y + distance
+        return (chip // 4, chip % 4) if chip < 16 else None
+
+    return to
 
 
 def along_y(distance):
@@ -505,9 +522,7 @@
     first = jnp.reshape(lax.axis_index("pack") * ROWS, (1,)).astype(jnp.int32)
     kv = keys_values.reshape(ROWS, 2 * HD)
     nowhere = lambda x, y: None
-    below = moved(kv, along_y(1), along_x(1))
-    above = moved(kv, along_y(3), along_x(3))
-    across = moved(kv, along_y(2), along_x(2))
+    one, three, two = [moved(kv, along_tokens(d), along_x(d)) for d in (1, 3, 2)]
     y_local, run_keep, run_send, fac = pl.pallas_call(
         ssd_kernel,
         out_shape=(
@@ -518,13 +533,13 @@
         ),
         in_specs=[SMEM] * 4 + [VMEM] * 3,
         out_specs=(VMEM, VMEM, VMEM, VMEM),
-        compiler_params=big(),
+        compiler_params=big(62 * 2**20),
         cost_estimate=pl.CostEstimate(flops=10**9, bytes_accessed=4 * 10**6, transcendentals=10**6),
         name="ssd_local",
     )(lengths, decay_log, skip_gain, first, ssm_values, ssm_maps, step_size.T)
 
-    below, above, across = lax.optimization_barrier((below, above, across, fac))[:3]
-    line = jnp.concatenate([kv, below, above, across], axis=0)
+    one, three, two = lax.optimization_barrier((one, three, two, fac))[:3]
+    line = jnp.concatenate([kv, one, three, two], axis=0)
     fetched = lax.all_gather(line, "pack", axis=0, tiled=True, axis_index_groups=lines())
     line_got = swapped(line)
 
@@ -541,13 +556,13 @@
     sums = jax.ShapeDtypeStruct((2 * ROWS, 2 * HD), jnp.float32)
     split = jax.ShapeDtypeStruct((2 * ROWS, 2 * HD), jnp.bfloat16)
 
-    def attend(kernel, name, shapes, vmem, *args):
+    def attend(kernel, name, shapes, vmem, *args, scratch=()):
         out = pl.pallas_call(
             kernel,
             out_shape=shapes,
-            in_specs=[SMEM] * 2 + [VMEM] * vmem + [ANY],
+            in_specs=[SMEM] * 2 + [VMEM] * vmem + [ANY] * (len(args) - vmem),
             out_specs=(VMEM,) * len(shapes),
-            scratch_shapes=chunks_scratch,
+            scratch_shapes=chunks_scratch + list(scratch),
             compiler_params=big(),
             cost_estimate=pl.CostEstimate(flops=3 * 10**9, bytes_accessed=5 * 10**6, transcendentals=5 * 10**6),
             name=name,
@@ -585,7 +600,16 @@
 
     fetched = lax.optimization_barrier((fetched, act))[0]
     other = swapped(fetched)
-    (acc,) = attend(part_kernel, "part", (sums,), 2, queries_split, acc, fetched)
+    (acc,) = attend(
+        part_kernel,
+        "part",
+        (sums,),
+        0,
+        queries_split,
+        acc,
+        fetched,
+        scratch=[pltpu.VMEM((2 * ROWS, 2 * HD), jnp.bfloat16), pltpu.SemaphoreType.DMA((2,))],
+    )
 
     terms = pl.pallas_call(
         mix_kernel,

time: 185 us -> 187 us (1.011)
  starting transfers between devices: 27.7 us -> 32 us
  waiting for transfers between devices: 103 us -> 99 us
    reduce_scatter x1, waiting for transfers between devices: 90.5 us -> 87.6 us  [local(): return lax.psum_scatter(terms, 'tp', scatter_dimension=0, tiled=True)]
    ppermute x9, starting transfers between devices: 23.2 us -> 25.6 us  [moved(): return lax.ppermute(block, 'pack', pairs)]
    ppermute x4, starting transfers between devices: 4.41 us -> 6.29 us  [swapped(): return lax.ppermute(block, 'pack', [(i, i ^ 1) for i in range(32)])]
  transfers between devices with their start and end apart: 15 -> 15, of which waited for: 7 -> 6; matrix products, arithmetic and copies ran while one was open for 0% -> 0% of each run, Pallas kernels for 14% -> 15%
where the time goes in v9:
time: 187 us; the launch traced here: 188 us
  waiting for transfers between devices  99 us (53%)
  Pallas kernels  42.4 us (23%)
  starting transfers between devices  32 us (17%)
  between operations  13.5 us (7%)
    reduce_scatter x1, waiting for transfers between devices, local(): return lax.psum_scatter(terms, 'tp', scatter_dimension=0, tiled=True)  87.6 us
    ppermute x9, starting transfers between devices, moved(): return lax.ppermute(block, 'pack', pairs)  25.6 us
    pallas_call x1, Pallas kernels, local(): pl.pallas_call(mix_kernel, out_shape=jax.ShapeDtypeStruct((ROWS, DM), jnp...  15.1 us
    pallas_call x3, Pallas kernels, attend(): pl.pallas_call(kernel, out_shape=shapes, in_specs=[SMEM] * 2 + [VMEM] * v...  11.7 us
    ppermute x4, waiting for transfers between devices, swapped(): return lax.ppermute(block, 'pack', [(i, i ^ 1) for i in range(32)])  7.61 us
    ppermute x4, starting transfers between devices, swapped(): return lax.ppermute(block, 'pack', [(i, i ^ 1) for i in range(32)])  6.29 us
    pallas_call x1, Pallas kernels, local(): pl.pallas_call(ssd_kernel, out_shape=(jax.ShapeDtypeStruct((ROWS, HP), jn...  6.22 us
    pallas_call x3, Pallas kernels, call(): pl.pallas_call(kernel, out_shape=tuple((jax.ShapeDtypeStruct(shape, jnp.b...  5.89 us
  transfers between devices with their start and end apart: 15, of which 6 were waited for; matrix products, arithmetic and copies ran while one was open for 0% of the time, Pallas kernels for 15%

profile of v9, /device:TPU:1, one launch (start us, length us, event | category | flops | bytes accessed | tf_op | source)
XLA Modules:
  0.0 188.0 jit_solution(17758281807909520756)
XLA Ops:
  6.5 5.6 %collective-permute-start.2 = (bf16[512,256]{1,0:T(8,128)(2,1)}, bf16[512,256]{1,0:T(8,128)(2,1)S(1)}, u32[]{:S(2)}, u32[]{:S(2)}) collective-permute-start(bf16[512,256]{1,0:T(8,128)(2,1)} %bitcast.3), channel_id=1, source_target_pairs={{0,32},{8,136},{16,48},{24,152},{32,64},{40,168},{48,80},{56,184},... | collective-permute-start | bytes 786440 | tf_op jit(solution)/shard_map/ppermute | solution.py:469
  12.2 1.3 collective-permute-start.1
  13.5 1.6 collective-permute-start
  15.1 6.2 %ssd_local.1 = (f32[512,512]{1,0:T(8,128)}, bf16[272,256]{1,0:T(8,128)(2,1)}, bf16[272,256]{1,0:T(8,128)(2,1)}, f32[512,8]{1,0:T(8,128)}) custom-call(s32[4]{0:T(128)} %len_ref.9, f32[8]{0:T(128)} %dl_ref.1, f32[8]{0:T(128)} %skip_ref.1, s32[1]{0:T(128)} %bitcast.first_ref, bf16[512,512]{1,0:T(8,128)(2,1)} %x_ref.1, bf16[512,512]{1,0:T(8,128)(2,1)} %read_ref.1, ...), custom_call_target="tpu_custom_call" | custom-call | flops 1000000000 | bytes 4000000 | tf_op jit(solution)/shard_map/ssd_local/pallas_call | solution.py:526
  21.4 1.1 pad_maximum_fusion.line
  22.5 5.1 %collective-permute-start.10 = (bf16[2048,256]{1,0:T(8,128)(2,1)}, bf16[2048,256]{1,0:T(8,128)(2,1)}, u32[]{:S(2)}, u32[]{:S(2)}) collective-permute-start(bf16[2048,256]{1,0:T(8,128)(2,1)} %pad_maximum_fusion.line), channel_id=1, source_target_pairs={{0,8},{8,0},{16,24},{24,16},{32,40},{40,32},{48,56},{56,48},{64,72... | collective-permute-start | bytes 3145736 | tf_op jit(solution)/shard_map/ppermute | solution.py:495
  27.7 2.4 %collective-permute-done.3.other_ref = bf16[272,256]{1,0:T(8,128)(2,1)} collective-permute-done((bf16[272,256]{1,0:T(8,128)(2,1)S(1)}, bf16[272,256]{1,0:T(8,128)(2,1)}, u32[]{:S(2)}, u32[]{:S(2)}) %collective-permute-start.3) | collective-permute-done | bytes 139296 | tf_op jit(solution)/shard_map/ppermute | solution.py:495
  30.1 1.7 shard_map.109.mine_ref
  32.7 2.8 %collective-permute-start.5 = (bf16[272,256]{1,0:T(8,128)(2,1)}, bf16[272,256]{1,0:T(8,128)(2,1)}, u32[]{:S(2)}, u32[]{:S(2)}) collective-permute-start(bf16[272,256]{1,0:T(8,128)(2,1)} %shard_map.109.mine_ref), channel_id=1, source_target_pairs={{0,48},{8,56},{16,0},{24,8},{32,16},{40,24},{48,32},{56,40},{64,11... | collective-permute-start | bytes 417800 | tf_op jit(solution)/shard_map/ppermute | solution.py:469
  36.1 4.1 %own_line.1 = (f32[1024,256]{1,0:T(8,128)}, bf16[1024,256]{1,0:T(8,128)(2,1)}) custom-call(s32[4]{0:T(128)} %len_ref.9, s32[1]{0:T(128)} %bitcast.first_ref, bf16[512,256]{1,0:T(8,128)(2,1)} %q_ref.1, bf16[2048,256]{1,0:T(8,128)(2,1)} %pad_maximum_fusion.line), custom_call_target="tpu_custom_call" | custom-call | flops 3000000000 | bytes 5000000 | tf_op jit(solution)/shard_map/own_line/pallas_call | solution.py:560
  40.3 2.7 %collective-permute-done.5.above_ref = bf16[272,256]{1,0:T(8,128)(2,1)} collective-permute-done((bf16[272,256]{1,0:T(8,128)(2,1)}, bf16[272,256]{1,0:T(8,128)(2,1)}, u32[]{:S(2)}, u32[]{:S(2)}) %collective-permute-start.5) | collective-permute-done | bytes 139296 | tf_op jit(solution)/shard_map/ppermute | solution.py:469
  43.0 2.1 %shard_map.110 = (bf16[272,256]{1,0:T(8,128)(2,1)}, bf16[272,256]{1,0:T(8,128)(2,1)}) custom-call(s32[1]{0:T(128)} %bitcast.first_ref, bf16[272,256]{1,0:T(8,128)(2,1)} %shard_map.109.mine_ref, bf16[272,256]{1,0:T(8,128)(2,1)} %collective-permute-done.4.below_ref, bf16[272,256]{1,0:T(8,128)(2,1)} %collective-permute-done.5.above_ref, ...), custom_call_target="tpu_custom_call" | custom-call | flops 1000000 | bytes 1000000 | tf_op jit(solution)/shard_map/pallas_call | solution.py:499
  45.1 7.3 %collective-permute-start.9 = (bf16[272,256]{1,0:T(8,128)(2,1)}, bf16[272,256]{1,0:T(8,128)(2,1)}, u32[]{:S(2)}, u32[]{:S(2)}) collective-permute-start(bf16[272,256]{1,0:T(8,128)(2,1)} %get-tuple-element.40), channel_id=1, source_target_pairs={{0,64},{8,72},{16,80},{24,88},{32,96},{40,104},{48,112},{56,120},{... | collective-permute-start | bytes 417800 | tf_op jit(solution)/shard_map/ppermute | solution.py:469
  52.4 3.5 %collective-permute-start.8 = (bf16[272,256]{1,0:T(8,128)(2,1)}, bf16[272,256]{1,0:T(8,128)(2,1)}, u32[]{:S(2)}, u32[]{:S(2)}) collective-permute-start(bf16[272,256]{1,0:T(8,128)(2,1)} %get-tuple-element.40), channel_id=1, source_target_pairs={{0,128},{8,136},{16,144},{24,152},{32,160},{40,168},{48,176},{56,1... | collective-permute-start | bytes 417800 | tf_op jit(solution)/shard_map/ppermute | solution.py:469
  55.9 2.0 %collective-permute-start.7 = (bf16[272,256]{1,0:T(8,128)(2,1)}, bf16[272,256]{1,0:T(8,128)(2,1)}, u32[]{:S(2)}, u32[]{:S(2)}) collective-permute-start(bf16[272,256]{1,0:T(8,128)(2,1)} %get-tuple-element.40), channel_id=1, source_target_pairs={{0,192},{8,200},{16,208},{24,216},{32,224},{40,232},{48,240},{56,2... | collective-permute-start | bytes 417800 | tf_op jit(solution)/shard_map/ppermute | solution.py:469
  57.8 4.3 %other_line.1.before_hbm = f32[1024,256]{1,0:T(8,128)} custom-call(s32[4]{0:T(128)} %len_ref.9, s32[1]{0:T(128)} %bitcast.first_ref, bf16[1024,256]{1,0:T(8,128)(2,1)} %get-tuple-element.34.split_ref.split_hbm, f32[1024,256]{1,0:T(8,128)} %get-tuple-element.36.before_ref, bf16[2048,256]{1,0:T(8,128)(2,1)} %collective-permute-done.10.line_got), custom_call_target="tpu_custom_call" | custom-call | flops 3000000000 | bytes 5000000 | tf_op jit(solution)/shard_map/other_line/pallas_call | solution.py:560
  62.2 1.1 collective-permute-done.7.row3_ref
  63.3 2.1 %shard_map.111 = (bf16[256,256]{1,0:T(8,128)(2,1)}, bf16[256,256]{1,0:T(8,128)(2,1)}) custom-call(s32[1]{0:T(128)} %bitcast.first_ref, bf16[272,256]{1,0:T(8,128)(2,1)} %collective-permute-done.7.row3_ref, bf16[272,256]{1,0:T(8,128)(2,1)} %collective-permute-done.8.row2_ref, bf16[272,256]{1,0:T(8,128)(2,1)} %collective-permute-done.9.row1_ref, ...), custom_call_target="tpu_custom_call" | custom-call | flops 1000000 | bytes 1000000 | tf_op jit(solution)/shard_map/pallas_call | solution.py:499
  66.1 1.3 collective-permute-done.11.got_ref
  67.4 3.5 %gate.1.act_hbm = bf16[512,512]{1,0:T(8,128)(2,1)} custom-call(s32[1]{0:T(128)} %bitcast.first_ref, f32[512,512]{1,0:T(8,128)} %get-tuple-element.35.y_ref, bf16[512,512]{1,0:T(8,128)(2,1)} %z_ref.1, bf16[512,512]{1,0:T(8,128)(2,1)} %read_ref.1, f32[512,8]{1,0:T(8,128)} %get-tuple-element.27.fac_ref, bf16[256,256]{1,0:T(8,128)(2,1)} %get-tuple-element.46.keep_ref, ...), custom_call_target="tpu_custom_call" | custom-call | flops 100000000 | bytes 3000000 | tf_op jit(solution)/shard_map/gate/pallas_call | solution.py:582
  71.3 3.2 %part.1.before_hbm = f32[1024,256]{1,0:T(8,128)} custom-call(s32[4]{0:T(128)} %len_ref.9, s32[1]{0:T(128)} %bitcast.first_ref, bf16[1024,256]{1,0:T(8,128)(2,1)} %get-tuple-element.34.split_ref.split_hbm, f32[1024,256]{1,0:T(8,128)} %other_line.1.before_hbm, bf16[8192,256]{1,0:T(8,128)(2,1)} %all-gather.2.cloned.1.call-done.fetched), custom_call_target="tpu_custom_call" | custom-call | flops 3000000000 | bytes 5000000 | tf_op jit(solution)/shard_map/part/pallas_call | solution.py:560
  74.5 3.9 %collective-permute-done.12.other = bf16[8192,256]{1,0:T(8,128)(2,1)} collective-permute-done((bf16[8192,256]{1,0:T(8,128)(2,1)}, bf16[8192,256]{1,0:T(8,128)(2,1)}, u32[]{:S(2)}, u32[]{:S(2)}) %collective-permute-start.12) | collective-permute-done | bytes 4194336 | tf_op jit(solution)/shard_map/ppermute | solution.py:495
  78.4 15.1 %mix.1 = bf16[512,5120]{1,0:T(8,128)(2,1)} custom-call(s32[4]{0:T(128)} %len_ref.9, s32[1]{0:T(128)} %bitcast.first_ref, bf16[1024,256]{1,0:T(8,128)(2,1)} %get-tuple-element.34.split_ref.split_hbm, bf16[512,512]{1,0:T(8,128)(2,1)} %gate.1.act_hbm, f32[1024,256]{1,0:T(8,128)} %part.1.before_hbm, bf16[8192,256]{1,0:T(8,128)(2,1)} %all-gather.2.cloned.1.call-done.fetched, ...), custom_call_target="tpu_custom_call" | custom-call | flops 8999999488 | bytes 25000000 | tf_op jit(solution)/shard_map/mix/pallas_call | solution.py:614
  93.6 87.6 %reduce-scatter.2.cloned.1.call-done = bf16[64,5120]{1,0:T(8,128)(2,1)} async-done(((bf16[512,5120]{1,0:T(8,128)(2,1)}), bf16[64,5120]{1,0:T(8,128)(2,1)}) %reduce-scatter.2.cloned.1.call-update) | async-done | bytes 655376 | tf_op jit(solution)/shard_map/reduce_scatter | solution.py:635
  (22 shorter events, 2.8 us)
Async XLA Ops:
  6.5 14.8 %copy-start = (bf16[512,1,256]{2,0,1:T(8,128)(2,1)S(1)}, bf16[512,1,256]{2,0,1:T(8,128)(2,1)}, u32[]{:S(2)}) copy-start(bf16[512,1,256]{2,0,1:T(8,128)(2,1)} %param.12) | copy-start | bytes 786436
  6.5 64.4 %all-gather.2.cloned.1.call-start = ((), (), s32[]{:S(2)}) async-start(), calls=%async_computation.1 | async-start | bytes 5242880 | tf_op jit(solution)/shard_map/all_gather | solution.py:543
  6.5 14.8 %collective-permute-start.2 = (bf16[512,256]{1,0:T(8,128)(2,1)}, bf16[512,256]{1,0:T(8,128)(2,1)S(1)}, u32[]{:S(2)}, u32[]{:S(2)}) collective-permute-start(bf16[512,256]{1,0:T(8,128)(2,1)} %bitcast.3), channel_id=1, source_target_pairs={{0,32},{8,136},{16,48},{24,152},{32,64},{40,168},{48,80},{56,184},... | collective-permute-start | bytes 786440 | tf_op jit(solution)/shard_map/ppermute | solution.py:469
  12.2 9.2 %collective-permute-start.1 = (bf16[512,256]{1,0:T(8,128)(2,1)}, bf16[512,256]{1,0:T(8,128)(2,1)S(1)}, u32[]{:S(2)}, u32[]{:S(2)}) collective-permute-start(bf16[512,256]{1,0:T(8,128)(2,1)} %bitcast.4), channel_id=1, source_target_pairs={{0,48},{8,200},{16,64},{24,216},{32,80},{40,232},{48,96},{56,248},... | collective-permute-start | bytes 786440 | tf_op jit(solution)/shard_map/ppermute | solution.py:469
  13.5 7.9 %collective-permute-start = (bf16[512,256]{1,0:T(8,128)(2,1)}, bf16[512,256]{1,0:T(8,128)(2,1)S(1)}, u32[]{:S(2)}, u32[]{:S(2)}) collective-permute-start(bf16[512,256]{1,0:T(8,128)(2,1)} %bitcast.5), channel_id=1, source_target_pairs={{0,16},{8,72},{16,32},{24,88},{32,48},{40,104},{48,64},{56,120},{6... | collective-permute-start | bytes 786440 | tf_op jit(solution)/shard_map/ppermute | solution.py:469
  21.3 6.3 %copy-start.1 = (bf16[272,256]{1,0:T(8,128)(2,1)S(1)}, bf16[272,256]{1,0:T(8,128)(2,1)}, u32[]{:S(2)}) copy-start(bf16[272,256]{1,0:T(8,128)(2,1)} %get-tuple-element.32) | copy-start | bytes 417796
  22.4 158.7 %reduce-scatter.2.cloned.1.call-start = ((), (), s32[]{:S(2)}) async-start(), calls=%async_computation.2 | async-start | bytes 5898240 | tf_op jit(solution)/shard_map/reduce_scatter | solution.py:635
  22.5 35.3 %collective-permute-start.10 = (bf16[2048,256]{1,0:T(8,128)(2,1)}, bf16[2048,256]{1,0:T(8,128)(2,1)}, u32[]{:S(2)}, u32[]{:S(2)}) collective-permute-start(bf16[2048,256]{1,0:T(8,128)(2,1)} %pad_maximum_fusion.line), channel_id=1, source_target_pairs={{0,8},{8,0},{16,24},{24,16},{32,40},{40,32},{48,56},{56,48},{64,72... | collective-permute-start | bytes 3145736 | tf_op jit(solution)/shard_map/ppermute | solution.py:495
  27.6 2.5 %collective-permute-start.3 = (bf16[272,256]{1,0:T(8,128)(2,1)S(1)}, bf16[272,256]{1,0:T(8,128)(2,1)}, u32[]{:S(2)}, u32[]{:S(2)}) collective-permute-start(bf16[272,256]{1,0:T(8,128)(2,1)S(1)} %copy-done.1), channel_id=1, source_target_pairs={{0,8},{8,0},{16,24},{24,16},{32,40},{40,32},{48,56},{56,48},{64,72... | collective-permute-start | bytes 417800 | tf_op jit(solution)/shard_map/ppermute | solution.py:495
  31.8 8.5 %collective-permute-start.6 = (bf16[272,256]{1,0:T(8,128)(2,1)}, bf16[272,256]{1,0:T(8,128)(2,1)}, u32[]{:S(2)}, u32[]{:S(2)}) collective-permute-start(bf16[272,256]{1,0:T(8,128)(2,1)} %shard_map.109.mine_ref), channel_id=1, source_target_pairs={{0,32},{8,40},{16,48},{24,56},{32,0},{40,8},{48,16},{56,24},{64,96... | collective-permute-start | bytes 417800 | tf_op jit(solution)/shard_map/ppermute | solution.py:469
  32.7 10.2 %collective-permute-start.5 = (bf16[272,256]{1,0:T(8,128)(2,1)}, bf16[272,256]{1,0:T(8,128)(2,1)}, u32[]{:S(2)}, u32[]{:S(2)}) collective-permute-start(bf16[272,256]{1,0:T(8,128)(2,1)} %shard_map.109.mine_ref), channel_id=1, source_target_pairs={{0,48},{8,56},{16,0},{24,8},{32,16},{40,24},{48,32},{56,40},{64,11... | collective-permute-start | bytes 417800 | tf_op jit(solution)/shard_map/ppermute | solution.py:469
  35.6 7.4 %collective-permute-start.4 = (bf16[272,256]{1,0:T(8,128)(2,1)}, bf16[272,256]{1,0:T(8,128)(2,1)}, u32[]{:S(2)}, u32[]{:S(2)}) collective-permute-start(bf16[272,256]{1,0:T(8,128)(2,1)} %shard_map.109.mine_ref), channel_id=1, source_target_pairs={{0,16},{8,24},{16,32},{24,40},{32,48},{40,56},{48,0},{56,8},{64,80... | collective-permute-start | bytes 417800 | tf_op jit(solution)/shard_map/ppermute | solution.py:469
  45.1 17.1 %collective-permute-start.9 = (bf16[272,256]{1,0:T(8,128)(2,1)}, bf16[272,256]{1,0:T(8,128)(2,1)}, u32[]{:S(2)}, u32[]{:S(2)}) collective-permute-start(bf16[272,256]{1,0:T(8,128)(2,1)} %get-tuple-element.40), channel_id=1, source_target_pairs={{0,64},{8,72},{16,80},{24,88},{32,96},{40,104},{48,112},{56,120},{... | collective-permute-start | bytes 417800 | tf_op jit(solution)/shard_map/ppermute | solution.py:469
  52.4 9.8 %collective-permute-start.8 = (bf16[272,256]{1,0:T(8,128)(2,1)}, bf16[272,256]{1,0:T(8,128)(2,1)}, u32[]{:S(2)}, u32[]{:S(2)}) collective-permute-start(bf16[272,256]{1,0:T(8,128)(2,1)} %get-tuple-element.40), channel_id=1, source_target_pairs={{0,128},{8,136},{16,144},{24,152},{32,160},{40,168},{48,176},{56,1... | collective-permute-start | bytes 417800 | tf_op jit(solution)/shard_map/ppermute | solution.py:469
  55.9 7.4 %collective-permute-start.7 = (bf16[272,256]{1,0:T(8,128)(2,1)}, bf16[272,256]{1,0:T(8,128)(2,1)}, u32[]{:S(2)}, u32[]{:S(2)}) collective-permute-start(bf16[272,256]{1,0:T(8,128)(2,1)} %get-tuple-element.40), channel_id=1, source_target_pairs={{0,192},{8,200},{16,208},{24,216},{32,224},{40,232},{48,240},{56,2... | collective-permute-start | bytes 417800 | tf_op jit(solution)/shard_map/ppermute | solution.py:469
  65.3 2.1 %collective-permute-start.11 = (bf16[256,256]{1,0:T(8,128)(2,1)}, bf16[256,256]{1,0:T(8,128)(2,1)}, u32[]{:S(2)}, u32[]{:S(2)}) collective-permute-start(bf16[256,256]{1,0:T(8,128)(2,1)} %get-tuple-element.47), channel_id=1, source_target_pairs={{0,8},{8,0},{16,24},{24,16},{32,40},{40,32},{48,56},{56,48},{64,72... | collective-permute-start | bytes 393224 | tf_op jit(solution)/shard_map/ppermute | solution.py:495
  70.9 7.5 %collective-permute-start.12 = (bf16[8192,256]{1,0:T(8,128)(2,1)}, bf16[8192,256]{1,0:T(8,128)(2,1)}, u32[]{:S(2)}, u32[]{:S(2)}) collective-permute-start(bf16[8192,256]{1,0:T(8,128)(2,1)} %all-gather.2.cloned.1.call-done.fetched), channel_id=1, source_target_pairs={{0,8},{8,0},{16,24},{24,16},{32,40},{40,32},{48,56},{56,48},{64,72... | collective-permute-start | bytes 12582920 | tf_op jit(solution)/shard_map/ppermute | solution.py:495
Sparse Core Ops, SparseCore 0:
  22.6 43.2 all-gather.1
  93.7 87.4 reduce-scatter.1

commit v10 on v9

--- a/solution.py
+++ b/solution.py
@@ -15,7 +15,7 @@
 CHUNK = 512
 SLOTS = 18
 TILE = 256
-COLS = 1280
+COLS = 1024
 LOW = -1e30
 LOG2E = 1.4426950408889634
 HIGH = lax.Precision.HIGHEST
@@ -211,17 +211,17 @@
         return self.mine + jnp.where(core == 0, far, -far) - step * i
 
     def in_line(self, block):
-        row = self.mine // 2 - block // 2 <= 3
+        row = block // 8 == self.mine // 8
         column = (block // 2) % 4 == (self.mine // 2) % 4
         return jnp.where(block % 2 == 0, row, column)
 
     def place(self, block):
-        chip, even = block // 2, block % 2 == 0
+        x, y, even = block // 8, (block // 2) % 4, block % 2 == 0
         my_x, my_y = self.mine // 8, (self.mine // 2) % 4
-        distance = jnp.where(even, (my_y - chip) % 4, (my_x - chip // 4) % 4)
+        distance = jnp.where(even, (my_y - y) % 4, (my_x - x) % 4)
         place = distance ^ (distance >> 1)
         if not self.near_only:
-            place = place + 4 * jnp.where(even, (chip + distance) // 4, chip % 4)
+            place = place + 4 * jnp.where(even, x, y)
         return place
 
     def copy(self, far, place, slot):
@@ -234,7 +234,7 @@
             plain, masked = carry
             block = self.block(far, i)
             if self.near_only:
-                wanted = (block >= self.low) & (block <= self.mine)
+                wanted = (block >= self.low) & (block <= self.mine) & self.in_line(block)
             elif every:
                 wanted = block >= self.low
             else:
@@ -417,12 +417,12 @@
                 pltpu.make_async_copy(ws_hbm.at[:, cols], w_scr.at[pl.ds(2 * HD, HP), cols], w_sem.at[2 * i + 1]),
             )
         )
-    for copy in inputs[:2]:
-        copy.wait()
     inputs[2].start()
     for pair in weights:
         for copy in pair:
             copy.start()
+    for copy in inputs[:2]:
+        copy.wait()
 
     attention.add(acc_scr)
     total = acc_scr[:, HD:]
@@ -477,14 +477,6 @@
 
 def along_x(distance):
     return lambda x, y: (x + distance, y) if x + distance < 4 else None
-
-
-def along_tokens(distance):
-    def to(x, y):
-        chip = 4 * x + y + distance
-        return (chip // 4, chip % 4) if chip < 16 else None
-
-    return to
 
 
 def along_y(distance):
@@ -522,7 +514,9 @@
     first = jnp.reshape(lax.axis_index("pack") * ROWS, (1,)).astype(jnp.int32)
     kv = keys_values.reshape(ROWS, 2 * HD)
     nowhere = lambda x, y: None
-    one, three, two = [moved(kv, along_tokens(d), along_x(d)) for d in (1, 3, 2)]
+    below = moved(kv, along_y(1), along_x(1))
+    above = moved(kv, along_y(3), along_x(3))
+    across = moved(kv, along_y(2), along_x(2))
     y_local, run_keep, run_send, fac = pl.pallas_call(
         ssd_kernel,
         out_shape=(
@@ -538,8 +532,8 @@
         name="ssd_local",
     )(lengths, decay_log, skip_gain, first, ssm_values, ssm_maps, step_size.T)
 
-    one, three, two = lax.optimization_barrier((one, three, two, fac))[:3]
-    line = jnp.concatenate([kv, one, three, two], axis=0)
+    below, above, across = lax.optimization_barrier((below, above, across, fac))[:3]
+    line = jnp.concatenate([kv, below, above, across], axis=0)
     fetched = lax.all_gather(line, "pack", axis=0, tiled=True, axis_index_groups=lines())
     line_got = swapped(line)
 

time: 187 us -> 183 us (0.979)
  starting transfers between devices: 32 us -> 27.8 us
    ppermute x9, starting transfers between devices: 25.6 us -> 21.4 us  [moved(): return lax.ppermute(block, 'pack', pairs)]
  transfers between devices with their start and end apart: 15 -> 15, of which waited for: 6 -> 7; matrix products, arithmetic and copies ran while one was open for 0% -> 0% of each run, Pallas kernels for 15% -> 15%
where the time goes in v10:
time: 183 us
  waiting for transfers between devices  100 us (55%)
  Pallas kernels  40.9 us (22%)
  starting transfers between devices  27.8 us (15%)
  between operations  13.5 us (7%)
    reduce_scatter x1, waiting for transfers between devices, local(): return lax.psum_scatter(terms, 'tp', scatter_dimension=0, tiled=True)  88.7 us
    ppermute x9, starting transfers between devices, moved(): return lax.ppermute(block, 'pack', pairs)  21.4 us
    pallas_call x1, Pallas kernels, local(): pl.pallas_call(mix_kernel, out_shape=jax.ShapeDtypeStruct((ROWS, DM), jnp...  13.7 us
    pallas_call x3, Pallas kernels, attend(): pl.pallas_call(kernel, out_shape=shapes, in_specs=[SMEM] * 2 + [VMEM] * v...  11.7 us
    ppermute x4, waiting for transfers between devices, swapped(): return lax.ppermute(block, 'pack', [(i, i ^ 1) for i in range(32)])  7.6 us
    ppermute x4, starting transfers between devices, swapped(): return lax.ppermute(block, 'pack', [(i, i ^ 1) for i in range(32)])  6.37 us
    pallas_call x1, Pallas kernels, local(): pl.pallas_call(ssd_kernel, out_shape=(jax.ShapeDtypeStruct((ROWS, HP), jn...  6.22 us
    pallas_call x3, Pallas kernels, call(): pl.pallas_call(kernel, out_shape=tuple((jax.ShapeDtypeStruct(shape, jnp.b...  5.84 us
  transfers between devices with their start and end apart: 15, of which 7 were waited for; matrix products, arithmetic and copies ran while one was open for 0% of the time, Pallas kernels for 15%

profile of v10, /device:TPU:1, one launch (start us, length us, event | category | flops | bytes accessed | tf_op | source)
XLA Modules:
  0.0 183.4 jit_solution(11925527550903914948)
XLA Ops:
  6.5 5.6 %collective-permute-start.2 = (bf16[512,256]{1,0:T(8,128)(2,1)}, bf16[512,256]{1,0:T(8,128)(2,1)S(1)}, u32[]{:S(2)}, u32[]{:S(2)}) collective-permute-start(bf16[512,256]{1,0:T(8,128)(2,1)} %bitcast.3), channel_id=1, source_target_pairs={{0,32},{8,136},{16,48},{24,152},{32,0},{40,168},{48,16},{56,184},{... | collective-permute-start | bytes 786440 | tf_op jit(solution)/shard_map/ppermute | solution.py:469
  12.2 1.3 collective-permute-start.1
  13.5 1.6 collective-permute-start
  15.1 6.2 %ssd_local.1 = (f32[512,512]{1,0:T(8,128)}, bf16[272,256]{1,0:T(8,128)(2,1)}, bf16[272,256]{1,0:T(8,128)(2,1)}, f32[512,8]{1,0:T(8,128)}) custom-call(s32[4]{0:T(128)} %len_ref.9, f32[8]{0:T(128)} %dl_ref.1, f32[8]{0:T(128)} %skip_ref.1, s32[1]{0:T(128)} %bitcast.first_ref, bf16[512,512]{1,0:T(8,128)(2,1)} %x_ref.1, bf16[512,512]{1,0:T(8,128)(2,1)} %read_ref.1, ...), custom_call_target="tpu_custom_call" | custom-call | flops 1000000000 | bytes 4000000 | tf_op jit(solution)/shard_map/ssd_local/pallas_call | solution.py:520
  22.5 4.7 %collective-permute-start.10 = (bf16[2048,256]{1,0:T(8,128)(2,1)}, bf16[2048,256]{1,0:T(8,128)(2,1)}, u32[]{:S(2)}, u32[]{:S(2)}) collective-permute-start(bf16[2048,256]{1,0:T(8,128)(2,1)} %pad_maximum_fusion.line), channel_id=1, source_target_pairs={{0,8},{8,0},{16,24},{24,16},{32,40},{40,32},{48,56},{56,48},{64,72... | collective-permute-start | bytes 3145736 | tf_op jit(solution)/shard_map/ppermute | solution.py:487
  27.3 2.4 %collective-permute-done.3.other_ref = bf16[272,256]{1,0:T(8,128)(2,1)} collective-permute-done((bf16[272,256]{1,0:T(8,128)(2,1)S(1)}, bf16[272,256]{1,0:T(8,128)(2,1)}, u32[]{:S(2)}, u32[]{:S(2)}) %collective-permute-start.3) | collective-permute-done | bytes 139296 | tf_op jit(solution)/shard_map/ppermute | solution.py:487
  29.7 1.7 shard_map.109.mine_ref
  31.4 1.3 collective-permute-start.6
  34.1 4.1 %own_line.1 = (f32[1024,256]{1,0:T(8,128)}, bf16[1024,256]{1,0:T(8,128)(2,1)}) custom-call(s32[4]{0:T(128)} %len_ref.9, s32[1]{0:T(128)} %bitcast.first_ref, bf16[512,256]{1,0:T(8,128)(2,1)} %q_ref.1, bf16[2048,256]{1,0:T(8,128)(2,1)} %pad_maximum_fusion.line), custom_call_target="tpu_custom_call" | custom-call | flops 3000000000 | bytes 5000000 | tf_op jit(solution)/shard_map/own_line/pallas_call | solution.py:554
  38.2 2.0 %collective-permute-done.5.above_ref = bf16[272,256]{1,0:T(8,128)(2,1)} collective-permute-done((bf16[272,256]{1,0:T(8,128)(2,1)}, bf16[272,256]{1,0:T(8,128)(2,1)}, u32[]{:S(2)}, u32[]{:S(2)}) %collective-permute-start.5) | collective-permute-done | bytes 139296 | tf_op jit(solution)/shard_map/ppermute | solution.py:469
  40.2 1.1 collective-permute-done.4.below_ref
  41.3 2.1 %shard_map.110 = (bf16[272,256]{1,0:T(8,128)(2,1)}, bf16[272,256]{1,0:T(8,128)(2,1)}) custom-call(s32[1]{0:T(128)} %bitcast.first_ref, bf16[272,256]{1,0:T(8,128)(2,1)} %shard_map.109.mine_ref, bf16[272,256]{1,0:T(8,128)(2,1)} %collective-permute-done.4.below_ref, bf16[272,256]{1,0:T(8,128)(2,1)} %collective-permute-done.5.above_ref, ...), custom_call_target="tpu_custom_call" | custom-call | flops 1000000 | bytes 1000000 | tf_op jit(solution)/shard_map/pallas_call | solution.py:491
  43.4 3.8 %collective-permute-start.9 = (bf16[272,256]{1,0:T(8,128)(2,1)}, bf16[272,256]{1,0:T(8,128)(2,1)}, u32[]{:S(2)}, u32[]{:S(2)}) collective-permute-start(bf16[272,256]{1,0:T(8,128)(2,1)} %get-tuple-element.40), channel_id=1, source_target_pairs={{0,64},{8,72},{16,80},{24,88},{32,96},{40,104},{48,112},{56,120},{... | collective-permute-start | bytes 417800 | tf_op jit(solution)/shard_map/ppermute | solution.py:469
  47.1 4.4 %collective-permute-start.8 = (bf16[272,256]{1,0:T(8,128)(2,1)}, bf16[272,256]{1,0:T(8,128)(2,1)}, u32[]{:S(2)}, u32[]{:S(2)}) collective-permute-start(bf16[272,256]{1,0:T(8,128)(2,1)} %get-tuple-element.40), channel_id=1, source_target_pairs={{0,128},{8,136},{16,144},{24,152},{32,160},{40,168},{48,176},{56,1... | collective-permute-start | bytes 417800 | tf_op jit(solution)/shard_map/ppermute | solution.py:469
  51.5 2.0 %collective-permute-start.7 = (bf16[272,256]{1,0:T(8,128)(2,1)}, bf16[272,256]{1,0:T(8,128)(2,1)}, u32[]{:S(2)}, u32[]{:S(2)}) collective-permute-start(bf16[272,256]{1,0:T(8,128)(2,1)} %get-tuple-element.40), channel_id=1, source_target_pairs={{0,192},{8,200},{16,208},{24,216},{32,224},{40,232},{48,240},{56,2... | collective-permute-start | bytes 417800 | tf_op jit(solution)/shard_map/ppermute | solution.py:469
  53.5 4.3 %other_line.1.before_hbm = f32[1024,256]{1,0:T(8,128)} custom-call(s32[4]{0:T(128)} %len_ref.9, s32[1]{0:T(128)} %bitcast.first_ref, bf16[1024,256]{1,0:T(8,128)(2,1)} %get-tuple-element.34.split_ref.split_hbm, f32[1024,256]{1,0:T(8,128)} %get-tuple-element.36.before_ref, bf16[2048,256]{1,0:T(8,128)(2,1)} %collective-permute-done.10.line_got), custom_call_target="tpu_custom_call" | custom-call | flops 3000000000 | bytes 5000000 | tf_op jit(solution)/shard_map/other_line/pallas_call | solution.py:554
  58.6 2.1 %shard_map.111 = (bf16[256,256]{1,0:T(8,128)(2,1)}, bf16[256,256]{1,0:T(8,128)(2,1)}) custom-call(s32[1]{0:T(128)} %bitcast.first_ref, bf16[272,256]{1,0:T(8,128)(2,1)} %collective-permute-done.7.row3_ref, bf16[272,256]{1,0:T(8,128)(2,1)} %collective-permute-done.8.row2_ref, bf16[272,256]{1,0:T(8,128)(2,1)} %collective-permute-done.9.row1_ref, ...), custom_call_target="tpu_custom_call" | custom-call | flops 1000000 | bytes 1000000 | tf_op jit(solution)/shard_map/pallas_call | solution.py:491
  60.6 1.2 collective-permute-start.11
  61.9 1.3 collective-permute-done.11.got_ref
  63.2 3.5 %gate.1.act_hbm = bf16[512,512]{1,0:T(8,128)(2,1)} custom-call(s32[1]{0:T(128)} %bitcast.first_ref, f32[512,512]{1,0:T(8,128)} %get-tuple-element.35.y_ref, bf16[512,512]{1,0:T(8,128)(2,1)} %z_ref.1, bf16[512,512]{1,0:T(8,128)(2,1)} %read_ref.1, f32[512,8]{1,0:T(8,128)} %get-tuple-element.27.fac_ref, bf16[256,256]{1,0:T(8,128)(2,1)} %get-tuple-element.46.keep_ref, ...), custom_call_target="tpu_custom_call" | custom-call | flops 100000000 | bytes 3000000 | tf_op jit(solution)/shard_map/gate/pallas_call | solution.py:576
  67.1 3.2 %part.1.before_hbm = f32[1024,256]{1,0:T(8,128)} custom-call(s32[4]{0:T(128)} %len_ref.9, s32[1]{0:T(128)} %bitcast.first_ref, bf16[1024,256]{1,0:T(8,128)(2,1)} %get-tuple-element.34.split_ref.split_hbm, f32[1024,256]{1,0:T(8,128)} %other_line.1.before_hbm, bf16[8192,256]{1,0:T(8,128)(2,1)} %all-gather.2.cloned.1.call-done.fetched), custom_call_target="tpu_custom_call" | custom-call | flops 3000000000 | bytes 5000000 | tf_op jit(solution)/shard_map/part/pallas_call | solution.py:554
  70.3 3.9 %collective-permute-done.12.other = bf16[8192,256]{1,0:T(8,128)(2,1)} collective-permute-done((bf16[8192,256]{1,0:T(8,128)(2,1)}, bf16[8192,256]{1,0:T(8,128)(2,1)}, u32[]{:S(2)}, u32[]{:S(2)}) %collective-permute-start.12) | collective-permute-done | bytes 4194336 | tf_op jit(solution)/shard_map/ppermute | solution.py:487
  74.2 13.7 %mix.1 = bf16[512,5120]{1,0:T(8,128)(2,1)} custom-call(s32[4]{0:T(128)} %len_ref.9, s32[1]{0:T(128)} %bitcast.first_ref, bf16[1024,256]{1,0:T(8,128)(2,1)} %get-tuple-element.34.split_ref.split_hbm, bf16[512,512]{1,0:T(8,128)(2,1)} %gate.1.act_hbm, f32[1024,256]{1,0:T(8,128)} %part.1.before_hbm, bf16[8192,256]{1,0:T(8,128)(2,1)} %all-gather.2.cloned.1.call-done.fetched, ...), custom_call_target="tpu_custom_call" | custom-call | flops 8999999488 | bytes 25000000 | tf_op jit(solution)/shard_map/mix/pallas_call | solution.py:608
  87.9 88.7 %reduce-scatter.2.cloned.1.call-done = bf16[64,5120]{1,0:T(8,128)(2,1)} async-done(((bf16[512,5120]{1,0:T(8,128)(2,1)}), bf16[64,5120]{1,0:T(8,128)(2,1)}) %reduce-scatter.2.cloned.1.call-update) | async-done | bytes 655376 | tf_op jit(solution)/shard_map/reduce_scatter | solution.py:629
  (22 shorter events, 3.9 us)
Async XLA Ops:
  6.5 14.8 %copy-start = (bf16[512,1,256]{2,0,1:T(8,128)(2,1)S(1)}, bf16[512,1,256]{2,0,1:T(8,128)(2,1)}, u32[]{:S(2)}) copy-start(bf16[512,1,256]{2,0,1:T(8,128)(2,1)} %param.12) | copy-start | bytes 786436
  6.5 60.2 %all-gather.2.cloned.1.call-start = ((), (), s32[]{:S(2)}) async-start(), calls=%async_computation.1 | async-start | bytes 5242880 | tf_op jit(solution)/shard_map/all_gather | solution.py:537
  6.5 14.8 %collective-permute-start.2 = (bf16[512,256]{1,0:T(8,128)(2,1)}, bf16[512,256]{1,0:T(8,128)(2,1)S(1)}, u32[]{:S(2)}, u32[]{:S(2)}) collective-permute-start(bf16[512,256]{1,0:T(8,128)(2,1)} %bitcast.3), channel_id=1, source_target_pairs={{0,32},{8,136},{16,48},{24,152},{32,0},{40,168},{48,16},{56,184},{... | collective-permute-start | bytes 786440 | tf_op jit(solution)/shard_map/ppermute | solution.py:469
  12.2 9.2 %collective-permute-start.1 = (bf16[512,256]{1,0:T(8,128)(2,1)}, bf16[512,256]{1,0:T(8,128)(2,1)S(1)}, u32[]{:S(2)}, u32[]{:S(2)}) collective-permute-start(bf16[512,256]{1,0:T(8,128)(2,1)} %bitcast.4), channel_id=1, source_target_pairs={{0,48},{8,200},{16,0},{24,216},{32,16},{40,232},{48,32},{56,248},{... | collective-permute-start | bytes 786440 | tf_op jit(solution)/shard_map/ppermute | solution.py:469
  13.5 7.9 %collective-permute-start = (bf16[512,256]{1,0:T(8,128)(2,1)}, bf16[512,256]{1,0:T(8,128)(2,1)S(1)}, u32[]{:S(2)}, u32[]{:S(2)}) collective-permute-start(bf16[512,256]{1,0:T(8,128)(2,1)} %bitcast.5), channel_id=1, source_target_pairs={{0,16},{8,72},{16,32},{24,88},{32,48},{40,104},{48,0},{56,120},{64... | collective-permute-start | bytes 786440 | tf_op jit(solution)/shard_map/ppermute | solution.py:469
  21.3 5.9 %copy-start.1 = (bf16[272,256]{1,0:T(8,128)(2,1)S(1)}, bf16[272,256]{1,0:T(8,128)(2,1)}, u32[]{:S(2)}) copy-start(bf16[272,256]{1,0:T(8,128)(2,1)} %get-tuple-element.32) | copy-start | bytes 417796
  22.4 154.2 %reduce-scatter.2.cloned.1.call-start = ((), (), s32[]{:S(2)}) async-start(), calls=%async_computation.2 | async-start | bytes 5898240 | tf_op jit(solution)/shard_map/reduce_scatter | solution.py:629
  22.5 31.0 %collective-permute-start.10 = (bf16[2048,256]{1,0:T(8,128)(2,1)}, bf16[2048,256]{1,0:T(8,128)(2,1)}, u32[]{:S(2)}, u32[]{:S(2)}) collective-permute-start(bf16[2048,256]{1,0:T(8,128)(2,1)} %pad_maximum_fusion.line), channel_id=1, source_target_pairs={{0,8},{8,0},{16,24},{24,16},{32,40},{40,32},{48,56},{56,48},{64,72... | collective-permute-start | bytes 3145736 | tf_op jit(solution)/shard_map/ppermute | solution.py:487
  27.2 2.5 %collective-permute-start.3 = (bf16[272,256]{1,0:T(8,128)(2,1)S(1)}, bf16[272,256]{1,0:T(8,128)(2,1)}, u32[]{:S(2)}, u32[]{:S(2)}) collective-permute-start(bf16[272,256]{1,0:T(8,128)(2,1)S(1)} %copy-done.1), channel_id=1, source_target_pairs={{0,8},{8,0},{16,24},{24,16},{32,40},{40,32},{48,56},{56,48},{64,72... | collective-permute-start | bytes 417800 | tf_op jit(solution)/shard_map/ppermute | solution.py:487
  31.4 6.9 %collective-permute-start.6 = (bf16[272,256]{1,0:T(8,128)(2,1)}, bf16[272,256]{1,0:T(8,128)(2,1)}, u32[]{:S(2)}, u32[]{:S(2)}) collective-permute-start(bf16[272,256]{1,0:T(8,128)(2,1)} %shard_map.109.mine_ref), channel_id=1, source_target_pairs={{0,32},{8,40},{16,48},{24,56},{32,0},{40,8},{48,16},{56,24},{64,96... | collective-permute-start | bytes 417800 | tf_op jit(solution)/shard_map/ppermute | solution.py:469
  32.6 7.6 %collective-permute-start.5 = (bf16[272,256]{1,0:T(8,128)(2,1)}, bf16[272,256]{1,0:T(8,128)(2,1)}, u32[]{:S(2)}, u32[]{:S(2)}) collective-permute-start(bf16[272,256]{1,0:T(8,128)(2,1)} %shard_map.109.mine_ref), channel_id=1, source_target_pairs={{0,48},{8,56},{16,0},{24,8},{32,16},{40,24},{48,32},{56,40},{64,11... | collective-permute-start | bytes 417800 | tf_op jit(solution)/shard_map/ppermute | solution.py:469
  33.6 7.7 %collective-permute-start.4 = (bf16[272,256]{1,0:T(8,128)(2,1)}, bf16[272,256]{1,0:T(8,128)(2,1)}, u32[]{:S(2)}, u32[]{:S(2)}) collective-permute-start(bf16[272,256]{1,0:T(8,128)(2,1)} %shard_map.109.mine_ref), channel_id=1, source_target_pairs={{0,16},{8,24},{16,32},{24,40},{32,48},{40,56},{48,0},{56,8},{64,80... | collective-permute-start | bytes 417800 | tf_op jit(solution)/shard_map/ppermute | solution.py:469
  43.4 14.5 %collective-permute-start.9 = (bf16[272,256]{1,0:T(8,128)(2,1)}, bf16[272,256]{1,0:T(8,128)(2,1)}, u32[]{:S(2)}, u32[]{:S(2)}) collective-permute-start(bf16[272,256]{1,0:T(8,128)(2,1)} %get-tuple-element.40), channel_id=1, source_target_pairs={{0,64},{8,72},{16,80},{24,88},{32,96},{40,104},{48,112},{56,120},{... | collective-permute-start | bytes 417800 | tf_op jit(solution)/shard_map/ppermute | solution.py:469
  47.1 10.7 %collective-permute-start.8 = (bf16[272,256]{1,0:T(8,128)(2,1)}, bf16[272,256]{1,0:T(8,128)(2,1)}, u32[]{:S(2)}, u32[]{:S(2)}) collective-permute-start(bf16[272,256]{1,0:T(8,128)(2,1)} %get-tuple-element.40), channel_id=1, source_target_pairs={{0,128},{8,136},{16,144},{24,152},{32,160},{40,168},{48,176},{56,1... | collective-permute-start | bytes 417800 | tf_op jit(solution)/shard_map/ppermute | solution.py:469
  51.5 7.1 %collective-permute-start.7 = (bf16[272,256]{1,0:T(8,128)(2,1)}, bf16[272,256]{1,0:T(8,128)(2,1)}, u32[]{:S(2)}, u32[]{:S(2)}) collective-permute-start(bf16[272,256]{1,0:T(8,128)(2,1)} %get-tuple-element.40), channel_id=1, source_target_pairs={{0,192},{8,200},{16,208},{24,216},{32,224},{40,232},{48,240},{56,2... | collective-permute-start | bytes 417800 | tf_op jit(solution)/shard_map/ppermute | solution.py:469
  60.6 2.5 %collective-permute-start.11 = (bf16[256,256]{1,0:T(8,128)(2,1)}, bf16[256,256]{1,0:T(8,128)(2,1)}, u32[]{:S(2)}, u32[]{:S(2)}) collective-permute-start(bf16[256,256]{1,0:T(8,128)(2,1)} %get-tuple-element.47), channel_id=1, source_target_pairs={{0,8},{8,0},{16,24},{24,16},{32,40},{40,32},{48,56},{56,48},{64,72... | collective-permute-start | bytes 393224 | tf_op jit(solution)/shard_map/ppermute | solution.py:487
  66.7 7.5 %collective-permute-start.12 = (bf16[8192,256]{1,0:T(8,128)(2,1)}, bf16[8192,256]{1,0:T(8,128)(2,1)}, u32[]{:S(2)}, u32[]{:S(2)}) collective-permute-start(bf16[8192,256]{1,0:T(8,128)(2,1)} %all-gather.2.cloned.1.call-done.fetched), channel_id=1, source_target_pairs={{0,8},{8,0},{16,24},{24,16},{32,40},{40,32},{48,56},{56,48},{64,72... | collective-permute-start | bytes 12582920 | tf_op jit(solution)/shard_map/ppermute | solution.py:487
Sparse Core Ops, SparseCore 0:
  22.6 39.6 all-gather.1
  88.1 88.5 reduce-scatter.1

commit v11 on v10

--- a/solution.py
+++ b/solution.py
@@ -20,6 +20,7 @@
 LOG2E = 1.4426950408889634
 HIGH = lax.Precision.HIGHEST
 LIMIT = 64 * 2**20 - 2**16
+EARLY = 62 * 2**20
 HALF = HP // 2
 STATE_ROWS = SN + 16
 VMEM = pl.BlockSpec(memory_space=pltpu.VMEM)
@@ -147,10 +148,11 @@
     return later[0] + later[1] * earlier[0], earlier[1] * later[1]
 
 
-def chip_kernel(first_ref, mine_ref, other_ref, out_ref):
+def chip_kernel(first_ref, mine_ref, other_ref, out_ref, token_ref):
     core = (first_ref[0] // ROWS) % 2
     mine, other = load_run(mine_ref), load_run(other_ref)
     store_run(out_ref, *after(pick(core == 0, mine, other), pick(core == 0, other, mine)))
+    token_ref[...] = jnp.zeros_like(token_ref)
 
 
 def row_kernel(first_ref, mine_ref, below_ref, above_ref, across_ref, prefix_ref, total_ref):
@@ -338,7 +340,7 @@
         lax.fori_loop(0, self.plain + self.masked, one_chunk, 0)
 
 
-def own_line_kernel(len_ref, first_ref, q_ref, line, acc_ref, split_ref, kv_scr, ids, kinds, kv_sem):
+def own_line_kernel(len_ref, first_ref, q_ref, line, _, acc_ref, split_ref, kv_scr, ids, kinds, kv_sem):
     attention = Attention(len_ref, first_ref, line, None, split_ref, kv_scr, ids, kinds, kv_sem, near_only=True)
     attention.fetch((0,))
     for g in range(2):
@@ -487,13 +489,13 @@
     return lax.ppermute(block, "pack", [(i, i ^ 1) for i in range(32)])
 
 
-def call(kernel, shapes, ins, *args):
+def call(kernel, shapes, ins, *args, limit=LIMIT):
     return pl.pallas_call(
         kernel,
         out_shape=tuple(jax.ShapeDtypeStruct(shape, jnp.bfloat16) for shape in shapes),
         in_specs=[SMEM] + [VMEM] * ins,
         out_specs=(VMEM,) * len(shapes),
-        compiler_params=big(),
+        compiler_params=big(limit),
         cost_estimate=pl.CostEstimate(flops=10**6, bytes_accessed=10**6, transcendentals=0),
     )(*args)
 
@@ -527,19 +529,19 @@
         ),
         in_specs=[SMEM] * 4 + [VMEM] * 3,
         out_specs=(VMEM, VMEM, VMEM, VMEM),
-        compiler_params=big(62 * 2**20),
+        compiler_params=big(EARLY),
         cost_estimate=pl.CostEstimate(flops=10**9, bytes_accessed=4 * 10**6, transcendentals=10**6),
         name="ssd_local",
     )(lengths, decay_log, skip_gain, first, ssm_values, ssm_maps, step_size.T)
 
-    below, above, across = lax.optimization_barrier((below, above, across, fac))[:3]
+    run = (STATE_ROWS, HALF)
+    run_got = swapped(run_send)
+    chip, token = call(chip_kernel, [run, (16, 128)], 2, first, run_keep, run_got, limit=EARLY)
+
+    below, above, across, token = lax.optimization_barrier((below, above, across, token))
     line = jnp.concatenate([kv, below, above, across], axis=0)
     fetched = lax.all_gather(line, "pack", axis=0, tiled=True, axis_index_groups=lines())
     line_got = swapped(line)
-
-    run = (STATE_ROWS, HALF)
-    run_got = swapped(run_send)
-    (chip,) = call(chip_kernel, [run], 2, first, run_keep, run_got)
     chips = [moved(chip, along_y(d), along_y(d)) for d in (1, 3, 2)]
     chunks_scratch = [
         pltpu.VMEM((SLOTS * CHUNK, 2 * HD), jnp.bfloat16),
@@ -563,8 +565,7 @@
         )(lengths, first, *args)
         return out
 
-    line = lax.optimization_barrier((line, chip))[0]
-    acc, queries_split = attend(own_line_kernel, "own_line", (sums, split), 1, queries, line)
+    acc, queries_split = attend(own_line_kernel, "own_line", (sums, split), 1, queries, line, token)
     chips = lax.optimization_barrier((*chips, acc))[:3]
     prefix, total = call(row_kernel, [run, run], 4, first, chip, *chips)
     rows = [moved(total, along_x(d), along_x(d)) for d in (3, 2, 1)]

time: 183 us -> 188 us (1.027)
  starting transfers between devices: 27.8 us -> 32.1 us
    ppermute x4, starting transfers between devices: 6.37 us -> 10.2 us  [swapped(): return lax.ppermute(block, 'pack', [(i, i ^ 1) for i in range(32)])]
  transfers between devices with their start and end apart: 15 -> 15, of which waited for: 7 -> 8; matrix products, arithmetic and copies ran while one was open for 0% -> 0% of each run, Pallas kernels for 15% -> 15%
where the time goes in v11:
time: 188 us; the launch traced here: 187 us
  waiting for transfers between devices  98.6 us (52%)
  Pallas kernels  41 us (22%)
  starting transfers between devices  32.1 us (17%)
  between operations  13.5 us (7%)
    reduce_scatter x1, waiting for transfers between devices, local(): return lax.psum_scatter(terms, 'tp', scatter_dimension=0, tiled=True)  88.6 us
    ppermute x9, starting transfers between devices, moved(): return lax.ppermute(block, 'pack', pairs)  21.9 us
    pallas_call x1, Pallas kernels, local(): pl.pallas_call(mix_kernel, out_shape=jax.ShapeDtypeStruct((ROWS, DM), jnp...  13.7 us
    pallas_call x3, Pallas kernels, attend(): pl.pallas_call(kernel, out_shape=shapes, in_specs=[SMEM] * 2 + [VMEM] * v...  11.7 us
    ppermute x4, starting transfers between devices, swapped(): return lax.ppermute(block, 'pack', [(i, i ^ 1) for i in range(32)])  10.2 us
    ppermute x4, waiting for transfers between devices, swapped(): return lax.ppermute(block, 'pack', [(i, i ^ 1) for i in range(32)])  6.42 us
    pallas_call x1, Pallas kernels, local(): pl.pallas_call(ssd_kernel, out_shape=(jax.ShapeDtypeStruct((ROWS, HP), jn...  6.22 us
    pallas_call x3, Pallas kernels, call(): pl.pallas_call(kernel, out_shape=tuple((jax.ShapeDtypeStruct(shape, jnp.b...  5.87 us
  transfers between devices with their start and end apart: 15, of which 8 were waited for; matrix products, arithmetic and copies ran while one was open for 0% of the time, Pallas kernels for 15%

profile of v11, /device:TPU:1, one launch (start us, length us, event | category | flops | bytes accessed | tf_op | source)
XLA Modules:
  0.0 186.9 jit_solution(7344042158786239098)
XLA Ops:
  6.5 5.6 %collective-permute-start.2 = (bf16[512,256]{1,0:T(8,128)(2,1)}, bf16[512,256]{1,0:T(8,128)(2,1)S(1)}, u32[]{:S(2)}, u32[]{:S(2)}) collective-permute-start(bf16[512,256]{1,0:T(8,128)(2,1)} %bitcast.3), channel_id=1, source_target_pairs={{0,32},{8,136},{16,48},{24,152},{32,0},{40,168},{48,16},{56,184},{... | collective-permute-start | bytes 786440 | tf_op jit(solution)/shard_map/ppermute | solution.py:471
  12.2 1.3 collective-permute-start.1
  13.5 1.6 collective-permute-start
  15.1 6.2 %ssd_local.1 = (f32[512,512]{1,0:T(8,128)}, bf16[272,256]{1,0:T(8,128)(2,1)}, bf16[272,256]{1,0:T(8,128)(2,1)}, f32[512,8]{1,0:T(8,128)}) custom-call(s32[4]{0:T(128)} %len_ref.9, f32[8]{0:T(128)} %dl_ref.1, f32[8]{0:T(128)} %skip_ref.1, s32[1]{0:T(128)} %bitcast.first_ref, bf16[512,512]{1,0:T(8,128)(2,1)} %x_ref.1, bf16[512,512]{1,0:T(8,128)(2,1)} %read_ref.1, ...), custom_call_target="tpu_custom_call" | custom-call | flops 1000000000 | bytes 4000000 | tf_op jit(solution)/shard_map/ssd_local/pallas_call | solution.py:522
  21.3 4.0 %collective-permute-start.3 = (bf16[272,256]{1,0:T(8,128)(2,1)}, bf16[272,256]{1,0:T(8,128)(2,1)S(1)}, u32[]{:S(2)}, u32[]{:S(2)}) collective-permute-start(bf16[272,256]{1,0:T(8,128)(2,1)} %get-tuple-element.30), channel_id=1, source_target_pairs={{0,8},{8,0},{16,24},{24,16},{32,40},{40,32},{48,56},{56,48},{64,72... | collective-permute-start | bytes 417800 | tf_op jit(solution)/shard_map/ppermute | solution.py:489
  25.4 1.2 collective-permute-done.3.other_ref
  27.2 1.7 shard_map.109
  30.5 1.8 collective-permute-start.6
  33.8 4.1 %own_line.1 = (f32[1024,256]{1,0:T(8,128)}, bf16[1024,256]{1,0:T(8,128)(2,1)}) custom-call(s32[4]{0:T(128)} %len_ref.9, s32[1]{0:T(128)} %bitcast.first_ref, bf16[512,256]{1,0:T(8,128)(2,1)} %q_ref.1, bf16[2048,256]{1,0:T(8,128)(2,1)} %pad_maximum_fusion.line, bf16[16,128]{1,0:T(8,128)(2,1)} %get-tuple-element.35._), custom_call_target="tpu_custom_call" | custom-call | flops 3000000000 | bytes 5000000 | tf_op jit(solution)/shard_map/own_line/pallas_call | solution.py:556
  37.9 2.2 %collective-permute-done.5.above_ref = bf16[272,256]{1,0:T(8,128)(2,1)} collective-permute-done((bf16[272,256]{1,0:T(8,128)(2,1)}, bf16[272,256]{1,0:T(8,128)(2,1)}, u32[]{:S(2)}, u32[]{:S(2)}) %collective-permute-start.5) | collective-permute-done | bytes 139296 | tf_op jit(solution)/shard_map/ppermute | solution.py:471
  40.4 2.0 %shard_map.110 = (bf16[272,256]{1,0:T(8,128)(2,1)}, bf16[272,256]{1,0:T(8,128)(2,1)}) custom-call(s32[1]{0:T(128)} %bitcast.first_ref, bf16[272,256]{1,0:T(8,128)(2,1)} %get-tuple-element.39.mine_ref, bf16[272,256]{1,0:T(8,128)(2,1)} %collective-permute-done.4.below_ref, bf16[272,256]{1,0:T(8,128)(2,1)} %collective-permute-done.5.above_ref, ...), custom_call_target="tpu_custom_call" | custom-call | flops 1000000 | bytes 1000000 | tf_op jit(solution)/shard_map/pallas_call | solution.py:493
  42.4 3.8 %collective-permute-start.9 = (bf16[272,256]{1,0:T(8,128)(2,1)}, bf16[272,256]{1,0:T(8,128)(2,1)}, u32[]{:S(2)}, u32[]{:S(2)}) collective-permute-start(bf16[272,256]{1,0:T(8,128)(2,1)} %get-tuple-element.44), channel_id=1, source_target_pairs={{0,64},{8,72},{16,80},{24,88},{32,96},{40,104},{48,112},{56,120},{... | collective-permute-start | bytes 417800 | tf_op jit(solution)/shard_map/ppermute | solution.py:471
  46.2 4.4 %collective-permute-start.8 = (bf16[272,256]{1,0:T(8,128)(2,1)}, bf16[272,256]{1,0:T(8,128)(2,1)}, u32[]{:S(2)}, u32[]{:S(2)}) collective-permute-start(bf16[272,256]{1,0:T(8,128)(2,1)} %get-tuple-element.44), channel_id=1, source_target_pairs={{0,128},{8,136},{16,144},{24,152},{32,160},{40,168},{48,176},{56,1... | collective-permute-start | bytes 417800 | tf_op jit(solution)/shard_map/ppermute | solution.py:471
  50.6 1.9 %collective-permute-start.7 = (bf16[272,256]{1,0:T(8,128)(2,1)}, bf16[272,256]{1,0:T(8,128)(2,1)}, u32[]{:S(2)}, u32[]{:S(2)}) collective-permute-start(bf16[272,256]{1,0:T(8,128)(2,1)} %get-tuple-element.44), channel_id=1, source_target_pairs={{0,192},{8,200},{16,208},{24,216},{32,224},{40,232},{48,240},{56,2... | collective-permute-start | bytes 417800 | tf_op jit(solution)/shard_map/ppermute | solution.py:471
  52.5 4.3 %other_line.1.before_hbm = f32[1024,256]{1,0:T(8,128)} custom-call(s32[4]{0:T(128)} %len_ref.9, s32[1]{0:T(128)} %bitcast.first_ref, bf16[1024,256]{1,0:T(8,128)(2,1)} %get-tuple-element.36.split_ref.split_hbm, f32[1024,256]{1,0:T(8,128)} %get-tuple-element.40.before_ref, bf16[2048,256]{1,0:T(8,128)(2,1)} %collective-permute-done.10.line_got), custom_call_target="tpu_custom_call" | custom-call | flops 3000000000 | bytes 5000000 | tf_op jit(solution)/shard_map/other_line/pallas_call | solution.py:556
  57.6 2.1 %shard_map.111 = (bf16[256,256]{1,0:T(8,128)(2,1)}, bf16[256,256]{1,0:T(8,128)(2,1)}) custom-call(s32[1]{0:T(128)} %bitcast.first_ref, bf16[272,256]{1,0:T(8,128)(2,1)} %collective-permute-done.7.row3_ref, bf16[272,256]{1,0:T(8,128)(2,1)} %collective-permute-done.8.row2_ref, bf16[272,256]{1,0:T(8,128)(2,1)} %collective-permute-done.9.row1_ref, ...), custom_call_target="tpu_custom_call" | custom-call | flops 1000000 | bytes 1000000 | tf_op jit(solution)/shard_map/pallas_call | solution.py:493
  59.7 1.3 collective-permute-start.11
  61.0 1.3 collective-permute-done.11.got_ref
  62.3 3.5 %gate.1.act_hbm = bf16[512,512]{1,0:T(8,128)(2,1)} custom-call(s32[1]{0:T(128)} %bitcast.first_ref, f32[512,512]{1,0:T(8,128)} %get-tuple-element.37.y_ref, bf16[512,512]{1,0:T(8,128)(2,1)} %z_ref.1, bf16[512,512]{1,0:T(8,128)(2,1)} %read_ref.1, f32[512,8]{1,0:T(8,128)} %get-tuple-element.38.fac_ref, bf16[256,256]{1,0:T(8,128)(2,1)} %get-tuple-element.50.keep_ref, ...), custom_call_target="tpu_custom_call" | custom-call | flops 100000000 | bytes 3000000 | tf_op jit(solution)/shard_map/gate/pallas_call | solution.py:577
  66.1 4.5 %collective-permute-start.12 = (bf16[8192,256]{1,0:T(8,128)(2,1)}, bf16[8192,256]{1,0:T(8,128)(2,1)}, u32[]{:S(2)}, u32[]{:S(2)}) collective-permute-start(bf16[8192,256]{1,0:T(8,128)(2,1)} %all-gather.2.cloned.1.call-done.fetched), channel_id=1, source_target_pairs={{0,8},{8,0},{16,24},{24,16},{32,40},{40,32},{48,56},{56,48},{64,72... | collective-permute-start | bytes 12582920 | tf_op jit(solution)/shard_map/ppermute | solution.py:489
  70.6 3.2 %part.1.before_hbm = f32[1024,256]{1,0:T(8,128)} custom-call(s32[4]{0:T(128)} %len_ref.9, s32[1]{0:T(128)} %bitcast.first_ref, bf16[1024,256]{1,0:T(8,128)(2,1)} %get-tuple-element.36.split_ref.split_hbm, f32[1024,256]{1,0:T(8,128)} %other_line.1.before_hbm, bf16[8192,256]{1,0:T(8,128)(2,1)} %all-gather.2.cloned.1.call-done.fetched), custom_call_target="tpu_custom_call" | custom-call | flops 3000000000 | bytes 5000000 | tf_op jit(solution)/shard_map/part/pallas_call | solution.py:556
  73.9 3.9 %collective-permute-done.12.other = bf16[8192,256]{1,0:T(8,128)(2,1)} collective-permute-done((bf16[8192,256]{1,0:T(8,128)(2,1)}, bf16[8192,256]{1,0:T(8,128)(2,1)}, u32[]{:S(2)}, u32[]{:S(2)}) %collective-permute-start.12) | collective-permute-done | bytes 4194336 | tf_op jit(solution)/shard_map/ppermute | solution.py:489
  77.7 13.7 %mix.1 = bf16[512,5120]{1,0:T(8,128)(2,1)} custom-call(s32[4]{0:T(128)} %len_ref.9, s32[1]{0:T(128)} %bitcast.first_ref, bf16[1024,256]{1,0:T(8,128)(2,1)} %get-tuple-element.36.split_ref.split_hbm, bf16[512,512]{1,0:T(8,128)(2,1)} %gate.1.act_hbm, f32[1024,256]{1,0:T(8,128)} %part.1.before_hbm, bf16[8192,256]{1,0:T(8,128)(2,1)} %all-gather.2.cloned.1.call-done.fetched, ...), custom_call_target="tpu_custom_call" | custom-call | flops 8999999488 | bytes 25000000 | tf_op jit(solution)/shard_map/mix/pallas_call | solution.py:609
  91.5 88.6 %reduce-scatter.2.cloned.1.call-done = bf16[64,5120]{1,0:T(8,128)(2,1)} async-done(((bf16[512,5120]{1,0:T(8,128)(2,1)}), bf16[64,5120]{1,0:T(8,128)(2,1)}) %reduce-scatter.2.cloned.1.call-update) | async-done | bytes 655376 | tf_op jit(solution)/shard_map/reduce_scatter | solution.py:630
  (22 shorter events, 5.0 us)
Async XLA Ops:
  6.5 22.4 %copy-start.1 = (bf16[512,1,256]{2,0,1:T(8,128)(2,1)S(1)}, bf16[512,1,256]{2,0,1:T(8,128)(2,1)}, u32[]{:S(2)}) copy-start(bf16[512,1,256]{2,0,1:T(8,128)(2,1)} %param.12) | copy-start | bytes 786436
  6.5 59.6 %all-gather.2.cloned.1.call-start = ((), (), s32[]{:S(2)}) async-start(), calls=%async_computation.1 | async-start | bytes 5242880 | tf_op jit(solution)/shard_map/all_gather | solution.py:543
  6.5 22.4 %collective-permute-start.2 = (bf16[512,256]{1,0:T(8,128)(2,1)}, bf16[512,256]{1,0:T(8,128)(2,1)S(1)}, u32[]{:S(2)}, u32[]{:S(2)}) collective-permute-start(bf16[512,256]{1,0:T(8,128)(2,1)} %bitcast.3), channel_id=1, source_target_pairs={{0,32},{8,136},{16,48},{24,152},{32,0},{40,168},{48,16},{56,184},{... | collective-permute-start | bytes 786440 | tf_op jit(solution)/shard_map/ppermute | solution.py:471
  12.2 16.8 %collective-permute-start.1 = (bf16[512,256]{1,0:T(8,128)(2,1)}, bf16[512,256]{1,0:T(8,128)(2,1)S(1)}, u32[]{:S(2)}, u32[]{:S(2)}) collective-permute-start(bf16[512,256]{1,0:T(8,128)(2,1)} %bitcast.4), channel_id=1, source_target_pairs={{0,48},{8,200},{16,0},{24,216},{32,16},{40,232},{48,32},{56,248},{... | collective-permute-start | bytes 786440 | tf_op jit(solution)/shard_map/ppermute | solution.py:471
  13.5 15.5 %collective-permute-start = (bf16[512,256]{1,0:T(8,128)(2,1)}, bf16[512,256]{1,0:T(8,128)(2,1)S(1)}, u32[]{:S(2)}, u32[]{:S(2)}) collective-permute-start(bf16[512,256]{1,0:T(8,128)(2,1)} %bitcast.5), channel_id=1, source_target_pairs={{0,16},{8,72},{16,32},{24,88},{32,48},{40,104},{48,0},{56,120},{64... | collective-permute-start | bytes 786440 | tf_op jit(solution)/shard_map/ppermute | solution.py:471
  21.3 5.3 %collective-permute-start.3 = (bf16[272,256]{1,0:T(8,128)(2,1)}, bf16[272,256]{1,0:T(8,128)(2,1)S(1)}, u32[]{:S(2)}, u32[]{:S(2)}) collective-permute-start(bf16[272,256]{1,0:T(8,128)(2,1)} %get-tuple-element.30), channel_id=1, source_target_pairs={{0,8},{8,0},{16,24},{24,16},{32,40},{40,32},{48,56},{56,48},{64,72... | collective-permute-start | bytes 417800 | tf_op jit(solution)/shard_map/ppermute | solution.py:489
  26.6 0.7 copy-start
  30.0 150.0 %reduce-scatter.2.cloned.1.call-start = ((), (), s32[]{:S(2)}) async-start(), calls=%async_computation.2 | async-start | bytes 5898240 | tf_op jit(solution)/shard_map/reduce_scatter | solution.py:630
  30.1 22.4 %collective-permute-start.10 = (bf16[2048,256]{1,0:T(8,128)(2,1)}, bf16[2048,256]{1,0:T(8,128)(2,1)}, u32[]{:S(2)}, u32[]{:S(2)}) collective-permute-start(bf16[2048,256]{1,0:T(8,128)(2,1)} %pad_maximum_fusion.line), channel_id=1, source_target_pairs={{0,8},{8,0},{16,24},{24,16},{32,40},{40,32},{48,56},{56,48},{64,72... | collective-permute-start | bytes 3145736 | tf_op jit(solution)/shard_map/ppermute | solution.py:489
  30.5 7.4 %collective-permute-start.6 = (bf16[272,256]{1,0:T(8,128)(2,1)}, bf16[272,256]{1,0:T(8,128)(2,1)}, u32[]{:S(2)}, u32[]{:S(2)}) collective-permute-start(bf16[272,256]{1,0:T(8,128)(2,1)} %get-tuple-element.39.mine_ref), channel_id=1, source_target_pairs={{0,32},{8,40},{16,48},{24,56},{32,0},{40,8},{48,16},{56,24},{64,96... | collective-permute-start | bytes 417800 | tf_op jit(solution)/shard_map/ppermute | solution.py:471
  32.3 7.8 %collective-permute-start.5 = (bf16[272,256]{1,0:T(8,128)(2,1)}, bf16[272,256]{1,0:T(8,128)(2,1)}, u32[]{:S(2)}, u32[]{:S(2)}) collective-permute-start(bf16[272,256]{1,0:T(8,128)(2,1)} %get-tuple-element.39.mine_ref), channel_id=1, source_target_pairs={{0,48},{8,56},{16,0},{24,8},{32,16},{40,24},{48,32},{56,40},{64,11... | collective-permute-start | bytes 417800 | tf_op jit(solution)/shard_map/ppermute | solution.py:471
  33.3 7.1 %collective-permute-start.4 = (bf16[272,256]{1,0:T(8,128)(2,1)}, bf16[272,256]{1,0:T(8,128)(2,1)}, u32[]{:S(2)}, u32[]{:S(2)}) collective-permute-start(bf16[272,256]{1,0:T(8,128)(2,1)} %get-tuple-element.39.mine_ref), channel_id=1, source_target_pairs={{0,16},{8,24},{16,32},{24,40},{32,48},{40,56},{48,0},{56,8},{64,80... | collective-permute-start | bytes 417800 | tf_op jit(solution)/shard_map/ppermute | solution.py:471
  42.4 14.4 %collective-permute-start.9 = (bf16[272,256]{1,0:T(8,128)(2,1)}, bf16[272,256]{1,0:T(8,128)(2,1)}, u32[]{:S(2)}, u32[]{:S(2)}) collective-permute-start(bf16[272,256]{1,0:T(8,128)(2,1)} %get-tuple-element.44), channel_id=1, source_target_pairs={{0,64},{8,72},{16,80},{24,88},{32,96},{40,104},{48,112},{56,120},{... | collective-permute-start | bytes 417800 | tf_op jit(solution)/shard_map/ppermute | solution.py:471
  46.2 10.7 %collective-permute-start.8 = (bf16[272,256]{1,0:T(8,128)(2,1)}, bf16[272,256]{1,0:T(8,128)(2,1)}, u32[]{:S(2)}, u32[]{:S(2)}) collective-permute-start(bf16[272,256]{1,0:T(8,128)(2,1)} %get-tuple-element.44), channel_id=1, source_target_pairs={{0,128},{8,136},{16,144},{24,152},{32,160},{40,168},{48,176},{56,1... | collective-permute-start | bytes 417800 | tf_op jit(solution)/shard_map/ppermute | solution.py:471
  50.6 7.0 %collective-permute-start.7 = (bf16[272,256]{1,0:T(8,128)(2,1)}, bf16[272,256]{1,0:T(8,128)(2,1)}, u32[]{:S(2)}, u32[]{:S(2)}) collective-permute-start(bf16[272,256]{1,0:T(8,128)(2,1)} %get-tuple-element.44), channel_id=1, source_target_pairs={{0,192},{8,200},{16,208},{24,216},{32,224},{40,232},{48,240},{56,2... | collective-permute-start | bytes 417800 | tf_op jit(solution)/shard_map/ppermute | solution.py:471
  59.7 2.6 %collective-permute-start.11 = (bf16[256,256]{1,0:T(8,128)(2,1)}, bf16[256,256]{1,0:T(8,128)(2,1)}, u32[]{:S(2)}, u32[]{:S(2)}) collective-permute-start(bf16[256,256]{1,0:T(8,128)(2,1)} %get-tuple-element.51), channel_id=1, source_target_pairs={{0,8},{8,0},{16,24},{24,16},{32,40},{40,32},{48,56},{56,48},{64,72... | collective-permute-start | bytes 393224 | tf_op jit(solution)/shard_map/ppermute | solution.py:489
  66.1 11.6 %collective-permute-start.12 = (bf16[8192,256]{1,0:T(8,128)(2,1)}, bf16[8192,256]{1,0:T(8,128)(2,1)}, u32[]{:S(2)}, u32[]{:S(2)}) collective-permute-start(bf16[8192,256]{1,0:T(8,128)(2,1)} %all-gather.2.cloned.1.call-done.fetched), channel_id=1, source_target_pairs={{0,8},{8,0},{16,24},{24,16},{32,40},{40,32},{48,56},{56,48},{64,72... | collective-permute-start | bytes 12582920 | tf_op jit(solution)/shard_map/ppermute | solution.py:489
Sparse Core Ops, SparseCore 0:
  30.2 35.9 all-gather.1
  91.6 88.4 reduce-scatter.1

commit v12 on v10

--- a/solution.py
+++ b/solution.py
@@ -532,13 +532,11 @@
         name="ssd_local",
     )(lengths, decay_log, skip_gain, first, ssm_values, ssm_maps, step_size.T)
 
-    below, above, across = lax.optimization_barrier((below, above, across, fac))[:3]
+    run = (STATE_ROWS, HALF)
+    run_got = swapped(run_send)
+    below, above, across, run_got = lax.optimization_barrier((below, above, across, run_got))
     line = jnp.concatenate([kv, below, above, across], axis=0)
     fetched = lax.all_gather(line, "pack", axis=0, tiled=True, axis_index_groups=lines())
-    line_got = swapped(line)
-
-    run = (STATE_ROWS, HALF)
-    run_got = swapped(run_send)
     (chip,) = call(chip_kernel, [run], 2, first, run_keep, run_got)
     chips = [moved(chip, along_y(d), along_y(d)) for d in (1, 3, 2)]
     chunks_scratch = [
@@ -564,6 +562,7 @@
         return out
 
     line = lax.optimization_barrier((line, chip))[0]
+    line_got = swapped(line)
     acc, queries_split = attend(own_line_kernel, "own_line", (sums, split), 1, queries, line)
     chips = lax.optimization_barrier((*chips, acc))[:3]
     prefix, total = call(row_kernel, [run, run], 4, first, chip, *chips)

time: 183 us -> 182 us (level)
  waiting for transfers between devices: 100 us -> 94.7 us
  starting transfers between devices: 27.8 us -> 30.8 us
    reduce_scatter x1, waiting for transfers between devices: 88.7 us -> 85 us  [local(): return lax.psum_scatter(terms, 'tp', scatter_dimension=0, tiled=True)]
    ppermute x4, starting transfers between devices: 6.37 us -> 8.86 us  [swapped(): return lax.ppermute(block, 'pack', [(i, i ^ 1) for i in range(32)])]
where the time goes in v12:
time: 182 us; the launch traced here: 181 us
  waiting for transfers between devices  94.7 us (52%)
  Pallas kernels  41 us (23%)
  starting transfers between devices  30.8 us (17%)
  between operations  13.5 us (7%)
    reduce_scatter x1, waiting for transfers between devices, local(): return lax.psum_scatter(terms, 'tp', scatter_dimension=0, tiled=True)  85 us
    ppermute x9, starting transfers between devices, moved(): return lax.ppermute(block, 'pack', pairs)  21.9 us
    pallas_call x1, Pallas kernels, local(): pl.pallas_call(mix_kernel, out_shape=jax.ShapeDtypeStruct((ROWS, DM), jnp...  13.7 us
    pallas_call x3, Pallas kernels, attend(): pl.pallas_call(kernel, out_shape=shapes, in_specs=[SMEM] * 2 + [VMEM] * v...  11.7 us
    ppermute x4, starting transfers between devices, swapped(): return lax.ppermute(block, 'pack', [(i, i ^ 1) for i in range(32)])  8.86 us
    ppermute x4, waiting for transfers between devices, swapped(): return lax.ppermute(block, 'pack', [(i, i ^ 1) for i in range(32)])  6.56 us
    pallas_call x1, Pallas kernels, local(): pl.pallas_call(ssd_kernel, out_shape=(jax.ShapeDtypeStruct((ROWS, HP), jn...  6.22 us
    pallas_call x3, Pallas kernels, call(): pl.pallas_call(kernel, out_shape=tuple((jax.ShapeDtypeStruct(shape, jnp.b...  5.86 us
  transfers between devices with their start and end apart: 15, of which 7 were waited for; matrix products, arithmetic and copies ran while one was open for 0% of the time, Pallas kernels for 15%

profile of v12, /device:TPU:1, one launch (start us, length us, event | category | flops | bytes accessed | tf_op | source)
XLA Modules:
  0.0 181.1 jit_solution(11410294811078773648)
XLA Ops:
  6.5 5.6 %collective-permute-start.2 = (bf16[512,256]{1,0:T(8,128)(2,1)}, bf16[512,256]{1,0:T(8,128)(2,1)S(1)}, u32[]{:S(2)}, u32[]{:S(2)}) collective-permute-start(bf16[512,256]{1,0:T(8,128)(2,1)} %bitcast.3), channel_id=1, source_target_pairs={{0,32},{8,136},{16,48},{24,152},{32,0},{40,168},{48,16},{56,184},{... | collective-permute-start | bytes 786440 | tf_op jit(solution)/shard_map/ppermute | solution.py:469
  12.2 1.3 collective-permute-start.1
  13.5 1.6 collective-permute-start
  15.1 6.2 %ssd_local.1 = (f32[512,512]{1,0:T(8,128)}, bf16[272,256]{1,0:T(8,128)(2,1)}, bf16[272,256]{1,0:T(8,128)(2,1)}, f32[512,8]{1,0:T(8,128)}) custom-call(s32[4]{0:T(128)} %len_ref.9, f32[8]{0:T(128)} %dl_ref.1, f32[8]{0:T(128)} %skip_ref.1, s32[1]{0:T(128)} %bitcast.first_ref, bf16[512,512]{1,0:T(8,128)(2,1)} %x_ref.1, bf16[512,512]{1,0:T(8,128)(2,1)} %read_ref.1, ...), custom_call_target="tpu_custom_call" | custom-call | flops 1000000000 | bytes 4000000 | tf_op jit(solution)/shard_map/ssd_local/pallas_call | solution.py:520
  21.3 4.0 %collective-permute-start.3 = (bf16[272,256]{1,0:T(8,128)(2,1)}, bf16[272,256]{1,0:T(8,128)(2,1)}, u32[]{:S(2)}, u32[]{:S(2)}) collective-permute-start(bf16[272,256]{1,0:T(8,128)(2,1)} %get-tuple-element.28), channel_id=1, source_target_pairs={{0,8},{8,0},{16,24},{24,16},{32,40},{40,32},{48,56},{56,48},{64,72... | collective-permute-start | bytes 417800 | tf_op jit(solution)/shard_map/ppermute | solution.py:487
  25.4 1.3 collective-permute-done.3.other_ref
  27.9 1.7 shard_map.109.mine_ref
  29.9 1.8 collective-permute-start.6
  33.2 4.1 %own_line.1 = (f32[1024,256]{1,0:T(8,128)}, bf16[1024,256]{1,0:T(8,128)(2,1)}) custom-call(s32[4]{0:T(128)} %len_ref.9, s32[1]{0:T(128)} %bitcast.first_ref, bf16[512,256]{1,0:T(8,128)(2,1)} %q_ref.1, bf16[2048,256]{1,0:T(8,128)(2,1)} %pad_maximum_fusion.line), custom_call_target="tpu_custom_call" | custom-call | flops 3000000000 | bytes 5000000 | tf_op jit(solution)/shard_map/own_line/pallas_call | solution.py:552
  37.3 2.2 %collective-permute-done.5.above_ref = bf16[272,256]{1,0:T(8,128)(2,1)} collective-permute-done((bf16[272,256]{1,0:T(8,128)(2,1)}, bf16[272,256]{1,0:T(8,128)(2,1)}, u32[]{:S(2)}, u32[]{:S(2)}) %collective-permute-start.5) | collective-permute-done | bytes 139296 | tf_op jit(solution)/shard_map/ppermute | solution.py:469
  39.8 2.0 %shard_map.110 = (bf16[272,256]{1,0:T(8,128)(2,1)}, bf16[272,256]{1,0:T(8,128)(2,1)}) custom-call(s32[1]{0:T(128)} %bitcast.first_ref, bf16[272,256]{1,0:T(8,128)(2,1)} %shard_map.109.mine_ref, bf16[272,256]{1,0:T(8,128)(2,1)} %collective-permute-done.4.below_ref, bf16[272,256]{1,0:T(8,128)(2,1)} %collective-permute-done.5.above_ref, ...), custom_call_target="tpu_custom_call" | custom-call | flops 1000000 | bytes 1000000 | tf_op jit(solution)/shard_map/pallas_call | solution.py:491
  41.8 3.8 %collective-permute-start.9 = (bf16[272,256]{1,0:T(8,128)(2,1)}, bf16[272,256]{1,0:T(8,128)(2,1)}, u32[]{:S(2)}, u32[]{:S(2)}) collective-permute-start(bf16[272,256]{1,0:T(8,128)(2,1)} %get-tuple-element.42), channel_id=1, source_target_pairs={{0,64},{8,72},{16,80},{24,88},{32,96},{40,104},{48,112},{56,120},{... | collective-permute-start | bytes 417800 | tf_op jit(solution)/shard_map/ppermute | solution.py:469
  45.6 4.4 %collective-permute-start.8 = (bf16[272,256]{1,0:T(8,128)(2,1)}, bf16[272,256]{1,0:T(8,128)(2,1)}, u32[]{:S(2)}, u32[]{:S(2)}) collective-permute-start(bf16[272,256]{1,0:T(8,128)(2,1)} %get-tuple-element.42), channel_id=1, source_target_pairs={{0,128},{8,136},{16,144},{24,152},{32,160},{40,168},{48,176},{56,1... | collective-permute-start | bytes 417800 | tf_op jit(solution)/shard_map/ppermute | solution.py:469
  50.0 2.0 %collective-permute-start.7 = (bf16[272,256]{1,0:T(8,128)(2,1)}, bf16[272,256]{1,0:T(8,128)(2,1)}, u32[]{:S(2)}, u32[]{:S(2)}) collective-permute-start(bf16[272,256]{1,0:T(8,128)(2,1)} %get-tuple-element.42), channel_id=1, source_target_pairs={{0,192},{8,200},{16,208},{24,216},{32,224},{40,232},{48,240},{56,2... | collective-permute-start | bytes 417800 | tf_op jit(solution)/shard_map/ppermute | solution.py:469
  51.9 4.3 %other_line.1.before_hbm = f32[1024,256]{1,0:T(8,128)} custom-call(s32[4]{0:T(128)} %len_ref.9, s32[1]{0:T(128)} %bitcast.first_ref, bf16[1024,256]{1,0:T(8,128)(2,1)} %get-tuple-element.35.split_ref.split_hbm, f32[1024,256]{1,0:T(8,128)} %get-tuple-element.38.before_ref, bf16[2048,256]{1,0:T(8,128)(2,1)} %collective-permute-done.10.line_got), custom_call_target="tpu_custom_call" | custom-call | flops 3000000000 | bytes 5000000 | tf_op jit(solution)/shard_map/other_line/pallas_call | solution.py:552
  57.0 2.1 %shard_map.111 = (bf16[256,256]{1,0:T(8,128)(2,1)}, bf16[256,256]{1,0:T(8,128)(2,1)}) custom-call(s32[1]{0:T(128)} %bitcast.first_ref, bf16[272,256]{1,0:T(8,128)(2,1)} %collective-permute-done.7.row3_ref, bf16[272,256]{1,0:T(8,128)(2,1)} %collective-permute-done.8.row2_ref, bf16[272,256]{1,0:T(8,128)(2,1)} %collective-permute-done.9.row1_ref, ...), custom_call_target="tpu_custom_call" | custom-call | flops 1000000 | bytes 1000000 | tf_op jit(solution)/shard_map/pallas_call | solution.py:491
  59.1 1.3 collective-permute-start.11
  60.4 1.3 collective-permute-done.11.got_ref
  61.8 3.5 %gate.1.act_hbm = bf16[512,512]{1,0:T(8,128)(2,1)} custom-call(s32[1]{0:T(128)} %bitcast.first_ref, f32[512,512]{1,0:T(8,128)} %get-tuple-element.36.y_ref, bf16[512,512]{1,0:T(8,128)(2,1)} %z_ref.1, bf16[512,512]{1,0:T(8,128)(2,1)} %read_ref.1, f32[512,8]{1,0:T(8,128)} %get-tuple-element.37.fac_ref, bf16[256,256]{1,0:T(8,128)(2,1)} %get-tuple-element.48.keep_ref, ...), custom_call_target="tpu_custom_call" | custom-call | flops 100000000 | bytes 3000000 | tf_op jit(solution)/shard_map/gate/pallas_call | solution.py:575
  65.3 3.1 %collective-permute-start.12 = (bf16[8192,256]{1,0:T(8,128)(2,1)}, bf16[8192,256]{1,0:T(8,128)(2,1)}, u32[]{:S(2)}, u32[]{:S(2)}) collective-permute-start(bf16[8192,256]{1,0:T(8,128)(2,1)} %all-gather.2.cloned.1.call-done.fetched), channel_id=1, source_target_pairs={{0,8},{8,0},{16,24},{24,16},{32,40},{40,32},{48,56},{56,48},{64,72... | collective-permute-start | bytes 12582920 | tf_op jit(solution)/shard_map/ppermute | solution.py:487
  68.4 3.2 %part.1.before_hbm = f32[1024,256]{1,0:T(8,128)} custom-call(s32[4]{0:T(128)} %len_ref.9, s32[1]{0:T(128)} %bitcast.first_ref, bf16[1024,256]{1,0:T(8,128)(2,1)} %get-tuple-element.35.split_ref.split_hbm, f32[1024,256]{1,0:T(8,128)} %other_line.1.before_hbm, bf16[8192,256]{1,0:T(8,128)(2,1)} %all-gather.2.cloned.1.call-done.fetched), custom_call_target="tpu_custom_call" | custom-call | flops 3000000000 | bytes 5000000 | tf_op jit(solution)/shard_map/part/pallas_call | solution.py:552
  71.6 3.9 %collective-permute-done.12.other = bf16[8192,256]{1,0:T(8,128)(2,1)} collective-permute-done((bf16[8192,256]{1,0:T(8,128)(2,1)}, bf16[8192,256]{1,0:T(8,128)(2,1)}, u32[]{:S(2)}, u32[]{:S(2)}) %collective-permute-start.12) | collective-permute-done | bytes 4194336 | tf_op jit(solution)/shard_map/ppermute | solution.py:487
  75.5 13.7 %mix.1 = bf16[512,5120]{1,0:T(8,128)(2,1)} custom-call(s32[4]{0:T(128)} %len_ref.9, s32[1]{0:T(128)} %bitcast.first_ref, bf16[1024,256]{1,0:T(8,128)(2,1)} %get-tuple-element.35.split_ref.split_hbm, bf16[512,512]{1,0:T(8,128)(2,1)} %gate.1.act_hbm, f32[1024,256]{1,0:T(8,128)} %part.1.before_hbm, bf16[8192,256]{1,0:T(8,128)(2,1)} %all-gather.2.cloned.1.call-done.fetched, ...), custom_call_target="tpu_custom_call" | custom-call | flops 8999999488 | bytes 25000000 | tf_op jit(solution)/shard_map/mix/pallas_call | solution.py:607
  89.3 85.0 %reduce-scatter.2.cloned.1.call-done = bf16[64,5120]{1,0:T(8,128)(2,1)} async-done(((bf16[512,5120]{1,0:T(8,128)(2,1)}), bf16[64,5120]{1,0:T(8,128)(2,1)}) %reduce-scatter.2.cloned.1.call-update) | async-done | bytes 655376 | tf_op jit(solution)/shard_map/reduce_scatter | solution.py:628
  (20 shorter events, 4.0 us)
Async XLA Ops:
  6.5 20.2 %copy-start = (bf16[512,1,256]{2,0,1:T(8,128)(2,1)S(1)}, bf16[512,1,256]{2,0,1:T(8,128)(2,1)}, u32[]{:S(2)}) copy-start(bf16[512,1,256]{2,0,1:T(8,128)(2,1)} %param.12) | copy-start | bytes 786436
  6.5 58.7 %all-gather.2.cloned.1.call-start = ((), (), s32[]{:S(2)}) async-start(), calls=%async_computation.1 | async-start | bytes 5242880 | tf_op jit(solution)/shard_map/all_gather | solution.py:539
  6.5 20.2 %collective-permute-start.2 = (bf16[512,256]{1,0:T(8,128)(2,1)}, bf16[512,256]{1,0:T(8,128)(2,1)S(1)}, u32[]{:S(2)}, u32[]{:S(2)}) collective-permute-start(bf16[512,256]{1,0:T(8,128)(2,1)} %bitcast.3), channel_id=1, source_target_pairs={{0,32},{8,136},{16,48},{24,152},{32,0},{40,168},{48,16},{56,184},{... | collective-permute-start | bytes 786440 | tf_op jit(solution)/shard_map/ppermute | solution.py:469
  12.2 14.5 %collective-permute-start.1 = (bf16[512,256]{1,0:T(8,128)(2,1)}, bf16[512,256]{1,0:T(8,128)(2,1)S(1)}, u32[]{:S(2)}, u32[]{:S(2)}) collective-permute-start(bf16[512,256]{1,0:T(8,128)(2,1)} %bitcast.4), channel_id=1, source_target_pairs={{0,48},{8,200},{16,0},{24,216},{32,16},{40,232},{48,32},{56,248},{... | collective-permute-start | bytes 786440 | tf_op jit(solution)/shard_map/ppermute | solution.py:469
  13.5 13.2 %collective-permute-start = (bf16[512,256]{1,0:T(8,128)(2,1)}, bf16[512,256]{1,0:T(8,128)(2,1)S(1)}, u32[]{:S(2)}, u32[]{:S(2)}) collective-permute-start(bf16[512,256]{1,0:T(8,128)(2,1)} %bitcast.5), channel_id=1, source_target_pairs={{0,16},{8,72},{16,32},{24,88},{32,48},{40,104},{48,0},{56,120},{64... | collective-permute-start | bytes 786440 | tf_op jit(solution)/shard_map/ppermute | solution.py:469
  21.3 5.4 %collective-permute-start.3 = (bf16[272,256]{1,0:T(8,128)(2,1)}, bf16[272,256]{1,0:T(8,128)(2,1)}, u32[]{:S(2)}, u32[]{:S(2)}) collective-permute-start(bf16[272,256]{1,0:T(8,128)(2,1)} %get-tuple-element.28), channel_id=1, source_target_pairs={{0,8},{8,0},{16,24},{24,16},{32,40},{40,32},{48,56},{56,48},{64,72... | collective-permute-start | bytes 417800 | tf_op jit(solution)/shard_map/ppermute | solution.py:487
  27.8 146.4 %reduce-scatter.2.cloned.1.call-start = ((), (), s32[]{:S(2)}) async-start(), calls=%async_computation.2 | async-start | bytes 5898240 | tf_op jit(solution)/shard_map/reduce_scatter | solution.py:628
  29.6 22.4 %collective-permute-start.10 = (bf16[2048,256]{1,0:T(8,128)(2,1)}, bf16[2048,256]{1,0:T(8,128)(2,1)}, u32[]{:S(2)}, u32[]{:S(2)}) collective-permute-start(bf16[2048,256]{1,0:T(8,128)(2,1)} %pad_maximum_fusion.line), channel_id=1, source_target_pairs={{0,8},{8,0},{16,24},{24,16},{32,40},{40,32},{48,56},{56,48},{64,72... | collective-permute-start | bytes 3145736 | tf_op jit(solution)/shard_map/ppermute | solution.py:487
  29.9 7.4 %collective-permute-start.6 = (bf16[272,256]{1,0:T(8,128)(2,1)}, bf16[272,256]{1,0:T(8,128)(2,1)}, u32[]{:S(2)}, u32[]{:S(2)}) collective-permute-start(bf16[272,256]{1,0:T(8,128)(2,1)} %shard_map.109.mine_ref), channel_id=1, source_target_pairs={{0,32},{8,40},{16,48},{24,56},{32,0},{40,8},{48,16},{56,24},{64,96... | collective-permute-start | bytes 417800 | tf_op jit(solution)/shard_map/ppermute | solution.py:469
  31.7 7.8 %collective-permute-start.5 = (bf16[272,256]{1,0:T(8,128)(2,1)}, bf16[272,256]{1,0:T(8,128)(2,1)}, u32[]{:S(2)}, u32[]{:S(2)}) collective-permute-start(bf16[272,256]{1,0:T(8,128)(2,1)} %shard_map.109.mine_ref), channel_id=1, source_target_pairs={{0,48},{8,56},{16,0},{24,8},{32,16},{40,24},{48,32},{56,40},{64,11... | collective-permute-start | bytes 417800 | tf_op jit(solution)/shard_map/ppermute | solution.py:469
  32.7 7.1 %collective-permute-start.4 = (bf16[272,256]{1,0:T(8,128)(2,1)}, bf16[272,256]{1,0:T(8,128)(2,1)}, u32[]{:S(2)}, u32[]{:S(2)}) collective-permute-start(bf16[272,256]{1,0:T(8,128)(2,1)} %shard_map.109.mine_ref), channel_id=1, source_target_pairs={{0,16},{8,24},{16,32},{24,40},{32,48},{40,56},{48,0},{56,8},{64,80... | collective-permute-start | bytes 417800 | tf_op jit(solution)/shard_map/ppermute | solution.py:469
  41.8 14.4 %collective-permute-start.9 = (bf16[272,256]{1,0:T(8,128)(2,1)}, bf16[272,256]{1,0:T(8,128)(2,1)}, u32[]{:S(2)}, u32[]{:S(2)}) collective-permute-start(bf16[272,256]{1,0:T(8,128)(2,1)} %get-tuple-element.42), channel_id=1, source_target_pairs={{0,64},{8,72},{16,80},{24,88},{32,96},{40,104},{48,112},{56,120},{... | collective-permute-start | bytes 417800 | tf_op jit(solution)/shard_map/ppermute | solution.py:469
  45.6 10.7 %collective-permute-start.8 = (bf16[272,256]{1,0:T(8,128)(2,1)}, bf16[272,256]{1,0:T(8,128)(2,1)}, u32[]{:S(2)}, u32[]{:S(2)}) collective-permute-start(bf16[272,256]{1,0:T(8,128)(2,1)} %get-tuple-element.42), channel_id=1, source_target_pairs={{0,128},{8,136},{16,144},{24,152},{32,160},{40,168},{48,176},{56,1... | collective-permute-start | bytes 417800 | tf_op jit(solution)/shard_map/ppermute | solution.py:469
  50.0 7.0 %collective-permute-start.7 = (bf16[272,256]{1,0:T(8,128)(2,1)}, bf16[272,256]{1,0:T(8,128)(2,1)}, u32[]{:S(2)}, u32[]{:S(2)}) collective-permute-start(bf16[272,256]{1,0:T(8,128)(2,1)} %get-tuple-element.42), channel_id=1, source_target_pairs={{0,192},{8,200},{16,208},{24,216},{32,224},{40,232},{48,240},{56,2... | collective-permute-start | bytes 417800 | tf_op jit(solution)/shard_map/ppermute | solution.py:469
  59.1 2.7 %collective-permute-start.11 = (bf16[256,256]{1,0:T(8,128)(2,1)}, bf16[256,256]{1,0:T(8,128)(2,1)}, u32[]{:S(2)}, u32[]{:S(2)}) collective-permute-start(bf16[256,256]{1,0:T(8,128)(2,1)} %get-tuple-element.49), channel_id=1, source_target_pairs={{0,8},{8,0},{16,24},{24,16},{32,40},{40,32},{48,56},{56,48},{64,72... | collective-permute-start | bytes 393224 | tf_op jit(solution)/shard_map/ppermute | solution.py:487
  65.3 10.3 %collective-permute-start.12 = (bf16[8192,256]{1,0:T(8,128)(2,1)}, bf16[8192,256]{1,0:T(8,128)(2,1)}, u32[]{:S(2)}, u32[]{:S(2)}) collective-permute-start(bf16[8192,256]{1,0:T(8,128)(2,1)} %all-gather.2.cloned.1.call-done.fetched), channel_id=1, source_target_pairs={{0,8},{8,0},{16,24},{24,16},{32,40},{40,32},{48,56},{56,48},{64,72... | collective-permute-start | bytes 12582920 | tf_op jit(solution)/shard_map/ppermute | solution.py:487
Sparse Core Ops, SparseCore 0:
  27.9 35.9 all-gather.1
  89.4 84.8 reduce-scatter.1

commit v13 on v10

--- a/solution.py
+++ b/solution.py
@@ -576,17 +576,17 @@
     act = pl.pallas_call(
         gate_kernel,
         out_shape=jax.ShapeDtypeStruct((ROWS, HP), jnp.bfloat16),
-        grid=(2,),
+        grid=(4,),
         in_specs=[
             SMEM,
-            pl.BlockSpec((ROWS // 2, HP), lambda i: (i, 0)),
-            pl.BlockSpec((ROWS // 2, HP), lambda i: (i, 0)),
-            pl.BlockSpec((ROWS // 2, SN), lambda i: (i, 1)),
-            pl.BlockSpec((ROWS // 2, HEADS), lambda i: (i, 0)),
+            pl.BlockSpec((ROWS // 4, HP), lambda i: (i, 0)),
+            pl.BlockSpec((ROWS // 4, HP), lambda i: (i, 0)),
+            pl.BlockSpec((ROWS // 4, SN), lambda i: (i, 1)),
+            pl.BlockSpec((ROWS // 4, HEADS), lambda i: (i, 0)),
             pl.BlockSpec((SN, HALF), lambda i: (0, 0)),
             pl.BlockSpec((SN, HALF), lambda i: (0, 0)),
         ],
-        out_specs=pl.BlockSpec((ROWS // 2, HP), lambda i: (i, 0)),
+        out_specs=pl.BlockSpec((ROWS // 4, HP), lambda i: (i, 0)),
         compiler_params=big(),
         cost_estimate=pl.CostEstimate(flops=10**8, bytes_accessed=3 * 10**6, transcendentals=3 * 10**5),
         name="gate",

time: 183 us -> 184 us (level); the launches traced: 183 us -> 182 us
  waiting for transfers between devices: 100 us -> 97.3 us
    reduce_scatter x1, waiting for transfers between devices: 88.7 us -> 86 us  [local(): return lax.psum_scatter(terms, 'tp', scatter_dimension=0, tiled=True)]
  transfers between devices with their start and end apart: 15 -> 15, of which waited for: 7 -> 7; matrix products, arithmetic and copies ran while one was open for 0% -> 0% of each run, Pallas kernels for 15% -> 16%
where the time goes in v13:
time: 184 us; the launch traced here: 182 us
  waiting for transfers between devices  97.3 us (53%)
  Pallas kernels  41.9 us (23%)
  starting transfers between devices  27.8 us (15%)
  between operations  13.5 us (7%)
    reduce_scatter x1, waiting for transfers between devices, local(): return lax.psum_scatter(terms, 'tp', scatter_dimension=0, tiled=True)  86 us
    ppermute x9, starting transfers between devices, moved(): return lax.ppermute(block, 'pack', pairs)  21.4 us
    pallas_call x1, Pallas kernels, local(): pl.pallas_call(mix_kernel, out_shape=jax.ShapeDtypeStruct((ROWS, DM), jnp...  13.6 us
    pallas_call x3, Pallas kernels, attend(): pl.pallas_call(kernel, out_shape=shapes, in_specs=[SMEM] * 2 + [VMEM] * v...  11.8 us
    ppermute x4, waiting for transfers between devices, swapped(): return lax.ppermute(block, 'pack', [(i, i ^ 1) for i in range(32)])  7.6 us
    ppermute x4, starting transfers between devices, swapped(): return lax.ppermute(block, 'pack', [(i, i ^ 1) for i in range(32)])  6.36 us
    pallas_call x1, Pallas kernels, local(): pl.pallas_call(ssd_kernel, out_shape=(jax.ShapeDtypeStruct((ROWS, HP), jn...  6.22 us
    pallas_call x3, Pallas kernels, call(): pl.pallas_call(kernel, out_shape=tuple((jax.ShapeDtypeStruct(shape, jnp.b...  5.84 us
  transfers between devices with their start and end apart: 15, of which 7 were waited for; matrix products, arithmetic and copies ran while one was open for 0% of the time, Pallas kernels for 16%

profile of v13, /device:TPU:1, one launch (start us, length us, event | category | flops | bytes accessed | tf_op | source)
XLA Modules:
  0.0 181.6 jit_solution(13499184945490130865)
XLA Ops:
  6.5 5.6 %collective-permute-start.2 = (bf16[512,256]{1,0:T(8,128)(2,1)}, bf16[512,256]{1,0:T(8,128)(2,1)S(1)}, u32[]{:S(2)}, u32[]{:S(2)}) collective-permute-start(bf16[512,256]{1,0:T(8,128)(2,1)} %bitcast.3), channel_id=1, source_target_pairs={{0,32},{8,136},{16,48},{24,152},{32,0},{40,168},{48,16},{56,184},{... | collective-permute-start | bytes 786440 | tf_op jit(solution)/shard_map/ppermute | solution.py:469
  12.2 1.3 collective-permute-start.1
  13.5 1.6 collective-permute-start
  15.1 6.2 %ssd_local.1 = (f32[512,512]{1,0:T(8,128)}, bf16[272,256]{1,0:T(8,128)(2,1)}, bf16[272,256]{1,0:T(8,128)(2,1)}, f32[512,8]{1,0:T(8,128)}) custom-call(s32[4]{0:T(128)} %len_ref.9, f32[8]{0:T(128)} %dl_ref.1, f32[8]{0:T(128)} %skip_ref.1, s32[1]{0:T(128)} %bitcast.first_ref, bf16[512,512]{1,0:T(8,128)(2,1)} %x_ref.1, bf16[512,512]{1,0:T(8,128)(2,1)} %read_ref.1, ...), custom_call_target="tpu_custom_call" | custom-call | flops 1000000000 | bytes 4000000 | tf_op jit(solution)/shard_map/ssd_local/pallas_call | solution.py:520
  22.5 4.7 %collective-permute-start.10 = (bf16[2048,256]{1,0:T(8,128)(2,1)}, bf16[2048,256]{1,0:T(8,128)(2,1)}, u32[]{:S(2)}, u32[]{:S(2)}) collective-permute-start(bf16[2048,256]{1,0:T(8,128)(2,1)} %pad_maximum_fusion.line), channel_id=1, source_target_pairs={{0,8},{8,0},{16,24},{24,16},{32,40},{40,32},{48,56},{56,48},{64,72... | collective-permute-start | bytes 3145736 | tf_op jit(solution)/shard_map/ppermute | solution.py:487
  27.3 2.4 %collective-permute-done.3.other_ref = bf16[272,256]{1,0:T(8,128)(2,1)} collective-permute-done((bf16[272,256]{1,0:T(8,128)(2,1)S(1)}, bf16[272,256]{1,0:T(8,128)(2,1)}, u32[]{:S(2)}, u32[]{:S(2)}) %collective-permute-start.3) | collective-permute-done | bytes 139296 | tf_op jit(solution)/shard_map/ppermute | solution.py:487
  29.7 1.7 shard_map.109.mine_ref
  31.4 1.3 collective-permute-start.6
  34.1 4.1 %own_line.1 = (f32[1024,256]{1,0:T(8,128)}, bf16[1024,256]{1,0:T(8,128)(2,1)}) custom-call(s32[4]{0:T(128)} %len_ref.9, s32[1]{0:T(128)} %bitcast.first_ref, bf16[512,256]{1,0:T(8,128)(2,1)} %q_ref.1, bf16[2048,256]{1,0:T(8,128)(2,1)} %pad_maximum_fusion.line), custom_call_target="tpu_custom_call" | custom-call | flops 3000000000 | bytes 5000000 | tf_op jit(solution)/shard_map/own_line/pallas_call | solution.py:554
  38.2 2.0 %collective-permute-done.5.above_ref = bf16[272,256]{1,0:T(8,128)(2,1)} collective-permute-done((bf16[272,256]{1,0:T(8,128)(2,1)}, bf16[272,256]{1,0:T(8,128)(2,1)}, u32[]{:S(2)}, u32[]{:S(2)}) %collective-permute-start.5) | collective-permute-done | bytes 139296 | tf_op jit(solution)/shard_map/ppermute | solution.py:469
  40.2 1.1 collective-permute-done.4.below_ref
  41.3 2.1 %shard_map.110 = (bf16[272,256]{1,0:T(8,128)(2,1)}, bf16[272,256]{1,0:T(8,128)(2,1)}) custom-call(s32[1]{0:T(128)} %bitcast.first_ref, bf16[272,256]{1,0:T(8,128)(2,1)} %shard_map.109.mine_ref, bf16[272,256]{1,0:T(8,128)(2,1)} %collective-permute-done.4.below_ref, bf16[272,256]{1,0:T(8,128)(2,1)} %collective-permute-done.5.above_ref, ...), custom_call_target="tpu_custom_call" | custom-call | flops 1000000 | bytes 1000000 | tf_op jit(solution)/shard_map/pallas_call | solution.py:491
  43.4 3.8 %collective-permute-start.9 = (bf16[272,256]{1,0:T(8,128)(2,1)}, bf16[272,256]{1,0:T(8,128)(2,1)}, u32[]{:S(2)}, u32[]{:S(2)}) collective-permute-start(bf16[272,256]{1,0:T(8,128)(2,1)} %get-tuple-element.40), channel_id=1, source_target_pairs={{0,64},{8,72},{16,80},{24,88},{32,96},{40,104},{48,112},{56,120},{... | collective-permute-start | bytes 417800 | tf_op jit(solution)/shard_map/ppermute | solution.py:469
  47.1 4.4 %collective-permute-start.8 = (bf16[272,256]{1,0:T(8,128)(2,1)}, bf16[272,256]{1,0:T(8,128)(2,1)}, u32[]{:S(2)}, u32[]{:S(2)}) collective-permute-start(bf16[272,256]{1,0:T(8,128)(2,1)} %get-tuple-element.40), channel_id=1, source_target_pairs={{0,128},{8,136},{16,144},{24,152},{32,160},{40,168},{48,176},{56,1... | collective-permute-start | bytes 417800 | tf_op jit(solution)/shard_map/ppermute | solution.py:469
  51.5 2.0 %collective-permute-start.7 = (bf16[272,256]{1,0:T(8,128)(2,1)}, bf16[272,256]{1,0:T(8,128)(2,1)}, u32[]{:S(2)}, u32[]{:S(2)}) collective-permute-start(bf16[272,256]{1,0:T(8,128)(2,1)} %get-tuple-element.40), channel_id=1, source_target_pairs={{0,192},{8,200},{16,208},{24,216},{32,224},{40,232},{48,240},{56,2... | collective-permute-start | bytes 417800 | tf_op jit(solution)/shard_map/ppermute | solution.py:469
  53.5 4.5 %other_line.1.before_hbm = f32[1024,256]{1,0:T(8,128)} custom-call(s32[4]{0:T(128)} %len_ref.9, s32[1]{0:T(128)} %bitcast.first_ref, bf16[1024,256]{1,0:T(8,128)(2,1)} %get-tuple-element.34.split_ref.split_hbm, f32[1024,256]{1,0:T(8,128)} %get-tuple-element.36.before_ref, bf16[2048,256]{1,0:T(8,128)(2,1)} %collective-permute-done.10.line_got), custom_call_target="tpu_custom_call" | custom-call | flops 3000000000 | bytes 5000000 | tf_op jit(solution)/shard_map/other_line/pallas_call | solution.py:554
  58.6 2.1 %shard_map.111 = (bf16[256,256]{1,0:T(8,128)(2,1)}, bf16[256,256]{1,0:T(8,128)(2,1)}) custom-call(s32[1]{0:T(128)} %bitcast.first_ref, bf16[272,256]{1,0:T(8,128)(2,1)} %collective-permute-done.7.row3_ref, bf16[272,256]{1,0:T(8,128)(2,1)} %collective-permute-done.8.row2_ref, bf16[272,256]{1,0:T(8,128)(2,1)} %collective-permute-done.9.row1_ref, ...), custom_call_target="tpu_custom_call" | custom-call | flops 1000000 | bytes 1000000 | tf_op jit(solution)/shard_map/pallas_call | solution.py:491
  60.6 1.2 collective-permute-start.11
  61.9 1.3 collective-permute-done.11.got_ref
  63.2 4.4 %gate.1.act_hbm = bf16[512,512]{1,0:T(8,128)(2,1)} custom-call(s32[1]{0:T(128)} %bitcast.first_ref, f32[512,512]{1,0:T(8,128)} %get-tuple-element.35.y_ref, bf16[512,512]{1,0:T(8,128)(2,1)} %z_ref.1, bf16[512,512]{1,0:T(8,128)(2,1)} %read_ref.1, f32[512,8]{1,0:T(8,128)} %get-tuple-element.27.fac_ref, bf16[256,256]{1,0:T(8,128)(2,1)} %get-tuple-element.46.keep_ref, ...), custom_call_target="tpu_custom_call" | custom-call | flops 100000000 | bytes 3000000 | tf_op jit(solution)/shard_map/gate/pallas_call | solution.py:576
  68.0 3.2 %part.1.before_hbm = f32[1024,256]{1,0:T(8,128)} custom-call(s32[4]{0:T(128)} %len_ref.9, s32[1]{0:T(128)} %bitcast.first_ref, bf16[1024,256]{1,0:T(8,128)(2,1)} %get-tuple-element.34.split_ref.split_hbm, f32[1024,256]{1,0:T(8,128)} %other_line.1.before_hbm, bf16[8192,256]{1,0:T(8,128)(2,1)} %all-gather.2.cloned.1.call-done.fetched), custom_call_target="tpu_custom_call" | custom-call | flops 3000000000 | bytes 5000000 | tf_op jit(solution)/shard_map/part/pallas_call | solution.py:554
  71.2 3.9 %collective-permute-done.12.other = bf16[8192,256]{1,0:T(8,128)(2,1)} collective-permute-done((bf16[8192,256]{1,0:T(8,128)(2,1)}, bf16[8192,256]{1,0:T(8,128)(2,1)}, u32[]{:S(2)}, u32[]{:S(2)}) %collective-permute-start.12) | collective-permute-done | bytes 4194336 | tf_op jit(solution)/shard_map/ppermute | solution.py:487
  75.1 13.6 %mix.1 = bf16[512,5120]{1,0:T(8,128)(2,1)} custom-call(s32[4]{0:T(128)} %len_ref.9, s32[1]{0:T(128)} %bitcast.first_ref, bf16[1024,256]{1,0:T(8,128)(2,1)} %get-tuple-element.34.split_ref.split_hbm, bf16[512,512]{1,0:T(8,128)(2,1)} %gate.1.act_hbm, f32[1024,256]{1,0:T(8,128)} %part.1.before_hbm, bf16[8192,256]{1,0:T(8,128)(2,1)} %all-gather.2.cloned.1.call-done.fetched, ...), custom_call_target="tpu_custom_call" | custom-call | flops 8999999488 | bytes 25000000 | tf_op jit(solution)/shard_map/mix/pallas_call | solution.py:608
  88.7 86.0 %reduce-scatter.2.cloned.1.call-done = bf16[64,5120]{1,0:T(8,128)(2,1)} async-done(((bf16[512,5120]{1,0:T(8,128)(2,1)}), bf16[64,5120]{1,0:T(8,128)(2,1)}) %reduce-scatter.2.cloned.1.call-update) | async-done | bytes 655376 | tf_op jit(solution)/shard_map/reduce_scatter | solution.py:629
  (22 shorter events, 3.8 us)
Async XLA Ops:
  6.5 14.8 %copy-start = (bf16[512,1,256]{2,0,1:T(8,128)(2,1)S(1)}, bf16[512,1,256]{2,0,1:T(8,128)(2,1)}, u32[]{:S(2)}) copy-start(bf16[512,1,256]{2,0,1:T(8,128)(2,1)} %param.12) | copy-start | bytes 786436
  6.5 61.0 %all-gather.2.cloned.1.call-start = ((), (), s32[]{:S(2)}) async-start(), calls=%async_computation.1 | async-start | bytes 5242880 | tf_op jit(solution)/shard_map/all_gather | solution.py:537
  6.5 14.8 %collective-permute-start.2 = (bf16[512,256]{1,0:T(8,128)(2,1)}, bf16[512,256]{1,0:T(8,128)(2,1)S(1)}, u32[]{:S(2)}, u32[]{:S(2)}) collective-permute-start(bf16[512,256]{1,0:T(8,128)(2,1)} %bitcast.3), channel_id=1, source_target_pairs={{0,32},{8,136},{16,48},{24,152},{32,0},{40,168},{48,16},{56,184},{... | collective-permute-start | bytes 786440 | tf_op jit(solution)/shard_map/ppermute | solution.py:469
  12.2 9.2 %collective-permute-start.1 = (bf16[512,256]{1,0:T(8,128)(2,1)}, bf16[512,256]{1,0:T(8,128)(2,1)S(1)}, u32[]{:S(2)}, u32[]{:S(2)}) collective-permute-start(bf16[512,256]{1,0:T(8,128)(2,1)} %bitcast.4), channel_id=1, source_target_pairs={{0,48},{8,200},{16,0},{24,216},{32,16},{40,232},{48,32},{56,248},{... | collective-permute-start | bytes 786440 | tf_op jit(solution)/shard_map/ppermute | solution.py:469
  13.5 7.9 %collective-permute-start = (bf16[512,256]{1,0:T(8,128)(2,1)}, bf16[512,256]{1,0:T(8,128)(2,1)S(1)}, u32[]{:S(2)}, u32[]{:S(2)}) collective-permute-start(bf16[512,256]{1,0:T(8,128)(2,1)} %bitcast.5), channel_id=1, source_target_pairs={{0,16},{8,72},{16,32},{24,88},{32,48},{40,104},{48,0},{56,120},{64... | collective-permute-start | bytes 786440 | tf_op jit(solution)/shard_map/ppermute | solution.py:469
  21.3 5.9 %copy-start.1 = (bf16[272,256]{1,0:T(8,128)(2,1)S(1)}, bf16[272,256]{1,0:T(8,128)(2,1)}, u32[]{:S(2)}) copy-start(bf16[272,256]{1,0:T(8,128)(2,1)} %get-tuple-element.32) | copy-start | bytes 417796
  22.4 152.3 %reduce-scatter.2.cloned.1.call-start = ((), (), s32[]{:S(2)}) async-start(), calls=%async_computation.2 | async-start | bytes 5898240 | tf_op jit(solution)/shard_map/reduce_scatter | solution.py:629
  22.5 31.0 %collective-permute-start.10 = (bf16[2048,256]{1,0:T(8,128)(2,1)}, bf16[2048,256]{1,0:T(8,128)(2,1)}, u32[]{:S(2)}, u32[]{:S(2)}) collective-permute-start(bf16[2048,256]{1,0:T(8,128)(2,1)} %pad_maximum_fusion.line), channel_id=1, source_target_pairs={{0,8},{8,0},{16,24},{24,16},{32,40},{40,32},{48,56},{56,48},{64,72... | collective-permute-start | bytes 3145736 | tf_op jit(solution)/shard_map/ppermute | solution.py:487
  27.2 2.5 %collective-permute-start.3 = (bf16[272,256]{1,0:T(8,128)(2,1)S(1)}, bf16[272,256]{1,0:T(8,128)(2,1)}, u32[]{:S(2)}, u32[]{:S(2)}) collective-permute-start(bf16[272,256]{1,0:T(8,128)(2,1)S(1)} %copy-done.1), channel_id=1, source_target_pairs={{0,8},{8,0},{16,24},{24,16},{32,40},{40,32},{48,56},{56,48},{64,72... | collective-permute-start | bytes 417800 | tf_op jit(solution)/shard_map/ppermute | solution.py:487
  31.4 6.9 %collective-permute-start.6 = (bf16[272,256]{1,0:T(8,128)(2,1)}, bf16[272,256]{1,0:T(8,128)(2,1)}, u32[]{:S(2)}, u32[]{:S(2)}) collective-permute-start(bf16[272,256]{1,0:T(8,128)(2,1)} %shard_map.109.mine_ref), channel_id=1, source_target_pairs={{0,32},{8,40},{16,48},{24,56},{32,0},{40,8},{48,16},{56,24},{64,96... | collective-permute-start | bytes 417800 | tf_op jit(solution)/shard_map/ppermute | solution.py:469
  32.6 7.6 %collective-permute-start.5 = (bf16[272,256]{1,0:T(8,128)(2,1)}, bf16[272,256]{1,0:T(8,128)(2,1)}, u32[]{:S(2)}, u32[]{:S(2)}) collective-permute-start(bf16[272,256]{1,0:T(8,128)(2,1)} %shard_map.109.mine_ref), channel_id=1, source_target_pairs={{0,48},{8,56},{16,0},{24,8},{32,16},{40,24},{48,32},{56,40},{64,11... | collective-permute-start | bytes 417800 | tf_op jit(solution)/shard_map/ppermute | solution.py:469
  33.6 7.7 %collective-permute-start.4 = (bf16[272,256]{1,0:T(8,128)(2,1)}, bf16[272,256]{1,0:T(8,128)(2,1)}, u32[]{:S(2)}, u32[]{:S(2)}) collective-permute-start(bf16[272,256]{1,0:T(8,128)(2,1)} %shard_map.109.mine_ref), channel_id=1, source_target_pairs={{0,16},{8,24},{16,32},{24,40},{32,48},{40,56},{48,0},{56,8},{64,80... | collective-permute-start | bytes 417800 | tf_op jit(solution)/shard_map/ppermute | solution.py:469
  43.4 14.6 %collective-permute-start.9 = (bf16[272,256]{1,0:T(8,128)(2,1)}, bf16[272,256]{1,0:T(8,128)(2,1)}, u32[]{:S(2)}, u32[]{:S(2)}) collective-permute-start(bf16[272,256]{1,0:T(8,128)(2,1)} %get-tuple-element.40), channel_id=1, source_target_pairs={{0,64},{8,72},{16,80},{24,88},{32,96},{40,104},{48,112},{56,120},{... | collective-permute-start | bytes 417800 | tf_op jit(solution)/shard_map/ppermute | solution.py:469
  47.1 10.8 %collective-permute-start.8 = (bf16[272,256]{1,0:T(8,128)(2,1)}, bf16[272,256]{1,0:T(8,128)(2,1)}, u32[]{:S(2)}, u32[]{:S(2)}) collective-permute-start(bf16[272,256]{1,0:T(8,128)(2,1)} %get-tuple-element.40), channel_id=1, source_target_pairs={{0,128},{8,136},{16,144},{24,152},{32,160},{40,168},{48,176},{56,1... | collective-permute-start | bytes 417800 | tf_op jit(solution)/shard_map/ppermute | solution.py:469
  51.5 7.1 %collective-permute-start.7 = (bf16[272,256]{1,0:T(8,128)(2,1)}, bf16[272,256]{1,0:T(8,128)(2,1)}, u32[]{:S(2)}, u32[]{:S(2)}) collective-permute-start(bf16[272,256]{1,0:T(8,128)(2,1)} %get-tuple-element.40), channel_id=1, source_target_pairs={{0,192},{8,200},{16,208},{24,216},{32,224},{40,232},{48,240},{56,2... | collective-permute-start | bytes 417800 | tf_op jit(solution)/shard_map/ppermute | solution.py:469
  60.6 2.5 %collective-permute-start.11 = (bf16[256,256]{1,0:T(8,128)(2,1)}, bf16[256,256]{1,0:T(8,128)(2,1)}, u32[]{:S(2)}, u32[]{:S(2)}) collective-permute-start(bf16[256,256]{1,0:T(8,128)(2,1)} %get-tuple-element.47), channel_id=1, source_target_pairs={{0,8},{8,0},{16,24},{24,16},{32,40},{40,32},{48,56},{56,48},{64,72... | collective-permute-start | bytes 393224 | tf_op jit(solution)/shard_map/ppermute | solution.py:487
  67.6 7.5 %collective-permute-start.12 = (bf16[8192,256]{1,0:T(8,128)(2,1)}, bf16[8192,256]{1,0:T(8,128)(2,1)}, u32[]{:S(2)}, u32[]{:S(2)}) collective-permute-start(bf16[8192,256]{1,0:T(8,128)(2,1)} %all-gather.2.cloned.1.call-done.fetched), channel_id=1, source_target_pairs={{0,8},{8,0},{16,24},{24,16},{32,40},{40,32},{48,56},{56,48},{64,72... | collective-permute-start | bytes 12582920 | tf_op jit(solution)/shard_map/ppermute | solution.py:487
Sparse Core Ops, SparseCore 0:
  22.6 39.6 all-gather.1
  88.8 85.8 reduce-scatter.1
